TPU v7x, 32 devices: a whole 2x2x4 slice. The times are simulated.
32 devices in a mesh: dp: 8 (over z, y), seq: 4 (over x, core).
Axes of the slice: x: 2, y: 2, z: 4, core: 2. Of those that a mesh axis runs over, the one named last changes fastest.
Arguments:
- queries: bfloat16 [4096, 2560], P(('dp', 'seq')), may hold values from -400 to 400
- key_states: bfloat16 [4096, 2560], P(('dp', 'seq')), may hold values from -400 to 400
- value_states: bfloat16 [4096, 2560], P(('dp', 'seq')), may hold values from -6 to 6
- query_tangent: bfloat16 [4096, 2560], P(('dp', 'seq')), may hold values from -6 to 6
- key_tangent: bfloat16 [4096, 2560], P(('dp', 'seq')), may hold values from -6 to 6
- value_tangent: bfloat16 [4096, 2560], P(('dp', 'seq')), may hold values from -6 to 6
- query_gain: float32 [2560], replicated, may hold values from 0.25 to 1.75
- key_gain: float32 [2560], replicated, may hold values from 0.25 to 1.75
- out_weight: bfloat16 [2560, 5120], P('seq', 'dp'), may hold values from -0.125 to 0.125
Outputs:
- projected: bfloat16 [4096, 5120], P(('dp', 'seq'))
- projected_tangent: bfloat16 [4096, 5120], P(('dp', 'seq'))
All inputs are finite; a program needn't handle non-finite values.
Results may differ from a plain program's by a relative error of at most 0.012.
The roundings to bfloat16 on the way count: a program that leaves them out, or rounds other values in their place, can miss the bound.
Values may be sent and summed in bfloat16 or wider, within the bound.
No kernel may reach another device: no remote copies, remote signals or barrier semaphores. Data moves between devices by JAX's collectives and lax.ppermute only.
A program may use at most 128 MiB of HBM per device.

v0:
```python
import functools

import jax
import jax.numpy as jnp
from jax import lax
from jax.experimental import pallas as pl
from jax.experimental.pallas import tpu as pltpu
from jax.sharding import PartitionSpec as P

HEADS = 20
EPS = 1e-06
VMEM_BYTES = 48 * 1024 * 1024
ROW_STEP = 32

LOW = jnp.bfloat16
WIDE = jnp.float32


def params():
    return pltpu.CompilerParams(vmem_limit_bytes=VMEM_BYTES)


def vmem_specs(count):
    return [pl.BlockSpec(memory_space=pltpu.VMEM)] * count


def pack_kernel(n_seq, chunks, core_ref, *refs):
    query_ref, key_ref, value_ref, dquery_ref, dkey_ref, dvalue_ref, query_gain_ref, key_gain_ref = refs[:8]
    out_refs = refs[8:]
    n_chunks = len(chunks)
    group = query_ref.shape[-1] // n_seq

    def statistics(primal_ref, tangent_ref):
        primal = primal_ref[...].astype(WIDE)
        tangent = tangent_ref[...].astype(WIDE)
        inverse = lax.rsqrt(jnp.mean(primal * primal, axis=-1, keepdims=True) + EPS)
        across = jnp.mean(primal * tangent, axis=-1, keepdims=True)
        return inverse, inverse * inverse * inverse * across

    query_stats = statistics(query_ref, dquery_ref)
    key_stats = statistics(key_ref, dkey_ref)

    def normed(primal_ref, tangent_ref, gain_ref, stats, lanes):
        primal = primal_ref[:, lanes].astype(WIDE)
        tangent = tangent_ref[:, lanes].astype(WIDE)
        gain = gain_ref[:, lanes]
        inverse, slope = stats
        return (primal * inverse * gain).astype(LOW), (gain * (tangent * inverse - primal * slope)).astype(LOW)

    for side in range(2):
        core = core_ref[0] if side == 0 else 1 - core_ref[0]
        queries_ref, *keyed_refs = out_refs[side * (1 + n_chunks) : (side + 1) * (1 + n_chunks)]
        for at in range(n_seq // 2):
            lanes = pl.ds(pl.multiple_of((2 * at + core) * group, 128), group)
            here = slice(at * group, (at + 1) * group)
            plain, dual = normed(query_ref, dquery_ref, query_gain_ref, query_stats, lanes)
            queries_ref[0, :, here] = plain
            queries_ref[1, :, here] = dual
            four = normed(key_ref, dkey_ref, key_gain_ref, key_stats, lanes)
            four += (value_ref[:, lanes], dvalue_ref[:, lanes])
            start = 0
            for keyed_ref, width in zip(keyed_refs, chunks):
                low, high = max(start, here.start), min(start + width, here.stop)
                if low < high:
                    for which, part in enumerate(four):
                        keyed_ref[which, :, low - start : high - start] = part[:, low - here.start : high - here.start]
                start += width


def pack(core, n_seq, chunks, arrays, gains):
    rows, features = arrays[0].shape
    step = min(rows, ROW_STEP)
    row_block = pl.BlockSpec((step, features), lambda i, c: (i, 0))
    gain_block = pl.BlockSpec((1, features), lambda i, c: (0, 0))
    kinds = [(2, features // 2)] + [(4, width) for width in chunks]
    kinds = kinds + kinds
    return pl.pallas_call(
        functools.partial(pack_kernel, n_seq, chunks),
        grid_spec=pltpu.PrefetchScalarGridSpec(
            num_scalar_prefetch=1,
            grid=(rows // step,),
            in_specs=[row_block] * 6 + [gain_block] * 2,
            out_specs=[pl.BlockSpec((count, step, width), lambda i, c: (0, i, 0)) for count, width in kinds],
        ),
        out_shape=[jax.ShapeDtypeStruct((count, rows, width), LOW) for count, width in kinds],
        compiler_params=params(),
    )(core, *arrays, *[gain.reshape(1, features) for gain in gains])


def attend_kernel(n_queries, *refs):
    query_refs, keyed_refs, out_ref = refs[:n_queries], refs[n_queries:-1], refs[-1]

    def stack(which, some_refs):
        return jnp.concatenate([ref[which] for ref in some_refs], axis=0)

    query, query_dual = (stack(which, query_refs) for which in range(2))
    key, key_dual, value, value_dual = (stack(which, keyed_refs) for which in range(4))
    factor = query.shape[-1] ** (-0.5)
    last = (((1,), (1,)), ((), ()))
    scores = lax.dot_general(query, key, last, preferred_element_type=WIDE) * factor
    dual_scores = (
        lax.dot_general(
            jnp.concatenate([query_dual, query], axis=1),
            jnp.concatenate([key, key_dual], axis=1),
            last,
            preferred_element_type=WIDE,
        )
        * factor
    )
    raised = jnp.exp(scores - jnp.max(scores, axis=-1, keepdims=True))
    probs = raised * (1.0 / jnp.sum(raised, axis=-1, keepdims=True))
    spread = probs * (dual_scores - jnp.sum(probs * dual_scores, axis=-1, keepdims=True))
    probs_low = probs.astype(LOW)
    spread_low = spread.astype(LOW)
    out_ref[0] = jnp.dot(probs_low, value, preferred_element_type=WIDE).astype(LOW)
    out_ref[1] = (
        jnp.dot(probs_low, value_dual, preferred_element_type=WIDE)
        + jnp.dot(spread_low, value, preferred_element_type=WIDE)
    ).astype(LOW)


def attend(start, hdim, queries, keyed):
    rows = queries[0].shape[1]
    width = keyed[0].shape[2]
    first = start // hdim
    return pl.pallas_call(
        functools.partial(attend_kernel, len(queries)),
        grid=(width // hdim,),
        in_specs=[pl.BlockSpec((2, rows, hdim), lambda h: (0, 0, first + h))] * len(queries)
        + [pl.BlockSpec((4, rows, hdim), lambda h: (0, 0, h))] * len(keyed),
        out_specs=pl.BlockSpec((2, len(queries) * rows, hdim), lambda h: (0, 0, h)),
        out_shape=jax.ShapeDtypeStruct((2, len(queries) * rows, width), LOW),
        compiler_params=params(),
    )(*queries, *keyed)


def assemble_kernel(chunks, flip_ref, *refs):
    part_refs, out_ref = refs[:-1], refs[-1]
    groups, rows_all, group = out_ref.shape
    rows = rows_all // 8
    start = 0
    for at, width in enumerate(chunks):
        for side in range(2):
            part_ref = part_refs[2 * at + side]
            for kind in range(2):
                for core in range(2):
                    first = (4 * core + 2 * side + kind) * rows
                    for g in range(groups):
                        low, high = max(start, g * group), min(start + width, (g + 1) * group)
                        if low < high:
                            out_ref[g ^ flip_ref[0], first : first + rows, low - g * group : high - g * group] = (
                                part_ref[kind, core * rows : (core + 1) * rows, low - start : high - start]
                            )
        start += width


def assemble(flip, groups, chunks, pairs):
    rows = 4 * pairs[0][0].shape[1]
    return pl.pallas_call(
        functools.partial(assemble_kernel, chunks),
        in_specs=[pl.BlockSpec(memory_space=pltpu.SMEM)] + vmem_specs(2 * len(pairs)),
        out_specs=vmem_specs(1)[0],
        out_shape=jax.ShapeDtypeStruct((groups, rows, sum(chunks) // groups), LOW),
        compiler_params=params(),
    )(flip, *[part for pair in pairs for part in pair])


def project_kernel(acts_ref, *refs):
    weight_refs, (keep_ref, send_ref) = refs[:-2], refs[-2:]
    rows = keep_ref.shape[0]
    beside = jnp.concatenate([ref[...] for ref in weight_refs[1:]], axis=0)
    total = jnp.dot(acts_ref[0], weight_refs[0][...], preferred_element_type=WIDE)
    total = total + jnp.dot(acts_ref[1], beside, preferred_element_type=WIDE)
    keep_ref[...] = total[:rows]
    send_ref[...] = total[rows:].astype(LOW)


def project(acts, weights):
    rows, n = acts.shape[1] // 2, weights[0].shape[1]
    return pl.pallas_call(
        project_kernel,
        in_specs=vmem_specs(1 + len(weights)),
        out_specs=vmem_specs(2),
        out_shape=[jax.ShapeDtypeStruct((rows, n), WIDE), jax.ShapeDtypeStruct((rows, n), LOW)],
        compiler_params=params(),
    )(acts, *weights)


def close_kernel(keep_ref, got_ref, mine_ref, other_ref):
    total = (keep_ref[...] + got_ref[...].astype(WIDE)).astype(LOW)
    half = total.shape[0] // 2
    mine_ref[...] = total[:half].reshape(mine_ref.shape)
    other_ref[...] = total[half:].reshape(other_ref.shape)


def close(keep, got):
    rows, n = keep.shape
    out = jax.ShapeDtypeStruct((2, rows // 4, n), LOW)
    return pl.pallas_call(
        close_kernel,
        in_specs=vmem_specs(2),
        out_specs=vmem_specs(2),
        out_shape=[out, out],
        compiler_params=params(),
    )(keep, got)


def place_kernel(n_pieces, where_ref, *refs):
    piece_refs = refs[:n_pieces]
    plain_ref, dual_ref = refs[n_pieces:]
    n = piece_refs[0].shape[-1]
    for at, piece_ref in enumerate(piece_refs):
        columns = pl.ds(pl.multiple_of(where_ref[at] * n, n), n)
        plain_ref[:, columns] = piece_ref[0]
        dual_ref[:, columns] = piece_ref[1]


def place(where, pieces):
    kinds, rows, n = pieces[0].shape
    width = n * len(pieces)
    if n % 128:
        out = jnp.zeros((kinds, rows, width), LOW)
        for at, piece in enumerate(pieces):
            out = lax.dynamic_update_slice(out, piece, (0, 0, where[at] * n))
        return out[0], out[1]
    out = jax.ShapeDtypeStruct((rows, width), LOW)
    return pl.pallas_call(
        functools.partial(place_kernel, len(pieces)),
        in_specs=[pl.BlockSpec(memory_space=pltpu.SMEM)] + vmem_specs(len(pieces)),
        out_specs=vmem_specs(2),
        out_shape=[out, out],
        compiler_params=params(),
    )(where, *pieces)


def body(
    n_dp,
    n_seq,
    queries,
    key_states,
    value_states,
    query_tangent,
    key_tangent,
    value_tangent,
    query_gain,
    key_gain,
    out_weight,
):
    dp = lax.axis_index("dp")
    seq = lax.axis_index("seq")
    n_ring = n_dp // 2
    groups = n_seq // 2
    features = queries.shape[1]
    hdim = features // HEADS
    group_heads = HEADS // n_seq
    few = group_heads * 2 // 5
    chunks = [group_heads * hdim] * (groups - 1) + [(group_heads - few) * hdim, few * hdim]
    starts = [sum(chunks[:at]) for at in range(len(chunks))]
    token = jnp.zeros((1,), jnp.int32)

    def far(array):
        return lax.ppermute(array, "seq", [(i, i ^ 2) for i in range(n_seq)])

    def near(array):
        return lax.ppermute(array, "seq", [(i, i ^ 1) for i in range(n_seq)])

    def across(array):
        return lax.ppermute(array, "dp", [(i, i ^ 1) for i in range(n_dp)])

    def onward(array):
        return lax.ppermute(array, "dp", [(i, (i + 2) % n_dp) for i in range(n_dp)])

    def wait(array):
        nonlocal token
        array, token = lax.optimization_barrier((array, token))
        return array

    def turn(ring, step):
        ring[step] = wait(ring[step])
        if step + 1 < n_ring:
            ring.append(onward(ring[step]))

    depth = out_weight.shape[0]
    cuts = [depth * 3 // 10 // 16 * 16, depth * 6 // 10 // 16 * 16]
    rings = [out_weight, onward(out_weight)]
    early = [far(out_weight[: cuts[0]])]

    core = jnp.stack([seq % 2])
    arrays = (queries, key_states, value_states, query_tangent, key_tangent, value_tangent)
    packs = [wait(array) for array in pack(core, n_seq, chunks, arrays, (query_gain, key_gain))]
    half = len(packs) // 2
    query_own, *keyed_own = packs[:half]
    query_other, *keyed_other = packs[half:]
    keyed_near = [wait(near(keyed_other[0]))]
    turn(early, 0)
    keyed_near += [wait(near(array)) for array in keyed_other[1:]]
    queries_both = [query_own, wait(near(query_other))]
    keyed_far = [[far(own), far(other)] for own, other in zip(keyed_own, keyed_near)]
    late = [far(out_weight[cuts[0] : cuts[1]])]
    rest = [far(out_weight[cuts[1] :])]

    acts, swapped = [], []

    def attention(chunk):
        keyed = [keyed_own[chunk], keyed_near[chunk], *keyed_far[chunk]]
        acts.append(wait(attend(starts[chunk], hdim, queries_both, keyed)))
        swapped.append(across(acts[-1]))

    def keyed_wait(chunk, at):
        keyed_far[chunk][at] = wait(keyed_far[chunk][at])

    turn(rings, 1)
    keyed_wait(0, 0)
    turn(early, 1)
    keyed_wait(0, 1)
    turn(rings, 2)
    keyed_wait(1, 0)
    attention(0)
    turn(early, 2)
    keyed_wait(1, 1)
    keyed_wait(2, 0)
    attention(1)
    keyed_wait(2, 1)
    swapped[0] = wait(swapped[0])
    for step in range(3, n_ring):
        turn(rings, step)
        turn(early, step)
    attention(2)
    rest.append(far(rings[1][cuts[1] :]))
    turn(late, 0)
    swapped[1] = wait(swapped[1])
    rest[0] = wait(rest[0])
    swapped[2] = wait(swapped[2])
    acts = assemble(jnp.stack([seq // 2]), groups, chunks, list(zip(acts, swapped)))

    keeps, sends, mine, other = [], [], [], []

    def columns(step):
        blocks = [rings[step], early[step], late[step], rest[step]]
        keep, send = project(acts, blocks)
        keeps.append(keep)
        sends.append(near(wait(send)))

    def finish(step):
        own, out = close(keeps[step], wait(sends[step]))
        mine.append(own)
        other.append(across(wait(out)))

    for step in range(1, n_ring):
        turn(late, step)
        columns(step - 1)
        if step + 1 < n_ring:
            rest.append(far(rings[step + 1][cuts[1] :]))
        rest[step] = wait(rest[step])
        finish(step - 1)
        if step > 1:
            other[step - 2] = wait(other[step - 2])
    columns(n_ring - 1)
    finish(n_ring - 1)

    pieces, where = [], []
    for step in range(n_ring):
        pair = (dp // 2 - step) % n_ring
        pieces += [mine[step], other[step]]
        where += [2 * pair + dp % 2, 2 * pair + 1 - dp % 2]
    return place(jnp.stack(where).astype(jnp.int32) + token, pieces)


def solution(mesh):
    rows = P(("dp", "seq"), None)
    return jax.shard_map(
        functools.partial(body, mesh.shape["dp"], mesh.shape["seq"]),
        mesh=mesh,
        in_specs=(rows,) * 6 + (P(), P(), P("seq", "dp")),
        out_specs=(rows, rows),
        check_vma=False,
    )
```

profile of v0, /device:TPU:0, one launch (start us, length us, event | category | flops | bytes accessed | tf_op | source)
XLA Modules:
  0.0 179.7 jit_solution(1685967297884489930)
XLA Ops:
  5.3 3.8 %shard_map.104 = (bf16[2,128,1280]{2,1,0:T(8,128)(2,1)S(1)}, bf16[4,128,640]{2,1,0:T(8,128)(2,1)S(1)}, bf16[4,128,384]{2,1,0:T(8,128)(2,1)S(1)}, bf16[4,128,256]...) custom-call(s32[1]{0:T(128)} %bitcast.9.core_ref, ...), custom_call_target="tpu_custom_call" | custom-call | tf_op jit(solution)/shard_map/pallas_call | solution.py:77
  9.7 2.6 %collective-permute-start.6 = (bf16[640,640]{1,0:T(8,128)(2,1)S(1)}, bf16[640,640]{1,0:T(8,128)(2,1)S(1)}, u32[]{:S(2)}, u32[]{:S(2)}) collective-permute-start(bf16[640,640]{1,0:T(8,128)(2,1)S(1)} %copy-done), channel_id=1, source_target_pairs={{0,8},{4,12},{8,16},{12,20},{16,24},{20,28},{24,0},{28,4},{1,9},{5... | collective-permute-start | bytes 2457608 | tf_op jit(solution)/shard_map/ppermute | solution.py:271
  13.0 1.6 collective-permute-start.3
  14.6 6.7 %collective-permute-done.3.refs_1_ = bf16[192,640]{1,0:T(8,128)(2,1)S(1)} collective-permute-done((bf16[192,640]{1,0:T(8,128)(2,1)S(1)}, bf16[192,640]{1,0:T(8,128)(2,1)S(1)}, u32[]{:S(2)}, u32[]{:S(2)}) %collective-permute-start.3) | collective-permute-done | bytes 245792 | tf_op jit(solution)/shard_map/ppermute | solution.py:262
  21.3 11.8 %collective-permute-done.6.refs_0_ = bf16[640,640]{1,0:T(8,128)(2,1)S(1)} collective-permute-done((bf16[640,640]{1,0:T(8,128)(2,1)S(1)}, bf16[640,640]{1,0:T(8,128)(2,1)S(1)}, u32[]{:S(2)}, u32[]{:S(2)}) %collective-permute-start.6) | collective-permute-done | bytes 819232 | tf_op jit(solution)/shard_map/ppermute | solution.py:271
  38.0 12.8 %collective-permute-done.5.refs_4_ = bf16[4,128,640]{2,1,0:T(8,128)(2,1)S(1)} collective-permute-done((bf16[4,128,640]{2,1,0:T(8,128)(2,1)S(1)}, bf16[4,128,640]{2,1,0:T(8,128)(2,1)S(1)}, u32[]{:S(2)}, u32[]{:S(2)}) %collective-permute-start.5) | collective-permute-done | bytes 655392 | tf_op jit(solution)/shard_map/ppermute | solution.py:262
  50.8 9.5 %collective-permute-done.8.refs_1_ = bf16[192,640]{1,0:T(8,128)(2,1)S(1)} collective-permute-done((bf16[192,640]{1,0:T(8,128)(2,1)S(1)}, bf16[192,640]{1,0:T(8,128)(2,1)S(1)}, u32[]{:S(2)}, u32[]{:S(2)}) %collective-permute-start.8) | collective-permute-done | bytes 245792 | tf_op jit(solution)/shard_map/ppermute | solution.py:271
  60.3 4.6 %collective-permute-done.7.refs_5_ = bf16[4,128,640]{2,1,0:T(8,128)(2,1)S(1)} collective-permute-done((bf16[4,128,640]{2,1,0:T(8,128)(2,1)S(1)}, bf16[4,128,640]{2,1,0:T(8,128)(2,1)S(1)}, u32[]{:S(2)}, u32[]{:S(2)}) %collective-permute-start.7) | collective-permute-done | bytes 655392 | tf_op jit(solution)/shard_map/ppermute | solution.py:262
  66.2 4.7 %shard_map.105.refs_0_ = bf16[2,256,640]{2,1,0:T(8,128)(2,1)S(1)} custom-call(bf16[2,128,1280]{2,1,0:T(8,128)(2,1)S(1)} %get-tuple-element.133.refs_0_, bf16[2,128,1280]{2,1,0:T(8,128)(2,1)S(1)} %collective-permute-done.refs_1_, bf16[4,128,640]{2,1,0:T(8,128)(2,1)S(1)} %get-tuple-element.158.refs_2_, ...), custom_call_target="tpu_custom_call" | custom-call | tf_op jit(solution)/shard_map/pallas_call | solution.py:126
  76.5 13.4 %collective-permute-done.14.refs_1_ = bf16[192,640]{1,0:T(8,128)(2,1)S(1)} collective-permute-done((bf16[192,640]{1,0:T(8,128)(2,1)S(1)}, bf16[192,640]{1,0:T(8,128)(2,1)S(1)}, u32[]{:S(2)}, u32[]{:S(2)}) %collective-permute-start.14) | collective-permute-done | bytes 245792 | tf_op jit(solution)/shard_map/ppermute | solution.py:271
  91.1 2.7 %collective-permute-start.18 = (bf16[192,640]{1,0:T(8,128)(2,1)S(1)}, bf16[192,640]{1,0:T(8,128)(2,1)S(1)}, u32[]{:S(2)}, u32[]{:S(2)}) collective-permute-start(bf16[192,640]{1,0:T(8,128)(2,1)S(1)} %collective-permute-done.14.refs_1_), channel_id=1, source_target_pairs={{0,8},{4,12},{8,16},{12,20},{16,24},{20,28},{24,0},{28,4},{1,9},{5... | collective-permute-start | bytes 737288 | tf_op jit(solution)/shard_map/ppermute | solution.py:271
  95.3 2.8 %shard_map.106.refs_2_ = bf16[2,256,384]{2,1,0:T(8,128)(2,1)S(1)} custom-call(bf16[2,128,1280]{2,1,0:T(8,128)(2,1)S(1)} %get-tuple-element.133.refs_0_, bf16[2,128,1280]{2,1,0:T(8,128)(2,1)S(1)} %collective-permute-done.refs_1_, bf16[4,128,384]{2,1,0:T(8,128)(2,1)S(1)} %get-tuple-element.167.refs_2_, ...), custom_call_target="tpu_custom_call" | custom-call | tf_op jit(solution)/shard_map/pallas_call | solution.py:126
  100.5 1.9 %collective-permute-start.21 = (bf16[256,640]{1,0:T(8,128)(2,1)}, bf16[256,640]{1,0:T(8,128)(2,1)}, u32[]{:S(2)}, u32[]{:S(2)}) collective-permute-start(bf16[256,640]{1,0:T(8,128)(2,1)} %slice.20), channel_id=1, source_target_pairs={{0,2},{1,3},{2,0},{3,1},{4,6},{5,7},{6,4},{7,5},{8,10},{9,11},{10,... | collective-permute-start | bytes 983048 | tf_op jit(solution)/shard_map/ppermute | solution.py:262
  102.4 2.5 %shard_map.107.refs_4_ = bf16[2,256,256]{2,1,0:T(8,128)(2,1)} custom-call(bf16[2,128,1280]{2,1,0:T(8,128)(2,1)S(1)} %get-tuple-element.133.refs_0_, bf16[2,128,1280]{2,1,0:T(8,128)(2,1)S(1)} %collective-permute-done.refs_1_, bf16[4,128,256]{2,1,0:T(8,128)(2,1)S(1)} %get-tuple-element.180.refs_2_, bf16[4,128,256]{2,1,0:T(8,128)(2,1)S(1)} %collective-permute-done.1.refs_3_, ...), custom_call_target="tpu_custom_call" | custom-call | tf_op jit(solution)/shard_map/pallas_call | solution.py:126
  105.7 2.0 %collective-permute-start.22 = (bf16[192,640]{1,0:T(8,128)(2,1)}, bf16[192,640]{1,0:T(8,128)(2,1)}, u32[]{:S(2)}, u32[]{:S(2)}) collective-permute-start(bf16[192,640]{1,0:T(8,128)(2,1)} %collective-permute-done.17.refs_2_), channel_id=1, source_target_pairs={{0,8},{4,12},{8,16},{12,20},{16,24},{20,28},{24,0},{28,4},{1,9},{5... | collective-permute-start | bytes 737288 | tf_op jit(solution)/shard_map/ppermute | solution.py:271
  108.7 3.7 %collective-permute-done.20.refs_5_ = bf16[2,256,256]{2,1,0:T(8,128)(2,1)} collective-permute-done((bf16[2,256,256]{2,1,0:T(8,128)(2,1)}, bf16[2,256,256]{2,1,0:T(8,128)(2,1)}, u32[]{:S(2)}, u32[]{:S(2)}) %collective-permute-start.20) | collective-permute-done | bytes 262176 | tf_op jit(solution)/shard_map/ppermute | solution.py:268
  112.4 1.7 collective-permute-done.22.refs_2_
  116.5 3.6 %shard_map.109 = (f32[512,640]{1,0:T(8,128)S(1)}, bf16[512,640]{1,0:T(8,128)(2,1)S(1)}) custom-call(bf16[2,1024,640]{2,1,0:T(8,128)(2,1)S(1)} %shard_map.108.acts_ref, bf16[640,640]{1,0:T(8,128)(2,1)S(1)} %copy-done, bf16[192,640]{1,0:T(8,128)(2,1)S(1)} %copy-done.11, bf16[192,640]{1,0:T(8,128)(2,1)} %collective-permute-done.17.refs_2_, ...), custom_call_target="tpu_custom_call" | custom-call | tf_op jit(solution)/shard_map/pallas_call | solution.py:180
  120.2 1.5 collective-permute-start.25
  122.0 8.4 %collective-permute-done.25.refs_3_ = bf16[256,640]{1,0:T(8,128)(2,1)S(1)} collective-permute-done((bf16[256,640]{1,0:T(8,128)(2,1)S(1)}, bf16[256,640]{1,0:T(8,128)(2,1)S(1)}, u32[]{:S(2)}, u32[]{:S(2)}) %collective-permute-start.25) | collective-permute-done | bytes 327712 | tf_op jit(solution)/shard_map/ppermute | solution.py:262
  130.4 3.4 %shard_map.111 = (f32[512,640]{1,0:T(8,128)S(1)}, bf16[512,640]{1,0:T(8,128)(2,1)S(1)}) custom-call(bf16[2,1024,640]{2,1,0:T(8,128)(2,1)S(1)} %shard_map.108.acts_ref, bf16[640,640]{1,0:T(8,128)(2,1)S(1)} %collective-permute-done.6.refs_0_, bf16[192,640]{1,0:T(8,128)(2,1)S(1)} %copy-done.15, bf16[192,640]{1,0:T(8,128)(2,1)} %collective-permute-done.22.refs_2_, ...), custom_call_target="tpu_custom_call" | custom-call | tf_op jit(solution)/shard_map/pallas_call | solution.py:180
  135.0 1.5 collective-permute-start.29
  137.4 7.0 %collective-permute-done.29.refs_3_ = bf16[256,640]{1,0:T(8,128)(2,1)S(1)} collective-permute-done((bf16[256,640]{1,0:T(8,128)(2,1)S(1)}, bf16[256,640]{1,0:T(8,128)(2,1)S(1)}, u32[]{:S(2)}, u32[]{:S(2)}) %collective-permute-start.29) | collective-permute-done | bytes 327712 | tf_op jit(solution)/shard_map/ppermute | solution.py:262
  144.4 2.5 %shard_map.113 = (f32[512,640]{1,0:T(8,128)S(1)}, bf16[512,640]{1,0:T(8,128)(2,1)S(1)}) custom-call(bf16[2,1024,640]{2,1,0:T(8,128)(2,1)S(1)} %shard_map.108.acts_ref, bf16[640,640]{1,0:T(8,128)(2,1)S(1)} %copy-done.2, bf16[192,640]{1,0:T(8,128)(2,1)S(1)} %copy-done.13, bf16[192,640]{1,0:T(8,128)(2,1)S(1)} %collective-permute-done.23.refs_2_, ...), custom_call_target="tpu_custom_call" | custom-call | tf_op jit(solution)/shard_map/pallas_call | solution.py:180
  147.2 1.5 collective-permute-start.30
  149.7 7.7 %collective-permute-done.30.refs_3_ = bf16[256,640]{1,0:T(8,128)(2,1)S(1)} collective-permute-done((bf16[256,640]{1,0:T(8,128)(2,1)S(1)}, bf16[256,640]{1,0:T(8,128)(2,1)S(1)}, u32[]{:S(2)}, u32[]{:S(2)}) %collective-permute-start.30) | collective-permute-done | bytes 327712 | tf_op jit(solution)/shard_map/ppermute | solution.py:262
  157.4 2.5 %shard_map.114 = (f32[512,640]{1,0:T(8,128)S(1)}, bf16[512,640]{1,0:T(8,128)(2,1)S(1)}) custom-call(bf16[2,1024,640]{2,1,0:T(8,128)(2,1)S(1)} %shard_map.108.acts_ref, bf16[640,640]{1,0:T(8,128)(2,1)S(1)} %collective-permute-done.19.refs_0_, bf16[192,640]{1,0:T(8,128)(2,1)S(1)} %copy-done.9, bf16[192,640]{1,0:T(8,128)(2,1)S(1)} %collective-permute-done.26.refs_2_, ...), custom_call_target="tpu_custom_call" | custom-call | tf_op jit(solution)/shard_map/pallas_call | solution.py:180
  160.1 2.1 %collective-permute-start.34 = (bf16[2,128,640]{2,1,0:T(8,128)(2,1)S(1)}, bf16[2,128,640]{2,1,0:T(8,128)(2,1)S(1)}, u32[]{:S(2)}, u32[]{:S(2)}) collective-permute-start(bf16[2,128,640]{2,1,0:T(8,128)(2,1)S(1)} %get-tuple-element.259), channel_id=1, source_target_pairs={{0,4},{4,0},{8,12},{12,8},{16,20},{20,16},{24,28},{28,24},{1,5},{5... | collective-permute-start | bytes 983048 | tf_op jit(solution)/shard_map/ppermute | solution.py:268
  162.3 2.1 %collective-permute-start.35 = (bf16[2,128,640]{2,1,0:T(8,128)(2,1)S(1)}, bf16[2,128,640]{2,1,0:T(8,128)(2,1)S(1)}, u32[]{:S(2)}, u32[]{:S(2)}) collective-permute-start(bf16[2,128,640]{2,1,0:T(8,128)(2,1)S(1)} %get-tuple-element.261), channel_id=1, source_target_pairs={{0,4},{4,0},{8,12},{12,8},{16,20},{20,16},{24,28},{28,24},{1,5},{5... | collective-permute-start | bytes 983048 | tf_op jit(solution)/shard_map/ppermute | solution.py:268
  164.4 6.3 %collective-permute-done.34.refs_5_ = bf16[2,128,640]{2,1,0:T(8,128)(2,1)S(1)} collective-permute-done((bf16[2,128,640]{2,1,0:T(8,128)(2,1)S(1)}, bf16[2,128,640]{2,1,0:T(8,128)(2,1)S(1)}, u32[]{:S(2)}, u32[]{:S(2)}) %collective-permute-start.34) | collective-permute-done | bytes 327712 | tf_op jit(solution)/shard_map/ppermute | solution.py:268
  170.7 6.7 %collective-permute-done.35.refs_7_ = bf16[2,128,640]{2,1,0:T(8,128)(2,1)S(1)} collective-permute-done((bf16[2,128,640]{2,1,0:T(8,128)(2,1)S(1)}, bf16[2,128,640]{2,1,0:T(8,128)(2,1)S(1)}, u32[]{:S(2)}, u32[]{:S(2)}) %collective-permute-start.35) | collective-permute-done | bytes 327712 | tf_op jit(solution)/shard_map/ppermute | solution.py:268
  177.5 2.2 %shard_map.117 = (bf16[128,5120]{1,0:T(8,128)(2,1)}, bf16[128,5120]{1,0:T(8,128)(2,1)}) custom-call(s32[8]{0:T(128)S(1)} %broadcast_add_fusion.where_ref, bf16[2,128,640]{2,1,0:T(8,128)(2,1)S(1)} %get-tuple-element.254.refs_0_, bf16[2,128,640]{2,1,0:T(8,128)(2,1)S(1)} %collective-permute-done.27.refs_1_, ...), custom_call_target="tpu_custom_call" | custom-call | tf_op jit(solution)/shard_map/pallas_call | solution.py:227
  (95 shorter events, 30.9 us)
Async XLA Ops:
  9.7 23.5 %collective-permute-start.6 = (bf16[640,640]{1,0:T(8,128)(2,1)S(1)}, bf16[640,640]{1,0:T(8,128)(2,1)S(1)}, u32[]{:S(2)}, u32[]{:S(2)}) collective-permute-start(bf16[640,640]{1,0:T(8,128)(2,1)S(1)} %copy-done), channel_id=1, source_target_pairs={{0,8},{4,12},{8,16},{12,20},{16,24},{20,28},{24,0},{28,4},{1,9},{5... | collective-permute-start | bytes 2457608 | tf_op jit(solution)/shard_map/ppermute | solution.py:271
  12.3 9.0 %collective-permute-start = (bf16[2,128,1280]{2,1,0:T(8,128)(2,1)S(1)}, bf16[2,128,1280]{2,1,0:T(8,128)(2,1)S(1)}, u32[]{:S(2)}, u32[]{:S(2)}) collective-permute-start(bf16[2,128,1280]{2,1,0:T(8,128)(2,1)S(1)} %get-tuple-element.142), channel_id=1, source_target_pairs={{0,1},{1,0},{2,3},{3,2},{4,5},{5,4},{6,7},{7,6},{8,9},{9,8},{10,11... | collective-permute-start | bytes 1966088 | tf_op jit(solution)/shard_map/ppermute | solution.py:265
  12.5 8.9 %collective-permute-start.1 = (bf16[4,128,256]{2,1,0:T(8,128)(2,1)S(1)}, bf16[4,128,256]{2,1,0:T(8,128)(2,1)S(1)}, u32[]{:S(2)}, u32[]{:S(2)}) collective-permute-start(bf16[4,128,256]{2,1,0:T(8,128)(2,1)S(1)} %get-tuple-element.149), channel_id=1, source_target_pairs={{0,1},{1,0},{2,3},{3,2},{4,5},{5,4},{6,7},{7,6},{8,9},{9,8},{10,11... | collective-permute-start | bytes 786440 | tf_op jit(solution)/shard_map/ppermute | solution.py:265
  12.8 8.5 %collective-permute-start.2 = (bf16[4,128,384]{2,1,0:T(8,128)(2,1)S(1)}, bf16[4,128,384]{2,1,0:T(8,128)(2,1)S(1)}, u32[]{:S(2)}, u32[]{:S(2)}) collective-permute-start(bf16[4,128,384]{2,1,0:T(8,128)(2,1)S(1)} %get-tuple-element.150), channel_id=1, source_target_pairs={{0,1},{1,0},{2,3},{3,2},{4,5},{5,4},{6,7},{7,6},{8,9},{9,8},{10,11... | collective-permute-start | bytes 1179656 | tf_op jit(solution)/shard_map/ppermute | solution.py:265
  13.0 8.3 %collective-permute-start.3 = (bf16[192,640]{1,0:T(8,128)(2,1)S(1)}, bf16[192,640]{1,0:T(8,128)(2,1)S(1)}, u32[]{:S(2)}, u32[]{:S(2)}) collective-permute-start(bf16[192,640]{1,0:T(8,128)(2,1)S(1)} %get-tuple-element.263), channel_id=1, source_target_pairs={{0,2},{1,3},{2,0},{3,1},{4,6},{5,7},{6,4},{7,5},{8,10},{9,11},{10,... | collective-permute-start | bytes 737288 | tf_op jit(solution)/shard_map/ppermute | solution.py:262
  33.2 31.7 %collective-permute-start.10 = (bf16[640,640]{1,0:T(8,128)(2,1)S(1)}, bf16[640,640]{1,0:T(8,128)(2,1)S(1)}, u32[]{:S(2)}, u32[]{:S(2)}) collective-permute-start(bf16[640,640]{1,0:T(8,128)(2,1)S(1)} %collective-permute-done.6.refs_0_), channel_id=1, source_target_pairs={{0,8},{4,12},{8,16},{12,20},{16,24},{20,28},{24,0},{28,4},{1,9},{5... | collective-permute-start | bytes 2457608 | tf_op jit(solution)/shard_map/ppermute | solution.py:271
  33.2 17.6 %collective-permute-start.5 = (bf16[4,128,640]{2,1,0:T(8,128)(2,1)S(1)}, bf16[4,128,640]{2,1,0:T(8,128)(2,1)S(1)}, u32[]{:S(2)}, u32[]{:S(2)}) collective-permute-start(bf16[4,128,640]{2,1,0:T(8,128)(2,1)S(1)} %get-tuple-element.158.refs_2_), channel_id=1, source_target_pairs={{0,2},{1,3},{2,0},{3,1},{4,6},{5,7},{6,4},{7,5},{8,10},{9,11},{10,... | collective-permute-start | bytes 1966088 | tf_op jit(solution)/shard_map/ppermute | solution.py:262
  34.7 30.2 %collective-permute-start.7 = (bf16[4,128,640]{2,1,0:T(8,128)(2,1)S(1)}, bf16[4,128,640]{2,1,0:T(8,128)(2,1)S(1)}, u32[]{:S(2)}, u32[]{:S(2)}) collective-permute-start(bf16[4,128,640]{2,1,0:T(8,128)(2,1)S(1)} %collective-permute-done.4.refs_3_), channel_id=1, source_target_pairs={{0,2},{1,3},{2,0},{3,1},{4,6},{5,7},{6,4},{7,5},{8,10},{9,11},{10,... | collective-permute-start | bytes 1966088 | tf_op jit(solution)/shard_map/ppermute | solution.py:262
  35.2 36.9 %collective-permute-start.9 = (bf16[4,128,384]{2,1,0:T(8,128)(2,1)S(1)}, bf16[4,128,384]{2,1,0:T(8,128)(2,1)S(1)}, u32[]{:S(2)}, u32[]{:S(2)}) collective-permute-start(bf16[4,128,384]{2,1,0:T(8,128)(2,1)S(1)} %get-tuple-element.167.refs_2_), channel_id=1, source_target_pairs={{0,2},{1,3},{2,0},{3,1},{4,6},{5,7},{6,4},{7,5},{8,10},{9,11},{10,... | collective-permute-start | bytes 1179656 | tf_op jit(solution)/shard_map/ppermute | solution.py:262
  36.7 23.5 %collective-permute-start.8 = (bf16[192,640]{1,0:T(8,128)(2,1)S(1)}, bf16[192,640]{1,0:T(8,128)(2,1)S(1)}, u32[]{:S(2)}, u32[]{:S(2)}) collective-permute-start(bf16[192,640]{1,0:T(8,128)(2,1)S(1)} %collective-permute-done.3.refs_1_), channel_id=1, source_target_pairs={{0,8},{4,12},{8,16},{12,20},{16,24},{20,28},{24,0},{28,4},{1,9},{5... | collective-permute-start | bytes 737288 | tf_op jit(solution)/shard_map/ppermute | solution.py:271
  64.9 40.1 %collective-permute-start.19 = (bf16[640,640]{1,0:T(8,128)(2,1)S(1)}, bf16[640,640]{1,0:T(8,128)(2,1)S(1)}, u32[]{:S(2)}, u32[]{:S(2)}) collective-permute-start(bf16[640,640]{1,0:T(8,128)(2,1)S(1)} %collective-permute-done.10.refs_0_), channel_id=1, source_target_pairs={{0,8},{4,12},{8,16},{12,20},{16,24},{20,28},{24,0},{28,4},{1,9},{5... | collective-permute-start | bytes 2457608 | tf_op jit(solution)/shard_map/ppermute | solution.py:271
  72.2 27.5 %collective-permute-start.11 = (bf16[2,256,640]{2,1,0:T(8,128)(2,1)S(1)}, bf16[2,256,640]{2,1,0:T(8,128)(2,1)S(1)}, u32[]{:S(2)}, u32[]{:S(2)}) collective-permute-start(bf16[2,256,640]{2,1,0:T(8,128)(2,1)S(1)} %shard_map.105.refs_0_), channel_id=1, source_target_pairs={{0,4},{4,0},{8,12},{12,8},{16,20},{20,16},{24,28},{28,24},{1,5},{5... | collective-permute-start | bytes 1966088 | tf_op jit(solution)/shard_map/ppermute | solution.py:268
  73.5 16.4 %collective-permute-start.14 = (bf16[192,640]{1,0:T(8,128)(2,1)S(1)}, bf16[192,640]{1,0:T(8,128)(2,1)S(1)}, u32[]{:S(2)}, u32[]{:S(2)}) collective-permute-start(bf16[192,640]{1,0:T(8,128)(2,1)S(1)} %collective-permute-done.8.refs_1_), channel_id=1, source_target_pairs={{0,8},{4,12},{8,16},{12,20},{16,24},{20,28},{24,0},{28,4},{1,9},{5... | collective-permute-start | bytes 737288 | tf_op jit(solution)/shard_map/ppermute | solution.py:271
  74.5 19.3 %collective-permute-start.13 = (bf16[4,128,384]{2,1,0:T(8,128)(2,1)S(1)}, bf16[4,128,384]{2,1,0:T(8,128)(2,1)S(1)}, u32[]{:S(2)}, u32[]{:S(2)}) collective-permute-start(bf16[4,128,384]{2,1,0:T(8,128)(2,1)S(1)} %collective-permute-done.2.refs_3_), channel_id=1, source_target_pairs={{0,2},{1,3},{2,0},{3,1},{4,6},{5,7},{6,4},{7,5},{8,10},{9,11},{10,... | collective-permute-start | bytes 1179656 | tf_op jit(solution)/shard_map/ppermute | solution.py:262
  76.0 15.2 %collective-permute-start.15 = (bf16[4,128,256]{2,1,0:T(8,128)(2,1)S(1)}, bf16[4,128,256]{2,1,0:T(8,128)(2,1)S(1)}, u32[]{:S(2)}, u32[]{:S(2)}) collective-permute-start(bf16[4,128,256]{2,1,0:T(8,128)(2,1)S(1)} %get-tuple-element.180.refs_2_), channel_id=1, source_target_pairs={{0,2},{1,3},{2,0},{3,1},{4,6},{5,7},{6,4},{7,5},{8,10},{9,11},{10,... | collective-permute-start | bytes 786440 | tf_op jit(solution)/shard_map/ppermute | solution.py:262
  89.9 8.3 %collective-permute-start.12 = (bf16[4,128,256]{2,1,0:T(8,128)(2,1)S(1)}, bf16[4,128,256]{2,1,0:T(8,128)(2,1)S(1)}, u32[]{:S(2)}, u32[]{:S(2)}) collective-permute-start(bf16[4,128,256]{2,1,0:T(8,128)(2,1)S(1)} %collective-permute-done.1.refs_3_), channel_id=1, source_target_pairs={{0,2},{1,3},{2,0},{3,1},{4,6},{5,7},{6,4},{7,5},{8,10},{9,11},{10,... | collective-permute-start | bytes 786440 | tf_op jit(solution)/shard_map/ppermute | solution.py:262
  91.1 13.8 %collective-permute-start.18 = (bf16[192,640]{1,0:T(8,128)(2,1)S(1)}, bf16[192,640]{1,0:T(8,128)(2,1)S(1)}, u32[]{:S(2)}, u32[]{:S(2)}) collective-permute-start(bf16[192,640]{1,0:T(8,128)(2,1)S(1)} %collective-permute-done.14.refs_1_), channel_id=1, source_target_pairs={{0,8},{4,12},{8,16},{12,20},{16,24},{20,28},{24,0},{28,4},{1,9},{5... | collective-permute-start | bytes 737288 | tf_op jit(solution)/shard_map/ppermute | solution.py:271
  93.8 11.9 %collective-permute-start.17 = (bf16[192,640]{1,0:T(8,128)(2,1)S(1)}, bf16[192,640]{1,0:T(8,128)(2,1)}, u32[]{:S(2)}, u32[]{:S(2)}) collective-permute-start(bf16[192,640]{1,0:T(8,128)(2,1)S(1)} %get-tuple-element.262), channel_id=1, source_target_pairs={{0,2},{1,3},{2,0},{3,1},{4,6},{5,7},{6,4},{7,5},{8,10},{9,11},{10,... | collective-permute-start | bytes 737288 | tf_op jit(solution)/shard_map/ppermute | solution.py:262
  98.2 10.4 %collective-permute-start.16 = (bf16[2,256,384]{2,1,0:T(8,128)(2,1)S(1)}, bf16[2,256,384]{2,1,0:T(8,128)(2,1)}, u32[]{:S(2)}, u32[]{:S(2)}) collective-permute-start(bf16[2,256,384]{2,1,0:T(8,128)(2,1)S(1)} %shard_map.106.refs_2_), channel_id=1, source_target_pairs={{0,4},{4,0},{8,12},{12,8},{16,20},{20,16},{24,28},{28,24},{1,5},{5... | collective-permute-start | bytes 1179656 | tf_op jit(solution)/shard_map/ppermute | solution.py:268
  105.7 8.3 %collective-permute-start.22 = (bf16[192,640]{1,0:T(8,128)(2,1)}, bf16[192,640]{1,0:T(8,128)(2,1)}, u32[]{:S(2)}, u32[]{:S(2)}) collective-permute-start(bf16[192,640]{1,0:T(8,128)(2,1)} %collective-permute-done.17.refs_2_), channel_id=1, source_target_pairs={{0,8},{4,12},{8,16},{12,20},{16,24},{20,28},{24,0},{28,4},{1,9},{5... | collective-permute-start | bytes 737288 | tf_op jit(solution)/shard_map/ppermute | solution.py:271
  120.1 13.7 %collective-permute-start.24 = (bf16[512,640]{1,0:T(8,128)(2,1)S(1)}, bf16[512,640]{1,0:T(8,128)(2,1)S(1)}, u32[]{:S(2)}, u32[]{:S(2)}) collective-permute-start(bf16[512,640]{1,0:T(8,128)(2,1)S(1)} %get-tuple-element.210), channel_id=1, source_target_pairs={{0,1},{1,0},{2,3},{3,2},{4,5},{5,4},{6,7},{7,6},{8,9},{9,8},{10,11... | collective-permute-start | bytes 1966088 | tf_op jit(solution)/shard_map/ppermute | solution.py:265
  120.2 10.2 %collective-permute-start.25 = (bf16[256,640]{1,0:T(8,128)(2,1)S(1)}, bf16[256,640]{1,0:T(8,128)(2,1)S(1)}, u32[]{:S(2)}, u32[]{:S(2)}) collective-permute-start(bf16[256,640]{1,0:T(8,128)(2,1)S(1)} %slice.21), channel_id=1, source_target_pairs={{0,2},{1,3},{2,0},{3,1},{4,6},{5,7},{6,4},{7,5},{8,10},{9,11},{10,... | collective-permute-start | bytes 983048 | tf_op jit(solution)/shard_map/ppermute | solution.py:262
  121.7 12.3 %collective-permute-start.23 = (bf16[192,640]{1,0:T(8,128)(2,1)}, bf16[192,640]{1,0:T(8,128)(2,1)S(1)}, u32[]{:S(2)}, u32[]{:S(2)}) collective-permute-start(bf16[192,640]{1,0:T(8,128)(2,1)} %collective-permute-done.22.refs_2_), channel_id=1, source_target_pairs={{0,8},{4,12},{8,16},{12,20},{16,24},{20,28},{24,0},{28,4},{1,9},{5... | collective-permute-start | bytes 737288 | tf_op jit(solution)/shard_map/ppermute | solution.py:271
  134.0 12.9 %collective-permute-start.28 = (bf16[512,640]{1,0:T(8,128)(2,1)S(1)}, bf16[512,640]{1,0:T(8,128)(2,1)S(1)}, u32[]{:S(2)}, u32[]{:S(2)}) collective-permute-start(bf16[512,640]{1,0:T(8,128)(2,1)S(1)} %get-tuple-element.223), channel_id=1, source_target_pairs={{0,1},{1,0},{2,3},{3,2},{4,5},{5,4},{6,7},{7,6},{8,9},{9,8},{10,11... | collective-permute-start | bytes 1966088 | tf_op jit(solution)/shard_map/ppermute | solution.py:265
  135.0 9.4 %collective-permute-start.29 = (bf16[256,640]{1,0:T(8,128)(2,1)S(1)}, bf16[256,640]{1,0:T(8,128)(2,1)S(1)}, u32[]{:S(2)}, u32[]{:S(2)}) collective-permute-start(bf16[256,640]{1,0:T(8,128)(2,1)S(1)} %slice.22), channel_id=1, source_target_pairs={{0,2},{1,3},{2,0},{3,1},{4,6},{5,7},{6,4},{7,5},{8,10},{9,11},{10,... | collective-permute-start | bytes 983048 | tf_op jit(solution)/shard_map/ppermute | solution.py:262
  136.5 10.5 %collective-permute-start.27 = (bf16[2,128,640]{2,1,0:T(8,128)(2,1)S(1)}, bf16[2,128,640]{2,1,0:T(8,128)(2,1)S(1)}, u32[]{:S(2)}, u32[]{:S(2)}) collective-permute-start(bf16[2,128,640]{2,1,0:T(8,128)(2,1)S(1)} %get-tuple-element.218), channel_id=1, source_target_pairs={{0,4},{4,0},{8,12},{12,8},{16,20},{20,16},{24,28},{28,24},{1,5},{5... | collective-permute-start | bytes 983048 | tf_op jit(solution)/shard_map/ppermute | solution.py:268
  137.4 9.7 %collective-permute-start.26 = (bf16[192,640]{1,0:T(8,128)(2,1)S(1)}, bf16[192,640]{1,0:T(8,128)(2,1)S(1)}, u32[]{:S(2)}, u32[]{:S(2)}) collective-permute-start(bf16[192,640]{1,0:T(8,128)(2,1)S(1)} %collective-permute-done.23.refs_2_), channel_id=1, source_target_pairs={{0,8},{4,12},{8,16},{12,20},{16,24},{20,28},{24,0},{28,4},{1,9},{5... | collective-permute-start | bytes 737288 | tf_op jit(solution)/shard_map/ppermute | solution.py:271
  147.1 12.8 %collective-permute-start.32 = (bf16[512,640]{1,0:T(8,128)(2,1)S(1)}, bf16[512,640]{1,0:T(8,128)(2,1)S(1)}, u32[]{:S(2)}, u32[]{:S(2)}) collective-permute-start(bf16[512,640]{1,0:T(8,128)(2,1)S(1)} %get-tuple-element.241), channel_id=1, source_target_pairs={{0,1},{1,0},{2,3},{3,2},{4,5},{5,4},{6,7},{7,6},{8,9},{9,8},{10,11... | collective-permute-start | bytes 1966088 | tf_op jit(solution)/shard_map/ppermute | solution.py:265
  147.2 10.2 %collective-permute-start.30 = (bf16[256,640]{1,0:T(8,128)(2,1)S(1)}, bf16[256,640]{1,0:T(8,128)(2,1)S(1)}, u32[]{:S(2)}, u32[]{:S(2)}) collective-permute-start(bf16[256,640]{1,0:T(8,128)(2,1)S(1)} %slice.23), channel_id=1, source_target_pairs={{0,2},{1,3},{2,0},{3,1},{4,6},{5,7},{6,4},{7,5},{8,10},{9,11},{10,... | collective-permute-start | bytes 983048 | tf_op jit(solution)/shard_map/ppermute | solution.py:262
  148.7 11.3 %collective-permute-start.31 = (bf16[2,128,640]{2,1,0:T(8,128)(2,1)S(1)}, bf16[2,128,640]{2,1,0:T(8,128)(2,1)S(1)}, u32[]{:S(2)}, u32[]{:S(2)}) collective-permute-start(bf16[2,128,640]{2,1,0:T(8,128)(2,1)S(1)} %get-tuple-element.239), channel_id=1, source_target_pairs={{0,4},{4,0},{8,12},{12,8},{16,20},{20,16},{24,28},{28,24},{1,5},{5... | collective-permute-start | bytes 983048 | tf_op jit(solution)/shard_map/ppermute | solution.py:268
  160.1 10.6 %collective-permute-start.34 = (bf16[2,128,640]{2,1,0:T(8,128)(2,1)S(1)}, bf16[2,128,640]{2,1,0:T(8,128)(2,1)S(1)}, u32[]{:S(2)}, u32[]{:S(2)}) collective-permute-start(bf16[2,128,640]{2,1,0:T(8,128)(2,1)S(1)} %get-tuple-element.259), channel_id=1, source_target_pairs={{0,4},{4,0},{8,12},{12,8},{16,20},{20,16},{24,28},{28,24},{1,5},{5... | collective-permute-start | bytes 983048 | tf_op jit(solution)/shard_map/ppermute | solution.py:268
  162.3 15.2 %collective-permute-start.35 = (bf16[2,128,640]{2,1,0:T(8,128)(2,1)S(1)}, bf16[2,128,640]{2,1,0:T(8,128)(2,1)S(1)}, u32[]{:S(2)}, u32[]{:S(2)}) collective-permute-start(bf16[2,128,640]{2,1,0:T(8,128)(2,1)S(1)} %get-tuple-element.261), channel_id=1, source_target_pairs={{0,4},{4,0},{8,12},{12,8},{16,20},{20,16},{24,28},{28,24},{1,5},{5... | collective-permute-start | bytes 983048 | tf_op jit(solution)/shard_map/ppermute | solution.py:268
  (20 other events, 145.7 us)
where the time goes:
time: 180 us
  waiting for transfers between devices  103 us (57%)
  starting transfers between devices  36.8 us (20%)
  Pallas kernels  29.9 us (17%)
  local copies, waits for them, and re-layouts  9.22 us (5%)
    ppermute x12, waiting for transfers between devices, far(): return lax.ppermute(array, 'seq', [(i, i ^ 2) for i in range(n_seq)])  48.7 us
    ppermute x9, waiting for transfers between devices, onward(): return lax.ppermute(array, 'dp', [(i, (i + 2) % n_dp) for i in range(n_dp)])  36.4 us
    ppermute x7, waiting for transfers between devices, across(): return lax.ppermute(array, 'dp', [(i, i ^ 1) for i in range(n_dp)])  17.7 us
    ppermute x12, starting transfers between devices, far(): return lax.ppermute(array, 'seq', [(i, i ^ 2) for i in range(n_seq)])  16.2 us
    pallas_call x4, Pallas kernels, project(): pl.pallas_call(project_kernel, in_specs=vmem_specs(1 + len(weights)), out...  12 us
    ppermute x9, starting transfers between devices, onward(): return lax.ppermute(array, 'dp', [(i, (i + 2) % n_dp) for i in range(n_dp)])  11.1 us
    pallas_call x3, Pallas kernels, attend(): pl.pallas_call(functools.partial(attend_kernel, len(queries)), grid=(widt...  10 us
    ppermute x7, starting transfers between devices, across(): return lax.ppermute(array, 'dp', [(i, i ^ 1) for i in range(n_dp)])  8.01 us
  transfers between devices with their start and end apart: 36, of which 16 were waited for; matrix products, arithmetic and copies ran while one was open for 1% of the time, Pallas kernels for 10%

commit v1 on v0

--- a/solution.py
+++ b/solution.py
@@ -14,6 +14,7 @@
 
 LOW = jnp.bfloat16
 WIDE = jnp.float32
+LIGHT = pl.CostEstimate(flops=1, transcendentals=0, bytes_accessed=1)
 
 
 def params():
@@ -84,6 +85,7 @@
         ),
         out_shape=[jax.ShapeDtypeStruct((count, rows, width), LOW) for count, width in kinds],
         compiler_params=params(),
+        cost_estimate=LIGHT,
     )(core, *arrays, *[gain.reshape(1, features) for gain in gains])
 
 
@@ -131,6 +133,7 @@
         out_specs=pl.BlockSpec((2, len(queries) * rows, hdim), lambda h: (0, 0, h)),
         out_shape=jax.ShapeDtypeStruct((2, len(queries) * rows, width), LOW),
         compiler_params=params(),
+        cost_estimate=LIGHT,
     )(*queries, *keyed)
 
 
@@ -162,27 +165,31 @@
         out_specs=vmem_specs(1)[0],
         out_shape=jax.ShapeDtypeStruct((groups, rows, sum(chunks) // groups), LOW),
         compiler_params=params(),
+        cost_estimate=LIGHT,
     )(flip, *[part for pair in pairs for part in pair])
 
 
-def project_kernel(acts_ref, *refs):
-    weight_refs, (keep_ref, send_ref) = refs[:-2], refs[-2:]
+def project_kernel(pieces, acts_ref, *refs):
+    weight_refs, (keep_ref, send_ref) = list(refs[:-2]), refs[-2:]
     rows = keep_ref.shape[0]
-    beside = jnp.concatenate([ref[...] for ref in weight_refs[1:]], axis=0)
-    total = jnp.dot(acts_ref[0], weight_refs[0][...], preferred_element_type=WIDE)
-    total = total + jnp.dot(acts_ref[1], beside, preferred_element_type=WIDE)
+    total = 0.0
+    for at, count in enumerate(pieces):
+        weight = jnp.concatenate([weight_refs.pop(0)[...] for _ in range(count)], axis=0)
+        total = total + jnp.dot(acts_ref[at], weight, preferred_element_type=WIDE)
     keep_ref[...] = total[:rows]
     send_ref[...] = total[rows:].astype(LOW)
 
 
-def project(acts, weights):
+def project(acts, blocks):
+    weights = [piece for block in blocks for piece in block]
     rows, n = acts.shape[1] // 2, weights[0].shape[1]
     return pl.pallas_call(
-        project_kernel,
+        functools.partial(project_kernel, [len(block) for block in blocks]),
         in_specs=vmem_specs(1 + len(weights)),
         out_specs=vmem_specs(2),
         out_shape=[jax.ShapeDtypeStruct((rows, n), WIDE), jax.ShapeDtypeStruct((rows, n), LOW)],
         compiler_params=params(),
+        cost_estimate=LIGHT,
     )(acts, *weights)
 
 
@@ -202,6 +209,7 @@
         out_specs=vmem_specs(2),
         out_shape=[out, out],
         compiler_params=params(),
+        cost_estimate=LIGHT,
     )(keep, got)
 
 
@@ -230,6 +238,7 @@
         out_specs=vmem_specs(2),
         out_shape=[out, out],
         compiler_params=params(),
+        cost_estimate=LIGHT,
     )(where, *pieces)
 
 
@@ -275,6 +284,9 @@
         array, token = lax.optimization_barrier((array, token))
         return array
 
+    def after(array):
+        return lax.optimization_barrier((array, token))[0]
+
     def turn(ring, step):
         ring[step] = wait(ring[step])
         if step + 1 < n_ring:
@@ -282,8 +294,8 @@
 
     depth = out_weight.shape[0]
     cuts = [depth * 3 // 10 // 16 * 16, depth * 6 // 10 // 16 * 16]
-    rings = [out_weight, onward(out_weight)]
     early = [far(out_weight[: cuts[0]])]
+    turn(early, 0)
 
     core = jnp.stack([seq % 2])
     arrays = (queries, key_states, value_states, query_tangent, key_tangent, value_tangent)
@@ -291,13 +303,12 @@
     half = len(packs) // 2
     query_own, *keyed_own = packs[:half]
     query_other, *keyed_other = packs[half:]
-    keyed_near = [wait(near(keyed_other[0]))]
-    turn(early, 0)
-    keyed_near += [wait(near(array)) for array in keyed_other[1:]]
+    tops, lows = [out_weight[: depth // 2]], [out_weight[depth // 2 :]]
+    tops.append(onward(tops[0]))
+    lows.append(onward(lows[0]))
+    keyed_near = [wait(near(array)) for array in keyed_other]
     queries_both = [query_own, wait(near(query_other))]
     keyed_far = [[far(own), far(other)] for own, other in zip(keyed_own, keyed_near)]
-    late = [far(out_weight[cuts[0] : cuts[1]])]
-    rest = [far(out_weight[cuts[1] :])]
 
     acts, swapped = [], []
 
@@ -309,25 +320,30 @@
     def keyed_wait(chunk, at):
         keyed_far[chunk][at] = wait(keyed_far[chunk][at])
 
-    turn(rings, 1)
     keyed_wait(0, 0)
     turn(early, 1)
+    turn(tops, 1)
+    turn(lows, 1)
     keyed_wait(0, 1)
-    turn(rings, 2)
     keyed_wait(1, 0)
+    turn(early, 2)
+    turn(tops, 2)
     attention(0)
-    turn(early, 2)
+    turn(lows, 2)
     keyed_wait(1, 1)
+    late = [far(after(out_weight[cuts[0] : cuts[1]]))]
     keyed_wait(2, 0)
+    rest = [far(after(out_weight[cuts[1] :]))]
     attention(1)
     keyed_wait(2, 1)
     swapped[0] = wait(swapped[0])
+    turn(late, 0)
+    attention(2)
     for step in range(3, n_ring):
-        turn(rings, step)
         turn(early, step)
-    attention(2)
-    rest.append(far(rings[1][cuts[1] :]))
-    turn(late, 0)
+        turn(tops, step)
+        turn(lows, step)
+    rest.append(far(lows[1][cuts[1] - depth // 2 :]))
     swapped[1] = wait(swapped[1])
     rest[0] = wait(rest[0])
     swapped[2] = wait(swapped[2])
@@ -336,7 +352,7 @@
     keeps, sends, mine, other = [], [], [], []
 
     def columns(step):
-        blocks = [rings[step], early[step], late[step], rest[step]]
+        blocks = [[tops[step], lows[step]], [early[step], late[step], rest[step]]]
         keep, send = project(acts, blocks)
         keeps.append(keep)
         sends.append(near(wait(send)))
@@ -348,14 +364,16 @@
 
     for step in range(1, n_ring):
         turn(late, step)
+        if step + 1 < n_ring:
+            rest.append(far(lows[step + 1][cuts[1] - depth // 2 :]))
+        rest[step] = wait(rest[step])
         columns(step - 1)
-        if step + 1 < n_ring:
-            rest.append(far(rings[step + 1][cuts[1] :]))
-        rest[step] = wait(rest[step])
-        finish(step - 1)
         if step > 1:
-            other[step - 2] = wait(other[step - 2])
+            finish(step - 2)
+        if step > 2:
+            other[step - 3] = wait(other[step - 3])
     columns(n_ring - 1)
+    finish(n_ring - 2)
     finish(n_ring - 1)
 
     pieces, where = [], []

time: 180 us -> 164 us (0.911)
  waiting for transfers between devices: 103 us -> 94.7 us
  starting transfers between devices: 36.8 us -> 29 us
    ppermute x12, waiting for transfers between devices: 48.7 us -> 23.4 us  [far(): return lax.ppermute(array, 'seq', [(i, i ^ 2) for i in range(n_seq)])]
    ppermute x9 -> x12, waiting for transfers between devices: 36.4 us -> 46.7 us  [onward(): return lax.ppermute(array, 'dp', [(i, (i + 2) % n_dp) for i in range(n_dp)])]
    ppermute x12, starting transfers between devices: 16.2 us -> 10.1 us  [far(): return lax.ppermute(array, 'seq', [(i, i ^ 2) for i in range(n_seq)])]
    ppermute x7, waiting for transfers between devices: 17.7 us -> 23.8 us  [across(): return lax.ppermute(array, 'dp', [(i, i ^ 1) for i in range(n_dp)])]
    slice x5 -> x6, local copies, waits for them, and re-layouts: 0.89 us -> 2.81 us  [the longest x1 1.17 us: body(): late = [far(after(out_weight[cuts[0]:cuts[1]]))]]
    unnamed x32 -> x40, local copies, waits for them, and re-layouts: 6.81 us -> 4.9 us
    ppermute x9 -> x12, starting transfers between devices: 11.1 us -> 9.29 us  [onward(): return lax.ppermute(array, 'dp', [(i, (i + 2) % n_dp) for i in range(n_dp)])]
  transfers between devices with their start and end apart: 36 -> 39, of which waited for: 16 -> 19; matrix products, arithmetic and copies ran while one was open for 1% -> 2% of each run, Pallas kernels for 10% -> 17%
where the time goes in v1:
time: 164 us
  waiting for transfers between devices  94.7 us (58%)
  Pallas kernels  30 us (18%)
  starting transfers between devices  29 us (18%)
  local copies, waits for them, and re-layouts  9.23 us (6%)
    ppermute x12, waiting for transfers between devices, onward(): return lax.ppermute(array, 'dp', [(i, (i + 2) % n_dp) for i in range(n_dp)])  46.7 us
    ppermute x7, waiting for transfers between devices, across(): return lax.ppermute(array, 'dp', [(i, i ^ 1) for i in range(n_dp)])  23.8 us
    ppermute x12, waiting for transfers between devices, far(): return lax.ppermute(array, 'seq', [(i, i ^ 2) for i in range(n_seq)])  23.4 us
    pallas_call x4, Pallas kernels, project(): pl.pallas_call(functools.partial(project_kernel, [len(block) for block in...  12.2 us
    ppermute x12, starting transfers between devices, far(): return lax.ppermute(array, 'seq', [(i, i ^ 2) for i in range(n_seq)])  10.1 us
    pallas_call x3, Pallas kernels, attend(): pl.pallas_call(functools.partial(attend_kernel, len(queries)), grid=(widt...  9.36 us
    ppermute x12, starting transfers between devices, onward(): return lax.ppermute(array, 'dp', [(i, (i + 2) % n_dp) for i in range(n_dp)])  9.29 us
    ppermute x7, starting transfers between devices, across(): return lax.ppermute(array, 'dp', [(i, i ^ 1) for i in range(n_dp)])  7.87 us
  transfers between devices with their start and end apart: 39, of which 19 were waited for; matrix products, arithmetic and copies ran while one was open for 2% of the time, Pallas kernels for 17%

profile of v1, /device:TPU:0, one launch (start us, length us, event | category | flops | bytes accessed | tf_op | source)
XLA Modules:
  0.0 164.0 jit_solution(11882434275519552079)
XLA Ops:
  1.8 3.0 %collective-permute-start = (bf16[192,640]{1,0:T(8,128)(2,1)S(1)}, bf16[192,640]{1,0:T(8,128)(2,1)S(1)}, u32[]{:S(2)}, u32[]{:S(2)}) collective-permute-start(bf16[192,640]{1,0:T(8,128)(2,1)S(1)} %get-tuple-element.275), channel_id=1, source_target_pairs={{0,2},{1,3},{2,0},{3,1},{4,6},{5,7},{6,4},{7,5},{8,10},{9,11},{10,... | collective-permute-start | bytes 737288 | tf_op jit(solution)/shard_map/ppermute | solution.py:271
  8.4 3.8 %shard_map.104 = (bf16[2,128,1280]{2,1,0:T(8,128)(2,1)S(1)}, bf16[4,128,640]{2,1,0:T(8,128)(2,1)S(1)}, bf16[4,128,384]{2,1,0:T(8,128)(2,1)S(1)}, bf16[4,128,256]...) custom-call(s32[1]{0:T(128)} %bitcast.9.core_ref, ...), custom_call_target="tpu_custom_call" | custom-call | flops 1 | bytes 1 | tf_op jit(solution)/shard_map/pallas_call | solution.py:78
  17.1 1.6 collective-permute-start.9
  20.3 10.7 %collective-permute-done.5.refs_4_ = bf16[4,128,640]{2,1,0:T(8,128)(2,1)S(1)} collective-permute-done((bf16[4,128,640]{2,1,0:T(8,128)(2,1)S(1)}, bf16[4,128,640]{2,1,0:T(8,128)(2,1)S(1)}, u32[]{:S(2)}, u32[]{:S(2)}) %collective-permute-start.5) | collective-permute-done | bytes 655392 | tf_op jit(solution)/shard_map/ppermute | solution.py:271
  30.9 2.9 %collective-permute-done.9.refs_2_ = bf16[192,640]{1,0:T(8,128)(2,1)S(1)} collective-permute-done((bf16[192,640]{1,0:T(8,128)(2,1)S(1)}, bf16[192,640]{1,0:T(8,128)(2,1)S(1)}, u32[]{:S(2)}, u32[]{:S(2)}) %collective-permute-start.9) | collective-permute-done | bytes 245792 | tf_op jit(solution)/shard_map/ppermute | solution.py:280
  36.4 6.2 %collective-permute-done.7.refs_1_ = bf16[320,640]{1,0:T(8,128)(2,1)S(1)} collective-permute-done((bf16[320,640]{1,0:T(8,128)(2,1)S(1)}, bf16[320,640]{1,0:T(8,128)(2,1)S(1)}, u32[]{:S(2)}, u32[]{:S(2)}) %collective-permute-start.7) | collective-permute-done | bytes 409632 | tf_op jit(solution)/shard_map/ppermute | solution.py:280
  42.6 2.4 %collective-permute-done.6.refs_5_ = bf16[4,128,640]{2,1,0:T(8,128)(2,1)S(1)} collective-permute-done((bf16[4,128,640]{2,1,0:T(8,128)(2,1)S(1)}, bf16[4,128,640]{2,1,0:T(8,128)(2,1)S(1)}, u32[]{:S(2)}, u32[]{:S(2)}) %collective-permute-start.6) | collective-permute-done | bytes 655392 | tf_op jit(solution)/shard_map/ppermute | solution.py:271
  45.2 4.7 %shard_map.105.refs_0_ = bf16[2,256,640]{2,1,0:T(8,128)(2,1)S(1)} custom-call(bf16[2,128,1280]{2,1,0:T(8,128)(2,1)S(1)} %get-tuple-element.140.refs_0_, bf16[2,128,1280]{2,1,0:T(8,128)(2,1)S(1)} %collective-permute-done.1.refs_1_, bf16[4,128,640]{2,1,0:T(8,128)(2,1)S(1)} %get-tuple-element.164.refs_2_, ...), custom_call_target="tpu_custom_call" | custom-call | flops 1 | bytes 1 | tf_op jit(solution)/shard_map/pallas_call | solution.py:128
  49.9 3.6 %collective-permute-done.12.refs_4_ = bf16[4,128,384]{2,1,0:T(8,128)(2,1)S(1)} collective-permute-done((bf16[4,128,384]{2,1,0:T(8,128)(2,1)S(1)}, bf16[4,128,384]{2,1,0:T(8,128)(2,1)S(1)}, u32[]{:S(2)}, u32[]{:S(2)}) %collective-permute-start.12) | collective-permute-done | bytes 393248 | tf_op jit(solution)/shard_map/ppermute | solution.py:271
  53.4 3.2 %collective-permute-done.11.refs_2_ = bf16[192,640]{1,0:T(8,128)(2,1)S(1)} collective-permute-done((bf16[192,640]{1,0:T(8,128)(2,1)S(1)}, bf16[192,640]{1,0:T(8,128)(2,1)S(1)}, u32[]{:S(2)}, u32[]{:S(2)}) %collective-permute-start.11) | collective-permute-done | bytes 245792 | tf_op jit(solution)/shard_map/ppermute | solution.py:280
  56.6 1.6 collective-permute-start.13
  60.2 4.4 %collective-permute-done.16.refs_1_ = bf16[320,640]{1,0:T(8,128)(2,1)S(1)} collective-permute-done((bf16[320,640]{1,0:T(8,128)(2,1)S(1)}, bf16[320,640]{1,0:T(8,128)(2,1)S(1)}, u32[]{:S(2)}, u32[]{:S(2)}) %collective-permute-start.16) | collective-permute-done | bytes 409632 | tf_op jit(solution)/shard_map/ppermute | solution.py:280
  64.7 2.8 %collective-permute-done.17.refs_4_ = bf16[4,128,256]{2,1,0:T(8,128)(2,1)S(1)} collective-permute-done((bf16[4,128,256]{2,1,0:T(8,128)(2,1)S(1)}, bf16[4,128,256]{2,1,0:T(8,128)(2,1)S(1)}, u32[]{:S(2)}, u32[]{:S(2)}) %collective-permute-start.17) | collective-permute-done | bytes 262176 | tf_op jit(solution)/shard_map/ppermute | solution.py:271
  70.6 1.6 collective-permute-done.14.refs_5_
  72.5 2.8 %shard_map.106.refs_2_ = bf16[2,256,384]{2,1,0:T(8,128)(2,1)S(1)} custom-call(bf16[2,128,1280]{2,1,0:T(8,128)(2,1)S(1)} %get-tuple-element.140.refs_0_, bf16[2,128,1280]{2,1,0:T(8,128)(2,1)S(1)} %collective-permute-done.1.refs_1_, bf16[4,128,384]{2,1,0:T(8,128)(2,1)S(1)} %get-tuple-element.176.refs_2_, ...), custom_call_target="tpu_custom_call" | custom-call | flops 1 | bytes 1 | tf_op jit(solution)/shard_map/pallas_call | solution.py:128
  75.3 15.9 %collective-permute-done.21.refs_2_ = bf16[192,640]{1,0:T(8,128)(2,1)S(1)} collective-permute-done((bf16[192,640]{1,0:T(8,128)(2,1)S(1)}, bf16[192,640]{1,0:T(8,128)(2,1)S(1)}, u32[]{:S(2)}, u32[]{:S(2)}) %collective-permute-start.21) | collective-permute-done | bytes 245792 | tf_op jit(solution)/shard_map/ppermute | solution.py:280
  95.5 1.6 %collective-permute-start.27 = (bf16[256,640]{1,0:T(8,128)(2,1)}, bf16[256,640]{1,0:T(8,128)(2,1)}, u32[]{:S(2)}, u32[]{:S(2)}) collective-permute-start(bf16[256,640]{1,0:T(8,128)(2,1)} %slice.29), channel_id=1, source_target_pairs={{0,2},{1,3},{2,0},{3,1},{4,6},{5,7},{6,4},{7,5},{8,10},{9,11},{10,... | collective-permute-start | bytes 983048 | tf_op jit(solution)/shard_map/ppermute | solution.py:271
  97.2 1.9 %shard_map.107.refs_4_ = bf16[2,256,256]{2,1,0:T(8,128)(2,1)S(1)} custom-call(bf16[2,128,1280]{2,1,0:T(8,128)(2,1)S(1)} %get-tuple-element.140.refs_0_, bf16[2,128,1280]{2,1,0:T(8,128)(2,1)S(1)} %collective-permute-done.1.refs_1_, bf16[4,128,256]{2,1,0:T(8,128)(2,1)S(1)} %get-tuple-element.189.refs_2_, ...), custom_call_target="tpu_custom_call" | custom-call | flops 1 | bytes 1 | tf_op jit(solution)/shard_map/pallas_call | solution.py:128
  100.4 1.7 %collective-permute-done.18.refs_3_ = bf16[2,256,384]{2,1,0:T(8,128)(2,1)} collective-permute-done((bf16[2,256,384]{2,1,0:T(8,128)(2,1)S(1)}, bf16[2,256,384]{2,1,0:T(8,128)(2,1)}, u32[]{:S(2)}, u32[]{:S(2)}) %collective-permute-start.18) | collective-permute-done | bytes 393248 | tf_op jit(solution)/shard_map/ppermute | solution.py:277
  102.1 2.4 %collective-permute-done.24.refs_4_ = bf16[256,640]{1,0:T(8,128)(2,1)} collective-permute-done((bf16[256,640]{1,0:T(8,128)(2,1)}, bf16[256,640]{1,0:T(8,128)(2,1)}, u32[]{:S(2)}, u32[]{:S(2)}) %collective-permute-start.24) | collective-permute-done | bytes 327712 | tf_op jit(solution)/shard_map/ppermute | solution.py:271
  104.5 2.0 %collective-permute-done.23.refs_5_ = bf16[2,256,256]{2,1,0:T(8,128)(2,1)} collective-permute-done((bf16[2,256,256]{2,1,0:T(8,128)(2,1)S(1)}, bf16[2,256,256]{2,1,0:T(8,128)(2,1)}, u32[]{:S(2)}, u32[]{:S(2)}) %collective-permute-start.23) | collective-permute-done | bytes 262176 | tf_op jit(solution)/shard_map/ppermute | solution.py:277
  108.9 3.6 %shard_map.109 = (f32[512,640]{1,0:T(8,128)S(1)}, bf16[512,640]{1,0:T(8,128)(2,1)S(1)}) custom-call(bf16[2,1024,640]{2,1,0:T(8,128)(2,1)S(1)} %shard_map.108.acts_ref, bf16[320,640]{1,0:T(8,128)(2,1)S(1)} %get-tuple-element.276.refs_0_, bf16[320,640]{1,0:T(8,128)(2,1)S(1)} %get-tuple-element.277.refs_1_, bf16[192,640]{1,0:T(8,128)(2,1)S(1)} %copy-done.12, ...), custom_call_target="tpu_custom_call" | custom-call | flops 1 | bytes 1 | tf_op jit(solution)/shard_map/pallas_call | solution.py:186
  112.7 3.6 %shard_map.110 = (f32[512,640]{1,0:T(8,128)S(1)}, bf16[512,640]{1,0:T(8,128)(2,1)S(1)}) custom-call(bf16[2,1024,640]{2,1,0:T(8,128)(2,1)S(1)} %shard_map.108.acts_ref, bf16[320,640]{1,0:T(8,128)(2,1)S(1)} %copy-done.8, bf16[320,640]{1,0:T(8,128)(2,1)S(1)} %collective-permute-done.7.refs_1_, bf16[192,640]{1,0:T(8,128)(2,1)S(1)} %copy-done.16, ...), custom_call_target="tpu_custom_call" | custom-call | flops 1 | bytes 1 | tf_op jit(solution)/shard_map/pallas_call | solution.py:186
  116.3 6.7 %collective-permute-done.26.refs_3_ = bf16[192,640]{1,0:T(8,128)(2,1)S(1)} collective-permute-done((bf16[192,640]{1,0:T(8,128)(2,1)}, bf16[192,640]{1,0:T(8,128)(2,1)S(1)}, u32[]{:S(2)}, u32[]{:S(2)}) %collective-permute-start.26) | collective-permute-done | bytes 245792 | tf_op jit(solution)/shard_map/ppermute | solution.py:280
  123.3 1.6 collective-permute-start.32
  124.9 2.5 %shard_map.113 = (f32[512,640]{1,0:T(8,128)S(1)}, bf16[512,640]{1,0:T(8,128)(2,1)S(1)}) custom-call(bf16[2,1024,640]{2,1,0:T(8,128)(2,1)S(1)} %shard_map.108.acts_ref, bf16[320,640]{1,0:T(8,128)(2,1)S(1)} %copy-done.6, bf16[320,640]{1,0:T(8,128)(2,1)S(1)} %collective-permute-done.16.refs_1_, bf16[192,640]{1,0:T(8,128)(2,1)S(1)} %copy-done.14, ...), custom_call_target="tpu_custom_call" | custom-call | flops 1 | bytes 1 | tf_op jit(solution)/shard_map/pallas_call | solution.py:186
  127.4 7.4 %collective-permute-done.28.refs_3_ = bf16[192,640]{1,0:T(8,128)(2,1)S(1)} collective-permute-done((bf16[192,640]{1,0:T(8,128)(2,1)S(1)}, bf16[192,640]{1,0:T(8,128)(2,1)S(1)}, u32[]{:S(2)}, u32[]{:S(2)}) %collective-permute-start.28) | collective-permute-done | bytes 245792 | tf_op jit(solution)/shard_map/ppermute | solution.py:280
  134.8 2.5 %shard_map.112 = (f32[512,640]{1,0:T(8,128)S(1)}, bf16[512,640]{1,0:T(8,128)(2,1)S(1)}) custom-call(bf16[2,1024,640]{2,1,0:T(8,128)(2,1)S(1)} %shard_map.108.acts_ref, bf16[320,640]{1,0:T(8,128)(2,1)S(1)} %copy-done.10, bf16[320,640]{1,0:T(8,128)(2,1)S(1)} %collective-permute-done.19.refs_1_, bf16[192,640]{1,0:T(8,128)(2,1)S(1)} %copy-done.18, ...), custom_call_target="tpu_custom_call" | custom-call | flops 1 | bytes 1 | tf_op jit(solution)/shard_map/pallas_call | solution.py:186
  141.7 6.9 %collective-permute-done.36.refs_3_ = bf16[2,128,640]{2,1,0:T(8,128)(2,1)S(1)} collective-permute-done((bf16[2,128,640]{2,1,0:T(8,128)(2,1)S(1)}, bf16[2,128,640]{2,1,0:T(8,128)(2,1)S(1)}, u32[]{:S(2)}, u32[]{:S(2)}) %collective-permute-start.36) | collective-permute-done | bytes 327712 | tf_op jit(solution)/shard_map/ppermute | solution.py:277
  148.6 7.0 %collective-permute-done.37.refs_5_ = bf16[2,128,640]{2,1,0:T(8,128)(2,1)S(1)} collective-permute-done((bf16[2,128,640]{2,1,0:T(8,128)(2,1)S(1)}, bf16[2,128,640]{2,1,0:T(8,128)(2,1)S(1)}, u32[]{:S(2)}, u32[]{:S(2)}) %collective-permute-start.37) | collective-permute-done | bytes 327712 | tf_op jit(solution)/shard_map/ppermute | solution.py:277
  155.6 6.1 %collective-permute-done.38.refs_7_ = bf16[2,128,640]{2,1,0:T(8,128)(2,1)S(1)} collective-permute-done((bf16[2,128,640]{2,1,0:T(8,128)(2,1)}, bf16[2,128,640]{2,1,0:T(8,128)(2,1)S(1)}, u32[]{:S(2)}, u32[]{:S(2)}) %collective-permute-start.38) | collective-permute-done | bytes 327712 | tf_op jit(solution)/shard_map/ppermute | solution.py:277
  161.8 2.2 %shard_map.117 = (bf16[128,5120]{1,0:T(8,128)(2,1)}, bf16[128,5120]{1,0:T(8,128)(2,1)}) custom-call(s32[8]{0:T(128)S(1)} %broadcast_add_fusion.where_ref, bf16[2,128,640]{2,1,0:T(8,128)(2,1)S(1)} %get-tuple-element.266.refs_0_, bf16[2,128,640]{2,1,0:T(8,128)(2,1)S(1)} %collective-permute-done.32.refs_1_, ...), custom_call_target="tpu_custom_call" | custom-call | flops 1 | bytes 1 | tf_op jit(solution)/shard_map/pallas_call | solution.py:235
  (110 shorter events, 32.2 us)
Async XLA Ops:
  1.8 10.4 %collective-permute-start = (bf16[192,640]{1,0:T(8,128)(2,1)S(1)}, bf16[192,640]{1,0:T(8,128)(2,1)S(1)}, u32[]{:S(2)}, u32[]{:S(2)}) collective-permute-start(bf16[192,640]{1,0:T(8,128)(2,1)S(1)} %get-tuple-element.275), channel_id=1, source_target_pairs={{0,2},{1,3},{2,0},{3,1},{4,6},{5,7},{6,4},{7,5},{8,10},{9,11},{10,... | collective-permute-start | bytes 737288 | tf_op jit(solution)/shard_map/ppermute | solution.py:271
  13.4 17.6 %collective-permute-start.5 = (bf16[4,128,640]{2,1,0:T(8,128)(2,1)S(1)}, bf16[4,128,640]{2,1,0:T(8,128)(2,1)S(1)}, u32[]{:S(2)}, u32[]{:S(2)}) collective-permute-start(bf16[4,128,640]{2,1,0:T(8,128)(2,1)S(1)} %get-tuple-element.164.refs_2_), channel_id=1, source_target_pairs={{0,2},{1,3},{2,0},{3,1},{4,6},{5,7},{6,4},{7,5},{8,10},{9,11},{10,... | collective-permute-start | bytes 1966088 | tf_op jit(solution)/shard_map/ppermute | solution.py:271
  14.4 19.4 %collective-permute-start.8 = (bf16[320,640]{1,0:T(8,128)(2,1)S(1)}, bf16[320,640]{1,0:T(8,128)(2,1)S(1)}, u32[]{:S(2)}, u32[]{:S(2)}) collective-permute-start(bf16[320,640]{1,0:T(8,128)(2,1)S(1)} %get-tuple-element.276.refs_0_), channel_id=1, source_target_pairs={{0,8},{4,12},{8,16},{12,20},{16,24},{20,28},{24,0},{28,4},{1,9},{5... | collective-permute-start | bytes 1228808 | tf_op jit(solution)/shard_map/ppermute | solution.py:280
  16.0 29.0 %collective-permute-start.6 = (bf16[4,128,640]{2,1,0:T(8,128)(2,1)S(1)}, bf16[4,128,640]{2,1,0:T(8,128)(2,1)S(1)}, u32[]{:S(2)}, u32[]{:S(2)}) collective-permute-start(bf16[4,128,640]{2,1,0:T(8,128)(2,1)S(1)} %collective-permute-done.4.refs_3_), channel_id=1, source_target_pairs={{0,2},{1,3},{2,0},{3,1},{4,6},{5,7},{6,4},{7,5},{8,10},{9,11},{10,... | collective-permute-start | bytes 1966088 | tf_op jit(solution)/shard_map/ppermute | solution.py:271
  17.1 16.7 %collective-permute-start.9 = (bf16[192,640]{1,0:T(8,128)(2,1)S(1)}, bf16[192,640]{1,0:T(8,128)(2,1)S(1)}, u32[]{:S(2)}, u32[]{:S(2)}) collective-permute-start(bf16[192,640]{1,0:T(8,128)(2,1)S(1)} %collective-permute-done.refs_2_), channel_id=1, source_target_pairs={{0,8},{4,12},{8,16},{12,20},{16,24},{20,28},{24,0},{28,4},{1,9},{5... | collective-permute-start | bytes 737288 | tf_op jit(solution)/shard_map/ppermute | solution.py:280
  18.7 23.9 %collective-permute-start.7 = (bf16[320,640]{1,0:T(8,128)(2,1)S(1)}, bf16[320,640]{1,0:T(8,128)(2,1)S(1)}, u32[]{:S(2)}, u32[]{:S(2)}) collective-permute-start(bf16[320,640]{1,0:T(8,128)(2,1)S(1)} %get-tuple-element.277.refs_1_), channel_id=1, source_target_pairs={{0,8},{4,12},{8,16},{12,20},{16,24},{20,28},{24,0},{28,4},{1,9},{5... | collective-permute-start | bytes 1228808 | tf_op jit(solution)/shard_map/ppermute | solution.py:280
  33.8 22.8 %collective-permute-start.10 = (bf16[320,640]{1,0:T(8,128)(2,1)S(1)}, bf16[320,640]{1,0:T(8,128)(2,1)S(1)}, u32[]{:S(2)}, u32[]{:S(2)}) collective-permute-start(bf16[320,640]{1,0:T(8,128)(2,1)S(1)} %collective-permute-done.8.refs_0_), channel_id=1, source_target_pairs={{0,8},{4,12},{8,16},{12,20},{16,24},{20,28},{24,0},{28,4},{1,9},{5... | collective-permute-start | bytes 1228808 | tf_op jit(solution)/shard_map/ppermute | solution.py:280
  33.9 19.5 %collective-permute-start.12 = (bf16[4,128,384]{2,1,0:T(8,128)(2,1)S(1)}, bf16[4,128,384]{2,1,0:T(8,128)(2,1)S(1)}, u32[]{:S(2)}, u32[]{:S(2)}) collective-permute-start(bf16[4,128,384]{2,1,0:T(8,128)(2,1)S(1)} %get-tuple-element.176.refs_2_), channel_id=1, source_target_pairs={{0,2},{1,3},{2,0},{3,1},{4,6},{5,7},{6,4},{7,5},{8,10},{9,11},{10,... | collective-permute-start | bytes 1179656 | tf_op jit(solution)/shard_map/ppermute | solution.py:271
  35.1 21.6 %collective-permute-start.11 = (bf16[192,640]{1,0:T(8,128)(2,1)S(1)}, bf16[192,640]{1,0:T(8,128)(2,1)S(1)}, u32[]{:S(2)}, u32[]{:S(2)}) collective-permute-start(bf16[192,640]{1,0:T(8,128)(2,1)S(1)} %collective-permute-done.9.refs_2_), channel_id=1, source_target_pairs={{0,8},{4,12},{8,16},{12,20},{16,24},{20,28},{24,0},{28,4},{1,9},{5... | collective-permute-start | bytes 737288 | tf_op jit(solution)/shard_map/ppermute | solution.py:280
  42.6 22.1 %collective-permute-start.16 = (bf16[320,640]{1,0:T(8,128)(2,1)S(1)}, bf16[320,640]{1,0:T(8,128)(2,1)S(1)}, u32[]{:S(2)}, u32[]{:S(2)}) collective-permute-start(bf16[320,640]{1,0:T(8,128)(2,1)S(1)} %collective-permute-done.7.refs_1_), channel_id=1, source_target_pairs={{0,8},{4,12},{8,16},{12,20},{16,24},{20,28},{24,0},{28,4},{1,9},{5... | collective-permute-start | bytes 1228808 | tf_op jit(solution)/shard_map/ppermute | solution.py:280
  45.0 24.1 %collective-permute-start.15 = (bf16[4,128,384]{2,1,0:T(8,128)(2,1)S(1)}, bf16[4,128,384]{2,1,0:T(8,128)(2,1)S(1)}, u32[]{:S(2)}, u32[]{:S(2)}) collective-permute-start(bf16[4,128,384]{2,1,0:T(8,128)(2,1)S(1)} %collective-permute-done.3.refs_3_), channel_id=1, source_target_pairs={{0,2},{1,3},{2,0},{3,1},{4,6},{5,7},{6,4},{7,5},{8,10},{9,11},{10,... | collective-permute-start | bytes 1179656 | tf_op jit(solution)/shard_map/ppermute | solution.py:271
  56.6 38.0 %collective-permute-start.13 = (bf16[2,256,640]{2,1,0:T(8,128)(2,1)S(1)}, bf16[2,256,640]{2,1,0:T(8,128)(2,1)S(1)}, u32[]{:S(2)}, u32[]{:S(2)}) collective-permute-start(bf16[2,256,640]{2,1,0:T(8,128)(2,1)S(1)} %shard_map.105.refs_0_), channel_id=1, source_target_pairs={{0,4},{4,0},{8,12},{12,8},{16,20},{20,16},{24,28},{28,24},{1,5},{5... | collective-permute-start | bytes 1966088 | tf_op jit(solution)/shard_map/ppermute | solution.py:277
  58.2 9.2 %collective-permute-start.17 = (bf16[4,128,256]{2,1,0:T(8,128)(2,1)S(1)}, bf16[4,128,256]{2,1,0:T(8,128)(2,1)S(1)}, u32[]{:S(2)}, u32[]{:S(2)}) collective-permute-start(bf16[4,128,256]{2,1,0:T(8,128)(2,1)S(1)} %get-tuple-element.189.refs_2_), channel_id=1, source_target_pairs={{0,2},{1,3},{2,0},{3,1},{4,6},{5,7},{6,4},{7,5},{8,10},{9,11},{10,... | collective-permute-start | bytes 786440 | tf_op jit(solution)/shard_map/ppermute | solution.py:271
  59.3 12.9 %collective-permute-start.14 = (bf16[4,128,256]{2,1,0:T(8,128)(2,1)S(1)}, bf16[4,128,256]{2,1,0:T(8,128)(2,1)S(1)}, u32[]{:S(2)}, u32[]{:S(2)}) collective-permute-start(bf16[4,128,256]{2,1,0:T(8,128)(2,1)S(1)} %collective-permute-done.2.refs_3_), channel_id=1, source_target_pairs={{0,2},{1,3},{2,0},{3,1},{4,6},{5,7},{6,4},{7,5},{8,10},{9,11},{10,... | collective-permute-start | bytes 786440 | tf_op jit(solution)/shard_map/ppermute | solution.py:271
  64.7 34.4 %collective-permute-start.19 = (bf16[320,640]{1,0:T(8,128)(2,1)S(1)}, bf16[320,640]{1,0:T(8,128)(2,1)S(1)}, u32[]{:S(2)}, u32[]{:S(2)}) collective-permute-start(bf16[320,640]{1,0:T(8,128)(2,1)S(1)} %collective-permute-done.16.refs_1_), channel_id=1, source_target_pairs={{0,8},{4,12},{8,16},{12,20},{16,24},{20,28},{24,0},{28,4},{1,9},{5... | collective-permute-start | bytes 1228808 | tf_op jit(solution)/shard_map/ppermute | solution.py:280
  67.5 32.2 %collective-permute-start.20 = (bf16[320,640]{1,0:T(8,128)(2,1)S(1)}, bf16[320,640]{1,0:T(8,128)(2,1)S(1)}, u32[]{:S(2)}, u32[]{:S(2)}) collective-permute-start(bf16[320,640]{1,0:T(8,128)(2,1)S(1)} %collective-permute-done.10.refs_0_), channel_id=1, source_target_pairs={{0,8},{4,12},{8,16},{12,20},{16,24},{20,28},{24,0},{28,4},{1,9},{5... | collective-permute-start | bytes 1228808 | tf_op jit(solution)/shard_map/ppermute | solution.py:280
  69.0 22.2 %collective-permute-start.21 = (bf16[192,640]{1,0:T(8,128)(2,1)S(1)}, bf16[192,640]{1,0:T(8,128)(2,1)S(1)}, u32[]{:S(2)}, u32[]{:S(2)}) collective-permute-start(bf16[192,640]{1,0:T(8,128)(2,1)S(1)} %collective-permute-done.11.refs_2_), channel_id=1, source_target_pairs={{0,8},{4,12},{8,16},{12,20},{16,24},{20,28},{24,0},{28,4},{1,9},{5... | collective-permute-start | bytes 737288 | tf_op jit(solution)/shard_map/ppermute | solution.py:280
  72.2 21.3 %collective-permute-start.22 = (bf16[192,640]{1,0:T(8,128)(2,1)S(1)}, bf16[192,640]{1,0:T(8,128)(2,1)}, u32[]{:S(2)}, u32[]{:S(2)}) collective-permute-start(bf16[192,640]{1,0:T(8,128)(2,1)S(1)} %get-tuple-element.201), channel_id=1, source_target_pairs={{0,2},{1,3},{2,0},{3,1},{4,6},{5,7},{6,4},{7,5},{8,10},{9,11},{10,... | collective-permute-start | bytes 737288 | tf_op jit(solution)/shard_map/ppermute | solution.py:271
  91.3 10.9 %collective-permute-start.18 = (bf16[2,256,384]{2,1,0:T(8,128)(2,1)S(1)}, bf16[2,256,384]{2,1,0:T(8,128)(2,1)}, u32[]{:S(2)}, u32[]{:S(2)}) collective-permute-start(bf16[2,256,384]{2,1,0:T(8,128)(2,1)S(1)} %shard_map.106.refs_2_), channel_id=1, source_target_pairs={{0,4},{4,0},{8,12},{12,8},{16,20},{20,16},{24,28},{28,24},{1,5},{5... | collective-permute-start | bytes 1179656 | tf_op jit(solution)/shard_map/ppermute | solution.py:277
  93.5 11.0 %collective-permute-start.24 = (bf16[256,640]{1,0:T(8,128)(2,1)}, bf16[256,640]{1,0:T(8,128)(2,1)}, u32[]{:S(2)}, u32[]{:S(2)}) collective-permute-start(bf16[256,640]{1,0:T(8,128)(2,1)} %slice.28), channel_id=1, source_target_pairs={{0,2},{1,3},{2,0},{3,1},{4,6},{5,7},{6,4},{7,5},{8,10},{9,11},{10,... | collective-permute-start | bytes 983048 | tf_op jit(solution)/shard_map/ppermute | solution.py:271
  95.5 17.0 %collective-permute-start.27 = (bf16[256,640]{1,0:T(8,128)(2,1)}, bf16[256,640]{1,0:T(8,128)(2,1)}, u32[]{:S(2)}, u32[]{:S(2)}) collective-permute-start(bf16[256,640]{1,0:T(8,128)(2,1)} %slice.29), channel_id=1, source_target_pairs={{0,2},{1,3},{2,0},{3,1},{4,6},{5,7},{6,4},{7,5},{8,10},{9,11},{10,... | collective-permute-start | bytes 983048 | tf_op jit(solution)/shard_map/ppermute | solution.py:271
  100.4 12.1 %collective-permute-start.25 = (bf16[192,640]{1,0:T(8,128)(2,1)}, bf16[192,640]{1,0:T(8,128)(2,1)}, u32[]{:S(2)}, u32[]{:S(2)}) collective-permute-start(bf16[192,640]{1,0:T(8,128)(2,1)} %collective-permute-done.22.refs_3_), channel_id=1, source_target_pairs={{0,8},{4,12},{8,16},{12,20},{16,24},{20,28},{24,0},{28,4},{1,9},{5... | collective-permute-start | bytes 737288 | tf_op jit(solution)/shard_map/ppermute | solution.py:280
  102.1 20.9 %collective-permute-start.30 = (bf16[256,640]{1,0:T(8,128)(2,1)S(1)}, bf16[256,640]{1,0:T(8,128)(2,1)S(1)}, u32[]{:S(2)}, u32[]{:S(2)}) collective-permute-start(bf16[256,640]{1,0:T(8,128)(2,1)S(1)} %slice.30), channel_id=1, source_target_pairs={{0,2},{1,3},{2,0},{3,1},{4,6},{5,7},{6,4},{7,5},{8,10},{9,11},{10,... | collective-permute-start | bytes 983048 | tf_op jit(solution)/shard_map/ppermute | solution.py:271
  112.5 10.6 %collective-permute-start.29 = (bf16[512,640]{1,0:T(8,128)(2,1)S(1)}, bf16[512,640]{1,0:T(8,128)(2,1)S(1)}, u32[]{:S(2)}, u32[]{:S(2)}) collective-permute-start(bf16[512,640]{1,0:T(8,128)(2,1)S(1)} %get-tuple-element.227), channel_id=1, source_target_pairs={{0,1},{1,0},{2,3},{3,2},{4,5},{5,4},{6,7},{7,6},{8,9},{9,8},{10,11... | collective-permute-start | bytes 1966088 | tf_op jit(solution)/shard_map/ppermute | solution.py:274
  112.6 10.4 %collective-permute-start.26 = (bf16[192,640]{1,0:T(8,128)(2,1)}, bf16[192,640]{1,0:T(8,128)(2,1)S(1)}, u32[]{:S(2)}, u32[]{:S(2)}) collective-permute-start(bf16[192,640]{1,0:T(8,128)(2,1)} %collective-permute-done.25.refs_3_), channel_id=1, source_target_pairs={{0,8},{4,12},{8,16},{12,20},{16,24},{20,28},{24,0},{28,4},{1,9},{5... | collective-permute-start | bytes 737288 | tf_op jit(solution)/shard_map/ppermute | solution.py:280
  123.0 14.3 %collective-permute-start.33 = (bf16[512,640]{1,0:T(8,128)(2,1)S(1)}, bf16[512,640]{1,0:T(8,128)(2,1)S(1)}, u32[]{:S(2)}, u32[]{:S(2)}) collective-permute-start(bf16[512,640]{1,0:T(8,128)(2,1)S(1)} %get-tuple-element.244), channel_id=1, source_target_pairs={{0,1},{1,0},{2,3},{3,2},{4,5},{5,4},{6,7},{7,6},{8,9},{9,8},{10,11... | collective-permute-start | bytes 1966088 | tf_op jit(solution)/shard_map/ppermute | solution.py:274
  123.1 11.7 %collective-permute-start.31 = (bf16[256,640]{1,0:T(8,128)(2,1)S(1)}, bf16[256,640]{1,0:T(8,128)(2,1)S(1)}, u32[]{:S(2)}, u32[]{:S(2)}) collective-permute-start(bf16[256,640]{1,0:T(8,128)(2,1)S(1)} %slice.31), channel_id=1, source_target_pairs={{0,2},{1,3},{2,0},{3,1},{4,6},{5,7},{6,4},{7,5},{8,10},{9,11},{10,... | collective-permute-start | bytes 983048 | tf_op jit(solution)/shard_map/ppermute | solution.py:271
  123.3 14.1 %collective-permute-start.32 = (bf16[2,128,640]{2,1,0:T(8,128)(2,1)S(1)}, bf16[2,128,640]{2,1,0:T(8,128)(2,1)S(1)}, u32[]{:S(2)}, u32[]{:S(2)}) collective-permute-start(bf16[2,128,640]{2,1,0:T(8,128)(2,1)S(1)} %get-tuple-element.242), channel_id=1, source_target_pairs={{0,4},{4,0},{8,12},{12,8},{16,20},{20,16},{24,28},{28,24},{1,5},{5... | collective-permute-start | bytes 983048 | tf_op jit(solution)/shard_map/ppermute | solution.py:277
  124.9 9.9 %collective-permute-start.28 = (bf16[192,640]{1,0:T(8,128)(2,1)S(1)}, bf16[192,640]{1,0:T(8,128)(2,1)S(1)}, u32[]{:S(2)}, u32[]{:S(2)}) collective-permute-start(bf16[192,640]{1,0:T(8,128)(2,1)S(1)} %collective-permute-done.26.refs_3_), channel_id=1, source_target_pairs={{0,8},{4,12},{8,16},{12,20},{16,24},{20,28},{24,0},{28,4},{1,9},{5... | collective-permute-start | bytes 737288 | tf_op jit(solution)/shard_map/ppermute | solution.py:280
  138.0 10.6 %collective-permute-start.36 = (bf16[2,128,640]{2,1,0:T(8,128)(2,1)S(1)}, bf16[2,128,640]{2,1,0:T(8,128)(2,1)S(1)}, u32[]{:S(2)}, u32[]{:S(2)}) collective-permute-start(bf16[2,128,640]{2,1,0:T(8,128)(2,1)S(1)} %get-tuple-element.269), channel_id=1, source_target_pairs={{0,4},{4,0},{8,12},{12,8},{16,20},{20,16},{24,28},{28,24},{1,5},{5... | collective-permute-start | bytes 983048 | tf_op jit(solution)/shard_map/ppermute | solution.py:277
  138.7 16.9 %collective-permute-start.37 = (bf16[2,128,640]{2,1,0:T(8,128)(2,1)S(1)}, bf16[2,128,640]{2,1,0:T(8,128)(2,1)S(1)}, u32[]{:S(2)}, u32[]{:S(2)}) collective-permute-start(bf16[2,128,640]{2,1,0:T(8,128)(2,1)S(1)} %get-tuple-element.271), channel_id=1, source_target_pairs={{0,4},{4,0},{8,12},{12,8},{16,20},{20,16},{24,28},{28,24},{1,5},{5... | collective-permute-start | bytes 983048 | tf_op jit(solution)/shard_map/ppermute | solution.py:277
  141.0 20.7 %collective-permute-start.38 = (bf16[2,128,640]{2,1,0:T(8,128)(2,1)}, bf16[2,128,640]{2,1,0:T(8,128)(2,1)S(1)}, u32[]{:S(2)}, u32[]{:S(2)}) collective-permute-start(bf16[2,128,640]{2,1,0:T(8,128)(2,1)} %get-tuple-element.273), channel_id=1, source_target_pairs={{0,4},{4,0},{8,12},{12,8},{16,20},{20,16},{24,28},{28,24},{1,5},{5... | collective-permute-start | bytes 983048 | tf_op jit(solution)/shard_map/ppermute | solution.py:277
  (27 other events, 196.0 us)

commit v2 on v1

v2 whole, which is shorter than its diff:
```python
import functools

import jax
import jax.numpy as jnp
from jax import lax
from jax.experimental import pallas as pl
from jax.experimental.pallas import tpu as pltpu
from jax.sharding import PartitionSpec as P

HEADS = 20
EPS = 1e-06
VMEM_BYTES = 48 * 1024 * 1024
ROW_STEP = 32

LOW = jnp.bfloat16
WIDE = jnp.float32
LIGHT = pl.CostEstimate(flops=1, transcendentals=0, bytes_accessed=1)


def params():
    return pltpu.CompilerParams(vmem_limit_bytes=VMEM_BYTES)


def vmem_specs(count):
    return [pl.BlockSpec(memory_space=pltpu.VMEM)] * count


def pack_kernel(n_seq, chunks, core_ref, *refs):
    query_ref, key_ref, value_ref, dquery_ref, dkey_ref, dvalue_ref, gains_ref = refs[:7]
    out_refs = refs[7:]
    n_chunks = len(chunks)
    group = query_ref.shape[-1] // n_seq

    def statistics(primal_ref, tangent_ref):
        primal = primal_ref[...].astype(WIDE)
        tangent = tangent_ref[...].astype(WIDE)
        inverse = lax.rsqrt(jnp.mean(primal * primal, axis=-1, keepdims=True) + EPS)
        across = jnp.mean(primal * tangent, axis=-1, keepdims=True)
        return inverse, inverse * inverse * inverse * across

    query_stats = statistics(query_ref, dquery_ref)
    key_stats = statistics(key_ref, dkey_ref)

    def normed(primal_ref, tangent_ref, which, stats, lanes):
        primal = primal_ref[:, lanes].astype(WIDE)
        tangent = tangent_ref[:, lanes].astype(WIDE)
        gain = gains_ref[which : which + 1, lanes]
        inverse, slope = stats
        return (primal * inverse * gain).astype(LOW), (gain * (tangent * inverse - primal * slope)).astype(LOW)

    for side in range(2):
        core = core_ref[0] if side == 0 else 1 - core_ref[0]
        queries_ref, *keyed_refs = out_refs[side * (1 + n_chunks) : (side + 1) * (1 + n_chunks)]
        for at in range(n_seq // 2):
            lanes = pl.ds(pl.multiple_of((2 * at + core) * group, 128), group)
            here = slice(at * group, (at + 1) * group)
            plain, dual = normed(query_ref, dquery_ref, 0, query_stats, lanes)
            queries_ref[0, :, here] = plain
            queries_ref[1, :, here] = dual
            four = normed(key_ref, dkey_ref, 1, key_stats, lanes)
            four += (value_ref[:, lanes], dvalue_ref[:, lanes])
            start = 0
            for keyed_ref, width in zip(keyed_refs, chunks):
                low, high = max(start, here.start), min(start + width, here.stop)
                if low < high:
                    for which, part in enumerate(four):
                        keyed_ref[which, :, low - start : high - start] = part[:, low - here.start : high - here.start]
                start += width


def pack(core, n_seq, chunks, arrays, gains):
    rows, features = arrays[0].shape
    step = min(rows, ROW_STEP)
    row_block = pl.BlockSpec((step, features), lambda i, c: (i, 0))
    gain_block = pl.BlockSpec((2, features), lambda i, c: (0, 0))
    kinds = [(2, features // 2)] + [(4, width) for width in chunks]
    kinds = kinds + kinds
    return pl.pallas_call(
        functools.partial(pack_kernel, n_seq, chunks),
        grid_spec=pltpu.PrefetchScalarGridSpec(
            num_scalar_prefetch=1,
            grid=(rows // step,),
            in_specs=[row_block] * 6 + [gain_block],
            out_specs=[pl.BlockSpec((count, step, width), lambda i, c: (0, i, 0)) for count, width in kinds],
        ),
        out_shape=[jax.ShapeDtypeStruct((count, rows, width), LOW) for count, width in kinds],
        compiler_params=params(),
        cost_estimate=LIGHT,
    )(core, *arrays, gains)


def attend_kernel(n_queries, *refs):
    query_refs, keyed_refs, out_ref = refs[:n_queries], refs[n_queries:-1], refs[-1]

    def stack(which, some_refs, kinds):
        parts = [ref[at] for ref in some_refs for at in range(which, ref.shape[0], kinds)]
        return jnp.concatenate(parts, axis=0)

    query, query_dual = (stack(which, query_refs, 2) for which in range(2))
    key, key_dual, value, value_dual = (stack(which, keyed_refs, 4) for which in range(4))
    factor = query.shape[-1] ** (-0.5)
    last = (((1,), (1,)), ((), ()))
    scores = lax.dot_general(query, key, last, preferred_element_type=WIDE) * factor
    dual_scores = (
        lax.dot_general(
            jnp.concatenate([query_dual, query], axis=1),
            jnp.concatenate([key, key_dual], axis=1),
            last,
            preferred_element_type=WIDE,
        )
        * factor
    )
    raised = jnp.exp(scores - jnp.max(scores, axis=-1, keepdims=True))
    probs = raised * (1.0 / jnp.sum(raised, axis=-1, keepdims=True))
    spread = probs * (dual_scores - jnp.sum(probs * dual_scores, axis=-1, keepdims=True))
    probs_low = probs.astype(LOW)
    spread_low = spread.astype(LOW)
    out_ref[0] = jnp.dot(probs_low, value, preferred_element_type=WIDE).astype(LOW)
    out_ref[1] = (
        jnp.dot(probs_low, value_dual, preferred_element_type=WIDE)
        + jnp.dot(spread_low, value, preferred_element_type=WIDE)
    ).astype(LOW)


def attend(start, hdim, queries, keyed):
    rows = queries[0].shape[1]
    width = keyed[0].shape[2]
    first = start // hdim
    return pl.pallas_call(
        functools.partial(attend_kernel, len(queries)),
        grid=(width // hdim,),
        in_specs=[pl.BlockSpec((2, rows, hdim), lambda h: (0, 0, first + h))] * len(queries)
        + [pl.BlockSpec((array.shape[0], rows, hdim), lambda h: (0, 0, h)) for array in keyed],
        out_specs=pl.BlockSpec((2, len(queries) * rows, hdim), lambda h: (0, 0, h)),
        out_shape=jax.ShapeDtypeStruct((2, len(queries) * rows, width), LOW),
        compiler_params=params(),
        cost_estimate=LIGHT,
    )(*queries, *keyed)


def assemble_kernel(chunks, flip_ref, *refs):
    part_refs, out_ref = refs[:-1], refs[-1]
    groups, rows_all, group = out_ref.shape
    rows = rows_all // 8
    start = 0
    for at, width in enumerate(chunks):
        for side in range(2):
            part_ref = part_refs[2 * at + side]
            for kind in range(2):
                for core in range(2):
                    first = (4 * core + 2 * side + kind) * rows
                    for g in range(groups):
                        low, high = max(start, g * group), min(start + width, (g + 1) * group)
                        if low < high:
                            out_ref[g ^ flip_ref[0], first : first + rows, low - g * group : high - g * group] = (
                                part_ref[kind, core * rows : (core + 1) * rows, low - start : high - start]
                            )
        start += width


def assemble(flip, groups, chunks, pairs):
    rows = 4 * pairs[0][0].shape[1]
    return pl.pallas_call(
        functools.partial(assemble_kernel, chunks),
        in_specs=[pl.BlockSpec(memory_space=pltpu.SMEM)] + vmem_specs(2 * len(pairs)),
        out_specs=vmem_specs(1)[0],
        out_shape=jax.ShapeDtypeStruct((groups, rows, sum(chunks) // groups), LOW),
        compiler_params=params(),
        cost_estimate=LIGHT,
    )(flip, *[part for pair in pairs for part in pair])


def project_kernel(spans, acts_ref, *refs):
    weight_refs = refs[:-4]
    keep_mine_ref, keep_other_ref, send_mine_ref, send_other_ref = refs[-4:]
    rows = keep_mine_ref.shape[0]
    total = 0.0
    for at, block in enumerate(spans):
        weight = jnp.concatenate([weight_refs[which][low:high] for which, low, high in block], axis=0)
        total = total + jnp.dot(acts_ref[at], weight, preferred_element_type=WIDE)
    keep_mine_ref[...] = total[:rows]
    keep_other_ref[...] = total[rows : 2 * rows]
    send_mine_ref[...] = total[2 * rows : 3 * rows].astype(LOW)
    send_other_ref[...] = total[3 * rows :].astype(LOW)


def project(acts, *blocks):
    weights, spans = [], []
    for block in blocks:
        spans.append([])
        for weight, low, high in block:
            if not any(weight is known for known in weights):
                weights.append(weight)
            which = [weight is known for known in weights].index(True)
            spans[-1].append((which, low, high))
    rows, n = acts.shape[1] // 4, weights[0].shape[1]
    return pl.pallas_call(
        functools.partial(project_kernel, spans),
        in_specs=vmem_specs(1 + len(weights)),
        out_specs=vmem_specs(4),
        out_shape=[jax.ShapeDtypeStruct((rows, n), WIDE)] * 2 + [jax.ShapeDtypeStruct((rows, n), LOW)] * 2,
        compiler_params=params(),
        cost_estimate=LIGHT,
    )(acts, *weights)


def close_kernel(keep_ref, got_ref, out_ref):
    out_ref[...] = (keep_ref[...] + got_ref[...].astype(WIDE)).astype(LOW)


def close(keep, got):
    return pl.pallas_call(
        close_kernel,
        in_specs=vmem_specs(2),
        out_specs=vmem_specs(1)[0],
        out_shape=jax.ShapeDtypeStruct(keep.shape, LOW),
        compiler_params=params(),
        cost_estimate=LIGHT,
    )(keep, got)


def place_kernel(n_steps, where_ref, *refs):
    keep_refs, got_refs, other_refs = refs[:n_steps], refs[n_steps : 2 * n_steps], refs[2 * n_steps : -2]
    plain_ref, dual_ref = refs[-2:]
    rows, n = plain_ref.shape[0], other_refs[0].shape[-1]
    for step in range(n_steps):
        mine, others = (pl.ds(pl.multiple_of(where_ref[2 * step + side] * n, n), n) for side in range(2))
        for kind, out_ref in enumerate((plain_ref, dual_ref)):
            here = slice(kind * rows, (kind + 1) * rows)
            out_ref[:, mine] = (keep_refs[step][here] + got_refs[step][here].astype(WIDE)).astype(LOW)
            out_ref[:, others] = other_refs[step][here]


def place(where, keeps, gots, others):
    rows, n = others[0].shape[0] // 2, others[0].shape[1]
    width = 2 * n * len(others)
    if n % 128:
        out = jnp.zeros((2 * rows, width), LOW)
        for step, (keep, got, other) in enumerate(zip(keeps, gots, others)):
            for side, piece in enumerate((close(keep, got), other)):
                out = lax.dynamic_update_slice(out, piece, (0, where[2 * step + side] * n))
        return out[:rows], out[rows:]
    out = jax.ShapeDtypeStruct((rows, width), LOW)
    return pl.pallas_call(
        functools.partial(place_kernel, len(others)),
        in_specs=[pl.BlockSpec(memory_space=pltpu.SMEM)] + vmem_specs(3 * len(others)),
        out_specs=vmem_specs(2),
        out_shape=[out, out],
        compiler_params=params(),
        cost_estimate=LIGHT,
    )(where, *keeps, *gots, *others)


def body(
    n_dp,
    n_seq,
    queries,
    key_states,
    value_states,
    query_tangent,
    key_tangent,
    value_tangent,
    query_gain,
    key_gain,
    out_weight,
):
    dp = lax.axis_index("dp")
    seq = lax.axis_index("seq")
    n_ring = n_dp // 2
    groups = n_seq // 2
    features = queries.shape[1]
    hdim = features // HEADS
    group_heads = HEADS // n_seq
    few = group_heads * 2 // 5
    chunks = [group_heads * hdim] * (groups - 1) + [(group_heads - few) * hdim, few * hdim]
    starts = [sum(chunks[:at]) for at in range(len(chunks))]
    token = jnp.zeros((1,), jnp.int32)

    def far(array):
        return lax.ppermute(array, "seq", [(i, i ^ 2) for i in range(n_seq)])

    def near(array):
        return lax.ppermute(array, "seq", [(i, i ^ 1) for i in range(n_seq)])

    def across(array):
        return lax.ppermute(array, "dp", [(i, i ^ 1) for i in range(n_dp)])

    def onward(array):
        return lax.ppermute(array, "dp", [(i, (i + 2) % n_dp) for i in range(n_dp)])

    def wait(array):
        nonlocal token
        array, token = lax.optimization_barrier((array, token))
        return array

    def after(array):
        return lax.optimization_barrier((array, token))[0]

    def turn(ring, step):
        ring[step] = wait(ring[step])
        if step + 1 < n_ring:
            ring.append(onward(ring[step]))

    depth = out_weight.shape[0]
    cut = depth * 3 // 5 // 16 * 16
    upper, lower = [out_weight[:cut]], [out_weight[cut:]]
    lower.append(onward(lower[0]))
    beside = [wait(far(upper[0]))]
    turn(lower, 1)

    core = jnp.stack([seq % 2])
    arrays = (queries, key_states, value_states, query_tangent, key_tangent, value_tangent)
    packs = [wait(array) for array in pack(core, n_seq, chunks, arrays, jnp.stack([query_gain, key_gain]))]
    half = len(packs) // 2
    query_own, *keyed_own = packs[:half]
    query_other, *keyed_other = packs[half:]
    keyed_near = [wait(near(array)) for array in keyed_other]
    queries_both = [query_own, wait(near(query_other))]
    keyed_far = [[far(keyed_own[0]), far(keyed_near[0])]]
    keyed_far += [[far(jnp.concatenate(pair))] for pair in zip(keyed_own[1:], keyed_near[1:])]
    upper.append(onward(upper[0]))
    beside.append(onward(beside[0]))
    turn(lower, 2)

    acts, swapped = [], []

    def attention(chunk):
        keyed_far[chunk][-1] = wait(keyed_far[chunk][-1])
        blocks = [keyed_own[chunk], keyed_near[chunk], *keyed_far[chunk]]
        acts.append(wait(attend(starts[chunk], hdim, queries_both, blocks)))
        swapped.append(across(acts[-1]))

    turn(upper, 1)
    keyed_far[0][0] = wait(keyed_far[0][0])
    turn(beside, 1)
    attention(0)
    for step in range(3, n_ring):
        turn(lower, step)
    later = [wait(jnp.concatenate(lower[step : step + 2])) for step in range(2, n_ring, 2)]
    turn(upper, 2)
    rest = [far(after(lower[0]))]
    attention(1)
    turn(beside, 2)
    swapped[0] = wait(swapped[0])
    swapped[1] = wait(swapped[1])
    attention(2)
    rest += [far(after(piece)) for piece in lower[1:2] + later]
    for step in range(3, n_ring):
        turn(upper, step)
    rest[0] = wait(rest[0])
    swapped[2] = wait(swapped[2])
    acts = wait(assemble(jnp.stack([seq // 2]), groups, chunks, list(zip(acts, swapped))))

    keeps, mine_sends, sends, mine_got, other = [], [], [], [], []

    def columns(step):
        own = [(upper[step], 0, cut), (lower[step], 0, depth - cut)]
        start = step % 2 * (depth - cut) if step > 1 else 0
        got = rest[step] if step < 2 else rest[1 + step // 2]
        theirs = [(beside[step], 0, cut), (got, start, start + depth - cut)]
        keep_mine, keep_other, send_mine, send_other = project(acts, own, theirs)
        keeps.append((keep_mine, keep_other))
        sends.append(near(wait(send_other)))
        mine_sends.append(send_mine)

    def finish(step):
        other.append(across(wait(close(keeps[step][1], wait(sends[step])))))
        mine_got.append(near(mine_sends[step]))

    columns(0)
    rest[1] = wait(rest[1])
    columns(1)
    finish(0)
    finish(1)
    for step in range(2, n_ring, 2):
        for ahead in range(max(step, 3), step + 2):
            turn(beside, ahead)
        rest[1 + step // 2] = wait(rest[1 + step // 2])
        columns(step)
        other[step - 2] = wait(other[step - 2])
        finish(step)
        columns(step + 1)
        other[step - 1] = wait(other[step - 1])
        mine_got[step - 2] = wait(mine_got[step - 2])
        mine_got[step - 1] = wait(mine_got[step - 1])
        finish(step + 1)

    where = []
    for step in range(n_ring):
        pair = (dp // 2 - step) % n_ring
        where += [2 * pair + dp % 2, 2 * pair + 1 - dp % 2]
    where = jnp.stack(where).astype(jnp.int32) + token
    return place(where, [keep for keep, _ in keeps], mine_got, other)


def solution(mesh):
    rows = P(("dp", "seq"), None)
    return jax.shard_map(
        functools.partial(body, mesh.shape["dp"], mesh.shape["seq"]),
        mesh=mesh,
        in_specs=(rows,) * 6 + (P(), P(), P("seq", "dp")),
        out_specs=(rows, rows),
        check_vma=False,
    )
```

time: 164 us -> 156 us (0.951)
  waiting for transfers between devices: 94.7 us -> 76.1 us
  local copies, waits for them, and re-layouts: 9.23 us -> 14.7 us
  Pallas kernels: 30 us -> 34.9 us
  starting transfers between devices: 29 us -> 27 us
    ppermute x12 -> x8, waiting for transfers between devices: 23.4 us -> 7.58 us  [far(): return lax.ppermute(array, 'seq', [(i, i ^ 2) for i in range(n_seq)])]
    unnamed x40 -> x72, local copies, waits for them, and re-layouts: 4.9 us -> 12.4 us
    ppermute x7, waiting for transfers between devices: 23.8 us -> 17.5 us  [across(): return lax.ppermute(array, 'dp', [(i, i ^ 1) for i in range(n_dp)])]
    pallas_call x5, Pallas kernels: 14.4 us -> 20.3 us  [the longest x4 17.4 us: project(): pl.pallas_call(functools.partial(project_kernel, spans), in_specs=vmem_sp...]
    ppermute x12 -> x9, starting transfers between devices: 9.29 us -> 5.39 us  [onward(): return lax.ppermute(array, 'dp', [(i, (i + 2) % n_dp) for i in range(n_dp)])]
    ppermute x12 -> x9, waiting for transfers between devices: 46.7 us -> 50.1 us  [onward(): return lax.ppermute(array, 'dp', [(i, (i + 2) % n_dp) for i in range(n_dp)])]
    ppermute x7, starting transfers between devices: 7.87 us -> 10.1 us  [across(): return lax.ppermute(array, 'dp', [(i, i ^ 1) for i in range(n_dp)])]
    ppermute x12 -> x8, starting transfers between devices: 10.1 us -> 8.88 us  [far(): return lax.ppermute(array, 'seq', [(i, i ^ 2) for i in range(n_seq)])]
  transfers between devices with their start and end apart: 39 -> 36, of which waited for: 19 -> 15; matrix products, arithmetic and copies ran while one was open for 2% -> 1% of each run, Pallas kernels for 17% -> 21%
where the time goes in v2:
time: 156 us; the launch traced here: 155 us
  waiting for transfers between devices  76.1 us (49%)
  Pallas kernels  34.9 us (22%)
  starting transfers between devices  27 us (17%)
  local copies, waits for them, and re-layouts  14.7 us (9%)
    ppermute x9, waiting for transfers between devices, onward(): return lax.ppermute(array, 'dp', [(i, (i + 2) % n_dp) for i in range(n_dp)])  50.1 us
    ppermute x7, waiting for transfers between devices, across(): return lax.ppermute(array, 'dp', [(i, i ^ 1) for i in range(n_dp)])  17.5 us
    pallas_call x4, Pallas kernels, project(): pl.pallas_call(functools.partial(project_kernel, spans), in_specs=vmem_sp...  17.4 us
    unnamed x72, local copies, waits for them, and re-layouts  12.4 us
    ppermute x7, starting transfers between devices, across(): return lax.ppermute(array, 'dp', [(i, i ^ 1) for i in range(n_dp)])  10.1 us
    pallas_call x3, Pallas kernels, attend(): pl.pallas_call(functools.partial(attend_kernel, len(queries)), grid=(widt...  9.41 us
    ppermute x8, starting transfers between devices, far(): return lax.ppermute(array, 'seq', [(i, i ^ 2) for i in range(n_seq)])  8.88 us
    ppermute x8, waiting for transfers between devices, far(): return lax.ppermute(array, 'seq', [(i, i ^ 2) for i in range(n_seq)])  7.58 us
  transfers between devices with their start and end apart: 36, of which 15 were waited for; matrix products, arithmetic and copies ran while one was open for 1% of the time, Pallas kernels for 21%

profile of v2, /device:TPU:0, one launch (start us, length us, event | category | flops | bytes accessed | tf_op | source)
XLA Modules:
  0.0 154.9 jit_solution(9598006945477421430)
XLA Ops:
  1.9 3.0 %collective-permute-start.1 = (bf16[384,640]{1,0:T(8,128)(2,1)S(1)}, bf16[384,640]{1,0:T(8,128)(2,1)S(1)}, u32[]{:S(2)}, u32[]{:S(2)}) collective-permute-start(bf16[384,640]{1,0:T(8,128)(2,1)S(1)} %slice.7.refs_0_), channel_id=1, source_target_pairs={{0,2},{1,3},{2,0},{3,1},{4,6},{5,7},{6,4},{7,5},{8,10},{9,11},{10,... | collective-permute-start | bytes 1474568 | tf_op jit(solution)/shard_map/ppermute | solution.py:280
  5.9 1.6 %collective-permute-start = (bf16[256,640]{1,0:T(8,128)(2,1)S(1)}, bf16[256,640]{1,0:T(8,128)(2,1)}, u32[]{:S(2)}, u32[]{:S(2)}) collective-permute-start(bf16[256,640]{1,0:T(8,128)(2,1)S(1)} %slice.6.refs_1_), channel_id=1, source_target_pairs={{0,8},{4,12},{8,16},{12,20},{16,24},{20,28},{24,0},{28,4},{1,9},{5... | collective-permute-start | bytes 983048 | tf_op jit(solution)/shard_map/ppermute | solution.py:289
  8.7 3.7 %shard_map.104 = (bf16[2,128,1280]{2,1,0:T(8,128)(2,1)S(1)}, bf16[4,128,640]{2,1,0:T(8,128)(2,1)S(1)}, bf16[4,128,384]{2,1,0:T(8,128)(2,1)S(1)}, bf16[4,128,256]...) custom-call(s32[1]{0:T(128)} %bitcast.9.core_ref, ...), custom_call_target="tpu_custom_call" | custom-call | flops 1 | bytes 1 | tf_op jit(solution)/shard_map/pallas_call | solution.py:78
  12.4 3.6 %collective-permute-done.1.refs_2_ = bf16[384,640]{1,0:T(8,128)(2,1)S(1)} collective-permute-done((bf16[384,640]{1,0:T(8,128)(2,1)S(1)}, bf16[384,640]{1,0:T(8,128)(2,1)S(1)}, u32[]{:S(2)}, u32[]{:S(2)}) %collective-permute-start.1) | collective-permute-done | bytes 491552 | tf_op jit(solution)/shard_map/ppermute | solution.py:280
  20.5 1.6 %collective-permute-start.7 = (bf16[384,640]{1,0:T(8,128)(2,1)S(1)}, bf16[384,640]{1,0:T(8,128)(2,1)S(1)}, u32[]{:S(2)}, u32[]{:S(2)}) collective-permute-start(bf16[384,640]{1,0:T(8,128)(2,1)S(1)} %slice.7.refs_0_), channel_id=1, source_target_pairs={{0,8},{4,12},{8,16},{12,20},{16,24},{20,28},{24,0},{28,4},{1,9},{5... | collective-permute-start | bytes 1474568 | tf_op jit(solution)/shard_map/ppermute | solution.py:289
  22.7 8.0 %collective-permute-done.8.refs_1_ = bf16[256,640]{1,0:T(8,128)(2,1)S(1)} collective-permute-done((bf16[256,640]{1,0:T(8,128)(2,1)}, bf16[256,640]{1,0:T(8,128)(2,1)S(1)}, u32[]{:S(2)}, u32[]{:S(2)}) %collective-permute-start.8) | collective-permute-done | bytes 327712 | tf_op jit(solution)/shard_map/ppermute | solution.py:289
  31.4 9.8 %collective-permute-done.7.refs_0_ = bf16[384,640]{1,0:T(8,128)(2,1)S(1)} collective-permute-done((bf16[384,640]{1,0:T(8,128)(2,1)S(1)}, bf16[384,640]{1,0:T(8,128)(2,1)S(1)}, u32[]{:S(2)}, u32[]{:S(2)}) %collective-permute-start.7) | collective-permute-done | bytes 491552 | tf_op jit(solution)/shard_map/ppermute | solution.py:289
  41.8 9.9 %collective-permute-done.10.refs_2_ = bf16[384,640]{1,0:T(8,128)(2,1)S(1)} collective-permute-done((bf16[384,640]{1,0:T(8,128)(2,1)S(1)}, bf16[384,640]{1,0:T(8,128)(2,1)S(1)}, u32[]{:S(2)}, u32[]{:S(2)}) %collective-permute-start.10) | collective-permute-done | bytes 491552 | tf_op jit(solution)/shard_map/ppermute | solution.py:289
  51.7 4.7 %shard_map.105.refs_0_ = bf16[2,256,640]{2,1,0:T(8,128)(2,1)S(1)} custom-call(bf16[2,128,1280]{2,1,0:T(8,128)(2,1)S(1)} %get-tuple-element.138.refs_0_, bf16[2,128,1280]{2,1,0:T(8,128)(2,1)S(1)} %collective-permute-done.2.refs_1_, bf16[4,128,640]{2,1,0:T(8,128)(2,1)S(1)} %get-tuple-element.162.refs_2_, ...), custom_call_target="tpu_custom_call" | custom-call | flops 1 | bytes 1 | tf_op jit(solution)/shard_map/pallas_call | solution.py:129
  56.4 1.6 %collective-permute-start.11 = (bf16[2,256,640]{2,1,0:T(8,128)(2,1)S(1)}, bf16[2,256,640]{2,1,0:T(8,128)(2,1)S(1)}, u32[]{:S(2)}, u32[]{:S(2)}) collective-permute-start(bf16[2,256,640]{2,1,0:T(8,128)(2,1)S(1)} %shard_map.105.refs_0_), channel_id=1, source_target_pairs={{0,4},{4,0},{8,12},{12,8},{16,20},{20,16},{24,28},{28,24},{1,5},{5... | collective-permute-start | bytes 1966088 | tf_op jit(solution)/shard_map/ppermute | solution.py:286
  58.9 9.4 %collective-permute-done.15.refs_1_ = bf16[256,640]{1,0:T(8,128)(2,1)S(1)} collective-permute-done((bf16[256,640]{1,0:T(8,128)(2,1)S(1)}, bf16[256,640]{1,0:T(8,128)(2,1)S(1)}, u32[]{:S(2)}, u32[]{:S(2)}) %collective-permute-start.15) | collective-permute-done | bytes 327712 | tf_op jit(solution)/shard_map/ppermute | solution.py:289
  69.2 2.8 %shard_map.106.refs_2_ = bf16[2,256,384]{2,1,0:T(8,128)(2,1)S(1)} custom-call(bf16[2,128,1280]{2,1,0:T(8,128)(2,1)S(1)} %get-tuple-element.138.refs_0_, bf16[2,128,1280]{2,1,0:T(8,128)(2,1)S(1)} %collective-permute-done.2.refs_1_, bf16[4,128,384]{2,1,0:T(8,128)(2,1)S(1)} %get-tuple-element.176.refs_2_, ...), custom_call_target="tpu_custom_call" | custom-call | flops 1 | bytes 1 | tf_op jit(solution)/shard_map/pallas_call | solution.py:129
  72.1 1.6 %collective-permute-start.16 = (bf16[2,256,384]{2,1,0:T(8,128)(2,1)S(1)}, bf16[2,256,384]{2,1,0:T(8,128)(2,1)S(1)}, u32[]{:S(2)}, u32[]{:S(2)}) collective-permute-start(bf16[2,256,384]{2,1,0:T(8,128)(2,1)S(1)} %shard_map.106.refs_2_), channel_id=1, source_target_pairs={{0,4},{4,0},{8,12},{12,8},{16,20},{20,16},{24,28},{28,24},{1,5},{5... | collective-permute-start | bytes 1179656 | tf_op jit(solution)/shard_map/ppermute | solution.py:286
  74.4 10.0 %collective-permute-done.12.refs_2_ = bf16[384,640]{1,0:T(8,128)(2,1)} collective-permute-done((bf16[384,640]{1,0:T(8,128)(2,1)S(1)}, bf16[384,640]{1,0:T(8,128)(2,1)}, u32[]{:S(2)}, u32[]{:S(2)}) %collective-permute-start.12) | collective-permute-done | bytes 491552 | tf_op jit(solution)/shard_map/ppermute | solution.py:289
  85.3 1.9 %shard_map.107.refs_4_ = bf16[2,256,256]{2,1,0:T(8,128)(2,1)S(1)} custom-call(bf16[2,128,1280]{2,1,0:T(8,128)(2,1)S(1)} %get-tuple-element.138.refs_0_, bf16[2,128,1280]{2,1,0:T(8,128)(2,1)S(1)} %collective-permute-done.2.refs_1_, bf16[4,128,256]{2,1,0:T(8,128)(2,1)S(1)} %get-tuple-element.193.refs_2_, ...), custom_call_target="tpu_custom_call" | custom-call | flops 1 | bytes 1 | tf_op jit(solution)/shard_map/pallas_call | solution.py:129
  87.2 1.2 collective-permute-start.22
  89.3 1.5 collective-permute-start.18
  90.9 2.1 %collective-permute-done.20.refs_0_ = bf16[384,640]{1,0:T(8,128)(2,1)S(1)} collective-permute-done((bf16[384,640]{1,0:T(8,128)(2,1)S(1)}, bf16[384,640]{1,0:T(8,128)(2,1)S(1)}, u32[]{:S(2)}, u32[]{:S(2)}) %collective-permute-start.20) | collective-permute-done | bytes 491552 | tf_op jit(solution)/shard_map/ppermute | solution.py:289
  93.7 1.4 collective-permute-done.19.refs_3_
  97.9 1.2 shard_map.108.acts_ref
  99.2 3.8 %shard_map.109 = (f32[256,640]{1,0:T(8,128)S(1)}, f32[256,640]{1,0:T(8,128)S(1)}, bf16[256,640]{1,0:T(8,128)(2,1)S(1)}, bf16[256,640]{1,0:T(8,128)(2,1)S(1)}) custom-call(bf16[2,1024,640]{2,1,0:T(8,128)(2,1)S(1)} %shard_map.108.acts_ref, bf16[384,640]{1,0:T(8,128)(2,1)S(1)} %slice.7.refs_0_, bf16[256,640]{1,0:T(8,128)(2,1)S(1)} %slice.6.refs_1_, ...), custom_call_target="tpu_custom_call" | custom-call | flops 1 | bytes 1 | tf_op jit(solution)/shard_map/pallas_call | solution.py:197
  103.1 3.7 %shard_map.110 = (f32[256,640]{1,0:T(8,128)S(1)}, f32[256,640]{1,0:T(8,128)S(1)}, bf16[256,640]{1,0:T(8,128)(2,1)S(1)}, bf16[256,640]{1,0:T(8,128)(2,1)S(1)}) custom-call(bf16[2,1024,640]{2,1,0:T(8,128)(2,1)S(1)} %shard_map.108.acts_ref, bf16[384,640]{1,0:T(8,128)(2,1)S(1)} %copy-done.17, bf16[256,640]{1,0:T(8,128)(2,1)} %collective-permute-done.refs_1_, ...), custom_call_target="tpu_custom_call" | custom-call | flops 1 | bytes 1 | tf_op jit(solution)/shard_map/pallas_call | solution.py:197
  107.2 1.6 %collective-permute-start.27 = (bf16[256,640]{1,0:T(8,128)(2,1)S(1)}, bf16[256,640]{1,0:T(8,128)(2,1)S(1)}, u32[]{:S(2)}, u32[]{:S(2)}) collective-permute-start(bf16[256,640]{1,0:T(8,128)(2,1)S(1)} %shard_map.111), channel_id=1, source_target_pairs={{0,4},{4,0},{8,12},{12,8},{16,20},{20,16},{24,28},{28,24},{1,5},{5... | collective-permute-start | bytes 983048 | tf_op jit(solution)/shard_map/ppermute | solution.py:286
  108.9 2.5 %collective-permute-done.25.refs_3_ = bf16[512,640]{1,0:T(8,128)(2,1)S(1)} collective-permute-done((bf16[512,640]{1,0:T(8,128)(2,1)}, bf16[512,640]{1,0:T(8,128)(2,1)S(1)}, u32[]{:S(2)}, u32[]{:S(2)}) %collective-permute-start.25) | collective-permute-done | bytes 655392 | tf_op jit(solution)/shard_map/ppermute | solution.py:280
  111.4 5.0 %shard_map.114 = (f32[256,640]{1,0:T(8,128)S(1)}, f32[256,640]{1,0:T(8,128)S(1)}, bf16[256,640]{1,0:T(8,128)(2,1)}, bf16[256,640]{1,0:T(8,128)(2,1)S(1)}) custom-call(bf16[2,1024,640]{2,1,0:T(8,128)(2,1)} %copy-done, bf16[384,640]{1,0:T(8,128)(2,1)S(1)} %copy-done.11, bf16[256,640]{1,0:T(8,128)(2,1)S(1)} %collective-permute-done.8.refs_1_, ...), custom_call_target="tpu_custom_call" | custom-call | flops 1 | bytes 1 | tf_op jit(solution)/shard_map/pallas_call | solution.py:197
  116.9 1.5 collective-permute-start.31
  118.4 5.0 %shard_map.113 = (f32[256,640]{1,0:T(8,128)S(1)}, f32[256,640]{1,0:T(8,128)S(1)}, bf16[256,640]{1,0:T(8,128)(2,1)}, bf16[256,640]{1,0:T(8,128)(2,1)S(1)}) custom-call(bf16[2,1024,640]{2,1,0:T(8,128)(2,1)} %copy-done, bf16[384,640]{1,0:T(8,128)(2,1)S(1)} %copy-done.13, bf16[256,640]{1,0:T(8,128)(2,1)S(1)} %collective-permute-done.15.refs_1_, ...), custom_call_target="tpu_custom_call" | custom-call | flops 1 | bytes 1 | tf_op jit(solution)/shard_map/pallas_call | solution.py:197
  124.1 2.9 %collective-permute-done.31.refs_9_ = bf16[256,640]{1,0:T(8,128)(2,1)S(1)} collective-permute-done((bf16[256,640]{1,0:T(8,128)(2,1)S(1)}, bf16[256,640]{1,0:T(8,128)(2,1)S(1)}, u32[]{:S(2)}, u32[]{:S(2)}) %collective-permute-start.31) | collective-permute-done | bytes 327712 | tf_op jit(solution)/shard_map/ppermute | solution.py:286
  127.1 1.6 %collective-permute-start.34 = (bf16[256,640]{1,0:T(8,128)(2,1)S(1)}, bf16[256,640]{1,0:T(8,128)(2,1)}, u32[]{:S(2)}, u32[]{:S(2)}) collective-permute-start(bf16[256,640]{1,0:T(8,128)(2,1)S(1)} %shard_map.115), channel_id=1, source_target_pairs={{0,4},{4,0},{8,12},{12,8},{16,20},{20,16},{24,28},{28,24},{1,5},{5... | collective-permute-start | bytes 983048 | tf_op jit(solution)/shard_map/ppermute | solution.py:286
  130.4 7.4 %collective-permute-done.34.refs_10_ = bf16[256,640]{1,0:T(8,128)(2,1)} collective-permute-done((bf16[256,640]{1,0:T(8,128)(2,1)S(1)}, bf16[256,640]{1,0:T(8,128)(2,1)}, u32[]{:S(2)}, u32[]{:S(2)}) %collective-permute-start.34) | collective-permute-done | bytes 327712 | tf_op jit(solution)/shard_map/ppermute | solution.py:286
  137.8 6.5 %collective-permute-done.35.refs_11_ = bf16[256,640]{1,0:T(8,128)(2,1)S(1)} collective-permute-done((bf16[256,640]{1,0:T(8,128)(2,1)S(1)}, bf16[256,640]{1,0:T(8,128)(2,1)S(1)}, u32[]{:S(2)}, u32[]{:S(2)}) %collective-permute-start.35) | collective-permute-done | bytes 327712 | tf_op jit(solution)/shard_map/ppermute | solution.py:286
  151.9 2.9 %shard_map.117 = (bf16[128,5120]{1,0:T(8,128)(2,1)}, bf16[128,5120]{1,0:T(8,128)(2,1)}) custom-call(s32[8]{0:T(128)S(1)} %broadcast_add_fusion.where_ref, f32[256,640]{1,0:T(8,128)S(1)} %copy-done.5, f32[256,640]{1,0:T(8,128)S(1)} %get-tuple-element.257.refs_1_, f32[256,640]{1,0:T(8,128)S(1)} %get-tuple-element.258.refs_2_, f32[256,640]{1,0:T(8,128)S(1)} %copy-done.7, ...), custom_call_target="tpu_custom_call" | custom-call | flops 1 | bytes 1 | tf_op jit(solution)/shard_map/pallas_call | solution.py:244
  (136 shorter events, 28.7 us)
Async XLA Ops:
  1.9 14.2 %collective-permute-start.1 = (bf16[384,640]{1,0:T(8,128)(2,1)S(1)}, bf16[384,640]{1,0:T(8,128)(2,1)S(1)}, u32[]{:S(2)}, u32[]{:S(2)}) collective-permute-start(bf16[384,640]{1,0:T(8,128)(2,1)S(1)} %slice.7.refs_0_), channel_id=1, source_target_pairs={{0,2},{1,3},{2,0},{3,1},{4,6},{5,7},{6,4},{7,5},{8,10},{9,11},{10,... | collective-permute-start | bytes 1474568 | tf_op jit(solution)/shard_map/ppermute | solution.py:280
  5.9 11.2 %collective-permute-start = (bf16[256,640]{1,0:T(8,128)(2,1)S(1)}, bf16[256,640]{1,0:T(8,128)(2,1)}, u32[]{:S(2)}, u32[]{:S(2)}) collective-permute-start(bf16[256,640]{1,0:T(8,128)(2,1)S(1)} %slice.6.refs_1_), channel_id=1, source_target_pairs={{0,8},{4,12},{8,16},{12,20},{16,24},{20,28},{24,0},{28,4},{1,9},{5... | collective-permute-start | bytes 983048 | tf_op jit(solution)/shard_map/ppermute | solution.py:289
  17.6 13.9 %collective-permute-start.2 = (bf16[2,128,1280]{2,1,0:T(8,128)(2,1)S(1)}, bf16[2,128,1280]{2,1,0:T(8,128)(2,1)S(1)}, u32[]{:S(2)}, u32[]{:S(2)}) collective-permute-start(bf16[2,128,1280]{2,1,0:T(8,128)(2,1)S(1)} %get-tuple-element.147), channel_id=1, source_target_pairs={{0,1},{1,0},{2,3},{3,2},{4,5},{5,4},{6,7},{7,6},{8,9},{9,8},{10,11... | collective-permute-start | bytes 1966088 | tf_op jit(solution)/shard_map/ppermute | solution.py:283
  17.6 4.5 %collective-permute-start.3 = (bf16[4,128,256]{2,1,0:T(8,128)(2,1)S(1)}, bf16[4,128,256]{2,1,0:T(8,128)(2,1)S(1)}, u32[]{:S(2)}, u32[]{:S(2)}) collective-permute-start(bf16[4,128,256]{2,1,0:T(8,128)(2,1)S(1)} %get-tuple-element.154), channel_id=1, source_target_pairs={{0,1},{1,0},{2,3},{3,2},{4,5},{5,4},{6,7},{7,6},{8,9},{9,8},{10,11... | collective-permute-start | bytes 786440 | tf_op jit(solution)/shard_map/ppermute | solution.py:283
  18.1 12.6 %collective-permute-start.8 = (bf16[256,640]{1,0:T(8,128)(2,1)}, bf16[256,640]{1,0:T(8,128)(2,1)S(1)}, u32[]{:S(2)}, u32[]{:S(2)}) collective-permute-start(bf16[256,640]{1,0:T(8,128)(2,1)} %collective-permute-done.refs_1_), channel_id=1, source_target_pairs={{0,8},{4,12},{8,16},{12,20},{16,24},{20,28},{24,0},{28,4},{1,9},{5... | collective-permute-start | bytes 983048 | tf_op jit(solution)/shard_map/ppermute | solution.py:289
  19.7 21.5 %collective-permute-start.6 = (bf16[4,128,640]{2,1,0:T(8,128)(2,1)S(1)}, bf16[4,128,640]{2,1,0:T(8,128)(2,1)S(1)}, u32[]{:S(2)}, u32[]{:S(2)}) collective-permute-start(bf16[4,128,640]{2,1,0:T(8,128)(2,1)S(1)} %get-tuple-element.162.refs_2_), channel_id=1, source_target_pairs={{0,2},{1,3},{2,0},{3,1},{4,6},{5,7},{6,4},{7,5},{8,10},{9,11},{10,... | collective-permute-start | bytes 1966088 | tf_op jit(solution)/shard_map/ppermute | solution.py:280
  20.5 20.7 %collective-permute-start.7 = (bf16[384,640]{1,0:T(8,128)(2,1)S(1)}, bf16[384,640]{1,0:T(8,128)(2,1)S(1)}, u32[]{:S(2)}, u32[]{:S(2)}) collective-permute-start(bf16[384,640]{1,0:T(8,128)(2,1)S(1)} %slice.7.refs_0_), channel_id=1, source_target_pairs={{0,8},{4,12},{8,16},{12,20},{16,24},{20,28},{24,0},{28,4},{1,9},{5... | collective-permute-start | bytes 1474568 | tf_op jit(solution)/shard_map/ppermute | solution.py:289
  22.1 29.7 %collective-permute-start.9 = (bf16[4,128,640]{2,1,0:T(8,128)(2,1)S(1)}, bf16[4,128,640]{2,1,0:T(8,128)(2,1)S(1)}, u32[]{:S(2)}, u32[]{:S(2)}) collective-permute-start(bf16[4,128,640]{2,1,0:T(8,128)(2,1)S(1)} %collective-permute-done.5.refs_3_), channel_id=1, source_target_pairs={{0,2},{1,3},{2,0},{3,1},{4,6},{5,7},{6,4},{7,5},{8,10},{9,11},{10,... | collective-permute-start | bytes 1966088 | tf_op jit(solution)/shard_map/ppermute | solution.py:280
  30.7 38.6 %collective-permute-start.13 = (bf16[8,128,384]{2,1,0:T(8,128)(2,1)S(1)}, bf16[8,128,384]{2,1,0:T(8,128)(2,1)S(1)}, u32[]{:S(2)}, u32[]{:S(2)}) collective-permute-start(bf16[8,128,384]{2,1,0:T(8,128)(2,1)S(1)} %pad_maximum_fusion), channel_id=1, source_target_pairs={{0,2},{1,3},{2,0},{3,1},{4,6},{5,7},{6,4},{7,5},{8,10},{9,11},{10,... | collective-permute-start | bytes 2359304 | tf_op jit(solution)/shard_map/ppermute | solution.py:280
  31.4 20.3 %collective-permute-start.10 = (bf16[384,640]{1,0:T(8,128)(2,1)S(1)}, bf16[384,640]{1,0:T(8,128)(2,1)S(1)}, u32[]{:S(2)}, u32[]{:S(2)}) collective-permute-start(bf16[384,640]{1,0:T(8,128)(2,1)S(1)} %collective-permute-done.1.refs_2_), channel_id=1, source_target_pairs={{0,8},{4,12},{8,16},{12,20},{16,24},{20,28},{24,0},{28,4},{1,9},{5... | collective-permute-start | bytes 1474568 | tf_op jit(solution)/shard_map/ppermute | solution.py:289
  41.2 28.0 %collective-permute-start.14 = (bf16[384,640]{1,0:T(8,128)(2,1)S(1)}, bf16[384,640]{1,0:T(8,128)(2,1)S(1)}, u32[]{:S(2)}, u32[]{:S(2)}) collective-permute-start(bf16[384,640]{1,0:T(8,128)(2,1)S(1)} %collective-permute-done.7.refs_0_), channel_id=1, source_target_pairs={{0,8},{4,12},{8,16},{12,20},{16,24},{20,28},{24,0},{28,4},{1,9},{5... | collective-permute-start | bytes 1474568 | tf_op jit(solution)/shard_map/ppermute | solution.py:289
  41.2 27.1 %collective-permute-start.15 = (bf16[256,640]{1,0:T(8,128)(2,1)S(1)}, bf16[256,640]{1,0:T(8,128)(2,1)S(1)}, u32[]{:S(2)}, u32[]{:S(2)}) collective-permute-start(bf16[256,640]{1,0:T(8,128)(2,1)S(1)} %collective-permute-done.8.refs_1_), channel_id=1, source_target_pairs={{0,8},{4,12},{8,16},{12,20},{16,24},{20,28},{24,0},{28,4},{1,9},{5... | collective-permute-start | bytes 983048 | tf_op jit(solution)/shard_map/ppermute | solution.py:289
  56.4 28.9 %collective-permute-start.11 = (bf16[2,256,640]{2,1,0:T(8,128)(2,1)S(1)}, bf16[2,256,640]{2,1,0:T(8,128)(2,1)S(1)}, u32[]{:S(2)}, u32[]{:S(2)}) collective-permute-start(bf16[2,256,640]{2,1,0:T(8,128)(2,1)S(1)} %shard_map.105.refs_0_), channel_id=1, source_target_pairs={{0,4},{4,0},{8,12},{12,8},{16,20},{20,16},{24,28},{28,24},{1,5},{5... | collective-permute-start | bytes 1966088 | tf_op jit(solution)/shard_map/ppermute | solution.py:286
  58.1 27.2 %collective-permute-start.17 = (bf16[8,128,256]{2,1,0:T(8,128)(2,1)S(1)}, bf16[8,128,256]{2,1,0:T(8,128)(2,1)S(1)}, u32[]{:S(2)}, u32[]{:S(2)}) collective-permute-start(bf16[8,128,256]{2,1,0:T(8,128)(2,1)S(1)} %pad_maximum_fusion.2), channel_id=1, source_target_pairs={{0,2},{1,3},{2,0},{3,1},{4,6},{5,7},{6,4},{7,5},{8,10},{9,11},{10,... | collective-permute-start | bytes 1572872 | tf_op jit(solution)/shard_map/ppermute | solution.py:280
  68.3 16.1 %collective-permute-start.12 = (bf16[384,640]{1,0:T(8,128)(2,1)S(1)}, bf16[384,640]{1,0:T(8,128)(2,1)}, u32[]{:S(2)}, u32[]{:S(2)}) collective-permute-start(bf16[384,640]{1,0:T(8,128)(2,1)S(1)} %collective-permute-done.10.refs_2_), channel_id=1, source_target_pairs={{0,8},{4,12},{8,16},{12,20},{16,24},{20,28},{24,0},{28,4},{1,9},{5... | collective-permute-start | bytes 1474568 | tf_op jit(solution)/shard_map/ppermute | solution.py:289
  72.1 13.2 %collective-permute-start.16 = (bf16[2,256,384]{2,1,0:T(8,128)(2,1)S(1)}, bf16[2,256,384]{2,1,0:T(8,128)(2,1)S(1)}, u32[]{:S(2)}, u32[]{:S(2)}) collective-permute-start(bf16[2,256,384]{2,1,0:T(8,128)(2,1)S(1)} %shard_map.106.refs_2_), channel_id=1, source_target_pairs={{0,4},{4,0},{8,12},{12,8},{16,20},{20,16},{24,28},{28,24},{1,5},{5... | collective-permute-start | bytes 1179656 | tf_op jit(solution)/shard_map/ppermute | solution.py:286
  73.7 19.3 %collective-permute-start.20 = (bf16[384,640]{1,0:T(8,128)(2,1)S(1)}, bf16[384,640]{1,0:T(8,128)(2,1)S(1)}, u32[]{:S(2)}, u32[]{:S(2)}) collective-permute-start(bf16[384,640]{1,0:T(8,128)(2,1)S(1)} %collective-permute-done.14.refs_0_), channel_id=1, source_target_pairs={{0,8},{4,12},{8,16},{12,20},{16,24},{20,28},{24,0},{28,4},{1,9},{5... | collective-permute-start | bytes 1474568 | tf_op jit(solution)/shard_map/ppermute | solution.py:289
  84.4 10.8 %collective-permute-start.19 = (bf16[256,640]{1,0:T(8,128)(2,1)S(1)}, bf16[256,640]{1,0:T(8,128)(2,1)}, u32[]{:S(2)}, u32[]{:S(2)}) collective-permute-start(bf16[256,640]{1,0:T(8,128)(2,1)S(1)} %slice.6.refs_1_), channel_id=1, source_target_pairs={{0,2},{1,3},{2,0},{3,1},{4,6},{5,7},{6,4},{7,5},{8,10},{9,11},{10,... | collective-permute-start | bytes 983048 | tf_op jit(solution)/shard_map/ppermute | solution.py:280
  87.2 15.8 %collective-permute-start.22 = (bf16[256,640]{1,0:T(8,128)(2,1)}, bf16[256,640]{1,0:T(8,128)(2,1)}, u32[]{:S(2)}, u32[]{:S(2)}) collective-permute-start(bf16[256,640]{1,0:T(8,128)(2,1)} %collective-permute-done.refs_1_), channel_id=1, source_target_pairs={{0,2},{1,3},{2,0},{3,1},{4,6},{5,7},{6,4},{7,5},{8,10},{9,11},{10,... | collective-permute-start | bytes 983048 | tf_op jit(solution)/shard_map/ppermute | solution.py:280
  88.4 23.0 %collective-permute-start.25 = (bf16[512,640]{1,0:T(8,128)(2,1)}, bf16[512,640]{1,0:T(8,128)(2,1)S(1)}, u32[]{:S(2)}, u32[]{:S(2)}) collective-permute-start(bf16[512,640]{1,0:T(8,128)(2,1)} %pad_maximum_fusion.1), channel_id=1, source_target_pairs={{0,2},{1,3},{2,0},{3,1},{4,6},{5,7},{6,4},{7,5},{8,10},{9,11},{10,... | collective-permute-start | bytes 1966088 | tf_op jit(solution)/shard_map/ppermute | solution.py:280
  89.3 6.5 %collective-permute-start.18 = (bf16[2,256,256]{2,1,0:T(8,128)(2,1)S(1)}, bf16[2,256,256]{2,1,0:T(8,128)(2,1)}, u32[]{:S(2)}, u32[]{:S(2)}) collective-permute-start(bf16[2,256,256]{2,1,0:T(8,128)(2,1)S(1)} %shard_map.107.refs_4_), channel_id=1, source_target_pairs={{0,4},{4,0},{8,12},{12,8},{16,20},{20,16},{24,28},{28,24},{1,5},{5... | collective-permute-start | bytes 786440 | tf_op jit(solution)/shard_map/ppermute | solution.py:286
  93.7 15.2 %collective-permute-start.21 = (bf16[384,640]{1,0:T(8,128)(2,1)}, bf16[384,640]{1,0:T(8,128)(2,1)}, u32[]{:S(2)}, u32[]{:S(2)}) collective-permute-start(bf16[384,640]{1,0:T(8,128)(2,1)} %collective-permute-done.12.refs_2_), channel_id=1, source_target_pairs={{0,8},{4,12},{8,16},{12,20},{16,24},{20,28},{24,0},{28,4},{1,9},{5... | collective-permute-start | bytes 1474568 | tf_op jit(solution)/shard_map/ppermute | solution.py:289
  102.9 4.2 %collective-permute-start.24 = (bf16[256,640]{1,0:T(8,128)(2,1)S(1)}, bf16[256,640]{1,0:T(8,128)(2,1)S(1)}, u32[]{:S(2)}, u32[]{:S(2)}) collective-permute-start(bf16[256,640]{1,0:T(8,128)(2,1)S(1)} %get-tuple-element.220), channel_id=1, source_target_pairs={{0,1},{1,0},{2,3},{3,2},{4,5},{5,4},{6,7},{7,6},{8,9},{9,8},{10,11... | collective-permute-start | bytes 983048 | tf_op jit(solution)/shard_map/ppermute | solution.py:283
  107.2 16.2 %collective-permute-start.27 = (bf16[256,640]{1,0:T(8,128)(2,1)S(1)}, bf16[256,640]{1,0:T(8,128)(2,1)S(1)}, u32[]{:S(2)}, u32[]{:S(2)}) collective-permute-start(bf16[256,640]{1,0:T(8,128)(2,1)S(1)} %shard_map.111), channel_id=1, source_target_pairs={{0,4},{4,0},{8,12},{12,8},{16,20},{20,16},{24,28},{28,24},{1,5},{5... | collective-permute-start | bytes 983048 | tf_op jit(solution)/shard_map/ppermute | solution.py:286
  116.4 7.0 %collective-permute-start.26 = (bf16[256,640]{1,0:T(8,128)(2,1)S(1)}, bf16[256,640]{1,0:T(8,128)(2,1)S(1)}, u32[]{:S(2)}, u32[]{:S(2)}) collective-permute-start(bf16[256,640]{1,0:T(8,128)(2,1)S(1)} %get-tuple-element.238), channel_id=1, source_target_pairs={{0,1},{1,0},{2,3},{3,2},{4,5},{5,4},{6,7},{7,6},{8,9},{9,8},{10,11... | collective-permute-start | bytes 983048 | tf_op jit(solution)/shard_map/ppermute | solution.py:283
  116.4 10.6 %collective-permute-start.30 = (bf16[256,640]{1,0:T(8,128)(2,1)S(1)}, bf16[256,640]{1,0:T(8,128)(2,1)S(1)}, u32[]{:S(2)}, u32[]{:S(2)}) collective-permute-start(bf16[256,640]{1,0:T(8,128)(2,1)S(1)} %get-tuple-element.247), channel_id=1, source_target_pairs={{0,1},{1,0},{2,3},{3,2},{4,5},{5,4},{6,7},{7,6},{8,9},{9,8},{10,11... | collective-permute-start | bytes 983048 | tf_op jit(solution)/shard_map/ppermute | solution.py:283
  116.9 10.2 %collective-permute-start.29 = (bf16[256,640]{1,0:T(8,128)(2,1)S(1)}, bf16[256,640]{1,0:T(8,128)(2,1)S(1)}, u32[]{:S(2)}, u32[]{:S(2)}) collective-permute-start(bf16[256,640]{1,0:T(8,128)(2,1)S(1)} %get-tuple-element.246), channel_id=1, source_target_pairs={{0,1},{1,0},{2,3},{3,2},{4,5},{5,4},{6,7},{7,6},{8,9},{9,8},{10,11... | collective-permute-start | bytes 983048 | tf_op jit(solution)/shard_map/ppermute | solution.py:283
  116.9 10.1 %collective-permute-start.31 = (bf16[256,640]{1,0:T(8,128)(2,1)S(1)}, bf16[256,640]{1,0:T(8,128)(2,1)S(1)}, u32[]{:S(2)}, u32[]{:S(2)}) collective-permute-start(bf16[256,640]{1,0:T(8,128)(2,1)S(1)} %shard_map.112), channel_id=1, source_target_pairs={{0,4},{4,0},{8,12},{12,8},{16,20},{20,16},{24,28},{28,24},{1,5},{5... | collective-permute-start | bytes 983048 | tf_op jit(solution)/shard_map/ppermute | solution.py:286
  123.5 5.1 %collective-permute-start.28 = (bf16[256,640]{1,0:T(8,128)(2,1)S(1)}, bf16[256,640]{1,0:T(8,128)(2,1)S(1)}, u32[]{:S(2)}, u32[]{:S(2)}) collective-permute-start(bf16[256,640]{1,0:T(8,128)(2,1)S(1)} %get-tuple-element.245), channel_id=1, source_target_pairs={{0,1},{1,0},{2,3},{3,2},{4,5},{5,4},{6,7},{7,6},{8,9},{9,8},{10,11... | collective-permute-start | bytes 983048 | tf_op jit(solution)/shard_map/ppermute | solution.py:283
  123.8 5.8 %collective-permute-start.32 = (bf16[256,640]{1,0:T(8,128)(2,1)}, bf16[256,640]{1,0:T(8,128)(2,1)S(1)}, u32[]{:S(2)}, u32[]{:S(2)}) collective-permute-start(bf16[256,640]{1,0:T(8,128)(2,1)} %get-tuple-element.262), channel_id=1, source_target_pairs={{0,1},{1,0},{2,3},{3,2},{4,5},{5,4},{6,7},{7,6},{8,9},{9,8},{10,11... | collective-permute-start | bytes 983048 | tf_op jit(solution)/shard_map/ppermute | solution.py:283
  127.1 10.7 %collective-permute-start.34 = (bf16[256,640]{1,0:T(8,128)(2,1)S(1)}, bf16[256,640]{1,0:T(8,128)(2,1)}, u32[]{:S(2)}, u32[]{:S(2)}) collective-permute-start(bf16[256,640]{1,0:T(8,128)(2,1)S(1)} %shard_map.115), channel_id=1, source_target_pairs={{0,4},{4,0},{8,12},{12,8},{16,20},{20,16},{24,28},{28,24},{1,5},{5... | collective-permute-start | bytes 983048 | tf_op jit(solution)/shard_map/ppermute | solution.py:286
  128.8 15.5 %collective-permute-start.35 = (bf16[256,640]{1,0:T(8,128)(2,1)S(1)}, bf16[256,640]{1,0:T(8,128)(2,1)S(1)}, u32[]{:S(2)}, u32[]{:S(2)}) collective-permute-start(bf16[256,640]{1,0:T(8,128)(2,1)S(1)} %shard_map.116), channel_id=1, source_target_pairs={{0,4},{4,0},{8,12},{12,8},{16,20},{20,16},{24,28},{28,24},{1,5},{5... | collective-permute-start | bytes 983048 | tf_op jit(solution)/shard_map/ppermute | solution.py:286
  (40 other events, 195.0 us)

commit v3 on v2

--- a/solution.py
+++ b/solution.py
@@ -9,7 +9,7 @@
 
 HEADS = 20
 EPS = 1e-06
-VMEM_BYTES = 48 * 1024 * 1024
+VMEM_BYTES = 16 * 1024 * 1024
 ROW_STEP = 32
 
 LOW = jnp.bfloat16
@@ -138,33 +138,33 @@
     )(*queries, *keyed)
 
 
-def assemble_kernel(chunks, flip_ref, *refs):
+def assemble_kernel(groups, chunks, flip_ref, *refs):
     part_refs, out_ref = refs[:-1], refs[-1]
-    groups, rows_all, group = out_ref.shape
-    rows = rows_all // 8
+    rows, group = out_ref.shape[0] // 8, out_ref.shape[1] // groups
     start = 0
     for at, width in enumerate(chunks):
-        for side in range(2):
-            part_ref = part_refs[2 * at + side]
-            for kind in range(2):
-                for core in range(2):
-                    first = (4 * core + 2 * side + kind) * rows
-                    for g in range(groups):
-                        low, high = max(start, g * group), min(start + width, (g + 1) * group)
-                        if low < high:
-                            out_ref[g ^ flip_ref[0], first : first + rows, low - g * group : high - g * group] = (
-                                part_ref[kind, core * rows : (core + 1) * rows, low - start : high - start]
-                            )
+        for g in range(groups):
+            low, high = max(start, g * group), min(start + width, (g + 1) * group)
+            if low >= high:
+                continue
+            to = pl.ds(pl.multiple_of((g ^ flip_ref[0]) * group + low - g * group, 128), high - low)
+            for side in range(2):
+                for kind in range(2):
+                    for core in range(2):
+                        first = (4 * core + 2 * side + kind) * rows
+                        out_ref[first : first + rows, to] = part_refs[2 * at + side][
+                            kind, core * rows : (core + 1) * rows, low - start : high - start
+                        ]
         start += width
 
 
 def assemble(flip, groups, chunks, pairs):
     rows = 4 * pairs[0][0].shape[1]
     return pl.pallas_call(
-        functools.partial(assemble_kernel, chunks),
+        functools.partial(assemble_kernel, groups, chunks),
         in_specs=[pl.BlockSpec(memory_space=pltpu.SMEM)] + vmem_specs(2 * len(pairs)),
         out_specs=vmem_specs(1)[0],
-        out_shape=jax.ShapeDtypeStruct((groups, rows, sum(chunks) // groups), LOW),
+        out_shape=jax.ShapeDtypeStruct((rows, sum(chunks)), LOW),
         compiler_params=params(),
         cost_estimate=LIGHT,
     )(flip, *[part for pair in pairs for part in pair])
@@ -174,28 +174,17 @@
     weight_refs = refs[:-4]
     keep_mine_ref, keep_other_ref, send_mine_ref, send_other_ref = refs[-4:]
     rows = keep_mine_ref.shape[0]
-    total = 0.0
-    for at, block in enumerate(spans):
-        weight = jnp.concatenate([weight_refs[which][low:high] for which, low, high in block], axis=0)
-        total = total + jnp.dot(acts_ref[at], weight, preferred_element_type=WIDE)
-    keep_mine_ref[...] = total[:rows]
-    keep_other_ref[...] = total[rows : 2 * rows]
-    send_mine_ref[...] = total[2 * rows : 3 * rows].astype(LOW)
-    send_other_ref[...] = total[3 * rows :].astype(LOW)
-
-
-def project(acts, *blocks):
-    weights, spans = [], []
-    for block in blocks:
-        spans.append([])
-        for weight, low, high in block:
-            if not any(weight is known for known in weights):
-                weights.append(weight)
-            which = [weight is known for known in weights].index(True)
-            spans[-1].append((which, low, high))
-    rows, n = acts.shape[1] // 4, weights[0].shape[1]
-    return pl.pallas_call(
-        functools.partial(project_kernel, spans),
+    weight = jnp.concatenate([ref[low:high] for ref, (low, high) in zip(weight_refs, spans)], axis=0)
+    for at, out_ref in enumerate((keep_mine_ref, keep_other_ref, send_mine_ref, send_other_ref)):
+        part = jnp.dot(acts_ref[at * rows : (at + 1) * rows], weight, preferred_element_type=WIDE)
+        out_ref[...] = part.astype(out_ref.dtype)
+
+
+def project(acts, pieces):
+    weights = [weight for weight, _, _ in pieces]
+    rows, n = acts.shape[0] // 4, weights[0].shape[1]
+    return pl.pallas_call(
+        functools.partial(project_kernel, [(low, high) for _, low, high in pieces]),
         in_specs=vmem_specs(1 + len(weights)),
         out_specs=vmem_specs(4),
         out_shape=[jax.ShapeDtypeStruct((rows, n), WIDE)] * 2 + [jax.ShapeDtypeStruct((rows, n), LOW)] * 2,
@@ -219,36 +208,45 @@
     )(keep, got)
 
 
-def place_kernel(n_steps, where_ref, *refs):
-    keep_refs, got_refs, other_refs = refs[:n_steps], refs[n_steps : 2 * n_steps], refs[2 * n_steps : -2]
+def place_kernel(where_ref, keep_ref, got_ref, other_ref, *refs):
     plain_ref, dual_ref = refs[-2:]
-    rows, n = plain_ref.shape[0], other_refs[0].shape[-1]
-    for step in range(n_steps):
-        mine, others = (pl.ds(pl.multiple_of(where_ref[2 * step + side] * n, n), n) for side in range(2))
-        for kind, out_ref in enumerate((plain_ref, dual_ref)):
-            here = slice(kind * rows, (kind + 1) * rows)
-            out_ref[:, mine] = (keep_refs[step][here] + got_refs[step][here].astype(WIDE)).astype(LOW)
-            out_ref[:, others] = other_refs[step][here]
-
-
-def place(where, keeps, gots, others):
-    rows, n = others[0].shape[0] // 2, others[0].shape[1]
-    width = 2 * n * len(others)
+    rows = plain_ref.shape[0]
+
+    @pl.when(pl.program_id(0) == 0)
+    def _():
+        total = (keep_ref[...] + got_ref[...].astype(WIDE)).astype(LOW)
+        plain_ref[...] = total[:rows]
+        dual_ref[...] = total[rows:]
+
+    @pl.when(pl.program_id(0) == 1)
+    def _():
+        plain_ref[...] = other_ref[:rows]
+        dual_ref[...] = other_ref[rows:]
+
+
+def place(outs, width, where, keep, got, other):
+    rows, n = other.shape[0] // 2, other.shape[1]
     if n % 128:
-        out = jnp.zeros((2 * rows, width), LOW)
-        for step, (keep, got, other) in enumerate(zip(keeps, gots, others)):
-            for side, piece in enumerate((close(keep, got), other)):
-                out = lax.dynamic_update_slice(out, piece, (0, where[2 * step + side] * n))
-        return out[:rows], out[rows:]
-    out = jax.ShapeDtypeStruct((rows, width), LOW)
-    return pl.pallas_call(
-        functools.partial(place_kernel, len(others)),
-        in_specs=[pl.BlockSpec(memory_space=pltpu.SMEM)] + vmem_specs(3 * len(others)),
-        out_specs=vmem_specs(2),
-        out_shape=[out, out],
-        compiler_params=params(),
-        cost_estimate=LIGHT,
-    )(where, *keeps, *gots, *others)
+        outs = outs or [jnp.zeros((rows, width), LOW)] * 2
+        for side, piece in enumerate((close(keep, got), other)):
+            parts = (piece[:rows], piece[rows:])
+            outs = [lax.dynamic_update_slice(out, part, (0, where[side] * n)) for out, part in zip(outs, parts)]
+        return outs
+    full = pl.BlockSpec((2 * rows, n), lambda i, w: (0, 0))
+    block = pl.BlockSpec((rows, n), lambda i, w: (0, w[i]))
+    return pl.pallas_call(
+        place_kernel,
+        grid_spec=pltpu.PrefetchScalarGridSpec(
+            num_scalar_prefetch=1,
+            grid=(2,),
+            in_specs=[full] * 3 + [pl.BlockSpec(memory_space=pl.ANY)] * len(outs),
+            out_specs=[block] * 2,
+        ),
+        out_shape=[jax.ShapeDtypeStruct((rows, width), LOW)] * 2,
+        input_output_aliases={4 + at: at for at in range(len(outs))},
+        compiler_params=params(),
+        cost_estimate=LIGHT,
+    )(where, keep, got, other, *outs)
 
 
 def body(
@@ -305,33 +303,33 @@
     cut = depth * 3 // 5 // 16 * 16
     upper, lower = [out_weight[:cut]], [out_weight[cut:]]
     lower.append(onward(lower[0]))
+    upper.append(onward(upper[0]))
     beside = [wait(far(upper[0]))]
+    beside.append(onward(beside[0]))
     turn(lower, 1)
 
     core = jnp.stack([seq % 2])
     arrays = (queries, key_states, value_states, query_tangent, key_tangent, value_tangent)
     packs = [wait(array) for array in pack(core, n_seq, chunks, arrays, jnp.stack([query_gain, key_gain]))]
-    half = len(packs) // 2
-    query_own, *keyed_own = packs[:half]
-    query_other, *keyed_other = packs[half:]
-    keyed_near = [wait(near(array)) for array in keyed_other]
+    query_own, *keyed_own = packs[: 1 + len(chunks)]
+    query_other, *keyed_other = packs[1 + len(chunks) :]
+    there = wait(near(keyed_other[0]))
+    keyed = [[keyed_own[0], there, far(keyed_own[0]), far(there)]]
+    for own, other in zip(keyed_own[1:], keyed_other[1:]):
+        there = wait(near(other))
+        keyed.append([own, there, far(jnp.concatenate([own, there]))])
     queries_both = [query_own, wait(near(query_other))]
-    keyed_far = [[far(keyed_own[0]), far(keyed_near[0])]]
-    keyed_far += [[far(jnp.concatenate(pair))] for pair in zip(keyed_own[1:], keyed_near[1:])]
-    upper.append(onward(upper[0]))
-    beside.append(onward(beside[0]))
     turn(lower, 2)
 
     acts, swapped = [], []
 
     def attention(chunk):
-        keyed_far[chunk][-1] = wait(keyed_far[chunk][-1])
-        blocks = [keyed_own[chunk], keyed_near[chunk], *keyed_far[chunk]]
-        acts.append(wait(attend(starts[chunk], hdim, queries_both, blocks)))
+        keyed[chunk][-1] = wait(keyed[chunk][-1])
+        acts.append(wait(attend(starts[chunk], hdim, queries_both, keyed[chunk])))
         swapped.append(across(acts[-1]))
 
     turn(upper, 1)
-    keyed_far[0][0] = wait(keyed_far[0][0])
+    keyed[0][2] = wait(keyed[0][2])
     turn(beside, 1)
     attention(0)
     for step in range(3, n_ring):
@@ -340,10 +338,10 @@
     turn(upper, 2)
     rest = [far(after(lower[0]))]
     attention(1)
-    turn(beside, 2)
     swapped[0] = wait(swapped[0])
     swapped[1] = wait(swapped[1])
     attention(2)
+    turn(beside, 2)
     rest += [far(after(piece)) for piece in lower[1:2] + later]
     for step in range(3, n_ring):
         turn(upper, step)
@@ -358,7 +356,7 @@
         start = step % 2 * (depth - cut) if step > 1 else 0
         got = rest[step] if step < 2 else rest[1 + step // 2]
         theirs = [(beside[step], 0, cut), (got, start, start + depth - cut)]
-        keep_mine, keep_other, send_mine, send_other = project(acts, own, theirs)
+        keep_mine, keep_other, send_mine, send_other = project(acts, own + theirs)
         keeps.append((keep_mine, keep_other))
         sends.append(near(wait(send_other)))
         mine_sends.append(send_mine)
@@ -366,6 +364,13 @@
     def finish(step):
         other.append(across(wait(close(keeps[step][1], wait(sends[step])))))
         mine_got.append(near(mine_sends[step]))
+
+    outs = []
+
+    def put(step):
+        pair = (dp // 2 - step) % n_ring
+        where = jnp.stack([2 * pair + dp % 2, 2 * pair + 1 - dp % 2]).astype(jnp.int32) + token
+        return place(outs, n_dp * out_weight.shape[1], where, keeps[step][0], wait(mine_got[step]), wait(other[step]))
 
     columns(0)
     rest[1] = wait(rest[1])
@@ -377,20 +382,14 @@
             turn(beside, ahead)
         rest[1 + step // 2] = wait(rest[1 + step // 2])
         columns(step)
-        other[step - 2] = wait(other[step - 2])
+        outs = put(step - 2)
         finish(step)
         columns(step + 1)
-        other[step - 1] = wait(other[step - 1])
-        mine_got[step - 2] = wait(mine_got[step - 2])
-        mine_got[step - 1] = wait(mine_got[step - 1])
+        outs = put(step - 1)
         finish(step + 1)
-
-    where = []
-    for step in range(n_ring):
-        pair = (dp // 2 - step) % n_ring
-        where += [2 * pair + dp % 2, 2 * pair + 1 - dp % 2]
-    where = jnp.stack(where).astype(jnp.int32) + token
-    return place(where, [keep for keep, _ in keeps], mine_got, other)
+    for step in range(n_ring - 2, n_ring):
+        outs = put(step)
+    return tuple(outs)
 
 
 def solution(mesh):

time: 156 us -> 139 us (0.89)
  waiting for transfers between devices: 76.1 us -> 58.1 us
  Pallas kernels: 34.9 us -> 37.5 us
    ppermute x9, waiting for transfers between devices: 50.1 us -> 42.7 us  [onward(): return lax.ppermute(array, 'dp', [(i, (i + 2) % n_dp) for i in range(n_dp)])]
    ppermute x8, waiting for transfers between devices: 7.58 us -> 2.18 us  [far(): return lax.ppermute(array, 'seq', [(i, i ^ 2) for i in range(n_seq)])]
    ppermute x7, waiting for transfers between devices: 17.5 us -> 12.5 us  [across(): return lax.ppermute(array, 'dp', [(i, i ^ 1) for i in range(n_dp)])]
    pallas_call x4, Pallas kernels: 0.24 us -> 2.79 us  [close(): pl.pallas_call(close_kernel, in_specs=vmem_specs(2), out_specs=vmem_specs...]
    pallas_call x6 -> x9, Pallas kernels: 21.5 us -> 23.2 us  [the longest x4 15.2 us: project(): pl.pallas_call(functools.partial(project_kernel, [(low, high) for _, low,...]
    pallas_call x1, Pallas kernels: 3.74 us -> 2.07 us  [pack(): pl.pallas_call(functools.partial(pack_kernel, n_seq, chunks), grid_spec=p...]
    unnamed x72 -> x58, local copies, waits for them, and re-layouts: 12.4 us -> 11 us
  transfers between devices with their start and end apart: 36 -> 36, of which waited for: 15 -> 12; matrix products, arithmetic and copies ran while one was open for 1% -> 2% of each run, Pallas kernels for 21% -> 26%
where the time goes in v3:
time: 139 us
  waiting for transfers between devices  58.1 us (42%)
  Pallas kernels  37.5 us (27%)
  starting transfers between devices  27.7 us (20%)
  local copies, waits for them, and re-layouts  13.2 us (9%)
    ppermute x9, waiting for transfers between devices, onward(): return lax.ppermute(array, 'dp', [(i, (i + 2) % n_dp) for i in range(n_dp)])  42.7 us
    pallas_call x4, Pallas kernels, project(): pl.pallas_call(functools.partial(project_kernel, [(low, high) for _, low,...  15.2 us
    ppermute x7, waiting for transfers between devices, across(): return lax.ppermute(array, 'dp', [(i, i ^ 1) for i in range(n_dp)])  12.5 us
    unnamed x58, local copies, waits for them, and re-layouts  11 us
    ppermute x8, starting transfers between devices, far(): return lax.ppermute(array, 'seq', [(i, i ^ 2) for i in range(n_seq)])  9.72 us
    ppermute x7, starting transfers between devices, across(): return lax.ppermute(array, 'dp', [(i, i ^ 1) for i in range(n_dp)])  9.67 us
    pallas_call x3, Pallas kernels, attend(): pl.pallas_call(functools.partial(attend_kernel, len(queries)), grid=(widt...  9.37 us
    pallas_call x4, Pallas kernels, place(): pl.pallas_call(place_kernel, grid_spec=pltpu.PrefetchScalarGridSpec(num_s...  6.92 us
  transfers between devices with their start and end apart: 36, of which 12 were waited for; matrix products, arithmetic and copies ran while one was open for 2% of the time, Pallas kernels for 26%

profile of v3, /device:TPU:0, one launch (start us, length us, event | category | flops | bytes accessed | tf_op | source)
XLA Modules:
  0.0 138.7 jit_solution(12131210059911694362)
XLA Ops:
  0.7 1.2 slice.7.refs_0_
  1.9 3.0 %collective-permute-start.1 = (bf16[384,640]{1,0:T(8,128)(2,1)S(1)}, bf16[384,640]{1,0:T(8,128)(2,1)}, u32[]{:S(2)}, u32[]{:S(2)}) collective-permute-start(bf16[384,640]{1,0:T(8,128)(2,1)S(1)} %slice.7.refs_0_), channel_id=1, source_target_pairs={{0,2},{1,3},{2,0},{3,1},{4,6},{5,7},{6,4},{7,5},{8,10},{9,11},{10,... | collective-permute-start | bytes 1474568 | tf_op jit(solution)/shard_map/ppermute | solution.py:278
  5.9 1.6 %collective-permute-start = (bf16[256,640]{1,0:T(8,128)(2,1)S(1)}, bf16[256,640]{1,0:T(8,128)(2,1)}, u32[]{:S(2)}, u32[]{:S(2)}) collective-permute-start(bf16[256,640]{1,0:T(8,128)(2,1)S(1)} %slice.6.refs_1_), channel_id=1, source_target_pairs={{0,8},{4,12},{8,16},{12,20},{16,24},{20,28},{24,0},{28,4},{1,9},{5... | collective-permute-start | bytes 983048 | tf_op jit(solution)/shard_map/ppermute | solution.py:287
  11.9 2.1 %shard_map.104 = (bf16[2,128,1280]{2,1,0:T(8,128)(2,1)S(1)}, bf16[4,128,640]{2,1,0:T(8,128)(2,1)S(1)}, bf16[4,128,384]{2,1,0:T(8,128)(2,1)S(1)}, bf16[4,128,256]...) custom-call(s32[1]{0:T(128)} %bitcast.3.core_ref, ...), custom_call_target="tpu_custom_call" | custom-call | flops 1 | bytes 1 | tf_op jit(solution)/shard_map/pallas_call | solution.py:78
  14.0 2.2 %collective-permute-done.1.refs_2_ = bf16[384,640]{1,0:T(8,128)(2,1)} collective-permute-done((bf16[384,640]{1,0:T(8,128)(2,1)S(1)}, bf16[384,640]{1,0:T(8,128)(2,1)}, u32[]{:S(2)}, u32[]{:S(2)}) %collective-permute-start.1) | collective-permute-done | bytes 491552 | tf_op jit(solution)/shard_map/ppermute | solution.py:278
  20.6 1.6 %collective-permute-start.7 = (bf16[384,640]{1,0:T(8,128)(2,1)S(1)}, bf16[384,640]{1,0:T(8,128)(2,1)S(1)}, u32[]{:S(2)}, u32[]{:S(2)}) collective-permute-start(bf16[384,640]{1,0:T(8,128)(2,1)S(1)} %slice.7.refs_0_), channel_id=1, source_target_pairs={{0,8},{4,12},{8,16},{12,20},{16,24},{20,28},{24,0},{28,4},{1,9},{5... | collective-permute-start | bytes 1474568 | tf_op jit(solution)/shard_map/ppermute | solution.py:287
  22.8 7.9 %collective-permute-done.8.refs_1_ = bf16[256,640]{1,0:T(8,128)(2,1)S(1)} collective-permute-done((bf16[256,640]{1,0:T(8,128)(2,1)}, bf16[256,640]{1,0:T(8,128)(2,1)S(1)}, u32[]{:S(2)}, u32[]{:S(2)}) %collective-permute-start.8) | collective-permute-done | bytes 327712 | tf_op jit(solution)/shard_map/ppermute | solution.py:287
  31.5 9.7 %collective-permute-done.7.refs_0_ = bf16[384,640]{1,0:T(8,128)(2,1)S(1)} collective-permute-done((bf16[384,640]{1,0:T(8,128)(2,1)S(1)}, bf16[384,640]{1,0:T(8,128)(2,1)S(1)}, u32[]{:S(2)}, u32[]{:S(2)}) %collective-permute-start.7) | collective-permute-done | bytes 491552 | tf_op jit(solution)/shard_map/ppermute | solution.py:287
  41.9 9.8 %collective-permute-done.10.refs_2_ = bf16[384,640]{1,0:T(8,128)(2,1)S(1)} collective-permute-done((bf16[384,640]{1,0:T(8,128)(2,1)}, bf16[384,640]{1,0:T(8,128)(2,1)S(1)}, u32[]{:S(2)}, u32[]{:S(2)}) %collective-permute-start.10) | collective-permute-done | bytes 491552 | tf_op jit(solution)/shard_map/ppermute | solution.py:287
  51.7 4.7 %shard_map.105.refs_0_ = bf16[2,256,640]{2,1,0:T(8,128)(2,1)S(1)} custom-call(bf16[2,128,1280]{2,1,0:T(8,128)(2,1)S(1)} %get-tuple-element.149.refs_0_, bf16[2,128,1280]{2,1,0:T(8,128)(2,1)S(1)} %collective-permute-done.2.refs_1_, bf16[4,128,640]{2,1,0:T(8,128)(2,1)S(1)} %get-tuple-element.173.refs_2_, ...), custom_call_target="tpu_custom_call" | custom-call | flops 1 | bytes 1 | tf_op jit(solution)/shard_map/pallas_call | solution.py:129
  56.4 1.6 %collective-permute-start.11 = (bf16[2,256,640]{2,1,0:T(8,128)(2,1)S(1)}, bf16[2,256,640]{2,1,0:T(8,128)(2,1)S(1)}, u32[]{:S(2)}, u32[]{:S(2)}) collective-permute-start(bf16[2,256,640]{2,1,0:T(8,128)(2,1)S(1)} %shard_map.105.refs_0_), channel_id=1, source_target_pairs={{0,4},{4,0},{8,12},{12,8},{16,20},{20,16},{24,28},{28,24},{1,5},{5... | collective-permute-start | bytes 1966088 | tf_op jit(solution)/shard_map/ppermute | solution.py:284
  59.0 9.3 %collective-permute-done.14.refs_1_ = bf16[256,640]{1,0:T(8,128)(2,1)S(1)} collective-permute-done((bf16[256,640]{1,0:T(8,128)(2,1)S(1)}, bf16[256,640]{1,0:T(8,128)(2,1)S(1)}, u32[]{:S(2)}, u32[]{:S(2)}) %collective-permute-start.14) | collective-permute-done | bytes 327712 | tf_op jit(solution)/shard_map/ppermute | solution.py:287
  69.2 2.8 %shard_map.106.refs_2_ = bf16[2,256,384]{2,1,0:T(8,128)(2,1)S(1)} custom-call(bf16[2,128,1280]{2,1,0:T(8,128)(2,1)S(1)} %get-tuple-element.149.refs_0_, bf16[2,128,1280]{2,1,0:T(8,128)(2,1)S(1)} %collective-permute-done.2.refs_1_, bf16[4,128,384]{2,1,0:T(8,128)(2,1)S(1)} %get-tuple-element.186.refs_2_, ...), custom_call_target="tpu_custom_call" | custom-call | flops 1 | bytes 1 | tf_op jit(solution)/shard_map/pallas_call | solution.py:129
  72.1 1.6 %collective-permute-start.15 = (bf16[2,256,384]{2,1,0:T(8,128)(2,1)S(1)}, bf16[2,256,384]{2,1,0:T(8,128)(2,1)S(1)}, u32[]{:S(2)}, u32[]{:S(2)}) collective-permute-start(bf16[2,256,384]{2,1,0:T(8,128)(2,1)S(1)} %shard_map.106.refs_2_), channel_id=1, source_target_pairs={{0,4},{4,0},{8,12},{12,8},{16,20},{20,16},{24,28},{28,24},{1,5},{5... | collective-permute-start | bytes 1179656 | tf_op jit(solution)/shard_map/ppermute | solution.py:284
  74.4 1.5 %collective-permute-start.18 = (bf16[256,640]{1,0:T(8,128)(2,1)S(1)}, bf16[256,640]{1,0:T(8,128)(2,1)}, u32[]{:S(2)}, u32[]{:S(2)}) collective-permute-start(bf16[256,640]{1,0:T(8,128)(2,1)S(1)} %slice.6.refs_1_), channel_id=1, source_target_pairs={{0,2},{1,3},{2,0},{3,1},{4,6},{5,7},{6,4},{7,5},{8,10},{9,11},{10,... | collective-permute-start | bytes 983048 | tf_op jit(solution)/shard_map/ppermute | solution.py:278
  75.9 6.4 %collective-permute-done.15.refs_3_ = bf16[2,256,384]{2,1,0:T(8,128)(2,1)S(1)} collective-permute-done((bf16[2,256,384]{2,1,0:T(8,128)(2,1)S(1)}, bf16[2,256,384]{2,1,0:T(8,128)(2,1)S(1)}, u32[]{:S(2)}, u32[]{:S(2)}) %collective-permute-start.15) | collective-permute-done | bytes 393248 | tf_op jit(solution)/shard_map/ppermute | solution.py:284
  82.3 1.9 %shard_map.107.refs_4_ = bf16[2,256,256]{2,1,0:T(8,128)(2,1)S(1)} custom-call(bf16[2,128,1280]{2,1,0:T(8,128)(2,1)S(1)} %get-tuple-element.149.refs_0_, bf16[2,128,1280]{2,1,0:T(8,128)(2,1)S(1)} %collective-permute-done.2.refs_1_, bf16[4,128,256]{2,1,0:T(8,128)(2,1)S(1)} %get-tuple-element.202.refs_2_, ...), custom_call_target="tpu_custom_call" | custom-call | flops 1 | bytes 1 | tf_op jit(solution)/shard_map/pallas_call | solution.py:129
  86.4 1.5 %collective-permute-start.17 = (bf16[2,256,256]{2,1,0:T(8,128)(2,1)S(1)}, bf16[2,256,256]{2,1,0:T(8,128)(2,1)}, u32[]{:S(2)}, u32[]{:S(2)}) collective-permute-start(bf16[2,256,256]{2,1,0:T(8,128)(2,1)S(1)} %shard_map.107.refs_4_), channel_id=1, source_target_pairs={{0,4},{4,0},{8,12},{12,8},{16,20},{20,16},{24,28},{28,24},{1,5},{5... | collective-permute-start | bytes 786440 | tf_op jit(solution)/shard_map/ppermute | solution.py:284
  87.9 5.0 %collective-permute-done.19.refs_0_ = bf16[384,640]{1,0:T(8,128)(2,1)S(1)} collective-permute-done((bf16[384,640]{1,0:T(8,128)(2,1)S(1)}, bf16[384,640]{1,0:T(8,128)(2,1)S(1)}, u32[]{:S(2)}, u32[]{:S(2)}) %collective-permute-start.19) | collective-permute-done | bytes 491552 | tf_op jit(solution)/shard_map/ppermute | solution.py:287
  97.0 3.4 %shard_map.109 = (f32[256,640]{1,0:T(8,128)S(1)}, f32[256,640]{1,0:T(8,128)S(1)}, bf16[256,640]{1,0:T(8,128)(2,1)S(1)}, bf16[256,640]{1,0:T(8,128)(2,1)S(1)}) custom-call(bf16[1024,1280]{1,0:T(8,128)(2,1)S(1)} %shard_map.108.acts_ref, bf16[384,640]{1,0:T(8,128)(2,1)S(1)} %slice.7.refs_0_, bf16[256,640]{1,0:T(8,128)(2,1)S(1)} %slice.6.refs_1_, ...), custom_call_target="tpu_custom_call" | custom-call | flops 1 | bytes 1 | tf_op jit(solution)/shard_map/pallas_call | solution.py:186
  100.5 3.9 %shard_map.110 = (f32[256,640]{1,0:T(8,128)S(1)}, f32[256,640]{1,0:T(8,128)S(1)}, bf16[256,640]{1,0:T(8,128)(2,1)}, bf16[256,640]{1,0:T(8,128)(2,1)S(1)}) custom-call(bf16[1024,1280]{1,0:T(8,128)(2,1)S(1)} %shard_map.108.acts_ref, bf16[384,640]{1,0:T(8,128)(2,1)S(1)} %copy-done.17, bf16[256,640]{1,0:T(8,128)(2,1)} %collective-permute-done.refs_1_, ...), custom_call_target="tpu_custom_call" | custom-call | flops 1 | bytes 1 | tf_op jit(solution)/shard_map/pallas_call | solution.py:186
  105.0 1.6 %collective-permute-start.27 = (bf16[256,640]{1,0:T(8,128)(2,1)S(1)}, bf16[256,640]{1,0:T(8,128)(2,1)S(1)}, u32[]{:S(2)}, u32[]{:S(2)}) collective-permute-start(bf16[256,640]{1,0:T(8,128)(2,1)S(1)} %shard_map.111), channel_id=1, source_target_pairs={{0,4},{4,0},{8,12},{12,8},{16,20},{20,16},{24,28},{28,24},{1,5},{5... | collective-permute-start | bytes 983048 | tf_op jit(solution)/shard_map/ppermute | solution.py:284
  107.4 3.9 %shard_map.113 = (f32[256,640]{1,0:T(8,128)S(1)}, f32[256,640]{1,0:T(8,128)S(1)}, bf16[256,640]{1,0:T(8,128)(2,1)}, bf16[256,640]{1,0:T(8,128)(2,1)S(1)}) custom-call(bf16[1024,1280]{1,0:T(8,128)(2,1)S(1)} %shard_map.108.acts_ref, bf16[384,640]{1,0:T(8,128)(2,1)S(1)} %copy-done.13, bf16[256,640]{1,0:T(8,128)(2,1)S(1)} %collective-permute-done.8.refs_1_, ...), custom_call_target="tpu_custom_call" | custom-call | flops 1 | bytes 1 | tf_op jit(solution)/shard_map/pallas_call | solution.py:186
  112.7 1.3 collective-permute-start.32
  114.0 4.0 %shard_map.115 = (f32[256,640]{1,0:T(8,128)S(1)}, f32[256,640]{1,0:T(8,128)S(1)}, bf16[256,640]{1,0:T(8,128)(2,1)S(1)}, bf16[256,640]{1,0:T(8,128)(2,1)}) custom-call(bf16[1024,1280]{1,0:T(8,128)(2,1)S(1)} %shard_map.108.acts_ref, bf16[384,640]{1,0:T(8,128)(2,1)S(1)} %copy-done.15, bf16[256,640]{1,0:T(8,128)(2,1)S(1)} %collective-permute-done.14.refs_1_, ...), custom_call_target="tpu_custom_call" | custom-call | flops 1 | bytes 1 | tf_op jit(solution)/shard_map/pallas_call | solution.py:186
  123.0 1.5 %shard_map.117 = (bf16[128,5120]{1,0:T(8,128)(2,1)}, bf16[128,5120]{1,0:T(8,128)(2,1)}) custom-call(s32[2]{0:T(128)S(1)} %add_add_fusion.3.where_ref, f32[256,640]{1,0:T(8,128)S(1)} %get-tuple-element.281.keep_ref, bf16[256,640]{1,0:T(8,128)(2,1)S(1)} %copy-done.23, bf16[256,640]{1,0:T(8,128)(2,1)S(1)} %copy-done.25), custom_call_target="tpu_custom_call" | custom-call | flops 1 | bytes 1 | tf_op jit(solution)/shard_map/pallas_call | solution.py:237
  125.6 1.4 collective-permute-start.35
  127.0 2.5 %shard_map.118 = (bf16[128,5120]{1,0:T(8,128)(2,1)}, bf16[128,5120]{1,0:T(8,128)(2,1)}) custom-call(s32[2]{0:T(128)S(1)} %add_add_fusion.2.where_ref, f32[256,640]{1,0:T(8,128)S(1)} %get-tuple-element.278.keep_ref, bf16[256,640]{1,0:T(8,128)(2,1)S(1)} %collective-permute-done.33.got_ref, ...), custom_call_target="tpu_custom_call", output_to_operand_aliasing={{0}: (4, {}), {1}: (5, {})} | custom-call | flops 1 | bytes 1 | tf_op jit(solution)/shard_map/pallas_call | solution.py:237
  129.5 1.6 %collective-permute-done.29.other_ref = bf16[256,640]{1,0:T(8,128)(2,1)S(1)} collective-permute-done((bf16[256,640]{1,0:T(8,128)(2,1)}, bf16[256,640]{1,0:T(8,128)(2,1)S(1)}, u32[]{:S(2)}, u32[]{:S(2)}) %collective-permute-start.29) | collective-permute-done | bytes 327712 | tf_op jit(solution)/shard_map/ppermute | solution.py:284
  131.1 1.5 %shard_map.119 = (bf16[128,5120]{1,0:T(8,128)(2,1)}, bf16[128,5120]{1,0:T(8,128)(2,1)}) custom-call(s32[2]{0:T(128)S(1)} %add_add_fusion.1.where_ref, f32[256,640]{1,0:T(8,128)S(1)} %copy-done.9, bf16[256,640]{1,0:T(8,128)(2,1)S(1)} %collective-permute-done.30.got_ref, ...), custom_call_target="tpu_custom_call", output_to_operand_aliasing={{0}: (4, {}), {1}: (5, {})} | custom-call | flops 1 | bytes 1 | tf_op jit(solution)/shard_map/pallas_call | solution.py:237
  132.7 4.5 %collective-permute-done.35.other_ref = bf16[256,640]{1,0:T(8,128)(2,1)S(1)} collective-permute-done((bf16[256,640]{1,0:T(8,128)(2,1)S(1)}, bf16[256,640]{1,0:T(8,128)(2,1)S(1)}, u32[]{:S(2)}, u32[]{:S(2)}) %collective-permute-start.35) | collective-permute-done | bytes 327712 | tf_op jit(solution)/shard_map/ppermute | solution.py:284
  137.2 1.5 %shard_map.120 = (bf16[128,5120]{1,0:T(8,128)(2,1)}, bf16[128,5120]{1,0:T(8,128)(2,1)}) custom-call(s32[2]{0:T(128)S(1)} %add_add_fusion.where_ref, f32[256,640]{1,0:T(8,128)S(1)} %copy-done.7, bf16[256,640]{1,0:T(8,128)(2,1)S(1)} %collective-permute-done.34.got_ref, ...), custom_call_target="tpu_custom_call", output_to_operand_aliasing={{0}: (4, {}), {1}: (5, {})} | custom-call | flops 1 | bytes 1 | tf_op jit(solution)/shard_map/pallas_call | solution.py:237
  (127 shorter events, 30.1 us)
Async XLA Ops:
  1.9 14.3 %collective-permute-start.1 = (bf16[384,640]{1,0:T(8,128)(2,1)S(1)}, bf16[384,640]{1,0:T(8,128)(2,1)}, u32[]{:S(2)}, u32[]{:S(2)}) collective-permute-start(bf16[384,640]{1,0:T(8,128)(2,1)S(1)} %slice.7.refs_0_), channel_id=1, source_target_pairs={{0,2},{1,3},{2,0},{3,1},{4,6},{5,7},{6,4},{7,5},{8,10},{9,11},{10,... | collective-permute-start | bytes 1474568 | tf_op jit(solution)/shard_map/ppermute | solution.py:278
  5.9 11.2 %collective-permute-start = (bf16[256,640]{1,0:T(8,128)(2,1)S(1)}, bf16[256,640]{1,0:T(8,128)(2,1)}, u32[]{:S(2)}, u32[]{:S(2)}) collective-permute-start(bf16[256,640]{1,0:T(8,128)(2,1)S(1)} %slice.6.refs_1_), channel_id=1, source_target_pairs={{0,8},{4,12},{8,16},{12,20},{16,24},{20,28},{24,0},{28,4},{1,9},{5... | collective-permute-start | bytes 983048 | tf_op jit(solution)/shard_map/ppermute | solution.py:287
  17.6 14.0 %collective-permute-start.2 = (bf16[2,128,1280]{2,1,0:T(8,128)(2,1)S(1)}, bf16[2,128,1280]{2,1,0:T(8,128)(2,1)S(1)}, u32[]{:S(2)}, u32[]{:S(2)}) collective-permute-start(bf16[2,128,1280]{2,1,0:T(8,128)(2,1)S(1)} %get-tuple-element.158), channel_id=1, source_target_pairs={{0,1},{1,0},{2,3},{3,2},{4,5},{5,4},{6,7},{7,6},{8,9},{9,8},{10,11... | collective-permute-start | bytes 1966088 | tf_op jit(solution)/shard_map/ppermute | solution.py:281
  17.6 4.6 %collective-permute-start.3 = (bf16[4,128,256]{2,1,0:T(8,128)(2,1)S(1)}, bf16[4,128,256]{2,1,0:T(8,128)(2,1)S(1)}, u32[]{:S(2)}, u32[]{:S(2)}) collective-permute-start(bf16[4,128,256]{2,1,0:T(8,128)(2,1)S(1)} %get-tuple-element.165), channel_id=1, source_target_pairs={{0,1},{1,0},{2,3},{3,2},{4,5},{5,4},{6,7},{7,6},{8,9},{9,8},{10,11... | collective-permute-start | bytes 786440 | tf_op jit(solution)/shard_map/ppermute | solution.py:281
  18.1 12.6 %collective-permute-start.8 = (bf16[256,640]{1,0:T(8,128)(2,1)}, bf16[256,640]{1,0:T(8,128)(2,1)S(1)}, u32[]{:S(2)}, u32[]{:S(2)}) collective-permute-start(bf16[256,640]{1,0:T(8,128)(2,1)} %collective-permute-done.refs_1_), channel_id=1, source_target_pairs={{0,8},{4,12},{8,16},{12,20},{16,24},{20,28},{24,0},{28,4},{1,9},{5... | collective-permute-start | bytes 983048 | tf_op jit(solution)/shard_map/ppermute | solution.py:287
  19.7 21.5 %collective-permute-start.6 = (bf16[4,128,640]{2,1,0:T(8,128)(2,1)S(1)}, bf16[4,128,640]{2,1,0:T(8,128)(2,1)S(1)}, u32[]{:S(2)}, u32[]{:S(2)}) collective-permute-start(bf16[4,128,640]{2,1,0:T(8,128)(2,1)S(1)} %get-tuple-element.173.refs_2_), channel_id=1, source_target_pairs={{0,2},{1,3},{2,0},{3,1},{4,6},{5,7},{6,4},{7,5},{8,10},{9,11},{10,... | collective-permute-start | bytes 1966088 | tf_op jit(solution)/shard_map/ppermute | solution.py:278
  20.6 20.6 %collective-permute-start.7 = (bf16[384,640]{1,0:T(8,128)(2,1)S(1)}, bf16[384,640]{1,0:T(8,128)(2,1)S(1)}, u32[]{:S(2)}, u32[]{:S(2)}) collective-permute-start(bf16[384,640]{1,0:T(8,128)(2,1)S(1)} %slice.7.refs_0_), channel_id=1, source_target_pairs={{0,8},{4,12},{8,16},{12,20},{16,24},{20,28},{24,0},{28,4},{1,9},{5... | collective-permute-start | bytes 1474568 | tf_op jit(solution)/shard_map/ppermute | solution.py:287
  22.2 29.6 %collective-permute-start.9 = (bf16[4,128,640]{2,1,0:T(8,128)(2,1)S(1)}, bf16[4,128,640]{2,1,0:T(8,128)(2,1)S(1)}, u32[]{:S(2)}, u32[]{:S(2)}) collective-permute-start(bf16[4,128,640]{2,1,0:T(8,128)(2,1)S(1)} %collective-permute-done.5.refs_3_), channel_id=1, source_target_pairs={{0,2},{1,3},{2,0},{3,1},{4,6},{5,7},{6,4},{7,5},{8,10},{9,11},{10,... | collective-permute-start | bytes 1966088 | tf_op jit(solution)/shard_map/ppermute | solution.py:278
  30.7 38.6 %collective-permute-start.12 = (bf16[8,128,384]{2,1,0:T(8,128)(2,1)S(1)}, bf16[8,128,384]{2,1,0:T(8,128)(2,1)S(1)}, u32[]{:S(2)}, u32[]{:S(2)}) collective-permute-start(bf16[8,128,384]{2,1,0:T(8,128)(2,1)S(1)} %pad_maximum_fusion), channel_id=1, source_target_pairs={{0,2},{1,3},{2,0},{3,1},{4,6},{5,7},{6,4},{7,5},{8,10},{9,11},{10,... | collective-permute-start | bytes 2359304 | tf_op jit(solution)/shard_map/ppermute | solution.py:278
  31.5 20.2 %collective-permute-start.10 = (bf16[384,640]{1,0:T(8,128)(2,1)}, bf16[384,640]{1,0:T(8,128)(2,1)S(1)}, u32[]{:S(2)}, u32[]{:S(2)}) collective-permute-start(bf16[384,640]{1,0:T(8,128)(2,1)} %collective-permute-done.1.refs_2_), channel_id=1, source_target_pairs={{0,8},{4,12},{8,16},{12,20},{16,24},{20,28},{24,0},{28,4},{1,9},{5... | collective-permute-start | bytes 1474568 | tf_op jit(solution)/shard_map/ppermute | solution.py:287
  41.2 28.0 %collective-permute-start.13 = (bf16[384,640]{1,0:T(8,128)(2,1)S(1)}, bf16[384,640]{1,0:T(8,128)(2,1)S(1)}, u32[]{:S(2)}, u32[]{:S(2)}) collective-permute-start(bf16[384,640]{1,0:T(8,128)(2,1)S(1)} %collective-permute-done.7.refs_0_), channel_id=1, source_target_pairs={{0,8},{4,12},{8,16},{12,20},{16,24},{20,28},{24,0},{28,4},{1,9},{5... | collective-permute-start | bytes 1474568 | tf_op jit(solution)/shard_map/ppermute | solution.py:287
  41.2 27.1 %collective-permute-start.14 = (bf16[256,640]{1,0:T(8,128)(2,1)S(1)}, bf16[256,640]{1,0:T(8,128)(2,1)S(1)}, u32[]{:S(2)}, u32[]{:S(2)}) collective-permute-start(bf16[256,640]{1,0:T(8,128)(2,1)S(1)} %collective-permute-done.8.refs_1_), channel_id=1, source_target_pairs={{0,8},{4,12},{8,16},{12,20},{16,24},{20,28},{24,0},{28,4},{1,9},{5... | collective-permute-start | bytes 983048 | tf_op jit(solution)/shard_map/ppermute | solution.py:287
  56.4 18.0 %collective-permute-start.11 = (bf16[2,256,640]{2,1,0:T(8,128)(2,1)S(1)}, bf16[2,256,640]{2,1,0:T(8,128)(2,1)S(1)}, u32[]{:S(2)}, u32[]{:S(2)}) collective-permute-start(bf16[2,256,640]{2,1,0:T(8,128)(2,1)S(1)} %shard_map.105.refs_0_), channel_id=1, source_target_pairs={{0,4},{4,0},{8,12},{12,8},{16,20},{20,16},{24,28},{28,24},{1,5},{5... | collective-permute-start | bytes 1966088 | tf_op jit(solution)/shard_map/ppermute | solution.py:284
  58.1 24.3 %collective-permute-start.16 = (bf16[8,128,256]{2,1,0:T(8,128)(2,1)S(1)}, bf16[8,128,256]{2,1,0:T(8,128)(2,1)S(1)}, u32[]{:S(2)}, u32[]{:S(2)}) collective-permute-start(bf16[8,128,256]{2,1,0:T(8,128)(2,1)S(1)} %pad_maximum_fusion.2), channel_id=1, source_target_pairs={{0,2},{1,3},{2,0},{3,1},{4,6},{5,7},{6,4},{7,5},{8,10},{9,11},{10,... | collective-permute-start | bytes 1572872 | tf_op jit(solution)/shard_map/ppermute | solution.py:278
  68.3 16.1 %collective-permute-start.20 = (bf16[384,640]{1,0:T(8,128)(2,1)S(1)}, bf16[384,640]{1,0:T(8,128)(2,1)}, u32[]{:S(2)}, u32[]{:S(2)}) collective-permute-start(bf16[384,640]{1,0:T(8,128)(2,1)S(1)} %collective-permute-done.10.refs_2_), channel_id=1, source_target_pairs={{0,8},{4,12},{8,16},{12,20},{16,24},{20,28},{24,0},{28,4},{1,9},{5... | collective-permute-start | bytes 1474568 | tf_op jit(solution)/shard_map/ppermute | solution.py:287
  72.1 10.2 %collective-permute-start.15 = (bf16[2,256,384]{2,1,0:T(8,128)(2,1)S(1)}, bf16[2,256,384]{2,1,0:T(8,128)(2,1)S(1)}, u32[]{:S(2)}, u32[]{:S(2)}) collective-permute-start(bf16[2,256,384]{2,1,0:T(8,128)(2,1)S(1)} %shard_map.106.refs_2_), channel_id=1, source_target_pairs={{0,4},{4,0},{8,12},{12,8},{16,20},{20,16},{24,28},{28,24},{1,5},{5... | collective-permute-start | bytes 1179656 | tf_op jit(solution)/shard_map/ppermute | solution.py:284
  73.7 19.3 %collective-permute-start.19 = (bf16[384,640]{1,0:T(8,128)(2,1)S(1)}, bf16[384,640]{1,0:T(8,128)(2,1)S(1)}, u32[]{:S(2)}, u32[]{:S(2)}) collective-permute-start(bf16[384,640]{1,0:T(8,128)(2,1)S(1)} %collective-permute-done.13.refs_0_), channel_id=1, source_target_pairs={{0,8},{4,12},{8,16},{12,20},{16,24},{20,28},{24,0},{28,4},{1,9},{5... | collective-permute-start | bytes 1474568 | tf_op jit(solution)/shard_map/ppermute | solution.py:287
  74.4 19.3 %collective-permute-start.18 = (bf16[256,640]{1,0:T(8,128)(2,1)S(1)}, bf16[256,640]{1,0:T(8,128)(2,1)}, u32[]{:S(2)}, u32[]{:S(2)}) collective-permute-start(bf16[256,640]{1,0:T(8,128)(2,1)S(1)} %slice.6.refs_1_), channel_id=1, source_target_pairs={{0,2},{1,3},{2,0},{3,1},{4,6},{5,7},{6,4},{7,5},{8,10},{9,11},{10,... | collective-permute-start | bytes 983048 | tf_op jit(solution)/shard_map/ppermute | solution.py:278
  84.4 16.1 %collective-permute-start.23 = (bf16[256,640]{1,0:T(8,128)(2,1)}, bf16[256,640]{1,0:T(8,128)(2,1)}, u32[]{:S(2)}, u32[]{:S(2)}) collective-permute-start(bf16[256,640]{1,0:T(8,128)(2,1)} %collective-permute-done.refs_1_), channel_id=1, source_target_pairs={{0,2},{1,3},{2,0},{3,1},{4,6},{5,7},{6,4},{7,5},{8,10},{9,11},{10,... | collective-permute-start | bytes 983048 | tf_op jit(solution)/shard_map/ppermute | solution.py:278
  85.3 22.0 %collective-permute-start.21 = (bf16[512,640]{1,0:T(8,128)(2,1)}, bf16[512,640]{1,0:T(8,128)(2,1)S(1)}, u32[]{:S(2)}, u32[]{:S(2)}) collective-permute-start(bf16[512,640]{1,0:T(8,128)(2,1)} %pad_maximum_fusion.1), channel_id=1, source_target_pairs={{0,2},{1,3},{2,0},{3,1},{4,6},{5,7},{6,4},{7,5},{8,10},{9,11},{10,... | collective-permute-start | bytes 1966088 | tf_op jit(solution)/shard_map/ppermute | solution.py:278
  86.4 7.3 %collective-permute-start.17 = (bf16[2,256,256]{2,1,0:T(8,128)(2,1)S(1)}, bf16[2,256,256]{2,1,0:T(8,128)(2,1)}, u32[]{:S(2)}, u32[]{:S(2)}) collective-permute-start(bf16[2,256,256]{2,1,0:T(8,128)(2,1)S(1)} %shard_map.107.refs_4_), channel_id=1, source_target_pairs={{0,4},{4,0},{8,12},{12,8},{16,20},{20,16},{24,28},{28,24},{1,5},{5... | collective-permute-start | bytes 786440 | tf_op jit(solution)/shard_map/ppermute | solution.py:284
  93.7 13.6 %collective-permute-start.22 = (bf16[384,640]{1,0:T(8,128)(2,1)}, bf16[384,640]{1,0:T(8,128)(2,1)}, u32[]{:S(2)}, u32[]{:S(2)}) collective-permute-start(bf16[384,640]{1,0:T(8,128)(2,1)} %collective-permute-done.20.refs_2_), channel_id=1, source_target_pairs={{0,8},{4,12},{8,16},{12,20},{16,24},{20,28},{24,0},{28,4},{1,9},{5... | collective-permute-start | bytes 1474568 | tf_op jit(solution)/shard_map/ppermute | solution.py:287
  104.9 13.9 %collective-permute-start.28 = (bf16[256,640]{1,0:T(8,128)(2,1)S(1)}, bf16[256,640]{1,0:T(8,128)(2,1)S(1)}, u32[]{:S(2)}, u32[]{:S(2)}) collective-permute-start(bf16[256,640]{1,0:T(8,128)(2,1)S(1)} %get-tuple-element.247), channel_id=1, source_target_pairs={{0,1},{1,0},{2,3},{3,2},{4,5},{5,4},{6,7},{7,6},{8,9},{9,8},{10,11... | collective-permute-start | bytes 983048 | tf_op jit(solution)/shard_map/ppermute | solution.py:281
  105.0 13.8 %collective-permute-start.27 = (bf16[256,640]{1,0:T(8,128)(2,1)S(1)}, bf16[256,640]{1,0:T(8,128)(2,1)S(1)}, u32[]{:S(2)}, u32[]{:S(2)}) collective-permute-start(bf16[256,640]{1,0:T(8,128)(2,1)S(1)} %shard_map.111), channel_id=1, source_target_pairs={{0,4},{4,0},{8,12},{12,8},{16,20},{20,16},{24,28},{28,24},{1,5},{5... | collective-permute-start | bytes 983048 | tf_op jit(solution)/shard_map/ppermute | solution.py:284
  112.2 6.6 %collective-permute-start.26 = (bf16[256,640]{1,0:T(8,128)(2,1)S(1)}, bf16[256,640]{1,0:T(8,128)(2,1)S(1)}, u32[]{:S(2)}, u32[]{:S(2)}) collective-permute-start(bf16[256,640]{1,0:T(8,128)(2,1)S(1)} %get-tuple-element.245), channel_id=1, source_target_pairs={{0,1},{1,0},{2,3},{3,2},{4,5},{5,4},{6,7},{7,6},{8,9},{9,8},{10,11... | collective-permute-start | bytes 983048 | tf_op jit(solution)/shard_map/ppermute | solution.py:281
  112.4 8.6 %collective-permute-start.33 = (bf16[256,640]{1,0:T(8,128)(2,1)}, bf16[256,640]{1,0:T(8,128)(2,1)S(1)}, u32[]{:S(2)}, u32[]{:S(2)}) collective-permute-start(bf16[256,640]{1,0:T(8,128)(2,1)} %get-tuple-element.262), channel_id=1, source_target_pairs={{0,1},{1,0},{2,3},{3,2},{4,5},{5,4},{6,7},{7,6},{8,9},{9,8},{10,11... | collective-permute-start | bytes 983048 | tf_op jit(solution)/shard_map/ppermute | solution.py:281
  112.7 11.8 %collective-permute-start.32 = (bf16[256,640]{1,0:T(8,128)(2,1)}, bf16[256,640]{1,0:T(8,128)(2,1)}, u32[]{:S(2)}, u32[]{:S(2)}) collective-permute-start(bf16[256,640]{1,0:T(8,128)(2,1)} %shard_map.112), channel_id=1, source_target_pairs={{0,4},{4,0},{8,12},{12,8},{16,20},{20,16},{24,28},{28,24},{1,5},{5... | collective-permute-start | bytes 983048 | tf_op jit(solution)/shard_map/ppermute | solution.py:284
  119.7 4.8 %collective-permute-start.31 = (bf16[256,640]{1,0:T(8,128)(2,1)}, bf16[256,640]{1,0:T(8,128)(2,1)}, u32[]{:S(2)}, u32[]{:S(2)}) collective-permute-start(bf16[256,640]{1,0:T(8,128)(2,1)} %get-tuple-element.260), channel_id=1, source_target_pairs={{0,1},{1,0},{2,3},{3,2},{4,5},{5,4},{6,7},{7,6},{8,9},{9,8},{10,11... | collective-permute-start | bytes 983048 | tf_op jit(solution)/shard_map/ppermute | solution.py:281
  119.7 9.7 %collective-permute-start.30 = (bf16[256,640]{1,0:T(8,128)(2,1)}, bf16[256,640]{1,0:T(8,128)(2,1)S(1)}, u32[]{:S(2)}, u32[]{:S(2)}) collective-permute-start(bf16[256,640]{1,0:T(8,128)(2,1)} %get-tuple-element.254), channel_id=1, source_target_pairs={{0,1},{1,0},{2,3},{3,2},{4,5},{5,4},{6,7},{7,6},{8,9},{9,8},{10,11... | collective-permute-start | bytes 983048 | tf_op jit(solution)/shard_map/ppermute | solution.py:281
  120.3 10.8 %collective-permute-start.29 = (bf16[256,640]{1,0:T(8,128)(2,1)}, bf16[256,640]{1,0:T(8,128)(2,1)S(1)}, u32[]{:S(2)}, u32[]{:S(2)}) collective-permute-start(bf16[256,640]{1,0:T(8,128)(2,1)} %shard_map.114), channel_id=1, source_target_pairs={{0,4},{4,0},{8,12},{12,8},{16,20},{20,16},{24,28},{28,24},{1,5},{5... | collective-permute-start | bytes 983048 | tf_op jit(solution)/shard_map/ppermute | solution.py:284
  121.0 11.6 %collective-permute-start.34 = (bf16[256,640]{1,0:T(8,128)(2,1)}, bf16[256,640]{1,0:T(8,128)(2,1)S(1)}, u32[]{:S(2)}, u32[]{:S(2)}) collective-permute-start(bf16[256,640]{1,0:T(8,128)(2,1)} %copy-done.26), channel_id=1, source_target_pairs={{0,1},{1,0},{2,3},{3,2},{4,5},{5,4},{6,7},{7,6},{8,9},{9,8},{10,11... | collective-permute-start | bytes 983048 | tf_op jit(solution)/shard_map/ppermute | solution.py:281
  125.6 11.6 %collective-permute-start.35 = (bf16[256,640]{1,0:T(8,128)(2,1)S(1)}, bf16[256,640]{1,0:T(8,128)(2,1)S(1)}, u32[]{:S(2)}, u32[]{:S(2)}) collective-permute-start(bf16[256,640]{1,0:T(8,128)(2,1)S(1)} %shard_map.116), channel_id=1, source_target_pairs={{0,4},{4,0},{8,12},{12,8},{16,20},{20,16},{24,28},{28,24},{1,5},{5... | collective-permute-start | bytes 983048 | tf_op jit(solution)/shard_map/ppermute | solution.py:284
  (33 other events, 129.5 us)

commit v4 on v3

--- a/solution.py
+++ b/solution.py
@@ -138,74 +138,69 @@
     )(*queries, *keyed)
 
 
-def assemble_kernel(groups, chunks, flip_ref, *refs):
-    part_refs, out_ref = refs[:-1], refs[-1]
-    rows, group = out_ref.shape[0] // 8, out_ref.shape[1] // groups
-    start = 0
-    for at, width in enumerate(chunks):
-        for g in range(groups):
-            low, high = max(start, g * group), min(start + width, (g + 1) * group)
-            if low >= high:
-                continue
-            to = pl.ds(pl.multiple_of((g ^ flip_ref[0]) * group + low - g * group, 128), high - low)
-            for side in range(2):
-                for kind in range(2):
-                    for core in range(2):
-                        first = (4 * core + 2 * side + kind) * rows
-                        out_ref[first : first + rows, to] = part_refs[2 * at + side][
-                            kind, core * rows : (core + 1) * rows, low - start : high - start
-                        ]
-        start += width
-
-
-def assemble(flip, groups, chunks, pairs):
-    rows = 4 * pairs[0][0].shape[1]
-    return pl.pallas_call(
-        functools.partial(assemble_kernel, groups, chunks),
-        in_specs=[pl.BlockSpec(memory_space=pltpu.SMEM)] + vmem_specs(2 * len(pairs)),
-        out_specs=vmem_specs(1)[0],
-        out_shape=jax.ShapeDtypeStruct((rows, sum(chunks)), LOW),
-        compiler_params=params(),
-        cost_estimate=LIGHT,
-    )(flip, *[part for pair in pairs for part in pair])
-
-
-def project_kernel(spans, acts_ref, *refs):
-    weight_refs = refs[:-4]
-    keep_mine_ref, keep_other_ref, send_mine_ref, send_other_ref = refs[-4:]
-    rows = keep_mine_ref.shape[0]
-    weight = jnp.concatenate([ref[low:high] for ref, (low, high) in zip(weight_refs, spans)], axis=0)
-    for at, out_ref in enumerate((keep_mine_ref, keep_other_ref, send_mine_ref, send_other_ref)):
-        part = jnp.dot(acts_ref[at * rows : (at + 1) * rows], weight, preferred_element_type=WIDE)
-        out_ref[...] = part.astype(out_ref.dtype)
-
-
-def project(acts, pieces):
+def project_kernel(n_chunks, spans, flip_ref, *refs):
+    sides = refs[:n_chunks], refs[n_chunks : 2 * n_chunks]
+    weight_refs, out_refs, weight_ref = refs[2 * n_chunks : -6], refs[-6:-1], refs[-1]
+    rows = out_refs[0].shape[0] // 2
+    depth = weight_ref.shape[0] // 2
+    at = 0
+    for ref, (low, high) in zip(weight_refs, spans):
+        block, inside = at // depth, at % depth
+        first = pl.multiple_of((block ^ flip_ref[0]) * depth + inside, 16)
+        weight_ref[pl.ds(first, high - low)] = ref[low:high]
+        at += high - low
+    weight = weight_ref[...]
+    for side, parts in enumerate(sides):
+        acts = jnp.concatenate([ref[...].reshape(4 * rows, ref.shape[-1]) for ref in parts], axis=1)
+        total = jnp.dot(acts, weight, preferred_element_type=WIDE)
+        for kind in range(2):
+            first = 2 * kind * rows
+            here = slice(kind * rows, (kind + 1) * rows)
+            out_refs[side][here] = total[first : first + rows]
+            low = total[first + rows : first + 2 * rows].astype(LOW)
+            if side:
+                out_refs[3 + kind][...] = low
+            else:
+                out_refs[2][here] = low
+
+
+def project(flip, acts, pieces):
+    mine, theirs = zip(*acts)
     weights = [weight for weight, _, _ in pieces]
-    rows, n = acts.shape[0] // 4, weights[0].shape[1]
-    return pl.pallas_call(
-        functools.partial(project_kernel, [(low, high) for _, low, high in pieces]),
-        in_specs=vmem_specs(1 + len(weights)),
-        out_specs=vmem_specs(4),
-        out_shape=[jax.ShapeDtypeStruct((rows, n), WIDE)] * 2 + [jax.ShapeDtypeStruct((rows, n), LOW)] * 2,
-        compiler_params=params(),
-        cost_estimate=LIGHT,
-    )(acts, *weights)
-
-
-def close_kernel(keep_ref, got_ref, out_ref):
-    out_ref[...] = (keep_ref[...] + got_ref[...].astype(WIDE)).astype(LOW)
-
-
-def close(keep, got):
+    spans = [(low, high) for _, low, high in pieces]
+    rows, n = mine[0].shape[1], weights[0].shape[1]
+    depth = sum(high - low for low, high in spans)
+    return pl.pallas_call(
+        functools.partial(project_kernel, len(acts), spans),
+        in_specs=[pl.BlockSpec(memory_space=pltpu.SMEM)] + vmem_specs(2 * len(acts) + len(weights)),
+        out_specs=vmem_specs(5),
+        out_shape=[jax.ShapeDtypeStruct((rows, n), WIDE)] * 2
+        + [jax.ShapeDtypeStruct((rows, n), LOW)]
+        + [jax.ShapeDtypeStruct((rows // 2, n), LOW)] * 2,
+        scratch_shapes=[pltpu.VMEM((depth, n), LOW)],
+        compiler_params=params(),
+        cost_estimate=pl.CostEstimate(flops=8 * rows * depth * pl.cdiv(n, 256) * 256, transcendentals=0, bytes_accessed=1),
+    )(flip, *mine, *theirs, *weights)
+
+
+def close_kernel(keep_ref, *refs):
+    got_refs, out_ref = refs[:-1], refs[-1]
+    first = 0
+    for got_ref in got_refs:
+        here = slice(first, first + got_ref.shape[0])
+        out_ref[here] = (keep_ref[here] + got_ref[...].astype(WIDE)).astype(LOW)
+        first = here.stop
+
+
+def close(keep, *gots):
     return pl.pallas_call(
         close_kernel,
-        in_specs=vmem_specs(2),
+        in_specs=vmem_specs(1 + len(gots)),
         out_specs=vmem_specs(1)[0],
         out_shape=jax.ShapeDtypeStruct(keep.shape, LOW),
         compiler_params=params(),
         cost_estimate=LIGHT,
-    )(keep, got)
+    )(keep, *gots)
 
 
 def place_kernel(where_ref, keep_ref, got_ref, other_ref, *refs):
@@ -315,21 +310,21 @@
     query_other, *keyed_other = packs[1 + len(chunks) :]
     there = wait(near(keyed_other[0]))
     keyed = [[keyed_own[0], there, far(keyed_own[0]), far(there)]]
+    turn(lower, 2)
+
+    acts, swapped = [], []
+
+    def attention(chunk):
+        keyed[chunk][-1] = wait(keyed[chunk][-1])
+        acts.append(wait(attend(starts[chunk], hdim, queries_both, keyed[chunk])))
+        swapped.append(across(acts[-1]))
+
+    turn(upper, 1)
+    keyed[0][2] = wait(keyed[0][2])
     for own, other in zip(keyed_own[1:], keyed_other[1:]):
         there = wait(near(other))
         keyed.append([own, there, far(jnp.concatenate([own, there]))])
     queries_both = [query_own, wait(near(query_other))]
-    turn(lower, 2)
-
-    acts, swapped = [], []
-
-    def attention(chunk):
-        keyed[chunk][-1] = wait(keyed[chunk][-1])
-        acts.append(wait(attend(starts[chunk], hdim, queries_both, keyed[chunk])))
-        swapped.append(across(acts[-1]))
-
-    turn(upper, 1)
-    keyed[0][2] = wait(keyed[0][2])
     turn(beside, 1)
     attention(0)
     for step in range(3, n_ring):
@@ -339,15 +334,17 @@
     rest = [far(after(lower[0]))]
     attention(1)
     swapped[0] = wait(swapped[0])
+    attention(2)
     swapped[1] = wait(swapped[1])
-    attention(2)
     turn(beside, 2)
-    rest += [far(after(piece)) for piece in lower[1:2] + later]
+    rest.append(far(after(lower[1])))
     for step in range(3, n_ring):
         turn(upper, step)
     rest[0] = wait(rest[0])
     swapped[2] = wait(swapped[2])
-    acts = wait(assemble(jnp.stack([seq // 2]), groups, chunks, list(zip(acts, swapped))))
+    rest += [far(after(piece)) for piece in later]
+    acts = list(zip(acts, swapped))
+    flip = jnp.stack([seq // 2])
 
     keeps, mine_sends, sends, mine_got, other = [], [], [], [], []
 
@@ -356,39 +353,38 @@
         start = step % 2 * (depth - cut) if step > 1 else 0
         got = rest[step] if step < 2 else rest[1 + step // 2]
         theirs = [(beside[step], 0, cut), (got, start, start + depth - cut)]
-        keep_mine, keep_other, send_mine, send_other = project(acts, own + theirs)
+        keep_mine, keep_other, send_mine, *send_other = project(flip, acts, own + theirs)
         keeps.append((keep_mine, keep_other))
-        sends.append(near(wait(send_other)))
+        sends.append([near(wait(array)) for array in send_other])
         mine_sends.append(send_mine)
 
     def finish(step):
-        other.append(across(wait(close(keeps[step][1], wait(sends[step])))))
+        other.append(across(wait(close(keeps[step][1], *[wait(array) for array in sends[step]]))))
         mine_got.append(near(mine_sends[step]))
 
+    columns(0)
+    finish(0)
+    rest[1] = wait(rest[1])
+    columns(1)
+    finish(1)
+    for step in range(2, n_ring, 2):
+        other[step - 2] = wait(other[step - 2])
+        rest[1 + step // 2] = wait(rest[1 + step // 2])
+        for ahead in range(max(step, 3), step + 2):
+            turn(beside, ahead)
+        columns(step)
+        finish(step)
+        columns(step + 1)
+        other[step - 1] = wait(other[step - 1])
+        finish(step + 1)
     outs = []
-
-    def put(step):
+    for step in range(n_ring):
         pair = (dp // 2 - step) % n_ring
         where = jnp.stack([2 * pair + dp % 2, 2 * pair + 1 - dp % 2]).astype(jnp.int32) + token
-        return place(outs, n_dp * out_weight.shape[1], where, keeps[step][0], wait(mine_got[step]), wait(other[step]))
-
-    columns(0)
-    rest[1] = wait(rest[1])
-    columns(1)
-    finish(0)
-    finish(1)
-    for step in range(2, n_ring, 2):
-        for ahead in range(max(step, 3), step + 2):
-            turn(beside, ahead)
-        rest[1 + step // 2] = wait(rest[1 + step // 2])
-        columns(step)
-        outs = put(step - 2)
-        finish(step)
-        columns(step + 1)
-        outs = put(step - 1)
-        finish(step + 1)
-    for step in range(n_ring - 2, n_ring):
-        outs = put(step)
+        mine_got[step] = wait(mine_got[step])
+        if step + 2 >= n_ring:
+            other[step] = wait(other[step])
+        outs = place(outs, n_dp * out_weight.shape[1], where, keeps[step][0], mine_got[step], other[step])
     return tuple(outs)
 
 

time: 139 us -> 152 us (1.094)
  waiting for transfers between devices: 58.1 us -> 73.1 us
    ppermute x9, waiting for transfers between devices: 42.7 us -> 52.7 us  [onward(): return lax.ppermute(array, 'dp', [(i, (i + 2) % n_dp) for i in range(n_dp)])]
    ppermute x7, waiting for transfers between devices: 12.5 us -> 15.1 us  [across(): return lax.ppermute(array, 'dp', [(i, i ^ 1) for i in range(n_dp)])]
    ppermute x12 -> x16, waiting for transfers between devices: 0.71 us -> 2.77 us  [near(): return lax.ppermute(array, 'seq', [(i, i ^ 1) for i in range(n_seq)])]
    pallas_call x9 -> x8, Pallas kernels: 19.1 us -> 17.2 us  [the longest x4 16 us: project(): pl.pallas_call(functools.partial(project_kernel, len(acts), spans), in_sp...]
    unnamed x58 -> x54, local copies, waits for them, and re-layouts: 11 us -> 9.97 us
    ppermute x12 -> x16, starting transfers between devices: 2.62 us -> 3.42 us  [near(): return lax.ppermute(array, 'seq', [(i, i ^ 1) for i in range(n_seq)])]
  transfers between devices with their start and end apart: 36 -> 40, of which waited for: 12 -> 19; matrix products, arithmetic and copies ran while one was open for 2% -> 2% of each run, Pallas kernels for 26% -> 23%
where the time goes in v4:
time: 152 us; the launch traced here: 151 us
  waiting for transfers between devices  73.1 us (48%)
  Pallas kernels  36.6 us (24%)
  starting transfers between devices  27.1 us (18%)
  local copies, waits for them, and re-layouts  12.2 us (8%)
    ppermute x9, waiting for transfers between devices, onward(): return lax.ppermute(array, 'dp', [(i, (i + 2) % n_dp) for i in range(n_dp)])  52.7 us
    pallas_call x4, Pallas kernels, project(): pl.pallas_call(functools.partial(project_kernel, len(acts), spans), in_sp...  16 us
    ppermute x7, waiting for transfers between devices, across(): return lax.ppermute(array, 'dp', [(i, i ^ 1) for i in range(n_dp)])  15.1 us
    ppermute x8, starting transfers between devices, far(): return lax.ppermute(array, 'seq', [(i, i ^ 2) for i in range(n_seq)])  10.6 us
    unnamed x54, local copies, waits for them, and re-layouts  9.97 us
    pallas_call x3, Pallas kernels, attend(): pl.pallas_call(functools.partial(attend_kernel, len(queries)), grid=(widt...  9.38 us
    ppermute x7, starting transfers between devices, across(): return lax.ppermute(array, 'dp', [(i, i ^ 1) for i in range(n_dp)])  8.93 us
    pallas_call x4, Pallas kernels, place(): pl.pallas_call(place_kernel, grid_spec=pltpu.PrefetchScalarGridSpec(num_s...  7.86 us
  transfers between devices with their start and end apart: 40, of which 19 were waited for; matrix products, arithmetic and copies ran while one was open for 2% of the time, Pallas kernels for 23%

profile of v4, /device:TPU:0, one launch (start us, length us, event | category | flops | bytes accessed | tf_op | source)
XLA Modules:
  0.0 151.3 jit_solution(7164968645479189285)
XLA Ops:
  0.7 1.2 slice.7.refs_6_
  1.9 3.0 %collective-permute-start.1 = (bf16[384,640]{1,0:T(8,128)(2,1)S(1)}, bf16[384,640]{1,0:T(8,128)(2,1)}, u32[]{:S(2)}, u32[]{:S(2)}) collective-permute-start(bf16[384,640]{1,0:T(8,128)(2,1)S(1)} %slice.7.refs_6_), channel_id=1, source_target_pairs={{0,2},{1,3},{2,0},{3,1},{4,6},{5,7},{6,4},{7,5},{8,10},{9,11},{10,... | collective-permute-start | bytes 1474568 | tf_op jit(solution)/shard_map/ppermute | solution.py:273
  5.9 1.6 %collective-permute-start = (bf16[256,640]{1,0:T(8,128)(2,1)S(1)}, bf16[256,640]{1,0:T(8,128)(2,1)}, u32[]{:S(2)}, u32[]{:S(2)}) collective-permute-start(bf16[256,640]{1,0:T(8,128)(2,1)S(1)} %slice.6.refs_7_), channel_id=1, source_target_pairs={{0,8},{4,12},{8,16},{12,20},{16,24},{20,28},{24,0},{28,4},{1,9},{5... | collective-permute-start | bytes 983048 | tf_op jit(solution)/shard_map/ppermute | solution.py:282
  11.9 2.1 %shard_map.104 = (bf16[2,128,1280]{2,1,0:T(8,128)(2,1)S(1)}, bf16[4,128,640]{2,1,0:T(8,128)(2,1)S(1)}, bf16[4,128,384]{2,1,0:T(8,128)(2,1)S(1)}, bf16[4,128,256]...) custom-call(s32[1]{0:T(128)} %bitcast.3.core_ref, ...), custom_call_target="tpu_custom_call" | custom-call | flops 1 | bytes 1 | tf_op jit(solution)/shard_map/pallas_call | solution.py:78
  14.0 2.2 %collective-permute-done.1.refs_8_ = bf16[384,640]{1,0:T(8,128)(2,1)} collective-permute-done((bf16[384,640]{1,0:T(8,128)(2,1)S(1)}, bf16[384,640]{1,0:T(8,128)(2,1)}, u32[]{:S(2)}, u32[]{:S(2)}) %collective-permute-start.1) | collective-permute-done | bytes 491552 | tf_op jit(solution)/shard_map/ppermute | solution.py:273
  18.0 1.5 collective-permute-start.5
  19.5 1.6 %collective-permute-start.7 = (bf16[256,640]{1,0:T(8,128)(2,1)}, bf16[256,640]{1,0:T(8,128)(2,1)S(1)}, u32[]{:S(2)}, u32[]{:S(2)}) collective-permute-start(bf16[256,640]{1,0:T(8,128)(2,1)} %collective-permute-done.refs_7_), channel_id=1, source_target_pairs={{0,8},{4,12},{8,16},{12,20},{16,24},{20,28},{24,0},{28,4},{1,9},{5... | collective-permute-start | bytes 983048 | tf_op jit(solution)/shard_map/ppermute | solution.py:282
  21.6 11.3 %collective-permute-done.6.refs_6_ = bf16[384,640]{1,0:T(8,128)(2,1)S(1)} collective-permute-done((bf16[384,640]{1,0:T(8,128)(2,1)S(1)}, bf16[384,640]{1,0:T(8,128)(2,1)S(1)}, u32[]{:S(2)}, u32[]{:S(2)}) %collective-permute-start.6) | collective-permute-done | bytes 491552 | tf_op jit(solution)/shard_map/ppermute | solution.py:282
  33.7 5.8 %collective-permute-done.7.refs_7_ = bf16[256,640]{1,0:T(8,128)(2,1)S(1)} collective-permute-done((bf16[256,640]{1,0:T(8,128)(2,1)}, bf16[256,640]{1,0:T(8,128)(2,1)S(1)}, u32[]{:S(2)}, u32[]{:S(2)}) %collective-permute-start.7) | collective-permute-done | bytes 327712 | tf_op jit(solution)/shard_map/ppermute | solution.py:282
  41.1 13.4 %collective-permute-done.10.refs_8_ = bf16[384,640]{1,0:T(8,128)(2,1)} collective-permute-done((bf16[384,640]{1,0:T(8,128)(2,1)}, bf16[384,640]{1,0:T(8,128)(2,1)}, u32[]{:S(2)}, u32[]{:S(2)}) %collective-permute-start.10) | collective-permute-done | bytes 491552 | tf_op jit(solution)/shard_map/ppermute | solution.py:282
  54.5 4.7 %shard_map.105.refs_0_ = bf16[2,256,640]{2,1,0:T(8,128)(2,1)S(1)} custom-call(bf16[2,128,1280]{2,1,0:T(8,128)(2,1)S(1)} %get-tuple-element.167.refs_0_, bf16[2,128,1280]{2,1,0:T(8,128)(2,1)S(1)} %collective-permute-done.2.refs_1_, bf16[4,128,640]{2,1,0:T(8,128)(2,1)S(1)} %get-tuple-element.185.refs_2_, ...), custom_call_target="tpu_custom_call" | custom-call | flops 1 | bytes 1 | tf_op jit(solution)/shard_map/pallas_call | solution.py:129
  59.2 1.6 %collective-permute-start.15 = (bf16[2,256,640]{2,1,0:T(8,128)(2,1)S(1)}, bf16[2,256,640]{2,1,0:T(8,128)(2,1)S(1)}, u32[]{:S(2)}, u32[]{:S(2)}) collective-permute-start(bf16[2,256,640]{2,1,0:T(8,128)(2,1)S(1)} %shard_map.105.refs_0_), channel_id=1, source_target_pairs={{0,4},{4,0},{8,12},{12,8},{16,20},{20,16},{24,28},{28,24},{1,5},{5... | collective-permute-start | bytes 1966088 | tf_op jit(solution)/shard_map/ppermute | solution.py:279
  61.9 13.4 %collective-permute-done.13.refs_7_ = bf16[256,640]{1,0:T(8,128)(2,1)S(1)} collective-permute-done((bf16[256,640]{1,0:T(8,128)(2,1)S(1)}, bf16[256,640]{1,0:T(8,128)(2,1)S(1)}, u32[]{:S(2)}, u32[]{:S(2)}) %collective-permute-start.13) | collective-permute-done | bytes 327712 | tf_op jit(solution)/shard_map/ppermute | solution.py:282
  76.2 2.8 %shard_map.106.refs_1_ = bf16[2,256,384]{2,1,0:T(8,128)(2,1)S(1)} custom-call(bf16[2,128,1280]{2,1,0:T(8,128)(2,1)S(1)} %get-tuple-element.167.refs_0_, bf16[2,128,1280]{2,1,0:T(8,128)(2,1)S(1)} %collective-permute-done.2.refs_1_, bf16[4,128,384]{2,1,0:T(8,128)(2,1)S(1)} %get-tuple-element.204.refs_2_, ...), custom_call_target="tpu_custom_call" | custom-call | flops 1 | bytes 1 | tf_op jit(solution)/shard_map/pallas_call | solution.py:129
  79.1 1.6 %collective-permute-start.16 = (bf16[2,256,384]{2,1,0:T(8,128)(2,1)S(1)}, bf16[2,256,384]{2,1,0:T(8,128)(2,1)}, u32[]{:S(2)}, u32[]{:S(2)}) collective-permute-start(bf16[2,256,384]{2,1,0:T(8,128)(2,1)S(1)} %shard_map.106.refs_1_), channel_id=1, source_target_pairs={{0,4},{4,0},{8,12},{12,8},{16,20},{20,16},{24,28},{28,24},{1,5},{5... | collective-permute-start | bytes 1179656 | tf_op jit(solution)/shard_map/ppermute | solution.py:279
  81.8 1.9 %shard_map.107.refs_2_ = bf16[2,256,256]{2,1,0:T(8,128)(2,1)S(1)} custom-call(bf16[2,128,1280]{2,1,0:T(8,128)(2,1)S(1)} %get-tuple-element.167.refs_0_, bf16[2,128,1280]{2,1,0:T(8,128)(2,1)S(1)} %collective-permute-done.2.refs_1_, bf16[4,128,256]{2,1,0:T(8,128)(2,1)S(1)} %get-tuple-element.216.refs_2_, ...), custom_call_target="tpu_custom_call" | custom-call | flops 1 | bytes 1 | tf_op jit(solution)/shard_map/pallas_call | solution.py:129
  84.2 6.7 %collective-permute-done.16.refs_4_ = bf16[2,256,384]{2,1,0:T(8,128)(2,1)} collective-permute-done((bf16[2,256,384]{2,1,0:T(8,128)(2,1)S(1)}, bf16[2,256,384]{2,1,0:T(8,128)(2,1)}, u32[]{:S(2)}, u32[]{:S(2)}) %collective-permute-start.16) | collective-permute-done | bytes 393248 | tf_op jit(solution)/shard_map/ppermute | solution.py:279
  91.5 7.4 %collective-permute-done.19.refs_6_ = bf16[384,640]{1,0:T(8,128)(2,1)} collective-permute-done((bf16[384,640]{1,0:T(8,128)(2,1)}, bf16[384,640]{1,0:T(8,128)(2,1)}, u32[]{:S(2)}, u32[]{:S(2)}) %collective-permute-start.19) | collective-permute-done | bytes 491552 | tf_op jit(solution)/shard_map/ppermute | solution.py:282
  102.1 3.9 %shard_map.108 = (f32[256,640]{1,0:T(8,128)S(1)}, f32[256,640]{1,0:T(8,128)S(1)}, bf16[256,640]{1,0:T(8,128)(2,1)}, bf16[128,640]{1,0:T(8,128)(2,1)S(1)}, bf16[128,640]{1,0:T(8,128)(2,1)S(1)}) custom-call(s32[1]{0:T(128)} %bitcast.2.flip_ref, bf16[2,256,640]{2,1,0:T(8,128)(2,1)S(1)} %shard_map.105.refs_0_, bf16[2,256,384]{2,1,0:T(8,128)(2,1)S(1)} %shard_map.106.refs_1_, ...), custom_call_target="tpu_custom_call" | custom-call | flops 2013265920 | bytes 1 | tf_op jit(solution)/shard_map/pallas_call | solution.py:173
  107.8 1.6 %collective-permute-start.24 = (bf16[256,640]{1,0:T(8,128)(2,1)S(1)}, bf16[256,640]{1,0:T(8,128)(2,1)S(1)}, u32[]{:S(2)}, u32[]{:S(2)}) collective-permute-start(bf16[256,640]{1,0:T(8,128)(2,1)S(1)} %shard_map.109), channel_id=1, source_target_pairs={{0,4},{4,0},{8,12},{12,8},{16,20},{20,16},{24,28},{28,24},{1,5},{5... | collective-permute-start | bytes 983048 | tf_op jit(solution)/shard_map/ppermute | solution.py:279
  109.8 3.9 %shard_map.110 = (f32[256,640]{1,0:T(8,128)S(1)}, f32[256,640]{1,0:T(8,128)S(1)}, bf16[256,640]{1,0:T(8,128)(2,1)}, bf16[128,640]{1,0:T(8,128)(2,1)S(1)}, bf16[128,640]{1,0:T(8,128)(2,1)S(1)}) custom-call(s32[1]{0:T(128)} %bitcast.2.flip_ref, bf16[2,256,640]{2,1,0:T(8,128)(2,1)S(1)} %shard_map.105.refs_0_, bf16[2,256,384]{2,1,0:T(8,128)(2,1)S(1)} %shard_map.106.refs_1_, ...), custom_call_target="tpu_custom_call" | custom-call | flops 2013265920 | bytes 1 | tf_op jit(solution)/shard_map/pallas_call | solution.py:173
  115.7 2.0 %collective-permute-done.24.other_ref = bf16[256,640]{1,0:T(8,128)(2,1)S(1)} collective-permute-done((bf16[256,640]{1,0:T(8,128)(2,1)S(1)}, bf16[256,640]{1,0:T(8,128)(2,1)S(1)}, u32[]{:S(2)}, u32[]{:S(2)}) %collective-permute-start.24) | collective-permute-done | bytes 327712 | tf_op jit(solution)/shard_map/ppermute | solution.py:279
  118.5 1.5 %collective-permute-start.36 = (bf16[256,640]{1,0:T(8,128)(2,1)S(1)}, bf16[256,640]{1,0:T(8,128)(2,1)S(1)}, u32[]{:S(2)}, u32[]{:S(2)}) collective-permute-start(bf16[256,640]{1,0:T(8,128)(2,1)S(1)} %shard_map.111), channel_id=1, source_target_pairs={{0,4},{4,0},{8,12},{12,8},{16,20},{20,16},{24,28},{28,24},{1,5},{5... | collective-permute-start | bytes 983048 | tf_op jit(solution)/shard_map/ppermute | solution.py:279
  120.0 3.9 %shard_map.112 = (f32[256,640]{1,0:T(8,128)S(1)}, f32[256,640]{1,0:T(8,128)S(1)}, bf16[256,640]{1,0:T(8,128)(2,1)}, bf16[128,640]{1,0:T(8,128)(2,1)S(1)}, bf16[128,640]{1,0:T(8,128)(2,1)S(1)}) custom-call(s32[1]{0:T(128)} %bitcast.2.flip_ref, bf16[2,256,640]{2,1,0:T(8,128)(2,1)S(1)} %shard_map.105.refs_0_, bf16[2,256,384]{2,1,0:T(8,128)(2,1)S(1)} %shard_map.106.refs_1_, ...), custom_call_target="tpu_custom_call" | custom-call | flops 2013265920 | bytes 1 | tf_op jit(solution)/shard_map/pallas_call | solution.py:173
  126.3 4.2 %shard_map.114 = (f32[256,640]{1,0:T(8,128)S(1)}, f32[256,640]{1,0:T(8,128)S(1)}, bf16[256,640]{1,0:T(8,128)(2,1)S(1)}, bf16[128,640]{1,0:T(8,128)(2,1)}, bf16[128,640]{1,0:T(8,128)(2,1)}) custom-call(s32[1]{0:T(128)} %bitcast.2.flip_ref, bf16[2,256,640]{2,1,0:T(8,128)(2,1)S(1)} %shard_map.105.refs_0_, bf16[2,256,384]{2,1,0:T(8,128)(2,1)S(1)} %copy-done.9, ...), custom_call_target="tpu_custom_call" | custom-call | flops 2013265920 | bytes 1 | tf_op jit(solution)/shard_map/pallas_call | solution.py:173
  132.7 1.3 collective-permute-start.31
  136.9 2.5 %shard_map.116 = (bf16[128,5120]{1,0:T(8,128)(2,1)}, bf16[128,5120]{1,0:T(8,128)(2,1)}) custom-call(s32[2]{0:T(128)S(1)} %add_add_fusion.3.where_ref, f32[256,640]{1,0:T(8,128)S(1)} %get-tuple-element.317.keep_ref, bf16[256,640]{1,0:T(8,128)(2,1)} %collective-permute-done.34.got_ref, bf16[256,640]{1,0:T(8,128)(2,1)S(1)} %copy-done.16), custom_call_target="tpu_custom_call" | custom-call | flops 1 | bytes 1 | tf_op jit(solution)/shard_map/pallas_call | solution.py:232
  139.4 2.5 %shard_map.117 = (bf16[128,5120]{1,0:T(8,128)(2,1)}, bf16[128,5120]{1,0:T(8,128)(2,1)}) custom-call(s32[2]{0:T(128)S(1)} %add_add_fusion.2.where_ref, f32[256,640]{1,0:T(8,128)S(1)} %get-tuple-element.314.keep_ref, bf16[256,640]{1,0:T(8,128)(2,1)} %collective-permute-done.33.got_ref, ...), custom_call_target="tpu_custom_call", output_to_operand_aliasing={{0}: (4, {}), {1}: (5, {})} | custom-call | flops 1 | bytes 1 | tf_op jit(solution)/shard_map/pallas_call | solution.py:232
  142.0 1.5 collective-permute-done.31.other_ref
  143.5 1.5 shard_map.118
  145.0 4.8 %collective-permute-done.39.other_ref = bf16[256,640]{1,0:T(8,128)(2,1)S(1)} collective-permute-done((bf16[256,640]{1,0:T(8,128)(2,1)S(1)}, bf16[256,640]{1,0:T(8,128)(2,1)S(1)}, u32[]{:S(2)}, u32[]{:S(2)}) %collective-permute-start.39) | collective-permute-done | bytes 327712 | tf_op jit(solution)/shard_map/ppermute | solution.py:279
  149.8 1.5 shard_map.119
  (130 shorter events, 30.1 us)
Async XLA Ops:
  1.9 14.3 %collective-permute-start.1 = (bf16[384,640]{1,0:T(8,128)(2,1)S(1)}, bf16[384,640]{1,0:T(8,128)(2,1)}, u32[]{:S(2)}, u32[]{:S(2)}) collective-permute-start(bf16[384,640]{1,0:T(8,128)(2,1)S(1)} %slice.7.refs_6_), channel_id=1, source_target_pairs={{0,2},{1,3},{2,0},{3,1},{4,6},{5,7},{6,4},{7,5},{8,10},{9,11},{10,... | collective-permute-start | bytes 1474568 | tf_op jit(solution)/shard_map/ppermute | solution.py:273
  5.9 11.2 %collective-permute-start = (bf16[256,640]{1,0:T(8,128)(2,1)S(1)}, bf16[256,640]{1,0:T(8,128)(2,1)}, u32[]{:S(2)}, u32[]{:S(2)}) collective-permute-start(bf16[256,640]{1,0:T(8,128)(2,1)S(1)} %slice.6.refs_7_), channel_id=1, source_target_pairs={{0,8},{4,12},{8,16},{12,20},{16,24},{20,28},{24,0},{28,4},{1,9},{5... | collective-permute-start | bytes 983048 | tf_op jit(solution)/shard_map/ppermute | solution.py:282
  17.1 15.8 %collective-permute-start.6 = (bf16[384,640]{1,0:T(8,128)(2,1)S(1)}, bf16[384,640]{1,0:T(8,128)(2,1)S(1)}, u32[]{:S(2)}, u32[]{:S(2)}) collective-permute-start(bf16[384,640]{1,0:T(8,128)(2,1)S(1)} %slice.7.refs_6_), channel_id=1, source_target_pairs={{0,8},{4,12},{8,16},{12,20},{16,24},{20,28},{24,0},{28,4},{1,9},{5... | collective-permute-start | bytes 1474568 | tf_op jit(solution)/shard_map/ppermute | solution.py:282
  18.0 21.5 %collective-permute-start.5 = (bf16[4,128,640]{2,1,0:T(8,128)(2,1)S(1)}, bf16[4,128,640]{2,1,0:T(8,128)(2,1)S(1)}, u32[]{:S(2)}, u32[]{:S(2)}) collective-permute-start(bf16[4,128,640]{2,1,0:T(8,128)(2,1)S(1)} %get-tuple-element.185.refs_2_), channel_id=1, source_target_pairs={{0,2},{1,3},{2,0},{3,1},{4,6},{5,7},{6,4},{7,5},{8,10},{9,11},{10,... | collective-permute-start | bytes 1966088 | tf_op jit(solution)/shard_map/ppermute | solution.py:273
  19.5 20.0 %collective-permute-start.7 = (bf16[256,640]{1,0:T(8,128)(2,1)}, bf16[256,640]{1,0:T(8,128)(2,1)S(1)}, u32[]{:S(2)}, u32[]{:S(2)}) collective-permute-start(bf16[256,640]{1,0:T(8,128)(2,1)} %collective-permute-done.refs_7_), channel_id=1, source_target_pairs={{0,8},{4,12},{8,16},{12,20},{16,24},{20,28},{24,0},{28,4},{1,9},{5... | collective-permute-start | bytes 983048 | tf_op jit(solution)/shard_map/ppermute | solution.py:282
  21.1 18.4 %collective-permute-start.4 = (bf16[4,128,384]{2,1,0:T(8,128)(2,1)S(1)}, bf16[4,128,384]{2,1,0:T(8,128)(2,1)S(1)}, u32[]{:S(2)}, u32[]{:S(2)}) collective-permute-start(bf16[4,128,384]{2,1,0:T(8,128)(2,1)S(1)} %get-tuple-element.184), channel_id=1, source_target_pairs={{0,1},{1,0},{2,3},{3,2},{4,5},{5,4},{6,7},{7,6},{8,9},{9,8},{10,11... | collective-permute-start | bytes 1179656 | tf_op jit(solution)/shard_map/ppermute | solution.py:276
  21.1 20.0 %collective-permute-start.2 = (bf16[2,128,1280]{2,1,0:T(8,128)(2,1)S(1)}, bf16[2,128,1280]{2,1,0:T(8,128)(2,1)S(1)}, u32[]{:S(2)}, u32[]{:S(2)}) collective-permute-start(bf16[2,128,1280]{2,1,0:T(8,128)(2,1)S(1)} %get-tuple-element.176), channel_id=1, source_target_pairs={{0,1},{1,0},{2,3},{3,2},{4,5},{5,4},{6,7},{7,6},{8,9},{9,8},{10,11... | collective-permute-start | bytes 1966088 | tf_op jit(solution)/shard_map/ppermute | solution.py:276
  32.9 21.6 %collective-permute-start.9 = (bf16[4,128,640]{2,1,0:T(8,128)(2,1)S(1)}, bf16[4,128,640]{2,1,0:T(8,128)(2,1)S(1)}, u32[]{:S(2)}, u32[]{:S(2)}) collective-permute-start(bf16[4,128,640]{2,1,0:T(8,128)(2,1)S(1)} %collective-permute-done.8.refs_3_), channel_id=1, source_target_pairs={{0,2},{1,3},{2,0},{3,1},{4,6},{5,7},{6,4},{7,5},{8,10},{9,11},{10,... | collective-permute-start | bytes 1966088 | tf_op jit(solution)/shard_map/ppermute | solution.py:273
  39.5 15.0 %collective-permute-start.10 = (bf16[384,640]{1,0:T(8,128)(2,1)}, bf16[384,640]{1,0:T(8,128)(2,1)}, u32[]{:S(2)}, u32[]{:S(2)}) collective-permute-start(bf16[384,640]{1,0:T(8,128)(2,1)} %collective-permute-done.1.refs_8_), channel_id=1, source_target_pairs={{0,8},{4,12},{8,16},{12,20},{16,24},{20,28},{24,0},{28,4},{1,9},{5... | collective-permute-start | bytes 1474568 | tf_op jit(solution)/shard_map/ppermute | solution.py:282
  39.6 36.6 %collective-permute-start.11 = (bf16[8,128,384]{2,1,0:T(8,128)(2,1)S(1)}, bf16[8,128,384]{2,1,0:T(8,128)(2,1)S(1)}, u32[]{:S(2)}, u32[]{:S(2)}) collective-permute-start(bf16[8,128,384]{2,1,0:T(8,128)(2,1)S(1)} %pad_maximum_fusion), channel_id=1, source_target_pairs={{0,2},{1,3},{2,0},{3,1},{4,6},{5,7},{6,4},{7,5},{8,10},{9,11},{10,... | collective-permute-start | bytes 2359304 | tf_op jit(solution)/shard_map/ppermute | solution.py:273
  54.5 21.7 %collective-permute-start.12 = (bf16[384,640]{1,0:T(8,128)(2,1)S(1)}, bf16[384,640]{1,0:T(8,128)(2,1)}, u32[]{:S(2)}, u32[]{:S(2)}) collective-permute-start(bf16[384,640]{1,0:T(8,128)(2,1)S(1)} %collective-permute-done.6.refs_6_), channel_id=1, source_target_pairs={{0,8},{4,12},{8,16},{12,20},{16,24},{20,28},{24,0},{28,4},{1,9},{5... | collective-permute-start | bytes 1474568 | tf_op jit(solution)/shard_map/ppermute | solution.py:282
  59.2 21.5 %collective-permute-start.15 = (bf16[2,256,640]{2,1,0:T(8,128)(2,1)S(1)}, bf16[2,256,640]{2,1,0:T(8,128)(2,1)S(1)}, u32[]{:S(2)}, u32[]{:S(2)}) collective-permute-start(bf16[2,256,640]{2,1,0:T(8,128)(2,1)S(1)} %shard_map.105.refs_0_), channel_id=1, source_target_pairs={{0,4},{4,0},{8,12},{12,8},{16,20},{20,16},{24,28},{28,24},{1,5},{5... | collective-permute-start | bytes 1966088 | tf_op jit(solution)/shard_map/ppermute | solution.py:279
  60.7 14.5 %collective-permute-start.13 = (bf16[256,640]{1,0:T(8,128)(2,1)S(1)}, bf16[256,640]{1,0:T(8,128)(2,1)S(1)}, u32[]{:S(2)}, u32[]{:S(2)}) collective-permute-start(bf16[256,640]{1,0:T(8,128)(2,1)S(1)} %collective-permute-done.7.refs_7_), channel_id=1, source_target_pairs={{0,8},{4,12},{8,16},{12,20},{16,24},{20,28},{24,0},{28,4},{1,9},{5... | collective-permute-start | bytes 983048 | tf_op jit(solution)/shard_map/ppermute | solution.py:282
  60.8 21.0 %collective-permute-start.14 = (bf16[8,128,256]{2,1,0:T(8,128)(2,1)S(1)}, bf16[8,128,256]{2,1,0:T(8,128)(2,1)S(1)}, u32[]{:S(2)}, u32[]{:S(2)}) collective-permute-start(bf16[8,128,256]{2,1,0:T(8,128)(2,1)S(1)} %pad_maximum_fusion.2), channel_id=1, source_target_pairs={{0,2},{1,3},{2,0},{3,1},{4,6},{5,7},{6,4},{7,5},{8,10},{9,11},{10,... | collective-permute-start | bytes 1572872 | tf_op jit(solution)/shard_map/ppermute | solution.py:273
  75.3 16.3 %collective-permute-start.20 = (bf16[384,640]{1,0:T(8,128)(2,1)}, bf16[384,640]{1,0:T(8,128)(2,1)}, u32[]{:S(2)}, u32[]{:S(2)}) collective-permute-start(bf16[384,640]{1,0:T(8,128)(2,1)} %collective-permute-done.10.refs_8_), channel_id=1, source_target_pairs={{0,8},{4,12},{8,16},{12,20},{16,24},{20,28},{24,0},{28,4},{1,9},{5... | collective-permute-start | bytes 1474568 | tf_op jit(solution)/shard_map/ppermute | solution.py:282
  76.2 22.7 %collective-permute-start.19 = (bf16[384,640]{1,0:T(8,128)(2,1)}, bf16[384,640]{1,0:T(8,128)(2,1)}, u32[]{:S(2)}, u32[]{:S(2)}) collective-permute-start(bf16[384,640]{1,0:T(8,128)(2,1)} %collective-permute-done.12.refs_6_), channel_id=1, source_target_pairs={{0,8},{4,12},{8,16},{12,20},{16,24},{20,28},{24,0},{28,4},{1,9},{5... | collective-permute-start | bytes 1474568 | tf_op jit(solution)/shard_map/ppermute | solution.py:282
  79.1 11.9 %collective-permute-start.16 = (bf16[2,256,384]{2,1,0:T(8,128)(2,1)S(1)}, bf16[2,256,384]{2,1,0:T(8,128)(2,1)}, u32[]{:S(2)}, u32[]{:S(2)}) collective-permute-start(bf16[2,256,384]{2,1,0:T(8,128)(2,1)S(1)} %shard_map.106.refs_1_), channel_id=1, source_target_pairs={{0,4},{4,0},{8,12},{12,8},{16,20},{20,16},{24,28},{28,24},{1,5},{5... | collective-permute-start | bytes 1179656 | tf_op jit(solution)/shard_map/ppermute | solution.py:279
  80.7 18.3 %collective-permute-start.18 = (bf16[256,640]{1,0:T(8,128)(2,1)S(1)}, bf16[256,640]{1,0:T(8,128)(2,1)}, u32[]{:S(2)}, u32[]{:S(2)}) collective-permute-start(bf16[256,640]{1,0:T(8,128)(2,1)S(1)} %slice.6.refs_7_), channel_id=1, source_target_pairs={{0,2},{1,3},{2,0},{3,1},{4,6},{5,7},{6,4},{7,5},{8,10},{9,11},{10,... | collective-permute-start | bytes 983048 | tf_op jit(solution)/shard_map/ppermute | solution.py:273
  83.7 16.5 %collective-permute-start.17 = (bf16[2,256,256]{2,1,0:T(8,128)(2,1)S(1)}, bf16[2,256,256]{2,1,0:T(8,128)(2,1)}, u32[]{:S(2)}, u32[]{:S(2)}) collective-permute-start(bf16[2,256,256]{2,1,0:T(8,128)(2,1)S(1)} %shard_map.107.refs_2_), channel_id=1, source_target_pairs={{0,4},{4,0},{8,12},{12,8},{16,20},{20,16},{24,28},{28,24},{1,5},{5... | collective-permute-start | bytes 786440 | tf_op jit(solution)/shard_map/ppermute | solution.py:279
  99.0 10.9 %collective-permute-start.25 = (bf16[256,640]{1,0:T(8,128)(2,1)}, bf16[256,640]{1,0:T(8,128)(2,1)S(1)}, u32[]{:S(2)}, u32[]{:S(2)}) collective-permute-start(bf16[256,640]{1,0:T(8,128)(2,1)} %collective-permute-done.refs_7_), channel_id=1, source_target_pairs={{0,2},{1,3},{2,0},{3,1},{4,6},{5,7},{6,4},{7,5},{8,10},{9,11},{10,... | collective-permute-start | bytes 983048 | tf_op jit(solution)/shard_map/ppermute | solution.py:273
  100.1 19.9 %collective-permute-start.21 = (bf16[512,640]{1,0:T(8,128)(2,1)}, bf16[512,640]{1,0:T(8,128)(2,1)S(1)}, u32[]{:S(2)}, u32[]{:S(2)}) collective-permute-start(bf16[512,640]{1,0:T(8,128)(2,1)} %pad_maximum_fusion.1), channel_id=1, source_target_pairs={{0,2},{1,3},{2,0},{3,1},{4,6},{5,7},{6,4},{7,5},{8,10},{9,11},{10,... | collective-permute-start | bytes 1966088 | tf_op jit(solution)/shard_map/ppermute | solution.py:273
  106.6 18.2 %collective-permute-start.28 = (bf16[384,640]{1,0:T(8,128)(2,1)}, bf16[384,640]{1,0:T(8,128)(2,1)S(1)}, u32[]{:S(2)}, u32[]{:S(2)}) collective-permute-start(bf16[384,640]{1,0:T(8,128)(2,1)} %collective-permute-done.20.refs_8_), channel_id=1, source_target_pairs={{0,8},{4,12},{8,16},{12,20},{16,24},{20,28},{24,0},{28,4},{1,9},{5... | collective-permute-start | bytes 1474568 | tf_op jit(solution)/shard_map/ppermute | solution.py:282
  107.8 10.0 %collective-permute-start.24 = (bf16[256,640]{1,0:T(8,128)(2,1)S(1)}, bf16[256,640]{1,0:T(8,128)(2,1)S(1)}, u32[]{:S(2)}, u32[]{:S(2)}) collective-permute-start(bf16[256,640]{1,0:T(8,128)(2,1)S(1)} %shard_map.109), channel_id=1, source_target_pairs={{0,4},{4,0},{8,12},{12,8},{16,20},{20,16},{24,28},{28,24},{1,5},{5... | collective-permute-start | bytes 983048 | tf_op jit(solution)/shard_map/ppermute | solution.py:279
  115.1 20.0 %collective-permute-start.34 = (bf16[256,640]{1,0:T(8,128)(2,1)}, bf16[256,640]{1,0:T(8,128)(2,1)}, u32[]{:S(2)}, u32[]{:S(2)}) collective-permute-start(bf16[256,640]{1,0:T(8,128)(2,1)} %get-tuple-element.285), channel_id=1, source_target_pairs={{0,1},{1,0},{2,3},{3,2},{4,5},{5,4},{6,7},{7,6},{8,9},{9,8},{10,11... | collective-permute-start | bytes 983048 | tf_op jit(solution)/shard_map/ppermute | solution.py:276
  115.4 19.7 %collective-permute-start.33 = (bf16[256,640]{1,0:T(8,128)(2,1)}, bf16[256,640]{1,0:T(8,128)(2,1)}, u32[]{:S(2)}, u32[]{:S(2)}) collective-permute-start(bf16[256,640]{1,0:T(8,128)(2,1)} %get-tuple-element.284), channel_id=1, source_target_pairs={{0,1},{1,0},{2,3},{3,2},{4,5},{5,4},{6,7},{7,6},{8,9},{9,8},{10,11... | collective-permute-start | bytes 983048 | tf_op jit(solution)/shard_map/ppermute | solution.py:276
  118.5 12.8 %collective-permute-start.36 = (bf16[256,640]{1,0:T(8,128)(2,1)S(1)}, bf16[256,640]{1,0:T(8,128)(2,1)S(1)}, u32[]{:S(2)}, u32[]{:S(2)}) collective-permute-start(bf16[256,640]{1,0:T(8,128)(2,1)S(1)} %shard_map.111), channel_id=1, source_target_pairs={{0,4},{4,0},{8,12},{12,8},{16,20},{20,16},{24,28},{28,24},{1,5},{5... | collective-permute-start | bytes 983048 | tf_op jit(solution)/shard_map/ppermute | solution.py:279
  124.8 5.7 %collective-permute-start.29 = (bf16[128,640]{1,0:T(8,128)(2,1)S(1)}, bf16[128,640]{1,0:T(8,128)(2,1)S(1)}, u32[]{:S(2)}, u32[]{:S(2)}) collective-permute-start(bf16[128,640]{1,0:T(8,128)(2,1)S(1)} %get-tuple-element.273), channel_id=1, source_target_pairs={{0,1},{1,0},{2,3},{3,2},{4,5},{5,4},{6,7},{7,6},{8,9},{9,8},{10,11... | collective-permute-start | bytes 491528 | tf_op jit(solution)/shard_map/ppermute | solution.py:276
  124.8 5.7 %collective-permute-start.30 = (bf16[128,640]{1,0:T(8,128)(2,1)S(1)}, bf16[128,640]{1,0:T(8,128)(2,1)S(1)}, u32[]{:S(2)}, u32[]{:S(2)}) collective-permute-start(bf16[128,640]{1,0:T(8,128)(2,1)S(1)} %get-tuple-element.278), channel_id=1, source_target_pairs={{0,1},{1,0},{2,3},{3,2},{4,5},{5,4},{6,7},{7,6},{8,9},{9,8},{10,11... | collective-permute-start | bytes 491528 | tf_op jit(solution)/shard_map/ppermute | solution.py:276
  132.1 9.7 %collective-permute-start.32 = (bf16[256,640]{1,0:T(8,128)(2,1)}, bf16[256,640]{1,0:T(8,128)(2,1)S(1)}, u32[]{:S(2)}, u32[]{:S(2)}) collective-permute-start(bf16[256,640]{1,0:T(8,128)(2,1)} %get-tuple-element.283), channel_id=1, source_target_pairs={{0,1},{1,0},{2,3},{3,2},{4,5},{5,4},{6,7},{7,6},{8,9},{9,8},{10,11... | collective-permute-start | bytes 983048 | tf_op jit(solution)/shard_map/ppermute | solution.py:276
  132.3 12.6 %collective-permute-start.38 = (bf16[256,640]{1,0:T(8,128)(2,1)}, bf16[256,640]{1,0:T(8,128)(2,1)S(1)}, u32[]{:S(2)}, u32[]{:S(2)}) collective-permute-start(bf16[256,640]{1,0:T(8,128)(2,1)} %copy-done.24), channel_id=1, source_target_pairs={{0,1},{1,0},{2,3},{3,2},{4,5},{5,4},{6,7},{7,6},{8,9},{9,8},{10,11... | collective-permute-start | bytes 983048 | tf_op jit(solution)/shard_map/ppermute | solution.py:276
  132.7 10.7 %collective-permute-start.31 = (bf16[256,640]{1,0:T(8,128)(2,1)}, bf16[256,640]{1,0:T(8,128)(2,1)S(1)}, u32[]{:S(2)}, u32[]{:S(2)}) collective-permute-start(bf16[256,640]{1,0:T(8,128)(2,1)} %copy-done.12), channel_id=1, source_target_pairs={{0,4},{4,0},{8,12},{12,8},{16,20},{20,16},{24,28},{28,24},{1,5},{5... | collective-permute-start | bytes 983048 | tf_op jit(solution)/shard_map/ppermute | solution.py:279
  135.1 14.7 %collective-permute-start.39 = (bf16[256,640]{1,0:T(8,128)(2,1)S(1)}, bf16[256,640]{1,0:T(8,128)(2,1)S(1)}, u32[]{:S(2)}, u32[]{:S(2)}) collective-permute-start(bf16[256,640]{1,0:T(8,128)(2,1)S(1)} %shard_map.115), channel_id=1, source_target_pairs={{0,4},{4,0},{8,12},{12,8},{16,20},{20,16},{24,28},{28,24},{1,5},{5... | collective-permute-start | bytes 983048 | tf_op jit(solution)/shard_map/ppermute | solution.py:279
  (35 other events, 185.7 us)

commit v5 on v4

--- a/solution.py
+++ b/solution.py
@@ -140,8 +140,9 @@
 
 def project_kernel(n_chunks, spans, flip_ref, *refs):
     sides = refs[:n_chunks], refs[n_chunks : 2 * n_chunks]
-    weight_refs, out_refs, weight_ref = refs[2 * n_chunks : -6], refs[-6:-1], refs[-1]
-    rows = out_refs[0].shape[0] // 2
+    weight_refs = refs[2 * n_chunks : -7]
+    keep_mine_ref, keep_other_ref, send_mine_ref, first_ref, second_ref, weight_ref, send_other_ref = refs[-7:]
+    rows = first_ref.shape[0]
     depth = weight_ref.shape[0] // 2
     at = 0
     for ref, (low, high) in zip(weight_refs, spans):
@@ -149,19 +150,20 @@
         first = pl.multiple_of((block ^ flip_ref[0]) * depth + inside, 16)
         weight_ref[pl.ds(first, high - low)] = ref[low:high]
         at += high - low
-    weight = weight_ref[...]
-    for side, parts in enumerate(sides):
-        acts = jnp.concatenate([ref[...].reshape(4 * rows, ref.shape[-1]) for ref in parts], axis=1)
-        total = jnp.dot(acts, weight, preferred_element_type=WIDE)
-        for kind in range(2):
-            first = 2 * kind * rows
-            here = slice(kind * rows, (kind + 1) * rows)
-            out_refs[side][here] = total[first : first + rows]
-            low = total[first + rows : first + 2 * rows].astype(LOW)
-            if side:
-                out_refs[3 + kind][...] = low
-            else:
-                out_refs[2][here] = low
+
+    def one(kind, _):
+        acts = [jnp.concatenate([ref[kind] for ref in parts], axis=1) for parts in sides]
+        total = jnp.dot(jnp.concatenate(acts), weight_ref[...], preferred_element_type=WIDE)
+        here = pl.ds(pl.multiple_of(kind * rows, rows), rows)
+        keep_mine_ref[here] = total[:rows]
+        send_mine_ref[here] = total[rows : 2 * rows].astype(LOW)
+        keep_other_ref[here] = total[2 * rows : 3 * rows]
+        send_other_ref[kind] = total[3 * rows :].astype(LOW)
+        return 0
+
+    lax.fori_loop(0, 2, one, 0)
+    first_ref[...] = send_other_ref[0]
+    second_ref[...] = send_other_ref[1]
 
 
 def project(flip, acts, pieces):
@@ -177,7 +179,7 @@
         out_shape=[jax.ShapeDtypeStruct((rows, n), WIDE)] * 2
         + [jax.ShapeDtypeStruct((rows, n), LOW)]
         + [jax.ShapeDtypeStruct((rows // 2, n), LOW)] * 2,
-        scratch_shapes=[pltpu.VMEM((depth, n), LOW)],
+        scratch_shapes=[pltpu.VMEM((depth, n), LOW), pltpu.VMEM((2, rows // 2, n), LOW)],
         compiler_params=params(),
         cost_estimate=pl.CostEstimate(flops=8 * rows * depth * pl.cdiv(n, 256) * 256, transcendentals=0, bytes_accessed=1),
     )(flip, *mine, *theirs, *weights)
@@ -310,6 +312,10 @@
     query_other, *keyed_other = packs[1 + len(chunks) :]
     there = wait(near(keyed_other[0]))
     keyed = [[keyed_own[0], there, far(keyed_own[0]), far(there)]]
+    for own, other in zip(keyed_own[1:], keyed_other[1:]):
+        there = wait(near(other))
+        keyed.append([own, there, far(jnp.concatenate([own, there]))])
+    queries_both = [query_own, wait(near(query_other))]
     turn(lower, 2)
 
     acts, swapped = [], []
@@ -321,10 +327,6 @@
 
     turn(upper, 1)
     keyed[0][2] = wait(keyed[0][2])
-    for own, other in zip(keyed_own[1:], keyed_other[1:]):
-        there = wait(near(other))
-        keyed.append([own, there, far(jnp.concatenate([own, there]))])
-    queries_both = [query_own, wait(near(query_other))]
     turn(beside, 1)
     attention(0)
     for step in range(3, n_ring):
@@ -334,8 +336,8 @@
     rest = [far(after(lower[0]))]
     attention(1)
     swapped[0] = wait(swapped[0])
+    swapped[1] = wait(swapped[1])
     attention(2)
-    swapped[1] = wait(swapped[1])
     turn(beside, 2)
     rest.append(far(after(lower[1])))
     for step in range(3, n_ring):

time: 152 us -> 153 us (level)
  waiting for transfers between devices: 73.1 us -> 69.7 us
  local copies, waits for them, and re-layouts: 12.2 us -> 14.2 us
    ppermute x9, waiting for transfers between devices: 52.7 us -> 48.3 us  [onward(): return lax.ppermute(array, 'dp', [(i, (i + 2) % n_dp) for i in range(n_dp)])]
    ppermute x9, starting transfers between devices: 4.18 us -> 7.12 us  [onward(): return lax.ppermute(array, 'dp', [(i, (i + 2) % n_dp) for i in range(n_dp)])]
    unnamed x54 -> x62, local copies, waits for them, and re-layouts: 9.97 us -> 12 us
    ppermute x16, waiting for transfers between devices: 2.77 us -> 4.42 us  [near(): return lax.ppermute(array, 'seq', [(i, i ^ 1) for i in range(n_seq)])]
  transfers between devices with their start and end apart: 40 -> 40, of which waited for: 19 -> 20; matrix products, arithmetic and copies ran while one was open for 2% -> 2% of each run, Pallas kernels for 23% -> 24%
where the time goes in v5:
time: 153 us
  waiting for transfers between devices  69.7 us (46%)
  Pallas kernels  37.9 us (25%)
  starting transfers between devices  28.5 us (19%)
  local copies, waits for them, and re-layouts  14.2 us (9%)
    ppermute x9, waiting for transfers between devices, onward(): return lax.ppermute(array, 'dp', [(i, (i + 2) % n_dp) for i in range(n_dp)])  48.3 us
    pallas_call x4, Pallas kernels, project(): pl.pallas_call(functools.partial(project_kernel, len(acts), spans), in_sp...  17.4 us
    ppermute x7, waiting for transfers between devices, across(): return lax.ppermute(array, 'dp', [(i, i ^ 1) for i in range(n_dp)])  13.8 us
    unnamed x62, local copies, waits for them, and re-layouts  12 us
    ppermute x8, starting transfers between devices, far(): return lax.ppermute(array, 'seq', [(i, i ^ 2) for i in range(n_seq)])  9.49 us
    pallas_call x3, Pallas kernels, attend(): pl.pallas_call(functools.partial(attend_kernel, len(queries)), grid=(widt...  9.35 us
    ppermute x7, starting transfers between devices, across(): return lax.ppermute(array, 'dp', [(i, i ^ 1) for i in range(n_dp)])  7.92 us
    pallas_call x4, Pallas kernels, place(): pl.pallas_call(place_kernel, grid_spec=pltpu.PrefetchScalarGridSpec(num_s...  7.86 us
  transfers between devices with their start and end apart: 40, of which 20 were waited for; matrix products, arithmetic and copies ran while one was open for 2% of the time, Pallas kernels for 24%

profile of v5, /device:TPU:0, one launch (start us, length us, event | category | flops | bytes accessed | tf_op | source)
XLA Modules:
  0.0 152.6 jit_solution(2888371108025202929)
XLA Ops:
  1.9 3.0 %collective-permute-start.1 = (bf16[384,640]{1,0:T(8,128)(2,1)S(1)}, bf16[384,640]{1,0:T(8,128)(2,1)S(1)}, u32[]{:S(2)}, u32[]{:S(2)}) collective-permute-start(bf16[384,640]{1,0:T(8,128)(2,1)S(1)} %slice.7.refs_6_), channel_id=1, source_target_pairs={{0,2},{1,3},{2,0},{3,1},{4,6},{5,7},{6,4},{7,5},{8,10},{9,11},{10,... | collective-permute-start | bytes 1474568 | tf_op jit(solution)/shard_map/ppermute | solution.py:275
  5.9 1.6 %collective-permute-start = (bf16[256,640]{1,0:T(8,128)(2,1)S(1)}, bf16[256,640]{1,0:T(8,128)(2,1)}, u32[]{:S(2)}, u32[]{:S(2)}) collective-permute-start(bf16[256,640]{1,0:T(8,128)(2,1)S(1)} %slice.6.refs_7_), channel_id=1, source_target_pairs={{0,8},{4,12},{8,16},{12,20},{16,24},{20,28},{24,0},{28,4},{1,9},{5... | collective-permute-start | bytes 983048 | tf_op jit(solution)/shard_map/ppermute | solution.py:284
  11.9 2.1 %shard_map.104 = (bf16[2,128,1280]{2,1,0:T(8,128)(2,1)S(1)}, bf16[4,128,640]{2,1,0:T(8,128)(2,1)S(1)}, bf16[4,128,384]{2,1,0:T(8,128)(2,1)S(1)}, bf16[4,128,256]...) custom-call(s32[1]{0:T(128)} %bitcast.3.core_ref, ...), custom_call_target="tpu_custom_call" | custom-call | flops 1 | bytes 1 | tf_op jit(solution)/shard_map/pallas_call | solution.py:78
  14.0 2.0 %collective-permute-done.1.refs_8_ = bf16[384,640]{1,0:T(8,128)(2,1)S(1)} collective-permute-done((bf16[384,640]{1,0:T(8,128)(2,1)S(1)}, bf16[384,640]{1,0:T(8,128)(2,1)S(1)}, u32[]{:S(2)}, u32[]{:S(2)}) %collective-permute-start.1) | collective-permute-done | bytes 491552 | tf_op jit(solution)/shard_map/ppermute | solution.py:275
  18.9 2.1 %collective-permute-done.3.refs_3_ = bf16[4,128,256]{2,1,0:T(8,128)(2,1)S(1)} collective-permute-done((bf16[4,128,256]{2,1,0:T(8,128)(2,1)S(1)}, bf16[4,128,256]{2,1,0:T(8,128)(2,1)S(1)}, u32[]{:S(2)}, u32[]{:S(2)}) %collective-permute-start.3) | collective-permute-done | bytes 262176 | tf_op jit(solution)/shard_map/ppermute | solution.py:278
  21.8 1.6 %collective-permute-start.7 = (bf16[384,640]{1,0:T(8,128)(2,1)S(1)}, bf16[384,640]{1,0:T(8,128)(2,1)S(1)}, u32[]{:S(2)}, u32[]{:S(2)}) collective-permute-start(bf16[384,640]{1,0:T(8,128)(2,1)S(1)} %slice.7.refs_6_), channel_id=1, source_target_pairs={{0,8},{4,12},{8,16},{12,20},{16,24},{20,28},{24,0},{28,4},{1,9},{5... | collective-permute-start | bytes 1474568 | tf_op jit(solution)/shard_map/ppermute | solution.py:284
  23.9 6.7 %collective-permute-done.8.refs_7_ = bf16[256,640]{1,0:T(8,128)(2,1)S(1)} collective-permute-done((bf16[256,640]{1,0:T(8,128)(2,1)}, bf16[256,640]{1,0:T(8,128)(2,1)S(1)}, u32[]{:S(2)}, u32[]{:S(2)}) %collective-permute-start.8) | collective-permute-done | bytes 327712 | tf_op jit(solution)/shard_map/ppermute | solution.py:284
  31.6 9.6 %collective-permute-done.7.refs_6_ = bf16[384,640]{1,0:T(8,128)(2,1)S(1)} collective-permute-done((bf16[384,640]{1,0:T(8,128)(2,1)S(1)}, bf16[384,640]{1,0:T(8,128)(2,1)S(1)}, u32[]{:S(2)}, u32[]{:S(2)}) %collective-permute-start.7) | collective-permute-done | bytes 491552 | tf_op jit(solution)/shard_map/ppermute | solution.py:284
  41.8 10.0 %collective-permute-done.10.refs_8_ = bf16[384,640]{1,0:T(8,128)(2,1)} collective-permute-done((bf16[384,640]{1,0:T(8,128)(2,1)S(1)}, bf16[384,640]{1,0:T(8,128)(2,1)}, u32[]{:S(2)}, u32[]{:S(2)}) %collective-permute-start.10) | collective-permute-done | bytes 491552 | tf_op jit(solution)/shard_map/ppermute | solution.py:284
  52.6 4.7 %shard_map.105.refs_0_ = bf16[2,256,640]{2,1,0:T(8,128)(2,1)S(1)} custom-call(bf16[2,128,1280]{2,1,0:T(8,128)(2,1)S(1)} %get-tuple-element.167.refs_0_, bf16[2,128,1280]{2,1,0:T(8,128)(2,1)S(1)} %collective-permute-done.2.refs_1_, bf16[4,128,640]{2,1,0:T(8,128)(2,1)S(1)} %get-tuple-element.191.refs_2_, ...), custom_call_target="tpu_custom_call" | custom-call | flops 1 | bytes 1 | tf_op jit(solution)/shard_map/pallas_call | solution.py:129
  57.3 1.6 %collective-permute-start.16 = (bf16[2,256,640]{2,1,0:T(8,128)(2,1)S(1)}, bf16[2,256,640]{2,1,0:T(8,128)(2,1)S(1)}, u32[]{:S(2)}, u32[]{:S(2)}) collective-permute-start(bf16[2,256,640]{2,1,0:T(8,128)(2,1)S(1)} %shard_map.105.refs_0_), channel_id=1, source_target_pairs={{0,4},{4,0},{8,12},{12,8},{16,20},{20,16},{24,28},{28,24},{1,5},{5... | collective-permute-start | bytes 1966088 | tf_op jit(solution)/shard_map/ppermute | solution.py:281
  59.8 8.5 %collective-permute-done.13.refs_7_ = bf16[256,640]{1,0:T(8,128)(2,1)S(1)} collective-permute-done((bf16[256,640]{1,0:T(8,128)(2,1)S(1)}, bf16[256,640]{1,0:T(8,128)(2,1)S(1)}, u32[]{:S(2)}, u32[]{:S(2)}) %collective-permute-start.13) | collective-permute-done | bytes 327712 | tf_op jit(solution)/shard_map/ppermute | solution.py:284
  69.5 2.8 %shard_map.106.refs_1_ = bf16[2,256,384]{2,1,0:T(8,128)(2,1)S(1)} custom-call(bf16[2,128,1280]{2,1,0:T(8,128)(2,1)S(1)} %get-tuple-element.167.refs_0_, bf16[2,128,1280]{2,1,0:T(8,128)(2,1)S(1)} %collective-permute-done.2.refs_1_, bf16[4,128,384]{2,1,0:T(8,128)(2,1)S(1)} %get-tuple-element.204.refs_2_, ...), custom_call_target="tpu_custom_call" | custom-call | flops 1 | bytes 1 | tf_op jit(solution)/shard_map/pallas_call | solution.py:129
  72.3 1.6 %collective-permute-start.15 = (bf16[2,256,384]{2,1,0:T(8,128)(2,1)S(1)}, bf16[2,256,384]{2,1,0:T(8,128)(2,1)S(1)}, u32[]{:S(2)}, u32[]{:S(2)}) collective-permute-start(bf16[2,256,384]{2,1,0:T(8,128)(2,1)S(1)} %shard_map.106.refs_1_), channel_id=1, source_target_pairs={{0,4},{4,0},{8,12},{12,8},{16,20},{20,16},{24,28},{28,24},{1,5},{5... | collective-permute-start | bytes 1179656 | tf_op jit(solution)/shard_map/ppermute | solution.py:281
  74.8 1.6 %collective-permute-start.19 = (bf16[384,640]{1,0:T(8,128)(2,1)}, bf16[384,640]{1,0:T(8,128)(2,1)}, u32[]{:S(2)}, u32[]{:S(2)}) collective-permute-start(bf16[384,640]{1,0:T(8,128)(2,1)} %collective-permute-done.12.refs_6_), channel_id=1, source_target_pairs={{0,8},{4,12},{8,16},{12,20},{16,24},{20,28},{24,0},{28,4},{1,9},{5... | collective-permute-start | bytes 1474568 | tf_op jit(solution)/shard_map/ppermute | solution.py:284
  76.4 1.5 collective-permute-start.18
  77.9 4.5 %collective-permute-done.15.refs_4_ = bf16[2,256,384]{2,1,0:T(8,128)(2,1)S(1)} collective-permute-done((bf16[2,256,384]{2,1,0:T(8,128)(2,1)S(1)}, bf16[2,256,384]{2,1,0:T(8,128)(2,1)S(1)}, u32[]{:S(2)}, u32[]{:S(2)}) %collective-permute-start.15) | collective-permute-done | bytes 393248 | tf_op jit(solution)/shard_map/ppermute | solution.py:281
  82.3 1.9 %shard_map.107.refs_2_ = bf16[2,256,256]{2,1,0:T(8,128)(2,1)S(1)} custom-call(bf16[2,128,1280]{2,1,0:T(8,128)(2,1)S(1)} %get-tuple-element.167.refs_0_, bf16[2,128,1280]{2,1,0:T(8,128)(2,1)S(1)} %collective-permute-done.2.refs_1_, bf16[4,128,256]{2,1,0:T(8,128)(2,1)S(1)} %get-tuple-element.216.refs_2_, ...), custom_call_target="tpu_custom_call" | custom-call | flops 1 | bytes 1 | tf_op jit(solution)/shard_map/pallas_call | solution.py:129
  84.3 1.6 %collective-permute-start.17 = (bf16[2,256,256]{2,1,0:T(8,128)(2,1)S(1)}, bf16[2,256,256]{2,1,0:T(8,128)(2,1)}, u32[]{:S(2)}, u32[]{:S(2)}) collective-permute-start(bf16[2,256,256]{2,1,0:T(8,128)(2,1)S(1)} %shard_map.107.refs_2_), channel_id=1, source_target_pairs={{0,4},{4,0},{8,12},{12,8},{16,20},{20,16},{24,28},{28,24},{1,5},{5... | collective-permute-start | bytes 786440 | tf_op jit(solution)/shard_map/ppermute | solution.py:281
  85.9 4.3 %collective-permute-done.20.refs_8_ = bf16[384,640]{1,0:T(8,128)(2,1)} collective-permute-done((bf16[384,640]{1,0:T(8,128)(2,1)}, bf16[384,640]{1,0:T(8,128)(2,1)}, u32[]{:S(2)}, u32[]{:S(2)}) %collective-permute-start.20) | collective-permute-done | bytes 491552 | tf_op jit(solution)/shard_map/ppermute | solution.py:284
  90.2 8.1 %collective-permute-done.19.refs_6_ = bf16[384,640]{1,0:T(8,128)(2,1)} collective-permute-done((bf16[384,640]{1,0:T(8,128)(2,1)}, bf16[384,640]{1,0:T(8,128)(2,1)}, u32[]{:S(2)}, u32[]{:S(2)}) %collective-permute-start.19) | collective-permute-done | bytes 491552 | tf_op jit(solution)/shard_map/ppermute | solution.py:284
  103.5 4.3 %shard_map.108 = (f32[256,640]{1,0:T(8,128)S(1)}, f32[256,640]{1,0:T(8,128)S(1)}, bf16[256,640]{1,0:T(8,128)(2,1)}, bf16[128,640]{1,0:T(8,128)(2,1)S(1)}, bf16[128,640]{1,0:T(8,128)(2,1)S(1)}) custom-call(s32[1]{0:T(128)} %bitcast.2.flip_ref, bf16[2,256,640]{2,1,0:T(8,128)(2,1)S(1)} %shard_map.105.refs_0_, bf16[2,256,384]{2,1,0:T(8,128)(2,1)S(1)} %shard_map.106.refs_1_, ...), custom_call_target="tpu_custom_call" | custom-call | flops 2013265920 | bytes 1 | tf_op jit(solution)/shard_map/pallas_call | solution.py:175
  110.1 4.4 %shard_map.110 = (f32[256,640]{1,0:T(8,128)S(1)}, f32[256,640]{1,0:T(8,128)S(1)}, bf16[256,640]{1,0:T(8,128)(2,1)}, bf16[128,640]{1,0:T(8,128)(2,1)S(1)}, bf16[128,640]{1,0:T(8,128)(2,1)S(1)}) custom-call(s32[1]{0:T(128)} %bitcast.2.flip_ref, bf16[2,256,640]{2,1,0:T(8,128)(2,1)S(1)} %shard_map.105.refs_0_, bf16[2,256,384]{2,1,0:T(8,128)(2,1)S(1)} %shard_map.106.refs_1_, ...), custom_call_target="tpu_custom_call" | custom-call | flops 2013265920 | bytes 1 | tf_op jit(solution)/shard_map/pallas_call | solution.py:175
  116.5 3.0 %collective-permute-done.24.other_ref = bf16[256,640]{1,0:T(8,128)(2,1)S(1)} collective-permute-done((bf16[256,640]{1,0:T(8,128)(2,1)S(1)}, bf16[256,640]{1,0:T(8,128)(2,1)S(1)}, u32[]{:S(2)}, u32[]{:S(2)}) %collective-permute-start.24) | collective-permute-done | bytes 327712 | tf_op jit(solution)/shard_map/ppermute | solution.py:281
  120.7 4.4 %shard_map.112 = (f32[256,640]{1,0:T(8,128)S(1)}, f32[256,640]{1,0:T(8,128)S(1)}, bf16[256,640]{1,0:T(8,128)(2,1)}, bf16[128,640]{1,0:T(8,128)(2,1)S(1)}, bf16[128,640]{1,0:T(8,128)(2,1)S(1)}) custom-call(s32[1]{0:T(128)} %bitcast.2.flip_ref, bf16[2,256,640]{2,1,0:T(8,128)(2,1)S(1)} %shard_map.105.refs_0_, bf16[2,256,384]{2,1,0:T(8,128)(2,1)S(1)} %shard_map.106.refs_1_, ...), custom_call_target="tpu_custom_call" | custom-call | flops 2013265920 | bytes 1 | tf_op jit(solution)/shard_map/pallas_call | solution.py:175
  127.5 4.4 %shard_map.114 = (f32[256,640]{1,0:T(8,128)S(1)}, f32[256,640]{1,0:T(8,128)S(1)}, bf16[256,640]{1,0:T(8,128)(2,1)S(1)}, bf16[128,640]{1,0:T(8,128)(2,1)}, bf16[128,640]{1,0:T(8,128)(2,1)}) custom-call(s32[1]{0:T(128)} %bitcast.2.flip_ref, bf16[2,256,640]{2,1,0:T(8,128)(2,1)S(1)} %shard_map.105.refs_0_, bf16[2,256,384]{2,1,0:T(8,128)(2,1)S(1)} %copy-done.9, ...), custom_call_target="tpu_custom_call" | custom-call | flops 2013265920 | bytes 1 | tf_op jit(solution)/shard_map/pallas_call | solution.py:175
  134.0 1.5 collective-permute-start.31
  138.2 2.5 %shard_map.116 = (bf16[128,5120]{1,0:T(8,128)(2,1)}, bf16[128,5120]{1,0:T(8,128)(2,1)}) custom-call(s32[2]{0:T(128)S(1)} %add_add_fusion.3.where_ref, f32[256,640]{1,0:T(8,128)S(1)} %get-tuple-element.317.keep_ref, bf16[256,640]{1,0:T(8,128)(2,1)} %collective-permute-done.34.got_ref, bf16[256,640]{1,0:T(8,128)(2,1)S(1)} %copy-done.16), custom_call_target="tpu_custom_call" | custom-call | flops 1 | bytes 1 | tf_op jit(solution)/shard_map/pallas_call | solution.py:234
  140.7 2.5 %shard_map.117 = (bf16[128,5120]{1,0:T(8,128)(2,1)}, bf16[128,5120]{1,0:T(8,128)(2,1)}) custom-call(s32[2]{0:T(128)S(1)} %add_add_fusion.2.where_ref, f32[256,640]{1,0:T(8,128)S(1)} %get-tuple-element.314.keep_ref, bf16[256,640]{1,0:T(8,128)(2,1)} %collective-permute-done.33.got_ref, ...), custom_call_target="tpu_custom_call", output_to_operand_aliasing={{0}: (4, {}), {1}: (5, {})} | custom-call | flops 1 | bytes 1 | tf_op jit(solution)/shard_map/pallas_call | solution.py:234
  143.3 1.5 collective-permute-done.31.other_ref
  144.8 1.5 shard_map.118
  146.3 4.8 %collective-permute-done.39.other_ref = bf16[256,640]{1,0:T(8,128)(2,1)S(1)} collective-permute-done((bf16[256,640]{1,0:T(8,128)(2,1)S(1)}, bf16[256,640]{1,0:T(8,128)(2,1)S(1)}, u32[]{:S(2)}, u32[]{:S(2)}) %collective-permute-start.39) | collective-permute-done | bytes 327712 | tf_op jit(solution)/shard_map/ppermute | solution.py:281
  (138 shorter events, 35.6 us)
Async XLA Ops:
  1.9 14.2 %collective-permute-start.1 = (bf16[384,640]{1,0:T(8,128)(2,1)S(1)}, bf16[384,640]{1,0:T(8,128)(2,1)S(1)}, u32[]{:S(2)}, u32[]{:S(2)}) collective-permute-start(bf16[384,640]{1,0:T(8,128)(2,1)S(1)} %slice.7.refs_6_), channel_id=1, source_target_pairs={{0,2},{1,3},{2,0},{3,1},{4,6},{5,7},{6,4},{7,5},{8,10},{9,11},{10,... | collective-permute-start | bytes 1474568 | tf_op jit(solution)/shard_map/ppermute | solution.py:275
  5.9 11.2 %collective-permute-start = (bf16[256,640]{1,0:T(8,128)(2,1)S(1)}, bf16[256,640]{1,0:T(8,128)(2,1)}, u32[]{:S(2)}, u32[]{:S(2)}) collective-permute-start(bf16[256,640]{1,0:T(8,128)(2,1)S(1)} %slice.6.refs_7_), channel_id=1, source_target_pairs={{0,8},{4,12},{8,16},{12,20},{16,24},{20,28},{24,0},{28,4},{1,9},{5... | collective-permute-start | bytes 983048 | tf_op jit(solution)/shard_map/ppermute | solution.py:284
  17.1 13.7 %collective-permute-start.2 = (bf16[2,128,1280]{2,1,0:T(8,128)(2,1)S(1)}, bf16[2,128,1280]{2,1,0:T(8,128)(2,1)S(1)}, u32[]{:S(2)}, u32[]{:S(2)}) collective-permute-start(bf16[2,128,1280]{2,1,0:T(8,128)(2,1)S(1)} %get-tuple-element.176), channel_id=1, source_target_pairs={{0,1},{1,0},{2,3},{3,2},{4,5},{5,4},{6,7},{7,6},{8,9},{9,8},{10,11... | collective-permute-start | bytes 1966088 | tf_op jit(solution)/shard_map/ppermute | solution.py:278
  17.6 5.8 %collective-permute-start.4 = (bf16[4,128,384]{2,1,0:T(8,128)(2,1)S(1)}, bf16[4,128,384]{2,1,0:T(8,128)(2,1)S(1)}, u32[]{:S(2)}, u32[]{:S(2)}) collective-permute-start(bf16[4,128,384]{2,1,0:T(8,128)(2,1)S(1)} %get-tuple-element.184), channel_id=1, source_target_pairs={{0,1},{1,0},{2,3},{3,2},{4,5},{5,4},{6,7},{7,6},{8,9},{9,8},{10,11... | collective-permute-start | bytes 1179656 | tf_op jit(solution)/shard_map/ppermute | solution.py:278
  18.1 12.6 %collective-permute-start.8 = (bf16[256,640]{1,0:T(8,128)(2,1)}, bf16[256,640]{1,0:T(8,128)(2,1)S(1)}, u32[]{:S(2)}, u32[]{:S(2)}) collective-permute-start(bf16[256,640]{1,0:T(8,128)(2,1)} %collective-permute-done.refs_7_), channel_id=1, source_target_pairs={{0,8},{4,12},{8,16},{12,20},{16,24},{20,28},{24,0},{28,4},{1,9},{5... | collective-permute-start | bytes 983048 | tf_op jit(solution)/shard_map/ppermute | solution.py:284
  21.0 20.2 %collective-permute-start.6 = (bf16[4,128,640]{2,1,0:T(8,128)(2,1)S(1)}, bf16[4,128,640]{2,1,0:T(8,128)(2,1)S(1)}, u32[]{:S(2)}, u32[]{:S(2)}) collective-permute-start(bf16[4,128,640]{2,1,0:T(8,128)(2,1)S(1)} %get-tuple-element.191.refs_2_), channel_id=1, source_target_pairs={{0,2},{1,3},{2,0},{3,1},{4,6},{5,7},{6,4},{7,5},{8,10},{9,11},{10,... | collective-permute-start | bytes 1966088 | tf_op jit(solution)/shard_map/ppermute | solution.py:275
  21.8 19.4 %collective-permute-start.7 = (bf16[384,640]{1,0:T(8,128)(2,1)S(1)}, bf16[384,640]{1,0:T(8,128)(2,1)S(1)}, u32[]{:S(2)}, u32[]{:S(2)}) collective-permute-start(bf16[384,640]{1,0:T(8,128)(2,1)S(1)} %slice.7.refs_6_), channel_id=1, source_target_pairs={{0,8},{4,12},{8,16},{12,20},{16,24},{20,28},{24,0},{28,4},{1,9},{5... | collective-permute-start | bytes 1474568 | tf_op jit(solution)/shard_map/ppermute | solution.py:284
  23.4 29.3 %collective-permute-start.9 = (bf16[4,128,640]{2,1,0:T(8,128)(2,1)S(1)}, bf16[4,128,640]{2,1,0:T(8,128)(2,1)S(1)}, u32[]{:S(2)}, u32[]{:S(2)}) collective-permute-start(bf16[4,128,640]{2,1,0:T(8,128)(2,1)S(1)} %collective-permute-done.5.refs_3_), channel_id=1, source_target_pairs={{0,2},{1,3},{2,0},{3,1},{4,6},{5,7},{6,4},{7,5},{8,10},{9,11},{10,... | collective-permute-start | bytes 1966088 | tf_op jit(solution)/shard_map/ppermute | solution.py:275
  30.7 21.2 %collective-permute-start.10 = (bf16[384,640]{1,0:T(8,128)(2,1)S(1)}, bf16[384,640]{1,0:T(8,128)(2,1)}, u32[]{:S(2)}, u32[]{:S(2)}) collective-permute-start(bf16[384,640]{1,0:T(8,128)(2,1)S(1)} %collective-permute-done.1.refs_8_), channel_id=1, source_target_pairs={{0,8},{4,12},{8,16},{12,20},{16,24},{20,28},{24,0},{28,4},{1,9},{5... | collective-permute-start | bytes 1474568 | tf_op jit(solution)/shard_map/ppermute | solution.py:284
  30.8 38.7 %collective-permute-start.11 = (bf16[8,128,384]{2,1,0:T(8,128)(2,1)S(1)}, bf16[8,128,384]{2,1,0:T(8,128)(2,1)S(1)}, u32[]{:S(2)}, u32[]{:S(2)}) collective-permute-start(bf16[8,128,384]{2,1,0:T(8,128)(2,1)S(1)} %pad_maximum_fusion), channel_id=1, source_target_pairs={{0,2},{1,3},{2,0},{3,1},{4,6},{5,7},{6,4},{7,5},{8,10},{9,11},{10,... | collective-permute-start | bytes 2359304 | tf_op jit(solution)/shard_map/ppermute | solution.py:275
  41.2 28.1 %collective-permute-start.12 = (bf16[384,640]{1,0:T(8,128)(2,1)S(1)}, bf16[384,640]{1,0:T(8,128)(2,1)}, u32[]{:S(2)}, u32[]{:S(2)}) collective-permute-start(bf16[384,640]{1,0:T(8,128)(2,1)S(1)} %collective-permute-done.7.refs_6_), channel_id=1, source_target_pairs={{0,8},{4,12},{8,16},{12,20},{16,24},{20,28},{24,0},{28,4},{1,9},{5... | collective-permute-start | bytes 1474568 | tf_op jit(solution)/shard_map/ppermute | solution.py:284
  41.2 27.1 %collective-permute-start.13 = (bf16[256,640]{1,0:T(8,128)(2,1)S(1)}, bf16[256,640]{1,0:T(8,128)(2,1)S(1)}, u32[]{:S(2)}, u32[]{:S(2)}) collective-permute-start(bf16[256,640]{1,0:T(8,128)(2,1)S(1)} %collective-permute-done.8.refs_7_), channel_id=1, source_target_pairs={{0,8},{4,12},{8,16},{12,20},{16,24},{20,28},{24,0},{28,4},{1,9},{5... | collective-permute-start | bytes 983048 | tf_op jit(solution)/shard_map/ppermute | solution.py:284
  57.3 19.0 %collective-permute-start.16 = (bf16[2,256,640]{2,1,0:T(8,128)(2,1)S(1)}, bf16[2,256,640]{2,1,0:T(8,128)(2,1)S(1)}, u32[]{:S(2)}, u32[]{:S(2)}) collective-permute-start(bf16[2,256,640]{2,1,0:T(8,128)(2,1)S(1)} %shard_map.105.refs_0_), channel_id=1, source_target_pairs={{0,4},{4,0},{8,12},{12,8},{16,20},{20,16},{24,28},{28,24},{1,5},{5... | collective-permute-start | bytes 1966088 | tf_op jit(solution)/shard_map/ppermute | solution.py:281
  59.0 23.4 %collective-permute-start.14 = (bf16[8,128,256]{2,1,0:T(8,128)(2,1)S(1)}, bf16[8,128,256]{2,1,0:T(8,128)(2,1)S(1)}, u32[]{:S(2)}, u32[]{:S(2)}) collective-permute-start(bf16[8,128,256]{2,1,0:T(8,128)(2,1)S(1)} %pad_maximum_fusion.2), channel_id=1, source_target_pairs={{0,2},{1,3},{2,0},{3,1},{4,6},{5,7},{6,4},{7,5},{8,10},{9,11},{10,... | collective-permute-start | bytes 1572872 | tf_op jit(solution)/shard_map/ppermute | solution.py:275
  72.3 10.0 %collective-permute-start.15 = (bf16[2,256,384]{2,1,0:T(8,128)(2,1)S(1)}, bf16[2,256,384]{2,1,0:T(8,128)(2,1)S(1)}, u32[]{:S(2)}, u32[]{:S(2)}) collective-permute-start(bf16[2,256,384]{2,1,0:T(8,128)(2,1)S(1)} %shard_map.106.refs_1_), channel_id=1, source_target_pairs={{0,4},{4,0},{8,12},{12,8},{16,20},{20,16},{24,28},{28,24},{1,5},{5... | collective-permute-start | bytes 1179656 | tf_op jit(solution)/shard_map/ppermute | solution.py:281
  73.9 16.3 %collective-permute-start.20 = (bf16[384,640]{1,0:T(8,128)(2,1)}, bf16[384,640]{1,0:T(8,128)(2,1)}, u32[]{:S(2)}, u32[]{:S(2)}) collective-permute-start(bf16[384,640]{1,0:T(8,128)(2,1)} %collective-permute-done.10.refs_8_), channel_id=1, source_target_pairs={{0,8},{4,12},{8,16},{12,20},{16,24},{20,28},{24,0},{28,4},{1,9},{5... | collective-permute-start | bytes 1474568 | tf_op jit(solution)/shard_map/ppermute | solution.py:284
  74.8 23.6 %collective-permute-start.19 = (bf16[384,640]{1,0:T(8,128)(2,1)}, bf16[384,640]{1,0:T(8,128)(2,1)}, u32[]{:S(2)}, u32[]{:S(2)}) collective-permute-start(bf16[384,640]{1,0:T(8,128)(2,1)} %collective-permute-done.12.refs_6_), channel_id=1, source_target_pairs={{0,8},{4,12},{8,16},{12,20},{16,24},{20,28},{24,0},{28,4},{1,9},{5... | collective-permute-start | bytes 1474568 | tf_op jit(solution)/shard_map/ppermute | solution.py:284
  76.4 22.0 %collective-permute-start.18 = (bf16[256,640]{1,0:T(8,128)(2,1)S(1)}, bf16[256,640]{1,0:T(8,128)(2,1)}, u32[]{:S(2)}, u32[]{:S(2)}) collective-permute-start(bf16[256,640]{1,0:T(8,128)(2,1)S(1)} %slice.6.refs_7_), channel_id=1, source_target_pairs={{0,2},{1,3},{2,0},{3,1},{4,6},{5,7},{6,4},{7,5},{8,10},{9,11},{10,... | collective-permute-start | bytes 983048 | tf_op jit(solution)/shard_map/ppermute | solution.py:275
  84.3 15.1 %collective-permute-start.17 = (bf16[2,256,256]{2,1,0:T(8,128)(2,1)S(1)}, bf16[2,256,256]{2,1,0:T(8,128)(2,1)}, u32[]{:S(2)}, u32[]{:S(2)}) collective-permute-start(bf16[2,256,256]{2,1,0:T(8,128)(2,1)S(1)} %shard_map.107.refs_2_), channel_id=1, source_target_pairs={{0,4},{4,0},{8,12},{12,8},{16,20},{20,16},{24,28},{28,24},{1,5},{5... | collective-permute-start | bytes 786440 | tf_op jit(solution)/shard_map/ppermute | solution.py:281
  98.3 11.8 %collective-permute-start.25 = (bf16[256,640]{1,0:T(8,128)(2,1)}, bf16[256,640]{1,0:T(8,128)(2,1)S(1)}, u32[]{:S(2)}, u32[]{:S(2)}) collective-permute-start(bf16[256,640]{1,0:T(8,128)(2,1)} %collective-permute-done.refs_7_), channel_id=1, source_target_pairs={{0,2},{1,3},{2,0},{3,1},{4,6},{5,7},{6,4},{7,5},{8,10},{9,11},{10,... | collective-permute-start | bytes 983048 | tf_op jit(solution)/shard_map/ppermute | solution.py:275
  99.4 21.3 %collective-permute-start.21 = (bf16[512,640]{1,0:T(8,128)(2,1)}, bf16[512,640]{1,0:T(8,128)(2,1)S(1)}, u32[]{:S(2)}, u32[]{:S(2)}) collective-permute-start(bf16[512,640]{1,0:T(8,128)(2,1)} %pad_maximum_fusion.1), channel_id=1, source_target_pairs={{0,2},{1,3},{2,0},{3,1},{4,6},{5,7},{6,4},{7,5},{8,10},{9,11},{10,... | collective-permute-start | bytes 1966088 | tf_op jit(solution)/shard_map/ppermute | solution.py:275
  108.4 17.7 %collective-permute-start.28 = (bf16[384,640]{1,0:T(8,128)(2,1)}, bf16[384,640]{1,0:T(8,128)(2,1)S(1)}, u32[]{:S(2)}, u32[]{:S(2)}) collective-permute-start(bf16[384,640]{1,0:T(8,128)(2,1)} %collective-permute-done.20.refs_8_), channel_id=1, source_target_pairs={{0,8},{4,12},{8,16},{12,20},{16,24},{20,28},{24,0},{28,4},{1,9},{5... | collective-permute-start | bytes 1474568 | tf_op jit(solution)/shard_map/ppermute | solution.py:284
  109.5 10.0 %collective-permute-start.24 = (bf16[256,640]{1,0:T(8,128)(2,1)S(1)}, bf16[256,640]{1,0:T(8,128)(2,1)S(1)}, u32[]{:S(2)}, u32[]{:S(2)}) collective-permute-start(bf16[256,640]{1,0:T(8,128)(2,1)S(1)} %shard_map.109), channel_id=1, source_target_pairs={{0,4},{4,0},{8,12},{12,8},{16,20},{20,16},{24,28},{28,24},{1,5},{5... | collective-permute-start | bytes 983048 | tf_op jit(solution)/shard_map/ppermute | solution.py:281
  115.9 20.7 %collective-permute-start.34 = (bf16[256,640]{1,0:T(8,128)(2,1)}, bf16[256,640]{1,0:T(8,128)(2,1)}, u32[]{:S(2)}, u32[]{:S(2)}) collective-permute-start(bf16[256,640]{1,0:T(8,128)(2,1)} %get-tuple-element.285), channel_id=1, source_target_pairs={{0,1},{1,0},{2,3},{3,2},{4,5},{5,4},{6,7},{7,6},{8,9},{9,8},{10,11... | collective-permute-start | bytes 983048 | tf_op jit(solution)/shard_map/ppermute | solution.py:278
  116.1 20.5 %collective-permute-start.33 = (bf16[256,640]{1,0:T(8,128)(2,1)}, bf16[256,640]{1,0:T(8,128)(2,1)}, u32[]{:S(2)}, u32[]{:S(2)}) collective-permute-start(bf16[256,640]{1,0:T(8,128)(2,1)} %get-tuple-element.284), channel_id=1, source_target_pairs={{0,1},{1,0},{2,3},{3,2},{4,5},{5,4},{6,7},{7,6},{8,9},{9,8},{10,11... | collective-permute-start | bytes 983048 | tf_op jit(solution)/shard_map/ppermute | solution.py:278
  120.2 12.3 %collective-permute-start.36 = (bf16[256,640]{1,0:T(8,128)(2,1)S(1)}, bf16[256,640]{1,0:T(8,128)(2,1)S(1)}, u32[]{:S(2)}, u32[]{:S(2)}) collective-permute-start(bf16[256,640]{1,0:T(8,128)(2,1)S(1)} %shard_map.111), channel_id=1, source_target_pairs={{0,4},{4,0},{8,12},{12,8},{16,20},{20,16},{24,28},{28,24},{1,5},{5... | collective-permute-start | bytes 983048 | tf_op jit(solution)/shard_map/ppermute | solution.py:281
  126.0 5.9 %collective-permute-start.29 = (bf16[128,640]{1,0:T(8,128)(2,1)S(1)}, bf16[128,640]{1,0:T(8,128)(2,1)S(1)}, u32[]{:S(2)}, u32[]{:S(2)}) collective-permute-start(bf16[128,640]{1,0:T(8,128)(2,1)S(1)} %get-tuple-element.273), channel_id=1, source_target_pairs={{0,1},{1,0},{2,3},{3,2},{4,5},{5,4},{6,7},{7,6},{8,9},{9,8},{10,11... | collective-permute-start | bytes 491528 | tf_op jit(solution)/shard_map/ppermute | solution.py:278
  126.0 5.9 %collective-permute-start.30 = (bf16[128,640]{1,0:T(8,128)(2,1)S(1)}, bf16[128,640]{1,0:T(8,128)(2,1)S(1)}, u32[]{:S(2)}, u32[]{:S(2)}) collective-permute-start(bf16[128,640]{1,0:T(8,128)(2,1)S(1)} %get-tuple-element.278), channel_id=1, source_target_pairs={{0,1},{1,0},{2,3},{3,2},{4,5},{5,4},{6,7},{7,6},{8,9},{9,8},{10,11... | collective-permute-start | bytes 491528 | tf_op jit(solution)/shard_map/ppermute | solution.py:278
  133.5 9.7 %collective-permute-start.32 = (bf16[256,640]{1,0:T(8,128)(2,1)}, bf16[256,640]{1,0:T(8,128)(2,1)S(1)}, u32[]{:S(2)}, u32[]{:S(2)}) collective-permute-start(bf16[256,640]{1,0:T(8,128)(2,1)} %get-tuple-element.283), channel_id=1, source_target_pairs={{0,1},{1,0},{2,3},{3,2},{4,5},{5,4},{6,7},{7,6},{8,9},{9,8},{10,11... | collective-permute-start | bytes 983048 | tf_op jit(solution)/shard_map/ppermute | solution.py:278
  133.6 12.6 %collective-permute-start.38 = (bf16[256,640]{1,0:T(8,128)(2,1)}, bf16[256,640]{1,0:T(8,128)(2,1)S(1)}, u32[]{:S(2)}, u32[]{:S(2)}) collective-permute-start(bf16[256,640]{1,0:T(8,128)(2,1)} %copy-done.28), channel_id=1, source_target_pairs={{0,1},{1,0},{2,3},{3,2},{4,5},{5,4},{6,7},{7,6},{8,9},{9,8},{10,11... | collective-permute-start | bytes 983048 | tf_op jit(solution)/shard_map/ppermute | solution.py:278
  134.0 10.7 %collective-permute-start.31 = (bf16[256,640]{1,0:T(8,128)(2,1)}, bf16[256,640]{1,0:T(8,128)(2,1)S(1)}, u32[]{:S(2)}, u32[]{:S(2)}) collective-permute-start(bf16[256,640]{1,0:T(8,128)(2,1)} %copy-done.12), channel_id=1, source_target_pairs={{0,4},{4,0},{8,12},{12,8},{16,20},{20,16},{24,28},{28,24},{1,5},{5... | collective-permute-start | bytes 983048 | tf_op jit(solution)/shard_map/ppermute | solution.py:281
  136.6 14.6 %collective-permute-start.39 = (bf16[256,640]{1,0:T(8,128)(2,1)S(1)}, bf16[256,640]{1,0:T(8,128)(2,1)S(1)}, u32[]{:S(2)}, u32[]{:S(2)}) collective-permute-start(bf16[256,640]{1,0:T(8,128)(2,1)S(1)} %shard_map.115), channel_id=1, source_target_pairs={{0,4},{4,0},{8,12},{12,8},{16,20},{20,16},{24,28},{28,24},{1,5},{5... | collective-permute-start | bytes 983048 | tf_op jit(solution)/shard_map/ppermute | solution.py:281
  (39 other events, 233.2 us)

commit v6 on v4

--- a/solution.py
+++ b/solution.py
@@ -179,7 +179,7 @@
         + [jax.ShapeDtypeStruct((rows // 2, n), LOW)] * 2,
         scratch_shapes=[pltpu.VMEM((depth, n), LOW)],
         compiler_params=params(),
-        cost_estimate=pl.CostEstimate(flops=8 * rows * depth * pl.cdiv(n, 256) * 256, transcendentals=0, bytes_accessed=1),
+        cost_estimate=LIGHT,
     )(flip, *mine, *theirs, *weights)
 
 
@@ -310,6 +310,10 @@
     query_other, *keyed_other = packs[1 + len(chunks) :]
     there = wait(near(keyed_other[0]))
     keyed = [[keyed_own[0], there, far(keyed_own[0]), far(there)]]
+    for own, other in zip(keyed_own[1:], keyed_other[1:]):
+        there = wait(near(other))
+        keyed.append([own, there, far(jnp.concatenate([own, there]))])
+    queries_both = [query_own, wait(near(query_other))]
     turn(lower, 2)
 
     acts, swapped = [], []
@@ -321,10 +325,6 @@
 
     turn(upper, 1)
     keyed[0][2] = wait(keyed[0][2])
-    for own, other in zip(keyed_own[1:], keyed_other[1:]):
-        there = wait(near(other))
-        keyed.append([own, there, far(jnp.concatenate([own, there]))])
-    queries_both = [query_own, wait(near(query_other))]
     turn(beside, 1)
     attention(0)
     for step in range(3, n_ring):
@@ -337,12 +337,9 @@
     attention(2)
     swapped[1] = wait(swapped[1])
     turn(beside, 2)
-    rest.append(far(after(lower[1])))
-    for step in range(3, n_ring):
-        turn(upper, step)
+    rest += [far(after(piece)) for piece in lower[1:2] + later]
     rest[0] = wait(rest[0])
     swapped[2] = wait(swapped[2])
-    rest += [far(after(piece)) for piece in later]
     acts = list(zip(acts, swapped))
     flip = jnp.stack([seq // 2])
 
@@ -362,9 +359,18 @@
         other.append(across(wait(close(keeps[step][1], *[wait(array) for array in sends[step]]))))
         mine_got.append(near(mine_sends[step]))
 
+    outs = []
+
+    def put(step):
+        pair = (dp // 2 - step) % n_ring
+        where = jnp.stack([2 * pair + dp % 2, 2 * pair + 1 - dp % 2]).astype(jnp.int32) + token
+        return place(outs, n_dp * out_weight.shape[1], where, keeps[step][0], wait(mine_got[step]), wait(other[step]))
+
     columns(0)
+    for step in range(3, n_ring):
+        turn(upper, step)
+    rest[1] = wait(rest[1])
     finish(0)
-    rest[1] = wait(rest[1])
     columns(1)
     finish(1)
     for step in range(2, n_ring, 2):
@@ -377,14 +383,8 @@
         columns(step + 1)
         other[step - 1] = wait(other[step - 1])
         finish(step + 1)
-    outs = []
     for step in range(n_ring):
-        pair = (dp // 2 - step) % n_ring
-        where = jnp.stack([2 * pair + dp % 2, 2 * pair + 1 - dp % 2]).astype(jnp.int32) + token
-        mine_got[step] = wait(mine_got[step])
-        if step + 2 >= n_ring:
-            other[step] = wait(other[step])
-        outs = place(outs, n_dp * out_weight.shape[1], where, keeps[step][0], mine_got[step], other[step])
+        outs = put(step)
     return tuple(outs)
 
 

time: 152 us -> 139 us (0.914)
  waiting for transfers between devices: 73.1 us -> 63 us
  starting transfers between devices: 27.1 us -> 23.9 us
  local copies, waits for them, and re-layouts: 12.2 us -> 15 us
  Pallas kernels: 36.6 us -> 34.5 us
    ppermute x9, waiting for transfers between devices: 52.7 us -> 41.5 us  [onward(): return lax.ppermute(array, 'dp', [(i, (i + 2) % n_dp) for i in range(n_dp)])]
    ppermute x7, waiting for transfers between devices: 15.1 us -> 11 us  [across(): return lax.ppermute(array, 'dp', [(i, i ^ 1) for i in range(n_dp)])]
    ppermute x8, waiting for transfers between devices: 2.63 us -> 6.25 us  [far(): return lax.ppermute(array, 'seq', [(i, i ^ 2) for i in range(n_seq)])]
    unnamed x54 -> x74, local copies, waits for them, and re-layouts: 9.97 us -> 12.1 us
    ppermute x8, starting transfers between devices: 10.6 us -> 8.56 us  [far(): return lax.ppermute(array, 'seq', [(i, i ^ 2) for i in range(n_seq)])]
    ppermute x9, starting transfers between devices: 4.18 us -> 2.59 us  [onward(): return lax.ppermute(array, 'dp', [(i, (i + 2) % n_dp) for i in range(n_dp)])]
  transfers between devices with their start and end apart: 40 -> 40, of which waited for: 19 -> 20; matrix products, arithmetic and copies ran while one was open for 2% -> 2% of each run, Pallas kernels for 23% -> 24%
where the time goes in v6:
time: 139 us
  waiting for transfers between devices  63 us (45%)
  Pallas kernels  34.5 us (25%)
  starting transfers between devices  23.9 us (17%)
  local copies, waits for them, and re-layouts  15 us (11%)
    ppermute x9, waiting for transfers between devices, onward(): return lax.ppermute(array, 'dp', [(i, (i + 2) % n_dp) for i in range(n_dp)])  41.5 us
    pallas_call x4, Pallas kernels, project(): pl.pallas_call(functools.partial(project_kernel, len(acts), spans), in_sp...  15 us
    unnamed x74, local copies, waits for them, and re-layouts  12.1 us
    ppermute x7, waiting for transfers between devices, across(): return lax.ppermute(array, 'dp', [(i, i ^ 1) for i in range(n_dp)])  11 us
    pallas_call x3, Pallas kernels, attend(): pl.pallas_call(functools.partial(attend_kernel, len(queries)), grid=(widt...  9.35 us
    ppermute x7, starting transfers between devices, across(): return lax.ppermute(array, 'dp', [(i, i ^ 1) for i in range(n_dp)])  9.02 us
    ppermute x8, starting transfers between devices, far(): return lax.ppermute(array, 'seq', [(i, i ^ 2) for i in range(n_seq)])  8.56 us
    pallas_call x4, Pallas kernels, place(): pl.pallas_call(place_kernel, grid_spec=pltpu.PrefetchScalarGridSpec(num_s...  7.89 us
  transfers between devices with their start and end apart: 40, of which 20 were waited for; matrix products, arithmetic and copies ran while one was open for 2% of the time, Pallas kernels for 24%

profile of v6, /device:TPU:0, one launch (start us, length us, event | category | flops | bytes accessed | tf_op | source)
XLA Modules:
  0.0 138.8 jit_solution(12701263748141196716)
XLA Ops:
  1.9 3.0 %collective-permute-start.1 = (bf16[384,640]{1,0:T(8,128)(2,1)S(1)}, bf16[384,640]{1,0:T(8,128)(2,1)S(1)}, u32[]{:S(2)}, u32[]{:S(2)}) collective-permute-start(bf16[384,640]{1,0:T(8,128)(2,1)S(1)} %slice.7.refs_6_), channel_id=1, source_target_pairs={{0,2},{1,3},{2,0},{3,1},{4,6},{5,7},{6,4},{7,5},{8,10},{9,11},{10,... | collective-permute-start | bytes 1474568 | tf_op jit(solution)/shard_map/ppermute | solution.py:273
  4.9 1.7 %slice.6.refs_7_ = bf16[256,640]{1,0:T(8,128)(2,1)} slice(bf16[640,640]{1,0:T(8,128)(2,1)} %param.17), slice={[384:640], [0:640]} | slice | bytes 655360 | tf_op jit(solution)/shard_map/slice | solution.py:299
  6.6 1.6 %collective-permute-start = (bf16[256,640]{1,0:T(8,128)(2,1)}, bf16[256,640]{1,0:T(8,128)(2,1)}, u32[]{:S(2)}, u32[]{:S(2)}) collective-permute-start(bf16[256,640]{1,0:T(8,128)(2,1)} %slice.6.refs_7_), channel_id=1, source_target_pairs={{0,8},{4,12},{8,16},{12,20},{16,24},{20,28},{24,0},{28,4},{1,9},{5... | collective-permute-start | bytes 983048 | tf_op jit(solution)/shard_map/ppermute | solution.py:282
  12.6 2.1 %shard_map.104 = (bf16[2,128,1280]{2,1,0:T(8,128)(2,1)S(1)}, bf16[4,128,640]{2,1,0:T(8,128)(2,1)S(1)}, bf16[4,128,384]{2,1,0:T(8,128)(2,1)S(1)}, bf16[4,128,256]...) custom-call(s32[1]{0:T(128)} %bitcast.3.core_ref, ...), custom_call_target="tpu_custom_call" | custom-call | flops 1 | bytes 1 | tf_op jit(solution)/shard_map/pallas_call | solution.py:78
  14.7 1.4 %collective-permute-done.1.refs_8_ = bf16[384,640]{1,0:T(8,128)(2,1)S(1)} collective-permute-done((bf16[384,640]{1,0:T(8,128)(2,1)S(1)}, bf16[384,640]{1,0:T(8,128)(2,1)S(1)}, u32[]{:S(2)}, u32[]{:S(2)}) %collective-permute-start.1) | collective-permute-done | bytes 491552 | tf_op jit(solution)/shard_map/ppermute | solution.py:273
  16.1 1.8 %collective-permute-done.refs_7_ = bf16[256,640]{1,0:T(8,128)(2,1)} collective-permute-done((bf16[256,640]{1,0:T(8,128)(2,1)}, bf16[256,640]{1,0:T(8,128)(2,1)}, u32[]{:S(2)}, u32[]{:S(2)}) %collective-permute-start) | collective-permute-done | bytes 327712 | tf_op jit(solution)/shard_map/ppermute | solution.py:282
  23.4 8.2 %collective-permute-done.8.refs_7_ = bf16[256,640]{1,0:T(8,128)(2,1)S(1)} collective-permute-done((bf16[256,640]{1,0:T(8,128)(2,1)}, bf16[256,640]{1,0:T(8,128)(2,1)S(1)}, u32[]{:S(2)}, u32[]{:S(2)}) %collective-permute-start.8) | collective-permute-done | bytes 327712 | tf_op jit(solution)/shard_map/ppermute | solution.py:282
  32.3 9.8 %collective-permute-done.7.refs_6_ = bf16[384,640]{1,0:T(8,128)(2,1)S(1)} collective-permute-done((bf16[384,640]{1,0:T(8,128)(2,1)S(1)}, bf16[384,640]{1,0:T(8,128)(2,1)S(1)}, u32[]{:S(2)}, u32[]{:S(2)}) %collective-permute-start.7) | collective-permute-done | bytes 491552 | tf_op jit(solution)/shard_map/ppermute | solution.py:282
  42.2 10.5 %collective-permute-done.10.refs_8_ = bf16[384,640]{1,0:T(8,128)(2,1)S(1)} collective-permute-done((bf16[384,640]{1,0:T(8,128)(2,1)S(1)}, bf16[384,640]{1,0:T(8,128)(2,1)S(1)}, u32[]{:S(2)}, u32[]{:S(2)}) %collective-permute-start.10) | collective-permute-done | bytes 491552 | tf_op jit(solution)/shard_map/ppermute | solution.py:282
  52.6 4.7 %shard_map.105.refs_0_ = bf16[2,256,640]{2,1,0:T(8,128)(2,1)S(1)} custom-call(bf16[2,128,1280]{2,1,0:T(8,128)(2,1)S(1)} %get-tuple-element.171.refs_0_, bf16[2,128,1280]{2,1,0:T(8,128)(2,1)S(1)} %collective-permute-done.2.refs_1_, bf16[4,128,640]{2,1,0:T(8,128)(2,1)S(1)} %get-tuple-element.195.refs_2_, ...), custom_call_target="tpu_custom_call" | custom-call | flops 1 | bytes 1 | tf_op jit(solution)/shard_map/pallas_call | solution.py:129
  57.3 1.6 %collective-permute-start.15 = (bf16[2,256,640]{2,1,0:T(8,128)(2,1)S(1)}, bf16[2,256,640]{2,1,0:T(8,128)(2,1)S(1)}, u32[]{:S(2)}, u32[]{:S(2)}) collective-permute-start(bf16[2,256,640]{2,1,0:T(8,128)(2,1)S(1)} %shard_map.105.refs_0_), channel_id=1, source_target_pairs={{0,4},{4,0},{8,12},{12,8},{16,20},{20,16},{24,28},{28,24},{1,5},{5... | collective-permute-start | bytes 1966088 | tf_op jit(solution)/shard_map/ppermute | solution.py:279
  59.5 9.7 %collective-permute-done.13.refs_7_ = bf16[256,640]{1,0:T(8,128)(2,1)S(1)} collective-permute-done((bf16[256,640]{1,0:T(8,128)(2,1)S(1)}, bf16[256,640]{1,0:T(8,128)(2,1)S(1)}, u32[]{:S(2)}, u32[]{:S(2)}) %collective-permute-start.13) | collective-permute-done | bytes 327712 | tf_op jit(solution)/shard_map/ppermute | solution.py:282
  70.2 2.8 %shard_map.106.refs_1_ = bf16[2,256,384]{2,1,0:T(8,128)(2,1)S(1)} custom-call(bf16[2,128,1280]{2,1,0:T(8,128)(2,1)S(1)} %get-tuple-element.171.refs_0_, bf16[2,128,1280]{2,1,0:T(8,128)(2,1)S(1)} %collective-permute-done.2.refs_1_, bf16[4,128,384]{2,1,0:T(8,128)(2,1)S(1)} %get-tuple-element.208.refs_2_, ...), custom_call_target="tpu_custom_call" | custom-call | flops 1 | bytes 1 | tf_op jit(solution)/shard_map/pallas_call | solution.py:129
  73.0 1.6 %collective-permute-start.16 = (bf16[2,256,384]{2,1,0:T(8,128)(2,1)S(1)}, bf16[2,256,384]{2,1,0:T(8,128)(2,1)S(1)}, u32[]{:S(2)}, u32[]{:S(2)}) collective-permute-start(bf16[2,256,384]{2,1,0:T(8,128)(2,1)S(1)} %shard_map.106.refs_1_), channel_id=1, source_target_pairs={{0,4},{4,0},{8,12},{12,8},{16,20},{20,16},{24,28},{28,24},{1,5},{5... | collective-permute-start | bytes 1179656 | tf_op jit(solution)/shard_map/ppermute | solution.py:279
  75.9 3.9 %collective-permute-done.14.refs_4_ = bf16[8,128,256]{2,1,0:T(8,128)(2,1)S(1)} collective-permute-done((bf16[8,128,256]{2,1,0:T(8,128)(2,1)S(1)}, bf16[8,128,256]{2,1,0:T(8,128)(2,1)S(1)}, u32[]{:S(2)}, u32[]{:S(2)}) %collective-permute-start.14) | collective-permute-done | bytes 524320 | tf_op jit(solution)/shard_map/ppermute | solution.py:273
  79.7 1.9 %shard_map.107.refs_2_ = bf16[2,256,256]{2,1,0:T(8,128)(2,1)S(1)} custom-call(bf16[2,128,1280]{2,1,0:T(8,128)(2,1)S(1)} %get-tuple-element.171.refs_0_, bf16[2,128,1280]{2,1,0:T(8,128)(2,1)S(1)} %collective-permute-done.2.refs_1_, bf16[4,128,256]{2,1,0:T(8,128)(2,1)S(1)} %get-tuple-element.220.refs_2_, ...), custom_call_target="tpu_custom_call" | custom-call | flops 1 | bytes 1 | tf_op jit(solution)/shard_map/pallas_call | solution.py:129
  81.6 1.6 %collective-permute-start.17 = (bf16[2,256,256]{2,1,0:T(8,128)(2,1)S(1)}, bf16[2,256,256]{2,1,0:T(8,128)(2,1)S(1)}, u32[]{:S(2)}, u32[]{:S(2)}) collective-permute-start(bf16[2,256,256]{2,1,0:T(8,128)(2,1)S(1)} %shard_map.107.refs_2_), channel_id=1, source_target_pairs={{0,4},{4,0},{8,12},{12,8},{16,20},{20,16},{24,28},{28,24},{1,5},{5... | collective-permute-start | bytes 786440 | tf_op jit(solution)/shard_map/ppermute | solution.py:279
  83.6 1.6 %collective-permute-done.19.refs_8_ = bf16[384,640]{1,0:T(8,128)(2,1)S(1)} collective-permute-done((bf16[384,640]{1,0:T(8,128)(2,1)S(1)}, bf16[384,640]{1,0:T(8,128)(2,1)S(1)}, u32[]{:S(2)}, u32[]{:S(2)}) %collective-permute-start.19) | collective-permute-done | bytes 491552 | tf_op jit(solution)/shard_map/ppermute | solution.py:282
  86.5 1.5 %collective-permute-start.20 = (bf16[512,640]{1,0:T(8,128)(2,1)}, bf16[512,640]{1,0:T(8,128)(2,1)S(1)}, u32[]{:S(2)}, u32[]{:S(2)}) collective-permute-start(bf16[512,640]{1,0:T(8,128)(2,1)} %pad_maximum_fusion.1), channel_id=1, source_target_pairs={{0,2},{1,3},{2,0},{3,1},{4,6},{5,7},{6,4},{7,5},{8,10},{9,11},{10,... | collective-permute-start | bytes 1966088 | tf_op jit(solution)/shard_map/ppermute | solution.py:273
  90.9 3.7 %shard_map.108 = (f32[256,640]{1,0:T(8,128)S(1)}, f32[256,640]{1,0:T(8,128)S(1)}, bf16[256,640]{1,0:T(8,128)(2,1)}, bf16[128,640]{1,0:T(8,128)(2,1)S(1)}, bf16[128,640]{1,0:T(8,128)(2,1)S(1)}) custom-call(s32[1]{0:T(128)} %bitcast.2.flip_ref, bf16[2,256,640]{2,1,0:T(8,128)(2,1)S(1)} %shard_map.105.refs_0_, bf16[2,256,384]{2,1,0:T(8,128)(2,1)S(1)} %shard_map.106.refs_1_, ...), custom_call_target="tpu_custom_call" | custom-call | flops 1 | bytes 1 | tf_op jit(solution)/shard_map/pallas_call | solution.py:173
  97.1 1.6 %collective-permute-start.25 = (bf16[256,640]{1,0:T(8,128)(2,1)S(1)}, bf16[256,640]{1,0:T(8,128)(2,1)S(1)}, u32[]{:S(2)}, u32[]{:S(2)}) collective-permute-start(bf16[256,640]{1,0:T(8,128)(2,1)S(1)} %shard_map.109), channel_id=1, source_target_pairs={{0,4},{4,0},{8,12},{12,8},{16,20},{20,16},{24,28},{28,24},{1,5},{5... | collective-permute-start | bytes 983048 | tf_op jit(solution)/shard_map/ppermute | solution.py:279
  98.7 3.6 %shard_map.110 = (f32[256,640]{1,0:T(8,128)S(1)}, f32[256,640]{1,0:T(8,128)S(1)}, bf16[256,640]{1,0:T(8,128)(2,1)}, bf16[128,640]{1,0:T(8,128)(2,1)S(1)}, bf16[128,640]{1,0:T(8,128)(2,1)S(1)}) custom-call(s32[1]{0:T(128)} %bitcast.2.flip_ref, bf16[2,256,640]{2,1,0:T(8,128)(2,1)S(1)} %shard_map.105.refs_0_, bf16[2,256,384]{2,1,0:T(8,128)(2,1)S(1)} %shard_map.106.refs_1_, ...), custom_call_target="tpu_custom_call" | custom-call | flops 1 | bytes 1 | tf_op jit(solution)/shard_map/pallas_call | solution.py:173
  105.5 1.6 %collective-permute-done.25.other_ref = bf16[256,640]{1,0:T(8,128)(2,1)S(1)} collective-permute-done((bf16[256,640]{1,0:T(8,128)(2,1)S(1)}, bf16[256,640]{1,0:T(8,128)(2,1)S(1)}, u32[]{:S(2)}, u32[]{:S(2)}) %collective-permute-start.25) | collective-permute-done | bytes 327712 | tf_op jit(solution)/shard_map/ppermute | solution.py:279
  107.1 3.7 %shard_map.112 = (f32[256,640]{1,0:T(8,128)S(1)}, f32[256,640]{1,0:T(8,128)S(1)}, bf16[256,640]{1,0:T(8,128)(2,1)}, bf16[128,640]{1,0:T(8,128)(2,1)S(1)}, bf16[128,640]{1,0:T(8,128)(2,1)S(1)}) custom-call(s32[1]{0:T(128)} %bitcast.2.flip_ref, bf16[2,256,640]{2,1,0:T(8,128)(2,1)S(1)} %shard_map.105.refs_0_, bf16[2,256,384]{2,1,0:T(8,128)(2,1)S(1)} %shard_map.106.refs_1_, ...), custom_call_target="tpu_custom_call" | custom-call | flops 1 | bytes 1 | tf_op jit(solution)/shard_map/pallas_call | solution.py:173
  112.7 4.0 %shard_map.114 = (f32[256,640]{1,0:T(8,128)S(1)}, f32[256,640]{1,0:T(8,128)S(1)}, bf16[256,640]{1,0:T(8,128)(2,1)S(1)}, bf16[128,640]{1,0:T(8,128)(2,1)}, bf16[128,640]{1,0:T(8,128)(2,1)S(1)}) custom-call(s32[1]{0:T(128)} %bitcast.2.flip_ref, bf16[2,256,640]{2,1,0:T(8,128)(2,1)S(1)} %shard_map.105.refs_0_, bf16[2,256,384]{2,1,0:T(8,128)(2,1)S(1)} %shard_map.106.refs_1_, ...), custom_call_target="tpu_custom_call" | custom-call | flops 1 | bytes 1 | tf_op jit(solution)/shard_map/pallas_call | solution.py:173
  120.3 1.7 %collective-permute-start.31 = (bf16[256,640]{1,0:T(8,128)(2,1)S(1)}, bf16[256,640]{1,0:T(8,128)(2,1)S(1)}, u32[]{:S(2)}, u32[]{:S(2)}) collective-permute-start(bf16[256,640]{1,0:T(8,128)(2,1)S(1)} %shard_map.113), channel_id=1, source_target_pairs={{0,4},{4,0},{8,12},{12,8},{16,20},{20,16},{24,28},{28,24},{1,5},{5... | collective-permute-start | bytes 983048 | tf_op jit(solution)/shard_map/ppermute | solution.py:279
  122.6 2.5 %shard_map.116 = (bf16[128,5120]{1,0:T(8,128)(2,1)}, bf16[128,5120]{1,0:T(8,128)(2,1)}) custom-call(s32[2]{0:T(128)S(1)} %add_add_fusion.3.where_ref, f32[256,640]{1,0:T(8,128)S(1)} %copy-done.13, bf16[256,640]{1,0:T(8,128)(2,1)} %collective-permute-done.35.got_ref, bf16[256,640]{1,0:T(8,128)(2,1)S(1)} %copy-done.33), custom_call_target="tpu_custom_call" | custom-call | flops 1 | bytes 1 | tf_op jit(solution)/shard_map/pallas_call | solution.py:232
  125.1 2.5 %shard_map.117 = (bf16[128,5120]{1,0:T(8,128)(2,1)}, bf16[128,5120]{1,0:T(8,128)(2,1)}) custom-call(s32[2]{0:T(128)S(1)} %add_add_fusion.2.where_ref, f32[256,640]{1,0:T(8,128)S(1)} %copy-done.17, bf16[256,640]{1,0:T(8,128)(2,1)} %collective-permute-done.34.got_ref, bf16[256,640]{1,0:T(8,128)(2,1)S(1)} %copy-done.31, ...), custom_call_target="tpu_custom_call", output_to_operand_aliasing={{0}: (4, {}), {1}: (5, {})} | custom-call | flops 1 | bytes 1 | tf_op jit(solution)/shard_map/pallas_call | solution.py:232
  127.6 3.2 %collective-permute-done.31.other_ref = bf16[256,640]{1,0:T(8,128)(2,1)S(1)} collective-permute-done((bf16[256,640]{1,0:T(8,128)(2,1)S(1)}, bf16[256,640]{1,0:T(8,128)(2,1)S(1)}, u32[]{:S(2)}, u32[]{:S(2)}) %collective-permute-start.31) | collective-permute-done | bytes 327712 | tf_op jit(solution)/shard_map/ppermute | solution.py:279
  130.8 1.5 %shard_map.118 = (bf16[128,5120]{1,0:T(8,128)(2,1)}, bf16[128,5120]{1,0:T(8,128)(2,1)}) custom-call(s32[2]{0:T(128)S(1)} %add_add_fusion.1.where_ref, f32[256,640]{1,0:T(8,128)S(1)} %copy-done.19, bf16[256,640]{1,0:T(8,128)(2,1)S(1)} %collective-permute-done.32.got_ref, ...), custom_call_target="tpu_custom_call", output_to_operand_aliasing={{0}: (4, {}), {1}: (5, {})} | custom-call | flops 1 | bytes 1 | tf_op jit(solution)/shard_map/pallas_call | solution.py:232
  132.4 4.9 %collective-permute-done.39.other_ref = bf16[256,640]{1,0:T(8,128)(2,1)S(1)} collective-permute-done((bf16[256,640]{1,0:T(8,128)(2,1)S(1)}, bf16[256,640]{1,0:T(8,128)(2,1)S(1)}, u32[]{:S(2)}, u32[]{:S(2)}) %collective-permute-start.39) | collective-permute-done | bytes 327712 | tf_op jit(solution)/shard_map/ppermute | solution.py:279
  137.3 1.5 %shard_map.119 = (bf16[128,5120]{1,0:T(8,128)(2,1)}, bf16[128,5120]{1,0:T(8,128)(2,1)}) custom-call(s32[2]{0:T(128)S(1)} %add_add_fusion.where_ref, f32[256,640]{1,0:T(8,128)S(1)} %copy-done.21, bf16[256,640]{1,0:T(8,128)(2,1)S(1)} %collective-permute-done.38.got_ref, ...), custom_call_target="tpu_custom_call", output_to_operand_aliasing={{0}: (4, {}), {1}: (5, {})} | custom-call | flops 1 | bytes 1 | tf_op jit(solution)/shard_map/pallas_call | solution.py:232
  (150 shorter events, 31.1 us)
Async XLA Ops:
  1.9 14.2 %collective-permute-start.1 = (bf16[384,640]{1,0:T(8,128)(2,1)S(1)}, bf16[384,640]{1,0:T(8,128)(2,1)S(1)}, u32[]{:S(2)}, u32[]{:S(2)}) collective-permute-start(bf16[384,640]{1,0:T(8,128)(2,1)S(1)} %slice.7.refs_6_), channel_id=1, source_target_pairs={{0,2},{1,3},{2,0},{3,1},{4,6},{5,7},{6,4},{7,5},{8,10},{9,11},{10,... | collective-permute-start | bytes 1474568 | tf_op jit(solution)/shard_map/ppermute | solution.py:273
  6.6 11.3 %collective-permute-start = (bf16[256,640]{1,0:T(8,128)(2,1)}, bf16[256,640]{1,0:T(8,128)(2,1)}, u32[]{:S(2)}, u32[]{:S(2)}) collective-permute-start(bf16[256,640]{1,0:T(8,128)(2,1)} %slice.6.refs_7_), channel_id=1, source_target_pairs={{0,8},{4,12},{8,16},{12,20},{16,24},{20,28},{24,0},{28,4},{1,9},{5... | collective-permute-start | bytes 983048 | tf_op jit(solution)/shard_map/ppermute | solution.py:282
  17.9 13.7 %collective-permute-start.2 = (bf16[2,128,1280]{2,1,0:T(8,128)(2,1)S(1)}, bf16[2,128,1280]{2,1,0:T(8,128)(2,1)S(1)}, u32[]{:S(2)}, u32[]{:S(2)}) collective-permute-start(bf16[2,128,1280]{2,1,0:T(8,128)(2,1)S(1)} %get-tuple-element.180), channel_id=1, source_target_pairs={{0,1},{1,0},{2,3},{3,2},{4,5},{5,4},{6,7},{7,6},{8,9},{9,8},{10,11... | collective-permute-start | bytes 1966088 | tf_op jit(solution)/shard_map/ppermute | solution.py:276
  18.5 4.0 %collective-permute-start.4 = (bf16[4,128,384]{2,1,0:T(8,128)(2,1)S(1)}, bf16[4,128,384]{2,1,0:T(8,128)(2,1)S(1)}, u32[]{:S(2)}, u32[]{:S(2)}) collective-permute-start(bf16[4,128,384]{2,1,0:T(8,128)(2,1)S(1)} %get-tuple-element.188), channel_id=1, source_target_pairs={{0,1},{1,0},{2,3},{3,2},{4,5},{5,4},{6,7},{7,6},{8,9},{9,8},{10,11... | collective-permute-start | bytes 1179656 | tf_op jit(solution)/shard_map/ppermute | solution.py:276
  19.0 12.6 %collective-permute-start.8 = (bf16[256,640]{1,0:T(8,128)(2,1)}, bf16[256,640]{1,0:T(8,128)(2,1)S(1)}, u32[]{:S(2)}, u32[]{:S(2)}) collective-permute-start(bf16[256,640]{1,0:T(8,128)(2,1)} %collective-permute-done.refs_7_), channel_id=1, source_target_pairs={{0,8},{4,12},{8,16},{12,20},{16,24},{20,28},{24,0},{28,4},{1,9},{5... | collective-permute-start | bytes 983048 | tf_op jit(solution)/shard_map/ppermute | solution.py:282
  20.0 22.1 %collective-permute-start.6 = (bf16[4,128,640]{2,1,0:T(8,128)(2,1)S(1)}, bf16[4,128,640]{2,1,0:T(8,128)(2,1)S(1)}, u32[]{:S(2)}, u32[]{:S(2)}) collective-permute-start(bf16[4,128,640]{2,1,0:T(8,128)(2,1)S(1)} %get-tuple-element.195.refs_2_), channel_id=1, source_target_pairs={{0,2},{1,3},{2,0},{3,1},{4,6},{5,7},{6,4},{7,5},{8,10},{9,11},{10,... | collective-permute-start | bytes 1966088 | tf_op jit(solution)/shard_map/ppermute | solution.py:273
  21.9 30.7 %collective-permute-start.9 = (bf16[4,128,640]{2,1,0:T(8,128)(2,1)S(1)}, bf16[4,128,640]{2,1,0:T(8,128)(2,1)S(1)}, u32[]{:S(2)}, u32[]{:S(2)}) collective-permute-start(bf16[4,128,640]{2,1,0:T(8,128)(2,1)S(1)} %collective-permute-done.5.refs_3_), channel_id=1, source_target_pairs={{0,2},{1,3},{2,0},{3,1},{4,6},{5,7},{6,4},{7,5},{8,10},{9,11},{10,... | collective-permute-start | bytes 1966088 | tf_op jit(solution)/shard_map/ppermute | solution.py:273
  22.5 19.6 %collective-permute-start.7 = (bf16[384,640]{1,0:T(8,128)(2,1)S(1)}, bf16[384,640]{1,0:T(8,128)(2,1)S(1)}, u32[]{:S(2)}, u32[]{:S(2)}) collective-permute-start(bf16[384,640]{1,0:T(8,128)(2,1)S(1)} %slice.7.refs_6_), channel_id=1, source_target_pairs={{0,8},{4,12},{8,16},{12,20},{16,24},{20,28},{24,0},{28,4},{1,9},{5... | collective-permute-start | bytes 1474568 | tf_op jit(solution)/shard_map/ppermute | solution.py:282
  31.6 21.1 %collective-permute-start.10 = (bf16[384,640]{1,0:T(8,128)(2,1)S(1)}, bf16[384,640]{1,0:T(8,128)(2,1)S(1)}, u32[]{:S(2)}, u32[]{:S(2)}) collective-permute-start(bf16[384,640]{1,0:T(8,128)(2,1)S(1)} %collective-permute-done.1.refs_8_), channel_id=1, source_target_pairs={{0,8},{4,12},{8,16},{12,20},{16,24},{20,28},{24,0},{28,4},{1,9},{5... | collective-permute-start | bytes 1474568 | tf_op jit(solution)/shard_map/ppermute | solution.py:282
  31.7 38.5 %collective-permute-start.11 = (bf16[8,128,384]{2,1,0:T(8,128)(2,1)S(1)}, bf16[8,128,384]{2,1,0:T(8,128)(2,1)S(1)}, u32[]{:S(2)}, u32[]{:S(2)}) collective-permute-start(bf16[8,128,384]{2,1,0:T(8,128)(2,1)S(1)} %pad_maximum_fusion), channel_id=1, source_target_pairs={{0,2},{1,3},{2,0},{3,1},{4,6},{5,7},{6,4},{7,5},{8,10},{9,11},{10,... | collective-permute-start | bytes 2359304 | tf_op jit(solution)/shard_map/ppermute | solution.py:273
  42.1 28.1 %collective-permute-start.12 = (bf16[384,640]{1,0:T(8,128)(2,1)S(1)}, bf16[384,640]{1,0:T(8,128)(2,1)}, u32[]{:S(2)}, u32[]{:S(2)}) collective-permute-start(bf16[384,640]{1,0:T(8,128)(2,1)S(1)} %collective-permute-done.7.refs_6_), channel_id=1, source_target_pairs={{0,8},{4,12},{8,16},{12,20},{16,24},{20,28},{24,0},{28,4},{1,9},{5... | collective-permute-start | bytes 1474568 | tf_op jit(solution)/shard_map/ppermute | solution.py:282
  42.1 27.1 %collective-permute-start.13 = (bf16[256,640]{1,0:T(8,128)(2,1)S(1)}, bf16[256,640]{1,0:T(8,128)(2,1)S(1)}, u32[]{:S(2)}, u32[]{:S(2)}) collective-permute-start(bf16[256,640]{1,0:T(8,128)(2,1)S(1)} %collective-permute-done.8.refs_7_), channel_id=1, source_target_pairs={{0,8},{4,12},{8,16},{12,20},{16,24},{20,28},{24,0},{28,4},{1,9},{5... | collective-permute-start | bytes 983048 | tf_op jit(solution)/shard_map/ppermute | solution.py:282
  57.3 17.3 %collective-permute-start.15 = (bf16[2,256,640]{2,1,0:T(8,128)(2,1)S(1)}, bf16[2,256,640]{2,1,0:T(8,128)(2,1)S(1)}, u32[]{:S(2)}, u32[]{:S(2)}) collective-permute-start(bf16[2,256,640]{2,1,0:T(8,128)(2,1)S(1)} %shard_map.105.refs_0_), channel_id=1, source_target_pairs={{0,4},{4,0},{8,12},{12,8},{16,20},{20,16},{24,28},{28,24},{1,5},{5... | collective-permute-start | bytes 1966088 | tf_op jit(solution)/shard_map/ppermute | solution.py:279
  58.9 20.8 %collective-permute-start.14 = (bf16[8,128,256]{2,1,0:T(8,128)(2,1)S(1)}, bf16[8,128,256]{2,1,0:T(8,128)(2,1)S(1)}, u32[]{:S(2)}, u32[]{:S(2)}) collective-permute-start(bf16[8,128,256]{2,1,0:T(8,128)(2,1)S(1)} %pad_maximum_fusion.2), channel_id=1, source_target_pairs={{0,2},{1,3},{2,0},{3,1},{4,6},{5,7},{6,4},{7,5},{8,10},{9,11},{10,... | collective-permute-start | bytes 1572872 | tf_op jit(solution)/shard_map/ppermute | solution.py:273
  69.2 16.0 %collective-permute-start.19 = (bf16[384,640]{1,0:T(8,128)(2,1)S(1)}, bf16[384,640]{1,0:T(8,128)(2,1)S(1)}, u32[]{:S(2)}, u32[]{:S(2)}) collective-permute-start(bf16[384,640]{1,0:T(8,128)(2,1)S(1)} %collective-permute-done.10.refs_8_), channel_id=1, source_target_pairs={{0,8},{4,12},{8,16},{12,20},{16,24},{20,28},{24,0},{28,4},{1,9},{5... | collective-permute-start | bytes 1474568 | tf_op jit(solution)/shard_map/ppermute | solution.py:282
  73.0 10.6 %collective-permute-start.16 = (bf16[2,256,384]{2,1,0:T(8,128)(2,1)S(1)}, bf16[2,256,384]{2,1,0:T(8,128)(2,1)S(1)}, u32[]{:S(2)}, u32[]{:S(2)}) collective-permute-start(bf16[2,256,384]{2,1,0:T(8,128)(2,1)S(1)} %shard_map.106.refs_1_), channel_id=1, source_target_pairs={{0,4},{4,0},{8,12},{12,8},{16,20},{20,16},{24,28},{28,24},{1,5},{5... | collective-permute-start | bytes 1179656 | tf_op jit(solution)/shard_map/ppermute | solution.py:279
  74.6 21.4 %collective-permute-start.23 = (bf16[384,640]{1,0:T(8,128)(2,1)}, bf16[384,640]{1,0:T(8,128)(2,1)}, u32[]{:S(2)}, u32[]{:S(2)}) collective-permute-start(bf16[384,640]{1,0:T(8,128)(2,1)} %collective-permute-done.12.refs_6_), channel_id=1, source_target_pairs={{0,8},{4,12},{8,16},{12,20},{16,24},{20,28},{24,0},{28,4},{1,9},{5... | collective-permute-start | bytes 1474568 | tf_op jit(solution)/shard_map/ppermute | solution.py:282
  74.6 13.4 %collective-permute-start.18 = (bf16[256,640]{1,0:T(8,128)(2,1)}, bf16[256,640]{1,0:T(8,128)(2,1)}, u32[]{:S(2)}, u32[]{:S(2)}) collective-permute-start(bf16[256,640]{1,0:T(8,128)(2,1)} %slice.6.refs_7_), channel_id=1, source_target_pairs={{0,2},{1,3},{2,0},{3,1},{4,6},{5,7},{6,4},{7,5},{8,10},{9,11},{10,... | collective-permute-start | bytes 983048 | tf_op jit(solution)/shard_map/ppermute | solution.py:273
  81.6 7.2 %collective-permute-start.17 = (bf16[2,256,256]{2,1,0:T(8,128)(2,1)S(1)}, bf16[2,256,256]{2,1,0:T(8,128)(2,1)S(1)}, u32[]{:S(2)}, u32[]{:S(2)}) collective-permute-start(bf16[2,256,256]{2,1,0:T(8,128)(2,1)S(1)} %shard_map.107.refs_2_), channel_id=1, source_target_pairs={{0,4},{4,0},{8,12},{12,8},{16,20},{20,16},{24,28},{28,24},{1,5},{5... | collective-permute-start | bytes 786440 | tf_op jit(solution)/shard_map/ppermute | solution.py:279
  85.9 11.0 %collective-permute-start.22 = (bf16[256,640]{1,0:T(8,128)(2,1)}, bf16[256,640]{1,0:T(8,128)(2,1)}, u32[]{:S(2)}, u32[]{:S(2)}) collective-permute-start(bf16[256,640]{1,0:T(8,128)(2,1)} %collective-permute-done.refs_7_), channel_id=1, source_target_pairs={{0,2},{1,3},{2,0},{3,1},{4,6},{5,7},{6,4},{7,5},{8,10},{9,11},{10,... | collective-permute-start | bytes 983048 | tf_op jit(solution)/shard_map/ppermute | solution.py:273
  86.5 20.6 %collective-permute-start.20 = (bf16[512,640]{1,0:T(8,128)(2,1)}, bf16[512,640]{1,0:T(8,128)(2,1)S(1)}, u32[]{:S(2)}, u32[]{:S(2)}) collective-permute-start(bf16[512,640]{1,0:T(8,128)(2,1)} %pad_maximum_fusion.1), channel_id=1, source_target_pairs={{0,2},{1,3},{2,0},{3,1},{4,6},{5,7},{6,4},{7,5},{8,10},{9,11},{10,... | collective-permute-start | bytes 1966088 | tf_op jit(solution)/shard_map/ppermute | solution.py:273
  95.9 15.7 %collective-permute-start.28 = (bf16[384,640]{1,0:T(8,128)(2,1)S(1)}, bf16[384,640]{1,0:T(8,128)(2,1)S(1)}, u32[]{:S(2)}, u32[]{:S(2)}) collective-permute-start(bf16[384,640]{1,0:T(8,128)(2,1)S(1)} %copy-done.29), channel_id=1, source_target_pairs={{0,8},{4,12},{8,16},{12,20},{16,24},{20,28},{24,0},{28,4},{1,9},{5... | collective-permute-start | bytes 1474568 | tf_op jit(solution)/shard_map/ppermute | solution.py:282
  97.1 10.0 %collective-permute-start.25 = (bf16[256,640]{1,0:T(8,128)(2,1)S(1)}, bf16[256,640]{1,0:T(8,128)(2,1)S(1)}, u32[]{:S(2)}, u32[]{:S(2)}) collective-permute-start(bf16[256,640]{1,0:T(8,128)(2,1)S(1)} %shard_map.109), channel_id=1, source_target_pairs={{0,4},{4,0},{8,12},{12,8},{16,20},{20,16},{24,28},{28,24},{1,5},{5... | collective-permute-start | bytes 983048 | tf_op jit(solution)/shard_map/ppermute | solution.py:279
  104.9 14.0 %collective-permute-start.33 = (bf16[256,640]{1,0:T(8,128)(2,1)S(1)}, bf16[256,640]{1,0:T(8,128)(2,1)S(1)}, u32[]{:S(2)}, u32[]{:S(2)}) collective-permute-start(bf16[256,640]{1,0:T(8,128)(2,1)S(1)} %shard_map.111), channel_id=1, source_target_pairs={{0,4},{4,0},{8,12},{12,8},{16,20},{20,16},{24,28},{28,24},{1,5},{5... | collective-permute-start | bytes 983048 | tf_op jit(solution)/shard_map/ppermute | solution.py:279
  111.7 5.8 %collective-permute-start.29 = (bf16[128,640]{1,0:T(8,128)(2,1)S(1)}, bf16[128,640]{1,0:T(8,128)(2,1)S(1)}, u32[]{:S(2)}, u32[]{:S(2)}) collective-permute-start(bf16[128,640]{1,0:T(8,128)(2,1)S(1)} %get-tuple-element.277), channel_id=1, source_target_pairs={{0,1},{1,0},{2,3},{3,2},{4,5},{5,4},{6,7},{7,6},{8,9},{9,8},{10,11... | collective-permute-start | bytes 491528 | tf_op jit(solution)/shard_map/ppermute | solution.py:276
  111.7 5.8 %collective-permute-start.30 = (bf16[128,640]{1,0:T(8,128)(2,1)S(1)}, bf16[128,640]{1,0:T(8,128)(2,1)S(1)}, u32[]{:S(2)}, u32[]{:S(2)}) collective-permute-start(bf16[128,640]{1,0:T(8,128)(2,1)S(1)} %get-tuple-element.282), channel_id=1, source_target_pairs={{0,1},{1,0},{2,3},{3,2},{4,5},{5,4},{6,7},{7,6},{8,9},{9,8},{10,11... | collective-permute-start | bytes 491528 | tf_op jit(solution)/shard_map/ppermute | solution.py:276
  112.2 9.9 %collective-permute-start.35 = (bf16[256,640]{1,0:T(8,128)(2,1)}, bf16[256,640]{1,0:T(8,128)(2,1)}, u32[]{:S(2)}, u32[]{:S(2)}) collective-permute-start(bf16[256,640]{1,0:T(8,128)(2,1)} %get-tuple-element.299), channel_id=1, source_target_pairs={{0,1},{1,0},{2,3},{3,2},{4,5},{5,4},{6,7},{7,6},{8,9},{9,8},{10,11... | collective-permute-start | bytes 983048 | tf_op jit(solution)/shard_map/ppermute | solution.py:276
  112.2 9.9 %collective-permute-start.34 = (bf16[256,640]{1,0:T(8,128)(2,1)}, bf16[256,640]{1,0:T(8,128)(2,1)}, u32[]{:S(2)}, u32[]{:S(2)}) collective-permute-start(bf16[256,640]{1,0:T(8,128)(2,1)} %get-tuple-element.297), channel_id=1, source_target_pairs={{0,1},{1,0},{2,3},{3,2},{4,5},{5,4},{6,7},{7,6},{8,9},{9,8},{10,11... | collective-permute-start | bytes 983048 | tf_op jit(solution)/shard_map/ppermute | solution.py:276
  119.6 7.9 %collective-permute-start.32 = (bf16[256,640]{1,0:T(8,128)(2,1)}, bf16[256,640]{1,0:T(8,128)(2,1)S(1)}, u32[]{:S(2)}, u32[]{:S(2)}) collective-permute-start(bf16[256,640]{1,0:T(8,128)(2,1)} %get-tuple-element.287), channel_id=1, source_target_pairs={{0,1},{1,0},{2,3},{3,2},{4,5},{5,4},{6,7},{7,6},{8,9},{9,8},{10,11... | collective-permute-start | bytes 983048 | tf_op jit(solution)/shard_map/ppermute | solution.py:276
  120.1 12.2 %collective-permute-start.38 = (bf16[256,640]{1,0:T(8,128)(2,1)}, bf16[256,640]{1,0:T(8,128)(2,1)S(1)}, u32[]{:S(2)}, u32[]{:S(2)}) collective-permute-start(bf16[256,640]{1,0:T(8,128)(2,1)} %copy-done.34), channel_id=1, source_target_pairs={{0,1},{1,0},{2,3},{3,2},{4,5},{5,4},{6,7},{7,6},{8,9},{9,8},{10,11... | collective-permute-start | bytes 983048 | tf_op jit(solution)/shard_map/ppermute | solution.py:276
  120.3 10.5 %collective-permute-start.31 = (bf16[256,640]{1,0:T(8,128)(2,1)S(1)}, bf16[256,640]{1,0:T(8,128)(2,1)S(1)}, u32[]{:S(2)}, u32[]{:S(2)}) collective-permute-start(bf16[256,640]{1,0:T(8,128)(2,1)S(1)} %shard_map.113), channel_id=1, source_target_pairs={{0,4},{4,0},{8,12},{12,8},{16,20},{20,16},{24,28},{28,24},{1,5},{5... | collective-permute-start | bytes 983048 | tf_op jit(solution)/shard_map/ppermute | solution.py:279
  122.1 15.2 %collective-permute-start.39 = (bf16[256,640]{1,0:T(8,128)(2,1)S(1)}, bf16[256,640]{1,0:T(8,128)(2,1)S(1)}, u32[]{:S(2)}, u32[]{:S(2)}) collective-permute-start(bf16[256,640]{1,0:T(8,128)(2,1)S(1)} %shard_map.115), channel_id=1, source_target_pairs={{0,4},{4,0},{8,12},{12,8},{16,20},{20,16},{24,28},{28,24},{1,5},{5... | collective-permute-start | bytes 983048 | tf_op jit(solution)/shard_map/ppermute | solution.py:279
  (45 other events, 254.3 us)

commit v7 on v6

--- a/solution.py
+++ b/solution.py
@@ -9,7 +9,7 @@
 
 HEADS = 20
 EPS = 1e-06
-VMEM_BYTES = 16 * 1024 * 1024
+VMEM_BYTES = 10 * 1024 * 1024
 ROW_STEP = 32
 
 LOW = jnp.bfloat16
@@ -350,7 +350,7 @@
         start = step % 2 * (depth - cut) if step > 1 else 0
         got = rest[step] if step < 2 else rest[1 + step // 2]
         theirs = [(beside[step], 0, cut), (got, start, start + depth - cut)]
-        keep_mine, keep_other, send_mine, *send_other = project(flip, acts, own + theirs)
+        keep_mine, keep_other, send_mine, *send_other = project(after(flip), acts, own + theirs)
         keeps.append((keep_mine, keep_other))
         sends.append([near(wait(array)) for array in send_other])
         mine_sends.append(send_mine)
@@ -376,13 +376,15 @@
     for step in range(2, n_ring, 2):
         other[step - 2] = wait(other[step - 2])
         rest[1 + step // 2] = wait(rest[1 + step // 2])
-        for ahead in range(max(step, 3), step + 2):
-            turn(beside, ahead)
+        if step > 2:
+            turn(beside, step)
         columns(step)
         finish(step)
+        turn(beside, step + 1)
         columns(step + 1)
         other[step - 1] = wait(other[step - 1])
         finish(step + 1)
+    other[-2] = wait(other[-2])
     for step in range(n_ring):
         outs = put(step)
     return tuple(outs)

time: 139 us -> 138 us (level)
  waiting for transfers between devices: 63 us -> 57.9 us
  local copies, waits for them, and re-layouts: 15 us -> 17.9 us
    ppermute x7, waiting for transfers between devices: 11 us -> 4.56 us  [across(): return lax.ppermute(array, 'dp', [(i, i ^ 1) for i in range(n_dp)])]
    unnamed x74, local copies, waits for them, and re-layouts: 12.1 us -> 15 us
  transfers between devices with their start and end apart: 40 -> 40, of which waited for: 20 -> 21; matrix products, arithmetic and copies ran while one was open for 2% -> 2% of each run, Pallas kernels for 24% -> 24%
where the time goes in v7:
time: 138 us; the launch traced here: 137 us
  waiting for transfers between devices  57.9 us (42%)
  Pallas kernels  34.7 us (25%)
  starting transfers between devices  24.3 us (18%)
  local copies, waits for them, and re-layouts  17.9 us (13%)
  other arithmetic  1.39 us (1%)
    ppermute x9, waiting for transfers between devices, onward(): return lax.ppermute(array, 'dp', [(i, (i + 2) % n_dp) for i in range(n_dp)])  41.6 us
    unnamed x74, local copies, waits for them, and re-layouts  15 us
    pallas_call x4, Pallas kernels, project(): pl.pallas_call(functools.partial(project_kernel, len(acts), spans), in_sp...  14.4 us
    pallas_call x3, Pallas kernels, attend(): pl.pallas_call(functools.partial(attend_kernel, len(queries)), grid=(widt...  9.36 us
    ppermute x7, starting transfers between devices, across(): return lax.ppermute(array, 'dp', [(i, i ^ 1) for i in range(n_dp)])  9 us
    pallas_call x4, Pallas kernels, place(): pl.pallas_call(place_kernel, grid_spec=pltpu.PrefetchScalarGridSpec(num_s...  7.89 us
    ppermute x8, starting transfers between devices, far(): return lax.ppermute(array, 'seq', [(i, i ^ 2) for i in range(n_seq)])  7.84 us
    ppermute x8, waiting for transfers between devices, far(): return lax.ppermute(array, 'seq', [(i, i ^ 2) for i in range(n_seq)])  6.25 us
  transfers between devices with their start and end apart: 40, of which 21 were waited for; matrix products, arithmetic and copies ran while one was open for 2% of the time, Pallas kernels for 24%

profile of v7, /device:TPU:0, one launch (start us, length us, event | category | flops | bytes accessed | tf_op | source)
XLA Modules:
  0.0 137.2 jit_solution(1867576769444141196)
XLA Ops:
  1.9 3.0 %collective-permute-start.1 = (bf16[384,640]{1,0:T(8,128)(2,1)S(1)}, bf16[384,640]{1,0:T(8,128)(2,1)S(1)}, u32[]{:S(2)}, u32[]{:S(2)}) collective-permute-start(bf16[384,640]{1,0:T(8,128)(2,1)S(1)} %slice.7.refs_6_), channel_id=1, source_target_pairs={{0,2},{1,3},{2,0},{3,1},{4,6},{5,7},{6,4},{7,5},{8,10},{9,11},{10,... | collective-permute-start | bytes 1474568 | tf_op jit(solution)/shard_map/ppermute | solution.py:273
  4.9 1.7 %slice.6.refs_7_ = bf16[256,640]{1,0:T(8,128)(2,1)} slice(bf16[640,640]{1,0:T(8,128)(2,1)} %param.17), slice={[384:640], [0:640]} | slice | bytes 655360 | tf_op jit(solution)/shard_map/slice | solution.py:299
  6.6 1.6 %collective-permute-start = (bf16[256,640]{1,0:T(8,128)(2,1)}, bf16[256,640]{1,0:T(8,128)(2,1)}, u32[]{:S(2)}, u32[]{:S(2)}) collective-permute-start(bf16[256,640]{1,0:T(8,128)(2,1)} %slice.6.refs_7_), channel_id=1, source_target_pairs={{0,8},{4,12},{8,16},{12,20},{16,24},{20,28},{24,0},{28,4},{1,9},{5... | collective-permute-start | bytes 983048 | tf_op jit(solution)/shard_map/ppermute | solution.py:282
  12.6 2.1 %shard_map.104 = (bf16[2,128,1280]{2,1,0:T(8,128)(2,1)S(1)}, bf16[4,128,640]{2,1,0:T(8,128)(2,1)S(1)}, bf16[4,128,384]{2,1,0:T(8,128)(2,1)S(1)}, bf16[4,128,256]...) custom-call(s32[1]{0:T(128)} %bitcast.3.core_ref, ...), custom_call_target="tpu_custom_call" | custom-call | flops 1 | bytes 1 | tf_op jit(solution)/shard_map/pallas_call | solution.py:78
  14.7 1.4 collective-permute-done.1.refs_8_
  16.1 1.9 %collective-permute-done.refs_7_ = bf16[256,640]{1,0:T(8,128)(2,1)} collective-permute-done((bf16[256,640]{1,0:T(8,128)(2,1)}, bf16[256,640]{1,0:T(8,128)(2,1)}, u32[]{:S(2)}, u32[]{:S(2)}) %collective-permute-start) | collective-permute-done | bytes 327712 | tf_op jit(solution)/shard_map/ppermute | solution.py:282
  20.6 1.3 collective-permute-done.4.refs_3_
  23.4 8.2 %collective-permute-done.2.refs_7_ = bf16[256,640]{1,0:T(8,128)(2,1)S(1)} collective-permute-done((bf16[256,640]{1,0:T(8,128)(2,1)}, bf16[256,640]{1,0:T(8,128)(2,1)S(1)}, u32[]{:S(2)}, u32[]{:S(2)}) %collective-permute-start.2) | collective-permute-done | bytes 327712 | tf_op jit(solution)/shard_map/ppermute | solution.py:282
  32.3 9.8 %collective-permute-done.9.refs_6_ = bf16[384,640]{1,0:T(8,128)(2,1)S(1)} collective-permute-done((bf16[384,640]{1,0:T(8,128)(2,1)S(1)}, bf16[384,640]{1,0:T(8,128)(2,1)S(1)}, u32[]{:S(2)}, u32[]{:S(2)}) %collective-permute-start.9) | collective-permute-done | bytes 491552 | tf_op jit(solution)/shard_map/ppermute | solution.py:282
  42.2 10.5 %collective-permute-done.11.refs_8_ = bf16[384,640]{1,0:T(8,128)(2,1)S(1)} collective-permute-done((bf16[384,640]{1,0:T(8,128)(2,1)S(1)}, bf16[384,640]{1,0:T(8,128)(2,1)S(1)}, u32[]{:S(2)}, u32[]{:S(2)}) %collective-permute-start.11) | collective-permute-done | bytes 491552 | tf_op jit(solution)/shard_map/ppermute | solution.py:282
  52.6 4.7 %shard_map.105.refs_0_ = bf16[2,256,640]{2,1,0:T(8,128)(2,1)S(1)} custom-call(bf16[2,128,1280]{2,1,0:T(8,128)(2,1)S(1)} %get-tuple-element.202.refs_0_, bf16[2,128,1280]{2,1,0:T(8,128)(2,1)S(1)} %collective-permute-done.3.refs_1_, bf16[4,128,640]{2,1,0:T(8,128)(2,1)S(1)} %get-tuple-element.204.refs_2_, ...), custom_call_target="tpu_custom_call" | custom-call | flops 1 | bytes 1 | tf_op jit(solution)/shard_map/pallas_call | solution.py:129
  57.3 1.6 %collective-permute-start.17 = (bf16[2,256,640]{2,1,0:T(8,128)(2,1)S(1)}, bf16[2,256,640]{2,1,0:T(8,128)(2,1)S(1)}, u32[]{:S(2)}, u32[]{:S(2)}) collective-permute-start(bf16[2,256,640]{2,1,0:T(8,128)(2,1)S(1)} %shard_map.105.refs_0_), channel_id=1, source_target_pairs={{0,4},{4,0},{8,12},{12,8},{16,20},{20,16},{24,28},{28,24},{1,5},{5... | collective-permute-start | bytes 1966088 | tf_op jit(solution)/shard_map/ppermute | solution.py:279
  59.6 9.7 %collective-permute-done.7.refs_7_ = bf16[256,640]{1,0:T(8,128)(2,1)S(1)} collective-permute-done((bf16[256,640]{1,0:T(8,128)(2,1)S(1)}, bf16[256,640]{1,0:T(8,128)(2,1)S(1)}, u32[]{:S(2)}, u32[]{:S(2)}) %collective-permute-start.7) | collective-permute-done | bytes 327712 | tf_op jit(solution)/shard_map/ppermute | solution.py:282
  70.2 2.8 %shard_map.106.refs_1_ = bf16[2,256,384]{2,1,0:T(8,128)(2,1)S(1)} custom-call(bf16[2,128,1280]{2,1,0:T(8,128)(2,1)S(1)} %get-tuple-element.202.refs_0_, bf16[2,128,1280]{2,1,0:T(8,128)(2,1)S(1)} %collective-permute-done.3.refs_1_, bf16[4,128,384]{2,1,0:T(8,128)(2,1)S(1)} %get-tuple-element.219.refs_2_, ...), custom_call_target="tpu_custom_call" | custom-call | flops 1 | bytes 1 | tf_op jit(solution)/shard_map/pallas_call | solution.py:129
  73.0 1.6 %collective-permute-start.15 = (bf16[2,256,384]{2,1,0:T(8,128)(2,1)S(1)}, bf16[2,256,384]{2,1,0:T(8,128)(2,1)S(1)}, u32[]{:S(2)}, u32[]{:S(2)}) collective-permute-start(bf16[2,256,384]{2,1,0:T(8,128)(2,1)S(1)} %shard_map.106.refs_1_), channel_id=1, source_target_pairs={{0,4},{4,0},{8,12},{12,8},{16,20},{20,16},{24,28},{28,24},{1,5},{5... | collective-permute-start | bytes 1179656 | tf_op jit(solution)/shard_map/ppermute | solution.py:279
  75.9 3.9 %collective-permute-done.16.refs_4_ = bf16[8,128,256]{2,1,0:T(8,128)(2,1)S(1)} collective-permute-done((bf16[8,128,256]{2,1,0:T(8,128)(2,1)S(1)}, bf16[8,128,256]{2,1,0:T(8,128)(2,1)S(1)}, u32[]{:S(2)}, u32[]{:S(2)}) %collective-permute-start.16) | collective-permute-done | bytes 524320 | tf_op jit(solution)/shard_map/ppermute | solution.py:273
  79.8 1.9 %shard_map.107.refs_2_ = bf16[2,256,256]{2,1,0:T(8,128)(2,1)S(1)} custom-call(bf16[2,128,1280]{2,1,0:T(8,128)(2,1)S(1)} %get-tuple-element.202.refs_0_, bf16[2,128,1280]{2,1,0:T(8,128)(2,1)S(1)} %collective-permute-done.3.refs_1_, bf16[4,128,256]{2,1,0:T(8,128)(2,1)S(1)} %get-tuple-element.227.refs_2_, ...), custom_call_target="tpu_custom_call" | custom-call | flops 1 | bytes 1 | tf_op jit(solution)/shard_map/pallas_call | solution.py:129
  81.7 1.6 %collective-permute-start.19 = (bf16[2,256,256]{2,1,0:T(8,128)(2,1)S(1)}, bf16[2,256,256]{2,1,0:T(8,128)(2,1)S(1)}, u32[]{:S(2)}, u32[]{:S(2)}) collective-permute-start(bf16[2,256,256]{2,1,0:T(8,128)(2,1)S(1)} %shard_map.107.refs_2_), channel_id=1, source_target_pairs={{0,4},{4,0},{8,12},{12,8},{16,20},{20,16},{24,28},{28,24},{1,5},{5... | collective-permute-start | bytes 786440 | tf_op jit(solution)/shard_map/ppermute | solution.py:279
  83.6 1.6 %collective-permute-done.12.refs_8_ = bf16[384,640]{1,0:T(8,128)(2,1)S(1)} collective-permute-done((bf16[384,640]{1,0:T(8,128)(2,1)S(1)}, bf16[384,640]{1,0:T(8,128)(2,1)S(1)}, u32[]{:S(2)}, u32[]{:S(2)}) %collective-permute-start.12) | collective-permute-done | bytes 491552 | tf_op jit(solution)/shard_map/ppermute | solution.py:282
  86.5 1.5 %collective-permute-start.18 = (bf16[512,640]{1,0:T(8,128)(2,1)}, bf16[512,640]{1,0:T(8,128)(2,1)S(1)}, u32[]{:S(2)}, u32[]{:S(2)}) collective-permute-start(bf16[512,640]{1,0:T(8,128)(2,1)} %pad_maximum_fusion.1), channel_id=1, source_target_pairs={{0,2},{1,3},{2,0},{3,1},{4,6},{5,7},{6,4},{7,5},{8,10},{9,11},{10,... | collective-permute-start | bytes 1966088 | tf_op jit(solution)/shard_map/ppermute | solution.py:273
  90.9 3.7 %shard_map.108 = (f32[256,640]{1,0:T(8,128)S(1)}, f32[256,640]{1,0:T(8,128)S(1)}, bf16[256,640]{1,0:T(8,128)(2,1)}, bf16[128,640]{1,0:T(8,128)(2,1)S(1)}, bf16[128,640]{1,0:T(8,128)(2,1)S(1)}) custom-call(s32[1]{0:T(128)} %bitcast.2.flip_ref, bf16[2,256,640]{2,1,0:T(8,128)(2,1)S(1)} %shard_map.105.refs_0_, bf16[2,256,384]{2,1,0:T(8,128)(2,1)S(1)} %shard_map.106.refs_1_, ...), custom_call_target="tpu_custom_call" | custom-call | flops 1 | bytes 1 | tf_op jit(solution)/shard_map/pallas_call | solution.py:173
  97.1 1.6 %collective-permute-start.25 = (bf16[256,640]{1,0:T(8,128)(2,1)S(1)}, bf16[256,640]{1,0:T(8,128)(2,1)S(1)}, u32[]{:S(2)}, u32[]{:S(2)}) collective-permute-start(bf16[256,640]{1,0:T(8,128)(2,1)S(1)} %shard_map.109), channel_id=1, source_target_pairs={{0,4},{4,0},{8,12},{12,8},{16,20},{20,16},{24,28},{28,24},{1,5},{5... | collective-permute-start | bytes 983048 | tf_op jit(solution)/shard_map/ppermute | solution.py:279
  98.7 3.6 %shard_map.110 = (f32[256,640]{1,0:T(8,128)S(1)}, f32[256,640]{1,0:T(8,128)S(1)}, bf16[256,640]{1,0:T(8,128)(2,1)}, bf16[128,640]{1,0:T(8,128)(2,1)S(1)}, bf16[128,640]{1,0:T(8,128)(2,1)S(1)}) custom-call(s32[1]{0:T(128)} %bitcast.2.flip_ref, bf16[2,256,640]{2,1,0:T(8,128)(2,1)S(1)} %shard_map.105.refs_0_, bf16[2,256,384]{2,1,0:T(8,128)(2,1)S(1)} %shard_map.106.refs_1_, ...), custom_call_target="tpu_custom_call" | custom-call | flops 1 | bytes 1 | tf_op jit(solution)/shard_map/pallas_call | solution.py:173
  105.5 1.6 %collective-permute-done.25.other_ref = bf16[256,640]{1,0:T(8,128)(2,1)S(1)} collective-permute-done((bf16[256,640]{1,0:T(8,128)(2,1)S(1)}, bf16[256,640]{1,0:T(8,128)(2,1)S(1)}, u32[]{:S(2)}, u32[]{:S(2)}) %collective-permute-start.25) | collective-permute-done | bytes 327712 | tf_op jit(solution)/shard_map/ppermute | solution.py:279
  107.1 3.7 %shard_map.112 = (f32[256,640]{1,0:T(8,128)S(1)}, f32[256,640]{1,0:T(8,128)S(1)}, bf16[256,640]{1,0:T(8,128)(2,1)}, bf16[128,640]{1,0:T(8,128)(2,1)S(1)}, bf16[128,640]{1,0:T(8,128)(2,1)S(1)}) custom-call(s32[1]{0:T(128)} %bitcast.2.flip_ref, bf16[2,256,640]{2,1,0:T(8,128)(2,1)S(1)} %shard_map.105.refs_0_, bf16[2,256,384]{2,1,0:T(8,128)(2,1)S(1)} %shard_map.106.refs_1_, ...), custom_call_target="tpu_custom_call" | custom-call | flops 1 | bytes 1 | tf_op jit(solution)/shard_map/pallas_call | solution.py:173
  114.1 1.7 %collective-permute-start.30 = (bf16[256,640]{1,0:T(8,128)(2,1)}, bf16[256,640]{1,0:T(8,128)(2,1)}, u32[]{:S(2)}, u32[]{:S(2)}) collective-permute-start(bf16[256,640]{1,0:T(8,128)(2,1)} %shard_map.113), channel_id=1, source_target_pairs={{0,4},{4,0},{8,12},{12,8},{16,20},{20,16},{24,28},{28,24},{1,5},{5... | collective-permute-start | bytes 983048 | tf_op jit(solution)/shard_map/ppermute | solution.py:279
  115.8 3.4 %shard_map.114 = (f32[256,640]{1,0:T(8,128)S(1)}, f32[256,640]{1,0:T(8,128)S(1)}, bf16[256,640]{1,0:T(8,128)(2,1)S(1)}, bf16[128,640]{1,0:T(8,128)(2,1)S(1)}, bf16[128,640]{1,0:T(8,128)(2,1)S(1)}) custom-call(s32[1]{0:T(128)} %bitcast.2.flip_ref, bf16[2,256,640]{2,1,0:T(8,128)(2,1)S(1)} %shard_map.105.refs_0_, bf16[2,256,384]{2,1,0:T(8,128)(2,1)S(1)} %shard_map.106.refs_1_, ...), custom_call_target="tpu_custom_call" | custom-call | flops 1 | bytes 1 | tf_op jit(solution)/shard_map/pallas_call | solution.py:173
  127.4 2.5 %shard_map.116 = (bf16[128,5120]{1,0:T(8,128)(2,1)}, bf16[128,5120]{1,0:T(8,128)(2,1)}) custom-call(s32[2]{0:T(128)S(1)} %add_add_fusion.3.where_ref, f32[256,640]{1,0:T(8,128)S(1)} %copy-done.13, bf16[256,640]{1,0:T(8,128)(2,1)} %collective-permute-done.37.got_ref, bf16[256,640]{1,0:T(8,128)(2,1)S(1)} %copy-done.33), custom_call_target="tpu_custom_call" | custom-call | flops 1 | bytes 1 | tf_op jit(solution)/shard_map/pallas_call | solution.py:232
  129.9 1.5 %shard_map.117 = (bf16[128,5120]{1,0:T(8,128)(2,1)}, bf16[128,5120]{1,0:T(8,128)(2,1)}) custom-call(s32[2]{0:T(128)S(1)} %add_add_fusion.2.where_ref, f32[256,640]{1,0:T(8,128)S(1)} %copy-done.17, bf16[256,640]{1,0:T(8,128)(2,1)S(1)} %collective-permute-done.36.got_ref, ...), custom_call_target="tpu_custom_call", output_to_operand_aliasing={{0}: (4, {}), {1}: (5, {})} | custom-call | flops 1 | bytes 1 | tf_op jit(solution)/shard_map/pallas_call | solution.py:232
  131.5 2.5 %shard_map.118 = (bf16[128,5120]{1,0:T(8,128)(2,1)}, bf16[128,5120]{1,0:T(8,128)(2,1)}) custom-call(s32[2]{0:T(128)S(1)} %add_add_fusion.1.where_ref, f32[256,640]{1,0:T(8,128)S(1)} %copy-done.19, bf16[256,640]{1,0:T(8,128)(2,1)S(1)} %collective-permute-done.35.got_ref, ...), custom_call_target="tpu_custom_call", output_to_operand_aliasing={{0}: (4, {}), {1}: (5, {})} | custom-call | flops 1 | bytes 1 | tf_op jit(solution)/shard_map/pallas_call | solution.py:232
  134.0 1.7 %collective-permute-done.39.other_ref = bf16[256,640]{1,0:T(8,128)(2,1)S(1)} collective-permute-done((bf16[256,640]{1,0:T(8,128)(2,1)S(1)}, bf16[256,640]{1,0:T(8,128)(2,1)S(1)}, u32[]{:S(2)}, u32[]{:S(2)}) %collective-permute-start.39) | collective-permute-done | bytes 327712 | tf_op jit(solution)/shard_map/ppermute | solution.py:279
  135.8 1.5 %shard_map.119 = (bf16[128,5120]{1,0:T(8,128)(2,1)}, bf16[128,5120]{1,0:T(8,128)(2,1)}) custom-call(s32[2]{0:T(128)S(1)} %add_add_fusion.where_ref, f32[256,640]{1,0:T(8,128)S(1)} %copy-done.21, bf16[256,640]{1,0:T(8,128)(2,1)S(1)} %collective-permute-done.38.got_ref, ...), custom_call_target="tpu_custom_call", output_to_operand_aliasing={{0}: (4, {}), {1}: (5, {})} | custom-call | flops 1 | bytes 1 | tf_op jit(solution)/shard_map/pallas_call | solution.py:232
  (150 shorter events, 35.2 us)
Async XLA Ops:
  1.9 14.2 %collective-permute-start.1 = (bf16[384,640]{1,0:T(8,128)(2,1)S(1)}, bf16[384,640]{1,0:T(8,128)(2,1)S(1)}, u32[]{:S(2)}, u32[]{:S(2)}) collective-permute-start(bf16[384,640]{1,0:T(8,128)(2,1)S(1)} %slice.7.refs_6_), channel_id=1, source_target_pairs={{0,2},{1,3},{2,0},{3,1},{4,6},{5,7},{6,4},{7,5},{8,10},{9,11},{10,... | collective-permute-start | bytes 1474568 | tf_op jit(solution)/shard_map/ppermute | solution.py:273
  6.6 11.3 %collective-permute-start = (bf16[256,640]{1,0:T(8,128)(2,1)}, bf16[256,640]{1,0:T(8,128)(2,1)}, u32[]{:S(2)}, u32[]{:S(2)}) collective-permute-start(bf16[256,640]{1,0:T(8,128)(2,1)} %slice.6.refs_7_), channel_id=1, source_target_pairs={{0,8},{4,12},{8,16},{12,20},{16,24},{20,28},{24,0},{28,4},{1,9},{5... | collective-permute-start | bytes 983048 | tf_op jit(solution)/shard_map/ppermute | solution.py:282
  18.0 2.1 %collective-permute-start.6 = (bf16[4,128,640]{2,1,0:T(8,128)(2,1)S(1)}, bf16[4,128,640]{2,1,0:T(8,128)(2,1)S(1)}, u32[]{:S(2)}, u32[]{:S(2)}) collective-permute-start(bf16[4,128,640]{2,1,0:T(8,128)(2,1)S(1)} %get-tuple-element.195), channel_id=1, source_target_pairs={{0,1},{1,0},{2,3},{3,2},{4,5},{5,4},{6,7},{7,6},{8,9},{9,8},{10,11... | collective-permute-start | bytes 1966088 | tf_op jit(solution)/shard_map/ppermute | solution.py:276
  18.0 13.7 %collective-permute-start.3 = (bf16[2,128,1280]{2,1,0:T(8,128)(2,1)S(1)}, bf16[2,128,1280]{2,1,0:T(8,128)(2,1)S(1)}, u32[]{:S(2)}, u32[]{:S(2)}) collective-permute-start(bf16[2,128,1280]{2,1,0:T(8,128)(2,1)S(1)} %get-tuple-element.186), channel_id=1, source_target_pairs={{0,1},{1,0},{2,3},{3,2},{4,5},{5,4},{6,7},{7,6},{8,9},{9,8},{10,11... | collective-permute-start | bytes 1966088 | tf_op jit(solution)/shard_map/ppermute | solution.py:276
  18.5 4.0 %collective-permute-start.5 = (bf16[4,128,384]{2,1,0:T(8,128)(2,1)S(1)}, bf16[4,128,384]{2,1,0:T(8,128)(2,1)S(1)}, u32[]{:S(2)}, u32[]{:S(2)}) collective-permute-start(bf16[4,128,384]{2,1,0:T(8,128)(2,1)S(1)} %get-tuple-element.194), channel_id=1, source_target_pairs={{0,1},{1,0},{2,3},{3,2},{4,5},{5,4},{6,7},{7,6},{8,9},{9,8},{10,11... | collective-permute-start | bytes 1179656 | tf_op jit(solution)/shard_map/ppermute | solution.py:276
  18.5 3.5 %collective-permute-start.4 = (bf16[4,128,256]{2,1,0:T(8,128)(2,1)S(1)}, bf16[4,128,256]{2,1,0:T(8,128)(2,1)S(1)}, u32[]{:S(2)}, u32[]{:S(2)}) collective-permute-start(bf16[4,128,256]{2,1,0:T(8,128)(2,1)S(1)} %get-tuple-element.193), channel_id=1, source_target_pairs={{0,1},{1,0},{2,3},{3,2},{4,5},{5,4},{6,7},{7,6},{8,9},{9,8},{10,11... | collective-permute-start | bytes 786440 | tf_op jit(solution)/shard_map/ppermute | solution.py:276
  19.0 12.6 %collective-permute-start.2 = (bf16[256,640]{1,0:T(8,128)(2,1)}, bf16[256,640]{1,0:T(8,128)(2,1)S(1)}, u32[]{:S(2)}, u32[]{:S(2)}) collective-permute-start(bf16[256,640]{1,0:T(8,128)(2,1)} %collective-permute-done.refs_7_), channel_id=1, source_target_pairs={{0,8},{4,12},{8,16},{12,20},{16,24},{20,28},{24,0},{28,4},{1,9},{5... | collective-permute-start | bytes 983048 | tf_op jit(solution)/shard_map/ppermute | solution.py:282
  20.1 22.1 %collective-permute-start.8 = (bf16[4,128,640]{2,1,0:T(8,128)(2,1)S(1)}, bf16[4,128,640]{2,1,0:T(8,128)(2,1)S(1)}, u32[]{:S(2)}, u32[]{:S(2)}) collective-permute-start(bf16[4,128,640]{2,1,0:T(8,128)(2,1)S(1)} %get-tuple-element.204.refs_2_), channel_id=1, source_target_pairs={{0,2},{1,3},{2,0},{3,1},{4,6},{5,7},{6,4},{7,5},{8,10},{9,11},{10,... | collective-permute-start | bytes 1966088 | tf_op jit(solution)/shard_map/ppermute | solution.py:273
  21.9 30.7 %collective-permute-start.10 = (bf16[4,128,640]{2,1,0:T(8,128)(2,1)S(1)}, bf16[4,128,640]{2,1,0:T(8,128)(2,1)S(1)}, u32[]{:S(2)}, u32[]{:S(2)}) collective-permute-start(bf16[4,128,640]{2,1,0:T(8,128)(2,1)S(1)} %collective-permute-done.6.refs_3_), channel_id=1, source_target_pairs={{0,2},{1,3},{2,0},{3,1},{4,6},{5,7},{6,4},{7,5},{8,10},{9,11},{10,... | collective-permute-start | bytes 1966088 | tf_op jit(solution)/shard_map/ppermute | solution.py:273
  22.5 19.6 %collective-permute-start.9 = (bf16[384,640]{1,0:T(8,128)(2,1)S(1)}, bf16[384,640]{1,0:T(8,128)(2,1)S(1)}, u32[]{:S(2)}, u32[]{:S(2)}) collective-permute-start(bf16[384,640]{1,0:T(8,128)(2,1)S(1)} %slice.7.refs_6_), channel_id=1, source_target_pairs={{0,8},{4,12},{8,16},{12,20},{16,24},{20,28},{24,0},{28,4},{1,9},{5... | collective-permute-start | bytes 1474568 | tf_op jit(solution)/shard_map/ppermute | solution.py:282
  31.6 21.1 %collective-permute-start.11 = (bf16[384,640]{1,0:T(8,128)(2,1)S(1)}, bf16[384,640]{1,0:T(8,128)(2,1)S(1)}, u32[]{:S(2)}, u32[]{:S(2)}) collective-permute-start(bf16[384,640]{1,0:T(8,128)(2,1)S(1)} %collective-permute-done.1.refs_8_), channel_id=1, source_target_pairs={{0,8},{4,12},{8,16},{12,20},{16,24},{20,28},{24,0},{28,4},{1,9},{5... | collective-permute-start | bytes 1474568 | tf_op jit(solution)/shard_map/ppermute | solution.py:282
  31.7 38.5 %collective-permute-start.13 = (bf16[8,128,384]{2,1,0:T(8,128)(2,1)S(1)}, bf16[8,128,384]{2,1,0:T(8,128)(2,1)S(1)}, u32[]{:S(2)}, u32[]{:S(2)}) collective-permute-start(bf16[8,128,384]{2,1,0:T(8,128)(2,1)S(1)} %pad_maximum_fusion), channel_id=1, source_target_pairs={{0,2},{1,3},{2,0},{3,1},{4,6},{5,7},{6,4},{7,5},{8,10},{9,11},{10,... | collective-permute-start | bytes 2359304 | tf_op jit(solution)/shard_map/ppermute | solution.py:273
  42.1 28.1 %collective-permute-start.14 = (bf16[384,640]{1,0:T(8,128)(2,1)S(1)}, bf16[384,640]{1,0:T(8,128)(2,1)}, u32[]{:S(2)}, u32[]{:S(2)}) collective-permute-start(bf16[384,640]{1,0:T(8,128)(2,1)S(1)} %collective-permute-done.9.refs_6_), channel_id=1, source_target_pairs={{0,8},{4,12},{8,16},{12,20},{16,24},{20,28},{24,0},{28,4},{1,9},{5... | collective-permute-start | bytes 1474568 | tf_op jit(solution)/shard_map/ppermute | solution.py:282
  42.1 27.1 %collective-permute-start.7 = (bf16[256,640]{1,0:T(8,128)(2,1)S(1)}, bf16[256,640]{1,0:T(8,128)(2,1)S(1)}, u32[]{:S(2)}, u32[]{:S(2)}) collective-permute-start(bf16[256,640]{1,0:T(8,128)(2,1)S(1)} %collective-permute-done.2.refs_7_), channel_id=1, source_target_pairs={{0,8},{4,12},{8,16},{12,20},{16,24},{20,28},{24,0},{28,4},{1,9},{5... | collective-permute-start | bytes 983048 | tf_op jit(solution)/shard_map/ppermute | solution.py:282
  57.3 17.8 %collective-permute-start.17 = (bf16[2,256,640]{2,1,0:T(8,128)(2,1)S(1)}, bf16[2,256,640]{2,1,0:T(8,128)(2,1)S(1)}, u32[]{:S(2)}, u32[]{:S(2)}) collective-permute-start(bf16[2,256,640]{2,1,0:T(8,128)(2,1)S(1)} %shard_map.105.refs_0_), channel_id=1, source_target_pairs={{0,4},{4,0},{8,12},{12,8},{16,20},{20,16},{24,28},{28,24},{1,5},{5... | collective-permute-start | bytes 1966088 | tf_op jit(solution)/shard_map/ppermute | solution.py:279
  59.0 20.8 %collective-permute-start.16 = (bf16[8,128,256]{2,1,0:T(8,128)(2,1)S(1)}, bf16[8,128,256]{2,1,0:T(8,128)(2,1)S(1)}, u32[]{:S(2)}, u32[]{:S(2)}) collective-permute-start(bf16[8,128,256]{2,1,0:T(8,128)(2,1)S(1)} %pad_maximum_fusion.2), channel_id=1, source_target_pairs={{0,2},{1,3},{2,0},{3,1},{4,6},{5,7},{6,4},{7,5},{8,10},{9,11},{10,... | collective-permute-start | bytes 1572872 | tf_op jit(solution)/shard_map/ppermute | solution.py:273
  69.2 16.0 %collective-permute-start.12 = (bf16[384,640]{1,0:T(8,128)(2,1)S(1)}, bf16[384,640]{1,0:T(8,128)(2,1)S(1)}, u32[]{:S(2)}, u32[]{:S(2)}) collective-permute-start(bf16[384,640]{1,0:T(8,128)(2,1)S(1)} %collective-permute-done.11.refs_8_), channel_id=1, source_target_pairs={{0,8},{4,12},{8,16},{12,20},{16,24},{20,28},{24,0},{28,4},{1,9},{5... | collective-permute-start | bytes 1474568 | tf_op jit(solution)/shard_map/ppermute | solution.py:282
  73.0 10.6 %collective-permute-start.15 = (bf16[2,256,384]{2,1,0:T(8,128)(2,1)S(1)}, bf16[2,256,384]{2,1,0:T(8,128)(2,1)S(1)}, u32[]{:S(2)}, u32[]{:S(2)}) collective-permute-start(bf16[2,256,384]{2,1,0:T(8,128)(2,1)S(1)} %shard_map.106.refs_1_), channel_id=1, source_target_pairs={{0,4},{4,0},{8,12},{12,8},{16,20},{20,16},{24,28},{28,24},{1,5},{5... | collective-permute-start | bytes 1179656 | tf_op jit(solution)/shard_map/ppermute | solution.py:279
  74.6 13.4 %collective-permute-start.20 = (bf16[256,640]{1,0:T(8,128)(2,1)}, bf16[256,640]{1,0:T(8,128)(2,1)}, u32[]{:S(2)}, u32[]{:S(2)}) collective-permute-start(bf16[256,640]{1,0:T(8,128)(2,1)} %slice.6.refs_7_), channel_id=1, source_target_pairs={{0,2},{1,3},{2,0},{3,1},{4,6},{5,7},{6,4},{7,5},{8,10},{9,11},{10,... | collective-permute-start | bytes 983048 | tf_op jit(solution)/shard_map/ppermute | solution.py:273
  75.1 20.8 %collective-permute-start.23 = (bf16[384,640]{1,0:T(8,128)(2,1)}, bf16[384,640]{1,0:T(8,128)(2,1)}, u32[]{:S(2)}, u32[]{:S(2)}) collective-permute-start(bf16[384,640]{1,0:T(8,128)(2,1)} %collective-permute-done.14.refs_6_), channel_id=1, source_target_pairs={{0,8},{4,12},{8,16},{12,20},{16,24},{20,28},{24,0},{28,4},{1,9},{5... | collective-permute-start | bytes 1474568 | tf_op jit(solution)/shard_map/ppermute | solution.py:282
  81.7 7.2 %collective-permute-start.19 = (bf16[2,256,256]{2,1,0:T(8,128)(2,1)S(1)}, bf16[2,256,256]{2,1,0:T(8,128)(2,1)S(1)}, u32[]{:S(2)}, u32[]{:S(2)}) collective-permute-start(bf16[2,256,256]{2,1,0:T(8,128)(2,1)S(1)} %shard_map.107.refs_2_), channel_id=1, source_target_pairs={{0,4},{4,0},{8,12},{12,8},{16,20},{20,16},{24,28},{28,24},{1,5},{5... | collective-permute-start | bytes 786440 | tf_op jit(solution)/shard_map/ppermute | solution.py:279
  86.0 11.0 %collective-permute-start.22 = (bf16[256,640]{1,0:T(8,128)(2,1)}, bf16[256,640]{1,0:T(8,128)(2,1)}, u32[]{:S(2)}, u32[]{:S(2)}) collective-permute-start(bf16[256,640]{1,0:T(8,128)(2,1)} %collective-permute-done.refs_7_), channel_id=1, source_target_pairs={{0,2},{1,3},{2,0},{3,1},{4,6},{5,7},{6,4},{7,5},{8,10},{9,11},{10,... | collective-permute-start | bytes 983048 | tf_op jit(solution)/shard_map/ppermute | solution.py:273
  86.5 20.6 %collective-permute-start.18 = (bf16[512,640]{1,0:T(8,128)(2,1)}, bf16[512,640]{1,0:T(8,128)(2,1)S(1)}, u32[]{:S(2)}, u32[]{:S(2)}) collective-permute-start(bf16[512,640]{1,0:T(8,128)(2,1)} %pad_maximum_fusion.1), channel_id=1, source_target_pairs={{0,2},{1,3},{2,0},{3,1},{4,6},{5,7},{6,4},{7,5},{8,10},{9,11},{10,... | collective-permute-start | bytes 1966088 | tf_op jit(solution)/shard_map/ppermute | solution.py:273
  97.1 10.0 %collective-permute-start.25 = (bf16[256,640]{1,0:T(8,128)(2,1)S(1)}, bf16[256,640]{1,0:T(8,128)(2,1)S(1)}, u32[]{:S(2)}, u32[]{:S(2)}) collective-permute-start(bf16[256,640]{1,0:T(8,128)(2,1)S(1)} %shard_map.109), channel_id=1, source_target_pairs={{0,4},{4,0},{8,12},{12,8},{16,20},{20,16},{24,28},{28,24},{1,5},{5... | collective-permute-start | bytes 983048 | tf_op jit(solution)/shard_map/ppermute | solution.py:279
  98.7 17.1 %collective-permute-start.31 = (bf16[384,640]{1,0:T(8,128)(2,1)S(1)}, bf16[384,640]{1,0:T(8,128)(2,1)S(1)}, u32[]{:S(2)}, u32[]{:S(2)}) collective-permute-start(bf16[384,640]{1,0:T(8,128)(2,1)S(1)} %copy-done.25), channel_id=1, source_target_pairs={{0,8},{4,12},{8,16},{12,20},{16,24},{20,28},{24,0},{28,4},{1,9},{5... | collective-permute-start | bytes 1474568 | tf_op jit(solution)/shard_map/ppermute | solution.py:282
  104.9 17.2 %collective-permute-start.33 = (bf16[256,640]{1,0:T(8,128)(2,1)S(1)}, bf16[256,640]{1,0:T(8,128)(2,1)S(1)}, u32[]{:S(2)}, u32[]{:S(2)}) collective-permute-start(bf16[256,640]{1,0:T(8,128)(2,1)S(1)} %shard_map.111), channel_id=1, source_target_pairs={{0,4},{4,0},{8,12},{12,8},{16,20},{20,16},{24,28},{28,24},{1,5},{5... | collective-permute-start | bytes 983048 | tf_op jit(solution)/shard_map/ppermute | solution.py:279
  114.1 11.8 %collective-permute-start.30 = (bf16[256,640]{1,0:T(8,128)(2,1)}, bf16[256,640]{1,0:T(8,128)(2,1)}, u32[]{:S(2)}, u32[]{:S(2)}) collective-permute-start(bf16[256,640]{1,0:T(8,128)(2,1)} %shard_map.113), channel_id=1, source_target_pairs={{0,4},{4,0},{8,12},{12,8},{16,20},{20,16},{24,28},{28,24},{1,5},{5... | collective-permute-start | bytes 983048 | tf_op jit(solution)/shard_map/ppermute | solution.py:279
  115.8 10.5 %collective-permute-start.37 = (bf16[256,640]{1,0:T(8,128)(2,1)}, bf16[256,640]{1,0:T(8,128)(2,1)}, u32[]{:S(2)}, u32[]{:S(2)}) collective-permute-start(bf16[256,640]{1,0:T(8,128)(2,1)} %get-tuple-element.319), channel_id=1, source_target_pairs={{0,1},{1,0},{2,3},{3,2},{4,5},{5,4},{6,7},{7,6},{8,9},{9,8},{10,11... | collective-permute-start | bytes 983048 | tf_op jit(solution)/shard_map/ppermute | solution.py:276
  122.1 7.7 %collective-permute-start.36 = (bf16[256,640]{1,0:T(8,128)(2,1)}, bf16[256,640]{1,0:T(8,128)(2,1)S(1)}, u32[]{:S(2)}, u32[]{:S(2)}) collective-permute-start(bf16[256,640]{1,0:T(8,128)(2,1)} %get-tuple-element.317), channel_id=1, source_target_pairs={{0,1},{1,0},{2,3},{3,2},{4,5},{5,4},{6,7},{7,6},{8,9},{9,8},{10,11... | collective-permute-start | bytes 983048 | tf_op jit(solution)/shard_map/ppermute | solution.py:276
  123.4 8.0 %collective-permute-start.35 = (bf16[256,640]{1,0:T(8,128)(2,1)}, bf16[256,640]{1,0:T(8,128)(2,1)S(1)}, u32[]{:S(2)}, u32[]{:S(2)}) collective-permute-start(bf16[256,640]{1,0:T(8,128)(2,1)} %get-tuple-element.315), channel_id=1, source_target_pairs={{0,1},{1,0},{2,3},{3,2},{4,5},{5,4},{6,7},{7,6},{8,9},{9,8},{10,11... | collective-permute-start | bytes 983048 | tf_op jit(solution)/shard_map/ppermute | solution.py:276
  124.4 9.6 %collective-permute-start.38 = (bf16[256,640]{1,0:T(8,128)(2,1)}, bf16[256,640]{1,0:T(8,128)(2,1)S(1)}, u32[]{:S(2)}, u32[]{:S(2)}) collective-permute-start(bf16[256,640]{1,0:T(8,128)(2,1)} %copy-done.34), channel_id=1, source_target_pairs={{0,1},{1,0},{2,3},{3,2},{4,5},{5,4},{6,7},{7,6},{8,9},{9,8},{10,11... | collective-permute-start | bytes 983048 | tf_op jit(solution)/shard_map/ppermute | solution.py:276
  125.9 9.8 %collective-permute-start.39 = (bf16[256,640]{1,0:T(8,128)(2,1)S(1)}, bf16[256,640]{1,0:T(8,128)(2,1)S(1)}, u32[]{:S(2)}, u32[]{:S(2)}) collective-permute-start(bf16[256,640]{1,0:T(8,128)(2,1)S(1)} %shard_map.115), channel_id=1, source_target_pairs={{0,4},{4,0},{8,12},{12,8},{16,20},{20,16},{24,28},{28,24},{1,5},{5... | collective-permute-start | bytes 983048 | tf_op jit(solution)/shard_map/ppermute | solution.py:279
  (45 other events, 237.8 us)

commit v8 on v7

--- a/solution.py
+++ b/solution.py
@@ -140,28 +140,44 @@
 
 def project_kernel(n_chunks, spans, flip_ref, *refs):
     sides = refs[:n_chunks], refs[n_chunks : 2 * n_chunks]
-    weight_refs, out_refs, weight_ref = refs[2 * n_chunks : -6], refs[-6:-1], refs[-1]
-    rows = out_refs[0].shape[0] // 2
+    weight_refs = refs[2 * n_chunks : -10]
+    keep_mine_ref, keep_other_ref, send_mine_ref, first_ref, second_ref = refs[-10:-5]
+    weight_ref, keep_ref, send_ref, in_sems, out_sems = refs[-5:]
+    rows = first_ref.shape[0]
     depth = weight_ref.shape[0] // 2
+    loads = []
     at = 0
     for ref, (low, high) in zip(weight_refs, spans):
         block, inside = at // depth, at % depth
         first = pl.multiple_of((block ^ flip_ref[0]) * depth + inside, 16)
-        weight_ref[pl.ds(first, high - low)] = ref[low:high]
+        to = weight_ref.at[pl.ds(first, high - low)]
+        loads.append(pltpu.make_async_copy(ref.at[pl.ds(low, high - low)], to, in_sems.at[len(loads)]))
+        loads[-1].start()
         at += high - low
-    weight = weight_ref[...]
-    for side, parts in enumerate(sides):
-        acts = jnp.concatenate([ref[...].reshape(4 * rows, ref.shape[-1]) for ref in parts], axis=1)
-        total = jnp.dot(acts, weight, preferred_element_type=WIDE)
-        for kind in range(2):
-            first = 2 * kind * rows
-            here = slice(kind * rows, (kind + 1) * rows)
-            out_refs[side][here] = total[first : first + rows]
-            low = total[first + rows : first + 2 * rows].astype(LOW)
-            if side:
-                out_refs[3 + kind][...] = low
-            else:
-                out_refs[2][here] = low
+
+    def gather(parts):
+        return jnp.concatenate([ref[...].reshape(4 * rows, ref.shape[-1]) for ref in parts], axis=1)
+
+    acts = gather(sides[0])
+    for load in loads:
+        load.wait()
+    total = jnp.dot(acts, weight_ref[...], preferred_element_type=WIDE)
+    for kind in range(2):
+        here = slice(kind * rows, (kind + 1) * rows)
+        keep_ref[here] = total[2 * kind * rows : (2 * kind + 1) * rows]
+        send_ref[here] = total[(2 * kind + 1) * rows : (2 * kind + 2) * rows].astype(LOW)
+    stores = [
+        pltpu.make_async_copy(keep_ref, keep_mine_ref, out_sems.at[0]),
+        pltpu.make_async_copy(send_ref, send_mine_ref, out_sems.at[1]),
+    ]
+    for store in stores:
+        store.start()
+    total = jnp.dot(gather(sides[1]), weight_ref[...], preferred_element_type=WIDE)
+    for kind, out_ref in enumerate((first_ref, second_ref)):
+        keep_other_ref[kind * rows : (kind + 1) * rows] = total[2 * kind * rows : (2 * kind + 1) * rows]
+        out_ref[...] = total[(2 * kind + 1) * rows : (2 * kind + 2) * rows].astype(LOW)
+    for store in stores:
+        store.wait()
 
 
 def project(flip, acts, pieces):
@@ -170,14 +186,27 @@
     spans = [(low, high) for _, low, high in pieces]
     rows, n = mine[0].shape[1], weights[0].shape[1]
     depth = sum(high - low for low, high in spans)
+    wide, low, part = (rows, n), (rows, n), (rows // 2, n)
+    hbm = pl.BlockSpec(memory_space=pltpu.HBM)
+    vmem = pl.BlockSpec(memory_space=pltpu.VMEM)
     return pl.pallas_call(
         functools.partial(project_kernel, len(acts), spans),
-        in_specs=[pl.BlockSpec(memory_space=pltpu.SMEM)] + vmem_specs(2 * len(acts) + len(weights)),
-        out_specs=vmem_specs(5),
-        out_shape=[jax.ShapeDtypeStruct((rows, n), WIDE)] * 2
-        + [jax.ShapeDtypeStruct((rows, n), LOW)]
-        + [jax.ShapeDtypeStruct((rows // 2, n), LOW)] * 2,
-        scratch_shapes=[pltpu.VMEM((depth, n), LOW)],
+        in_specs=[pl.BlockSpec(memory_space=pltpu.SMEM)] + [vmem] * (2 * len(acts)) + [hbm] * len(weights),
+        out_specs=[hbm, vmem, hbm, vmem, vmem],
+        out_shape=[
+            jax.ShapeDtypeStruct(wide, WIDE),
+            jax.ShapeDtypeStruct(wide, WIDE),
+            jax.ShapeDtypeStruct(low, LOW),
+            jax.ShapeDtypeStruct(part, LOW),
+            jax.ShapeDtypeStruct(part, LOW),
+        ],
+        scratch_shapes=[
+            pltpu.VMEM((depth, n), LOW),
+            pltpu.VMEM(wide, WIDE),
+            pltpu.VMEM(low, LOW),
+            pltpu.SemaphoreType.DMA((len(weights),)),
+            pltpu.SemaphoreType.DMA((2,)),
+        ],
         compiler_params=params(),
         cost_estimate=LIGHT,
     )(flip, *mine, *theirs, *weights)
@@ -376,11 +405,10 @@
     for step in range(2, n_ring, 2):
         other[step - 2] = wait(other[step - 2])
         rest[1 + step // 2] = wait(rest[1 + step // 2])
-        if step > 2:
-            turn(beside, step)
+        for ahead in range(max(step, 3), step + 2):
+            turn(beside, ahead)
         columns(step)
         finish(step)
-        turn(beside, step + 1)
         columns(step + 1)
         other[step - 1] = wait(other[step - 1])
         finish(step + 1)

time: 138 us -> 145 us (1.051)
  Pallas kernels: 34.7 us -> 38.8 us
  waiting for transfers between devices: 57.9 us -> 60.5 us
    pallas_call x4, Pallas kernels: 14.4 us -> 18.5 us  [project(): pl.pallas_call(functools.partial(project_kernel, len(acts), spans), in_sp...]
    ppermute x9, waiting for transfers between devices: 41.6 us -> 45.6 us  [onward(): return lax.ppermute(array, 'dp', [(i, (i + 2) % n_dp) for i in range(n_dp)])]
  transfers between devices with their start and end apart: 40 -> 40, of which waited for: 21 -> 22; matrix products, arithmetic and copies ran while one was open for 2% -> 2% of each run, Pallas kernels for 24% -> 26%
where the time goes in v8:
time: 145 us; the launch traced here: 144 us
  waiting for transfers between devices  60.5 us (42%)
  Pallas kernels  38.8 us (27%)
  starting transfers between devices  24.4 us (17%)
  local copies, waits for them, and re-layouts  17.9 us (12%)
    ppermute x9, waiting for transfers between devices, onward(): return lax.ppermute(array, 'dp', [(i, (i + 2) % n_dp) for i in range(n_dp)])  45.6 us
    pallas_call x4, Pallas kernels, project(): pl.pallas_call(functools.partial(project_kernel, len(acts), spans), in_sp...  18.5 us
    unnamed x74, local copies, waits for them, and re-layouts  15 us
    pallas_call x3, Pallas kernels, attend(): pl.pallas_call(functools.partial(attend_kernel, len(queries)), grid=(widt...  9.36 us
    ppermute x7, starting transfers between devices, across(): return lax.ppermute(array, 'dp', [(i, i ^ 1) for i in range(n_dp)])  8.99 us
    ppermute x8, starting transfers between devices, far(): return lax.ppermute(array, 'seq', [(i, i ^ 2) for i in range(n_seq)])  8.55 us
    pallas_call x4, Pallas kernels, place(): pl.pallas_call(place_kernel, grid_spec=pltpu.PrefetchScalarGridSpec(num_s...  7.89 us
    ppermute x16, waiting for transfers between devices, near(): return lax.ppermute(array, 'seq', [(i, i ^ 1) for i in range(n_seq)])  6.46 us
  transfers between devices with their start and end apart: 40, of which 22 were waited for; matrix products, arithmetic and copies ran while one was open for 2% of the time, Pallas kernels for 26%

profile of v8, /device:TPU:0, one launch (start us, length us, event | category | flops | bytes accessed | tf_op | source)
XLA Modules:
  0.0 144.0 jit_solution(1868694771153194546)
XLA Ops:
  1.9 3.0 %collective-permute-start = (bf16[384,640]{1,0:T(8,128)(2,1)S(1)}, bf16[384,640]{1,0:T(8,128)(2,1)S(1)}, u32[]{:S(2)}, u32[]{:S(2)}) collective-permute-start(bf16[384,640]{1,0:T(8,128)(2,1)S(1)} %slice.6.refs_6_), channel_id=1, source_target_pairs={{0,2},{1,3},{2,0},{3,1},{4,6},{5,7},{6,4},{7,5},{8,10},{9,11},{10,... | collective-permute-start | bytes 1474568 | tf_op jit(solution)/shard_map/ppermute | solution.py:302
  4.9 1.7 %slice.7.refs_7_ = bf16[256,640]{1,0:T(8,128)(2,1)} slice(bf16[640,640]{1,0:T(8,128)(2,1)} %param.17), slice={[384:640], [0:640]} | slice | bytes 655360 | tf_op jit(solution)/shard_map/slice | solution.py:328
  6.6 1.6 %collective-permute-start.2 = (bf16[256,640]{1,0:T(8,128)(2,1)}, bf16[256,640]{1,0:T(8,128)(2,1)}, u32[]{:S(2)}, u32[]{:S(2)}) collective-permute-start(bf16[256,640]{1,0:T(8,128)(2,1)} %slice.7.refs_7_), channel_id=1, source_target_pairs={{0,8},{4,12},{8,16},{12,20},{16,24},{20,28},{24,0},{28,4},{1,9},{5... | collective-permute-start | bytes 983048 | tf_op jit(solution)/shard_map/ppermute | solution.py:311
  12.6 2.1 %shard_map.104 = (bf16[2,128,1280]{2,1,0:T(8,128)(2,1)S(1)}, bf16[4,128,640]{2,1,0:T(8,128)(2,1)S(1)}, bf16[4,128,384]{2,1,0:T(8,128)(2,1)S(1)}, bf16[4,128,256]...) custom-call(s32[1]{0:T(128)} %bitcast.3.core_ref, ...), custom_call_target="tpu_custom_call" | custom-call | flops 1 | bytes 1 | tf_op jit(solution)/shard_map/pallas_call | solution.py:78
  14.7 1.4 collective-permute-done.refs_8_
  16.1 1.9 %collective-permute-done.2.refs_7_ = bf16[256,640]{1,0:T(8,128)(2,1)} collective-permute-done((bf16[256,640]{1,0:T(8,128)(2,1)}, bf16[256,640]{1,0:T(8,128)(2,1)}, u32[]{:S(2)}, u32[]{:S(2)}) %collective-permute-start.2) | collective-permute-done | bytes 327712 | tf_op jit(solution)/shard_map/ppermute | solution.py:311
  20.6 1.3 collective-permute-done.7.refs_3_
  23.4 8.2 %collective-permute-done.5.refs_7_ = bf16[256,640]{1,0:T(8,128)(2,1)S(1)} collective-permute-done((bf16[256,640]{1,0:T(8,128)(2,1)}, bf16[256,640]{1,0:T(8,128)(2,1)S(1)}, u32[]{:S(2)}, u32[]{:S(2)}) %collective-permute-start.5) | collective-permute-done | bytes 327712 | tf_op jit(solution)/shard_map/ppermute | solution.py:311
  32.3 9.8 %collective-permute-done.4.refs_6_ = bf16[384,640]{1,0:T(8,128)(2,1)S(1)} collective-permute-done((bf16[384,640]{1,0:T(8,128)(2,1)S(1)}, bf16[384,640]{1,0:T(8,128)(2,1)S(1)}, u32[]{:S(2)}, u32[]{:S(2)}) %collective-permute-start.4) | collective-permute-done | bytes 491552 | tf_op jit(solution)/shard_map/ppermute | solution.py:311
  42.2 10.5 %collective-permute-done.1.refs_8_ = bf16[384,640]{1,0:T(8,128)(2,1)S(1)} collective-permute-done((bf16[384,640]{1,0:T(8,128)(2,1)S(1)}, bf16[384,640]{1,0:T(8,128)(2,1)S(1)}, u32[]{:S(2)}, u32[]{:S(2)}) %collective-permute-start.1) | collective-permute-done | bytes 491552 | tf_op jit(solution)/shard_map/ppermute | solution.py:311
  52.6 4.7 %shard_map.105.refs_0_ = bf16[2,256,640]{2,1,0:T(8,128)(2,1)S(1)} custom-call(bf16[2,128,1280]{2,1,0:T(8,128)(2,1)S(1)} %get-tuple-element.207.refs_0_, bf16[2,128,1280]{2,1,0:T(8,128)(2,1)S(1)} %collective-permute-done.6.refs_1_, bf16[4,128,640]{2,1,0:T(8,128)(2,1)S(1)} %get-tuple-element.180.refs_2_, ...), custom_call_target="tpu_custom_call" | custom-call | flops 1 | bytes 1 | tf_op jit(solution)/shard_map/pallas_call | solution.py:129
  57.3 1.6 %collective-permute-start.17 = (bf16[2,256,640]{2,1,0:T(8,128)(2,1)S(1)}, bf16[2,256,640]{2,1,0:T(8,128)(2,1)S(1)}, u32[]{:S(2)}, u32[]{:S(2)}) collective-permute-start(bf16[2,256,640]{2,1,0:T(8,128)(2,1)S(1)} %shard_map.105.refs_0_), channel_id=1, source_target_pairs={{0,4},{4,0},{8,12},{12,8},{16,20},{20,16},{24,28},{28,24},{1,5},{5... | collective-permute-start | bytes 1966088 | tf_op jit(solution)/shard_map/ppermute | solution.py:308
  59.6 9.7 %collective-permute-done.13.refs_7_ = bf16[256,640]{1,0:T(8,128)(2,1)S(1)} collective-permute-done((bf16[256,640]{1,0:T(8,128)(2,1)S(1)}, bf16[256,640]{1,0:T(8,128)(2,1)S(1)}, u32[]{:S(2)}, u32[]{:S(2)}) %collective-permute-start.13) | collective-permute-done | bytes 327712 | tf_op jit(solution)/shard_map/ppermute | solution.py:311
  70.2 2.8 %shard_map.106.refs_1_ = bf16[2,256,384]{2,1,0:T(8,128)(2,1)S(1)} custom-call(bf16[2,128,1280]{2,1,0:T(8,128)(2,1)S(1)} %get-tuple-element.207.refs_0_, bf16[2,128,1280]{2,1,0:T(8,128)(2,1)S(1)} %collective-permute-done.6.refs_1_, bf16[4,128,384]{2,1,0:T(8,128)(2,1)S(1)} %get-tuple-element.209.refs_2_, ...), custom_call_target="tpu_custom_call" | custom-call | flops 1 | bytes 1 | tf_op jit(solution)/shard_map/pallas_call | solution.py:129
  73.0 1.6 %collective-permute-start.15 = (bf16[2,256,384]{2,1,0:T(8,128)(2,1)S(1)}, bf16[2,256,384]{2,1,0:T(8,128)(2,1)S(1)}, u32[]{:S(2)}, u32[]{:S(2)}) collective-permute-start(bf16[2,256,384]{2,1,0:T(8,128)(2,1)S(1)} %shard_map.106.refs_1_), channel_id=1, source_target_pairs={{0,4},{4,0},{8,12},{12,8},{16,20},{20,16},{24,28},{28,24},{1,5},{5... | collective-permute-start | bytes 1179656 | tf_op jit(solution)/shard_map/ppermute | solution.py:308
  75.9 3.9 %collective-permute-done.16.refs_4_ = bf16[8,128,256]{2,1,0:T(8,128)(2,1)S(1)} collective-permute-done((bf16[8,128,256]{2,1,0:T(8,128)(2,1)S(1)}, bf16[8,128,256]{2,1,0:T(8,128)(2,1)S(1)}, u32[]{:S(2)}, u32[]{:S(2)}) %collective-permute-start.16) | collective-permute-done | bytes 524320 | tf_op jit(solution)/shard_map/ppermute | solution.py:302
  79.8 1.9 %shard_map.107.refs_2_ = bf16[2,256,256]{2,1,0:T(8,128)(2,1)S(1)} custom-call(bf16[2,128,1280]{2,1,0:T(8,128)(2,1)S(1)} %get-tuple-element.207.refs_0_, bf16[2,128,1280]{2,1,0:T(8,128)(2,1)S(1)} %collective-permute-done.6.refs_1_, bf16[4,128,256]{2,1,0:T(8,128)(2,1)S(1)} %get-tuple-element.226.refs_2_, ...), custom_call_target="tpu_custom_call" | custom-call | flops 1 | bytes 1 | tf_op jit(solution)/shard_map/pallas_call | solution.py:129
  81.7 1.6 %collective-permute-start.20 = (bf16[2,256,256]{2,1,0:T(8,128)(2,1)S(1)}, bf16[2,256,256]{2,1,0:T(8,128)(2,1)S(1)}, u32[]{:S(2)}, u32[]{:S(2)}) collective-permute-start(bf16[2,256,256]{2,1,0:T(8,128)(2,1)S(1)} %shard_map.107.refs_2_), channel_id=1, source_target_pairs={{0,4},{4,0},{8,12},{12,8},{16,20},{20,16},{24,28},{28,24},{1,5},{5... | collective-permute-start | bytes 786440 | tf_op jit(solution)/shard_map/ppermute | solution.py:308
  83.6 1.6 %collective-permute-done.10.refs_8_ = bf16[384,640]{1,0:T(8,128)(2,1)S(1)} collective-permute-done((bf16[384,640]{1,0:T(8,128)(2,1)S(1)}, bf16[384,640]{1,0:T(8,128)(2,1)S(1)}, u32[]{:S(2)}, u32[]{:S(2)}) %collective-permute-start.10) | collective-permute-done | bytes 491552 | tf_op jit(solution)/shard_map/ppermute | solution.py:311
  86.5 1.5 %collective-permute-start.19 = (bf16[512,640]{1,0:T(8,128)(2,1)}, bf16[512,640]{1,0:T(8,128)(2,1)S(1)}, u32[]{:S(2)}, u32[]{:S(2)}) collective-permute-start(bf16[512,640]{1,0:T(8,128)(2,1)} %pad_maximum_fusion.1), channel_id=1, source_target_pairs={{0,2},{1,3},{2,0},{3,1},{4,6},{5,7},{6,4},{7,5},{8,10},{9,11},{10,... | collective-permute-start | bytes 1966088 | tf_op jit(solution)/shard_map/ppermute | solution.py:302
  90.9 4.9 %shard_map.108 = (f32[256,640]{1,0:T(8,128)S(1)}, f32[256,640]{1,0:T(8,128)S(1)}, bf16[256,640]{1,0:T(8,128)(2,1)}, bf16[128,640]{1,0:T(8,128)(2,1)S(1)}, bf16[128,640]{1,0:T(8,128)(2,1)S(1)}) custom-call(s32[1]{0:T(128)} %bitcast.2.flip_ref, bf16[2,256,640]{2,1,0:T(8,128)(2,1)S(1)} %shard_map.105.refs_0_, bf16[2,256,384]{2,1,0:T(8,128)(2,1)S(1)} %shard_map.106.refs_1_, ...), custom_call_target="tpu_custom_call" | custom-call | flops 1 | bytes 1 | tf_op jit(solution)/shard_map/pallas_call | solution.py:192
  98.4 1.6 %collective-permute-start.26 = (bf16[256,640]{1,0:T(8,128)(2,1)S(1)}, bf16[256,640]{1,0:T(8,128)(2,1)S(1)}, u32[]{:S(2)}, u32[]{:S(2)}) collective-permute-start(bf16[256,640]{1,0:T(8,128)(2,1)S(1)} %shard_map.109), channel_id=1, source_target_pairs={{0,4},{4,0},{8,12},{12,8},{16,20},{20,16},{24,28},{28,24},{1,5},{5... | collective-permute-start | bytes 983048 | tf_op jit(solution)/shard_map/ppermute | solution.py:308
  100.0 4.9 %shard_map.110 = (f32[256,640]{1,0:T(8,128)S(1)}, f32[256,640]{1,0:T(8,128)S(1)}, bf16[256,640]{1,0:T(8,128)(2,1)}, bf16[128,640]{1,0:T(8,128)(2,1)S(1)}, bf16[128,640]{1,0:T(8,128)(2,1)S(1)}) custom-call(s32[1]{0:T(128)} %bitcast.2.flip_ref, bf16[2,256,640]{2,1,0:T(8,128)(2,1)S(1)} %shard_map.105.refs_0_, bf16[2,256,384]{2,1,0:T(8,128)(2,1)S(1)} %shard_map.106.refs_1_, ...), custom_call_target="tpu_custom_call" | custom-call | flops 1 | bytes 1 | tf_op jit(solution)/shard_map/pallas_call | solution.py:192
  108.3 4.0 %collective-permute-done.18.refs_8_ = bf16[384,640]{1,0:T(8,128)(2,1)S(1)} collective-permute-done((bf16[384,640]{1,0:T(8,128)(2,1)S(1)}, bf16[384,640]{1,0:T(8,128)(2,1)S(1)}, u32[]{:S(2)}, u32[]{:S(2)}) %collective-permute-start.18) | collective-permute-done | bytes 491552 | tf_op jit(solution)/shard_map/ppermute | solution.py:311
  112.4 4.3 %shard_map.112 = (f32[256,640]{1,0:T(8,128)S(1)}, f32[256,640]{1,0:T(8,128)S(1)}, bf16[256,640]{1,0:T(8,128)(2,1)}, bf16[128,640]{1,0:T(8,128)(2,1)S(1)}, bf16[128,640]{1,0:T(8,128)(2,1)S(1)}) custom-call(s32[1]{0:T(128)} %bitcast.2.flip_ref, bf16[2,256,640]{2,1,0:T(8,128)(2,1)S(1)} %shard_map.105.refs_0_, bf16[2,256,384]{2,1,0:T(8,128)(2,1)S(1)} %shard_map.106.refs_1_, ...), custom_call_target="tpu_custom_call" | custom-call | flops 1 | bytes 1 | tf_op jit(solution)/shard_map/pallas_call | solution.py:192
  120.0 1.5 %collective-permute-start.31 = (bf16[256,640]{1,0:T(8,128)(2,1)}, bf16[256,640]{1,0:T(8,128)(2,1)}, u32[]{:S(2)}, u32[]{:S(2)}) collective-permute-start(bf16[256,640]{1,0:T(8,128)(2,1)} %shard_map.113), channel_id=1, source_target_pairs={{0,4},{4,0},{8,12},{12,8},{16,20},{20,16},{24,28},{28,24},{1,5},{5... | collective-permute-start | bytes 983048 | tf_op jit(solution)/shard_map/ppermute | solution.py:308
  121.5 4.4 %shard_map.114 = (f32[256,640]{1,0:T(8,128)S(1)}, f32[256,640]{1,0:T(8,128)S(1)}, bf16[256,640]{1,0:T(8,128)(2,1)S(1)}, bf16[128,640]{1,0:T(8,128)(2,1)S(1)}, bf16[128,640]{1,0:T(8,128)(2,1)S(1)}) custom-call(s32[1]{0:T(128)} %bitcast.2.flip_ref, bf16[2,256,640]{2,1,0:T(8,128)(2,1)S(1)} %shard_map.105.refs_0_, bf16[2,256,384]{2,1,0:T(8,128)(2,1)S(1)} %shard_map.106.refs_1_, ...), custom_call_target="tpu_custom_call" | custom-call | flops 1 | bytes 1 | tf_op jit(solution)/shard_map/pallas_call | solution.py:192
  134.3 2.5 %shard_map.116 = (bf16[128,5120]{1,0:T(8,128)(2,1)}, bf16[128,5120]{1,0:T(8,128)(2,1)}) custom-call(s32[2]{0:T(128)S(1)} %add_add_fusion.3.where_ref, f32[256,640]{1,0:T(8,128)S(1)} %copy-done.13, bf16[256,640]{1,0:T(8,128)(2,1)} %collective-permute-done.37.got_ref, bf16[256,640]{1,0:T(8,128)(2,1)S(1)} %copy-done.33), custom_call_target="tpu_custom_call" | custom-call | flops 1 | bytes 1 | tf_op jit(solution)/shard_map/pallas_call | solution.py:261
  136.8 1.5 %shard_map.117 = (bf16[128,5120]{1,0:T(8,128)(2,1)}, bf16[128,5120]{1,0:T(8,128)(2,1)}) custom-call(s32[2]{0:T(128)S(1)} %add_add_fusion.2.where_ref, f32[256,640]{1,0:T(8,128)S(1)} %copy-done.17, bf16[256,640]{1,0:T(8,128)(2,1)S(1)} %collective-permute-done.36.got_ref, ...), custom_call_target="tpu_custom_call", output_to_operand_aliasing={{0}: (4, {}), {1}: (5, {})} | custom-call | flops 1 | bytes 1 | tf_op jit(solution)/shard_map/pallas_call | solution.py:261
  138.4 2.5 %shard_map.118 = (bf16[128,5120]{1,0:T(8,128)(2,1)}, bf16[128,5120]{1,0:T(8,128)(2,1)}) custom-call(s32[2]{0:T(128)S(1)} %add_add_fusion.1.where_ref, f32[256,640]{1,0:T(8,128)S(1)} %copy-done.19, bf16[256,640]{1,0:T(8,128)(2,1)S(1)} %collective-permute-done.35.got_ref, ...), custom_call_target="tpu_custom_call", output_to_operand_aliasing={{0}: (4, {}), {1}: (5, {})} | custom-call | flops 1 | bytes 1 | tf_op jit(solution)/shard_map/pallas_call | solution.py:261
  141.0 1.5 %collective-permute-done.39.other_ref = bf16[256,640]{1,0:T(8,128)(2,1)S(1)} collective-permute-done((bf16[256,640]{1,0:T(8,128)(2,1)S(1)}, bf16[256,640]{1,0:T(8,128)(2,1)S(1)}, u32[]{:S(2)}, u32[]{:S(2)}) %collective-permute-start.39) | collective-permute-done | bytes 327712 | tf_op jit(solution)/shard_map/ppermute | solution.py:308
  142.5 1.5 %shard_map.119 = (bf16[128,5120]{1,0:T(8,128)(2,1)}, bf16[128,5120]{1,0:T(8,128)(2,1)}) custom-call(s32[2]{0:T(128)S(1)} %add_add_fusion.where_ref, f32[256,640]{1,0:T(8,128)S(1)} %copy-done.21, bf16[256,640]{1,0:T(8,128)(2,1)S(1)} %collective-permute-done.38.got_ref, ...), custom_call_target="tpu_custom_call", output_to_operand_aliasing={{0}: (4, {}), {1}: (5, {})} | custom-call | flops 1 | bytes 1 | tf_op jit(solution)/shard_map/pallas_call | solution.py:261
  (150 shorter events, 35.8 us)
Async XLA Ops:
  1.9 14.2 %collective-permute-start = (bf16[384,640]{1,0:T(8,128)(2,1)S(1)}, bf16[384,640]{1,0:T(8,128)(2,1)S(1)}, u32[]{:S(2)}, u32[]{:S(2)}) collective-permute-start(bf16[384,640]{1,0:T(8,128)(2,1)S(1)} %slice.6.refs_6_), channel_id=1, source_target_pairs={{0,2},{1,3},{2,0},{3,1},{4,6},{5,7},{6,4},{7,5},{8,10},{9,11},{10,... | collective-permute-start | bytes 1474568 | tf_op jit(solution)/shard_map/ppermute | solution.py:302
  6.6 11.3 %collective-permute-start.2 = (bf16[256,640]{1,0:T(8,128)(2,1)}, bf16[256,640]{1,0:T(8,128)(2,1)}, u32[]{:S(2)}, u32[]{:S(2)}) collective-permute-start(bf16[256,640]{1,0:T(8,128)(2,1)} %slice.7.refs_7_), channel_id=1, source_target_pairs={{0,8},{4,12},{8,16},{12,20},{16,24},{20,28},{24,0},{28,4},{1,9},{5... | collective-permute-start | bytes 983048 | tf_op jit(solution)/shard_map/ppermute | solution.py:311
  18.0 2.1 %collective-permute-start.9 = (bf16[4,128,640]{2,1,0:T(8,128)(2,1)S(1)}, bf16[4,128,640]{2,1,0:T(8,128)(2,1)S(1)}, u32[]{:S(2)}, u32[]{:S(2)}) collective-permute-start(bf16[4,128,640]{2,1,0:T(8,128)(2,1)S(1)} %get-tuple-element.197), channel_id=1, source_target_pairs={{0,1},{1,0},{2,3},{3,2},{4,5},{5,4},{6,7},{7,6},{8,9},{9,8},{10,11... | collective-permute-start | bytes 1966088 | tf_op jit(solution)/shard_map/ppermute | solution.py:305
  18.0 13.7 %collective-permute-start.6 = (bf16[2,128,1280]{2,1,0:T(8,128)(2,1)S(1)}, bf16[2,128,1280]{2,1,0:T(8,128)(2,1)S(1)}, u32[]{:S(2)}, u32[]{:S(2)}) collective-permute-start(bf16[2,128,1280]{2,1,0:T(8,128)(2,1)S(1)} %get-tuple-element.188), channel_id=1, source_target_pairs={{0,1},{1,0},{2,3},{3,2},{4,5},{5,4},{6,7},{7,6},{8,9},{9,8},{10,11... | collective-permute-start | bytes 1966088 | tf_op jit(solution)/shard_map/ppermute | solution.py:305
  18.5 4.0 %collective-permute-start.8 = (bf16[4,128,384]{2,1,0:T(8,128)(2,1)S(1)}, bf16[4,128,384]{2,1,0:T(8,128)(2,1)S(1)}, u32[]{:S(2)}, u32[]{:S(2)}) collective-permute-start(bf16[4,128,384]{2,1,0:T(8,128)(2,1)S(1)} %get-tuple-element.196), channel_id=1, source_target_pairs={{0,1},{1,0},{2,3},{3,2},{4,5},{5,4},{6,7},{7,6},{8,9},{9,8},{10,11... | collective-permute-start | bytes 1179656 | tf_op jit(solution)/shard_map/ppermute | solution.py:305
  18.5 3.5 %collective-permute-start.7 = (bf16[4,128,256]{2,1,0:T(8,128)(2,1)S(1)}, bf16[4,128,256]{2,1,0:T(8,128)(2,1)S(1)}, u32[]{:S(2)}, u32[]{:S(2)}) collective-permute-start(bf16[4,128,256]{2,1,0:T(8,128)(2,1)S(1)} %get-tuple-element.195), channel_id=1, source_target_pairs={{0,1},{1,0},{2,3},{3,2},{4,5},{5,4},{6,7},{7,6},{8,9},{9,8},{10,11... | collective-permute-start | bytes 786440 | tf_op jit(solution)/shard_map/ppermute | solution.py:305
  19.0 12.6 %collective-permute-start.5 = (bf16[256,640]{1,0:T(8,128)(2,1)}, bf16[256,640]{1,0:T(8,128)(2,1)S(1)}, u32[]{:S(2)}, u32[]{:S(2)}) collective-permute-start(bf16[256,640]{1,0:T(8,128)(2,1)} %collective-permute-done.2.refs_7_), channel_id=1, source_target_pairs={{0,8},{4,12},{8,16},{12,20},{16,24},{20,28},{24,0},{28,4},{1,9},{5... | collective-permute-start | bytes 983048 | tf_op jit(solution)/shard_map/ppermute | solution.py:311
  20.1 22.1 %collective-permute-start.3 = (bf16[4,128,640]{2,1,0:T(8,128)(2,1)S(1)}, bf16[4,128,640]{2,1,0:T(8,128)(2,1)S(1)}, u32[]{:S(2)}, u32[]{:S(2)}) collective-permute-start(bf16[4,128,640]{2,1,0:T(8,128)(2,1)S(1)} %get-tuple-element.180.refs_2_), channel_id=1, source_target_pairs={{0,2},{1,3},{2,0},{3,1},{4,6},{5,7},{6,4},{7,5},{8,10},{9,11},{10,... | collective-permute-start | bytes 1966088 | tf_op jit(solution)/shard_map/ppermute | solution.py:302
  21.9 30.7 %collective-permute-start.14 = (bf16[4,128,640]{2,1,0:T(8,128)(2,1)S(1)}, bf16[4,128,640]{2,1,0:T(8,128)(2,1)S(1)}, u32[]{:S(2)}, u32[]{:S(2)}) collective-permute-start(bf16[4,128,640]{2,1,0:T(8,128)(2,1)S(1)} %collective-permute-done.9.refs_3_), channel_id=1, source_target_pairs={{0,2},{1,3},{2,0},{3,1},{4,6},{5,7},{6,4},{7,5},{8,10},{9,11},{10,... | collective-permute-start | bytes 1966088 | tf_op jit(solution)/shard_map/ppermute | solution.py:302
  22.5 19.6 %collective-permute-start.4 = (bf16[384,640]{1,0:T(8,128)(2,1)S(1)}, bf16[384,640]{1,0:T(8,128)(2,1)S(1)}, u32[]{:S(2)}, u32[]{:S(2)}) collective-permute-start(bf16[384,640]{1,0:T(8,128)(2,1)S(1)} %slice.6.refs_6_), channel_id=1, source_target_pairs={{0,8},{4,12},{8,16},{12,20},{16,24},{20,28},{24,0},{28,4},{1,9},{5... | collective-permute-start | bytes 1474568 | tf_op jit(solution)/shard_map/ppermute | solution.py:311
  31.6 21.1 %collective-permute-start.1 = (bf16[384,640]{1,0:T(8,128)(2,1)S(1)}, bf16[384,640]{1,0:T(8,128)(2,1)S(1)}, u32[]{:S(2)}, u32[]{:S(2)}) collective-permute-start(bf16[384,640]{1,0:T(8,128)(2,1)S(1)} %collective-permute-done.refs_8_), channel_id=1, source_target_pairs={{0,8},{4,12},{8,16},{12,20},{16,24},{20,28},{24,0},{28,4},{1,9},{5... | collective-permute-start | bytes 1474568 | tf_op jit(solution)/shard_map/ppermute | solution.py:311
  31.7 38.5 %collective-permute-start.11 = (bf16[8,128,384]{2,1,0:T(8,128)(2,1)S(1)}, bf16[8,128,384]{2,1,0:T(8,128)(2,1)S(1)}, u32[]{:S(2)}, u32[]{:S(2)}) collective-permute-start(bf16[8,128,384]{2,1,0:T(8,128)(2,1)S(1)} %pad_maximum_fusion), channel_id=1, source_target_pairs={{0,2},{1,3},{2,0},{3,1},{4,6},{5,7},{6,4},{7,5},{8,10},{9,11},{10,... | collective-permute-start | bytes 2359304 | tf_op jit(solution)/shard_map/ppermute | solution.py:302
  42.1 28.1 %collective-permute-start.12 = (bf16[384,640]{1,0:T(8,128)(2,1)S(1)}, bf16[384,640]{1,0:T(8,128)(2,1)}, u32[]{:S(2)}, u32[]{:S(2)}) collective-permute-start(bf16[384,640]{1,0:T(8,128)(2,1)S(1)} %collective-permute-done.4.refs_6_), channel_id=1, source_target_pairs={{0,8},{4,12},{8,16},{12,20},{16,24},{20,28},{24,0},{28,4},{1,9},{5... | collective-permute-start | bytes 1474568 | tf_op jit(solution)/shard_map/ppermute | solution.py:311
  42.1 27.1 %collective-permute-start.13 = (bf16[256,640]{1,0:T(8,128)(2,1)S(1)}, bf16[256,640]{1,0:T(8,128)(2,1)S(1)}, u32[]{:S(2)}, u32[]{:S(2)}) collective-permute-start(bf16[256,640]{1,0:T(8,128)(2,1)S(1)} %collective-permute-done.5.refs_7_), channel_id=1, source_target_pairs={{0,8},{4,12},{8,16},{12,20},{16,24},{20,28},{24,0},{28,4},{1,9},{5... | collective-permute-start | bytes 983048 | tf_op jit(solution)/shard_map/ppermute | solution.py:311
  57.3 17.3 %collective-permute-start.17 = (bf16[2,256,640]{2,1,0:T(8,128)(2,1)S(1)}, bf16[2,256,640]{2,1,0:T(8,128)(2,1)S(1)}, u32[]{:S(2)}, u32[]{:S(2)}) collective-permute-start(bf16[2,256,640]{2,1,0:T(8,128)(2,1)S(1)} %shard_map.105.refs_0_), channel_id=1, source_target_pairs={{0,4},{4,0},{8,12},{12,8},{16,20},{20,16},{24,28},{28,24},{1,5},{5... | collective-permute-start | bytes 1966088 | tf_op jit(solution)/shard_map/ppermute | solution.py:308
  59.0 20.8 %collective-permute-start.16 = (bf16[8,128,256]{2,1,0:T(8,128)(2,1)S(1)}, bf16[8,128,256]{2,1,0:T(8,128)(2,1)S(1)}, u32[]{:S(2)}, u32[]{:S(2)}) collective-permute-start(bf16[8,128,256]{2,1,0:T(8,128)(2,1)S(1)} %pad_maximum_fusion.2), channel_id=1, source_target_pairs={{0,2},{1,3},{2,0},{3,1},{4,6},{5,7},{6,4},{7,5},{8,10},{9,11},{10,... | collective-permute-start | bytes 1572872 | tf_op jit(solution)/shard_map/ppermute | solution.py:302
  69.2 16.0 %collective-permute-start.10 = (bf16[384,640]{1,0:T(8,128)(2,1)S(1)}, bf16[384,640]{1,0:T(8,128)(2,1)S(1)}, u32[]{:S(2)}, u32[]{:S(2)}) collective-permute-start(bf16[384,640]{1,0:T(8,128)(2,1)S(1)} %collective-permute-done.1.refs_8_), channel_id=1, source_target_pairs={{0,8},{4,12},{8,16},{12,20},{16,24},{20,28},{24,0},{28,4},{1,9},{5... | collective-permute-start | bytes 1474568 | tf_op jit(solution)/shard_map/ppermute | solution.py:311
  73.0 10.6 %collective-permute-start.15 = (bf16[2,256,384]{2,1,0:T(8,128)(2,1)S(1)}, bf16[2,256,384]{2,1,0:T(8,128)(2,1)S(1)}, u32[]{:S(2)}, u32[]{:S(2)}) collective-permute-start(bf16[2,256,384]{2,1,0:T(8,128)(2,1)S(1)} %shard_map.106.refs_1_), channel_id=1, source_target_pairs={{0,4},{4,0},{8,12},{12,8},{16,20},{20,16},{24,28},{28,24},{1,5},{5... | collective-permute-start | bytes 1179656 | tf_op jit(solution)/shard_map/ppermute | solution.py:308
  74.6 22.6 %collective-permute-start.24 = (bf16[384,640]{1,0:T(8,128)(2,1)}, bf16[384,640]{1,0:T(8,128)(2,1)}, u32[]{:S(2)}, u32[]{:S(2)}) collective-permute-start(bf16[384,640]{1,0:T(8,128)(2,1)} %collective-permute-done.12.refs_6_), channel_id=1, source_target_pairs={{0,8},{4,12},{8,16},{12,20},{16,24},{20,28},{24,0},{28,4},{1,9},{5... | collective-permute-start | bytes 1474568 | tf_op jit(solution)/shard_map/ppermute | solution.py:311
  74.6 13.4 %collective-permute-start.21 = (bf16[256,640]{1,0:T(8,128)(2,1)}, bf16[256,640]{1,0:T(8,128)(2,1)}, u32[]{:S(2)}, u32[]{:S(2)}) collective-permute-start(bf16[256,640]{1,0:T(8,128)(2,1)} %slice.7.refs_7_), channel_id=1, source_target_pairs={{0,2},{1,3},{2,0},{3,1},{4,6},{5,7},{6,4},{7,5},{8,10},{9,11},{10,... | collective-permute-start | bytes 983048 | tf_op jit(solution)/shard_map/ppermute | solution.py:302
  81.7 7.2 %collective-permute-start.20 = (bf16[2,256,256]{2,1,0:T(8,128)(2,1)S(1)}, bf16[2,256,256]{2,1,0:T(8,128)(2,1)S(1)}, u32[]{:S(2)}, u32[]{:S(2)}) collective-permute-start(bf16[2,256,256]{2,1,0:T(8,128)(2,1)S(1)} %shard_map.107.refs_2_), channel_id=1, source_target_pairs={{0,4},{4,0},{8,12},{12,8},{16,20},{20,16},{24,28},{28,24},{1,5},{5... | collective-permute-start | bytes 786440 | tf_op jit(solution)/shard_map/ppermute | solution.py:308
  86.0 11.2 %collective-permute-start.23 = (bf16[256,640]{1,0:T(8,128)(2,1)}, bf16[256,640]{1,0:T(8,128)(2,1)}, u32[]{:S(2)}, u32[]{:S(2)}) collective-permute-start(bf16[256,640]{1,0:T(8,128)(2,1)} %collective-permute-done.2.refs_7_), channel_id=1, source_target_pairs={{0,2},{1,3},{2,0},{3,1},{4,6},{5,7},{6,4},{7,5},{8,10},{9,11},{10,... | collective-permute-start | bytes 983048 | tf_op jit(solution)/shard_map/ppermute | solution.py:302
  86.5 21.8 %collective-permute-start.19 = (bf16[512,640]{1,0:T(8,128)(2,1)}, bf16[512,640]{1,0:T(8,128)(2,1)S(1)}, u32[]{:S(2)}, u32[]{:S(2)}) collective-permute-start(bf16[512,640]{1,0:T(8,128)(2,1)} %pad_maximum_fusion.1), channel_id=1, source_target_pairs={{0,2},{1,3},{2,0},{3,1},{4,6},{5,7},{6,4},{7,5},{8,10},{9,11},{10,... | collective-permute-start | bytes 1966088 | tf_op jit(solution)/shard_map/ppermute | solution.py:302
  97.2 15.2 %collective-permute-start.18 = (bf16[384,640]{1,0:T(8,128)(2,1)S(1)}, bf16[384,640]{1,0:T(8,128)(2,1)S(1)}, u32[]{:S(2)}, u32[]{:S(2)}) collective-permute-start(bf16[384,640]{1,0:T(8,128)(2,1)S(1)} %copy-done.29), channel_id=1, source_target_pairs={{0,8},{4,12},{8,16},{12,20},{16,24},{20,28},{24,0},{28,4},{1,9},{5... | collective-permute-start | bytes 1474568 | tf_op jit(solution)/shard_map/ppermute | solution.py:311
  98.4 10.0 %collective-permute-start.26 = (bf16[256,640]{1,0:T(8,128)(2,1)S(1)}, bf16[256,640]{1,0:T(8,128)(2,1)S(1)}, u32[]{:S(2)}, u32[]{:S(2)}) collective-permute-start(bf16[256,640]{1,0:T(8,128)(2,1)S(1)} %shard_map.109), channel_id=1, source_target_pairs={{0,4},{4,0},{8,12},{12,8},{16,20},{20,16},{24,28},{28,24},{1,5},{5... | collective-permute-start | bytes 983048 | tf_op jit(solution)/shard_map/ppermute | solution.py:308
  107.4 21.4 %collective-permute-start.33 = (bf16[256,640]{1,0:T(8,128)(2,1)S(1)}, bf16[256,640]{1,0:T(8,128)(2,1)S(1)}, u32[]{:S(2)}, u32[]{:S(2)}) collective-permute-start(bf16[256,640]{1,0:T(8,128)(2,1)S(1)} %shard_map.111), channel_id=1, source_target_pairs={{0,4},{4,0},{8,12},{12,8},{16,20},{20,16},{24,28},{28,24},{1,5},{5... | collective-permute-start | bytes 983048 | tf_op jit(solution)/shard_map/ppermute | solution.py:308
  120.0 12.7 %collective-permute-start.31 = (bf16[256,640]{1,0:T(8,128)(2,1)}, bf16[256,640]{1,0:T(8,128)(2,1)}, u32[]{:S(2)}, u32[]{:S(2)}) collective-permute-start(bf16[256,640]{1,0:T(8,128)(2,1)} %shard_map.113), channel_id=1, source_target_pairs={{0,4},{4,0},{8,12},{12,8},{16,20},{20,16},{24,28},{28,24},{1,5},{5... | collective-permute-start | bytes 983048 | tf_op jit(solution)/shard_map/ppermute | solution.py:308
  121.5 11.7 %collective-permute-start.37 = (bf16[256,640]{1,0:T(8,128)(2,1)}, bf16[256,640]{1,0:T(8,128)(2,1)}, u32[]{:S(2)}, u32[]{:S(2)}) collective-permute-start(bf16[256,640]{1,0:T(8,128)(2,1)} %get-tuple-element.319), channel_id=1, source_target_pairs={{0,1},{1,0},{2,3},{3,2},{4,5},{5,4},{6,7},{7,6},{8,9},{9,8},{10,11... | collective-permute-start | bytes 983048 | tf_op jit(solution)/shard_map/ppermute | solution.py:305
  128.8 7.9 %collective-permute-start.36 = (bf16[256,640]{1,0:T(8,128)(2,1)}, bf16[256,640]{1,0:T(8,128)(2,1)S(1)}, u32[]{:S(2)}, u32[]{:S(2)}) collective-permute-start(bf16[256,640]{1,0:T(8,128)(2,1)} %get-tuple-element.317), channel_id=1, source_target_pairs={{0,1},{1,0},{2,3},{3,2},{4,5},{5,4},{6,7},{7,6},{8,9},{9,8},{10,11... | collective-permute-start | bytes 983048 | tf_op jit(solution)/shard_map/ppermute | solution.py:305
  130.1 8.2 %collective-permute-start.35 = (bf16[256,640]{1,0:T(8,128)(2,1)}, bf16[256,640]{1,0:T(8,128)(2,1)S(1)}, u32[]{:S(2)}, u32[]{:S(2)}) collective-permute-start(bf16[256,640]{1,0:T(8,128)(2,1)} %get-tuple-element.315), channel_id=1, source_target_pairs={{0,1},{1,0},{2,3},{3,2},{4,5},{5,4},{6,7},{7,6},{8,9},{9,8},{10,11... | collective-permute-start | bytes 983048 | tf_op jit(solution)/shard_map/ppermute | solution.py:305
  131.1 9.7 %collective-permute-start.38 = (bf16[256,640]{1,0:T(8,128)(2,1)}, bf16[256,640]{1,0:T(8,128)(2,1)S(1)}, u32[]{:S(2)}, u32[]{:S(2)}) collective-permute-start(bf16[256,640]{1,0:T(8,128)(2,1)} %copy-done.34), channel_id=1, source_target_pairs={{0,1},{1,0},{2,3},{3,2},{4,5},{5,4},{6,7},{7,6},{8,9},{9,8},{10,11... | collective-permute-start | bytes 983048 | tf_op jit(solution)/shard_map/ppermute | solution.py:305
  132.7 9.8 %collective-permute-start.39 = (bf16[256,640]{1,0:T(8,128)(2,1)S(1)}, bf16[256,640]{1,0:T(8,128)(2,1)S(1)}, u32[]{:S(2)}, u32[]{:S(2)}) collective-permute-start(bf16[256,640]{1,0:T(8,128)(2,1)S(1)} %shard_map.115), channel_id=1, source_target_pairs={{0,4},{4,0},{8,12},{12,8},{16,20},{20,16},{24,28},{28,24},{1,5},{5... | collective-permute-start | bytes 983048 | tf_op jit(solution)/shard_map/ppermute | solution.py:308
  (45 other events, 243.7 us)

commit v9 on v7

--- a/solution.py
+++ b/solution.py
@@ -203,15 +203,14 @@
     )(keep, *gots)
 
 
-def place_kernel(where_ref, keep_ref, got_ref, other_ref, *refs):
+def place_kernel(where_ref, mine_ref, other_ref, *refs):
     plain_ref, dual_ref = refs[-2:]
     rows = plain_ref.shape[0]
 
     @pl.when(pl.program_id(0) == 0)
     def _():
-        total = (keep_ref[...] + got_ref[...].astype(WIDE)).astype(LOW)
-        plain_ref[...] = total[:rows]
-        dual_ref[...] = total[rows:]
+        plain_ref[...] = mine_ref[:rows]
+        dual_ref[...] = mine_ref[rows:]
 
     @pl.when(pl.program_id(0) == 1)
     def _():
@@ -219,11 +218,11 @@
         dual_ref[...] = other_ref[rows:]
 
 
-def place(outs, width, where, keep, got, other):
+def place(outs, width, where, mine, other):
     rows, n = other.shape[0] // 2, other.shape[1]
     if n % 128:
         outs = outs or [jnp.zeros((rows, width), LOW)] * 2
-        for side, piece in enumerate((close(keep, got), other)):
+        for side, piece in enumerate((mine, other)):
             parts = (piece[:rows], piece[rows:])
             outs = [lax.dynamic_update_slice(out, part, (0, where[side] * n)) for out, part in zip(outs, parts)]
         return outs
@@ -234,14 +233,14 @@
         grid_spec=pltpu.PrefetchScalarGridSpec(
             num_scalar_prefetch=1,
             grid=(2,),
-            in_specs=[full] * 3 + [pl.BlockSpec(memory_space=pl.ANY)] * len(outs),
+            in_specs=[full] * 2 + [pl.BlockSpec(memory_space=pl.ANY)] * len(outs),
             out_specs=[block] * 2,
         ),
         out_shape=[jax.ShapeDtypeStruct((rows, width), LOW)] * 2,
-        input_output_aliases={4 + at: at for at in range(len(outs))},
+        input_output_aliases={3 + at: at for at in range(len(outs))},
         compiler_params=params(),
         cost_estimate=LIGHT,
-    )(where, keep, got, other, *outs)
+    )(where, mine, other, *outs)
 
 
 def body(
@@ -343,51 +342,60 @@
     acts = list(zip(acts, swapped))
     flip = jnp.stack([seq // 2])
 
-    keeps, mine_sends, sends, mine_got, other = [], [], [], [], []
+    keeps, sends, mine_got, mine, other = [], [], [], [], []
 
     def columns(step):
-        own = [(upper[step], 0, cut), (lower[step], 0, depth - cut)]
+        own = [(upper[step], 0, cut), (lower[step], 0, depth - cut)] if step else [(out_weight, 0, depth)]
         start = step % 2 * (depth - cut) if step > 1 else 0
         got = rest[step] if step < 2 else rest[1 + step // 2]
         theirs = [(beside[step], 0, cut), (got, start, start + depth - cut)]
-        keep_mine, keep_other, send_mine, *send_other = project(after(flip), acts, own + theirs)
+        keep_mine, keep_other, *low = project(after(flip), acts, own + theirs)
         keeps.append((keep_mine, keep_other))
-        sends.append([near(wait(array)) for array in send_other])
-        mine_sends.append(send_mine)
-
-    def finish(step):
+        sends.append([near(wait(array)) for array in low[1:]])
+        mine_got.append([wait(array) for array in low[:1]])
+
+    def send(step):
+        if step > 2:
+            other[step - 1] = wait(other[step - 1])
         other.append(across(wait(close(keeps[step][1], *[wait(array) for array in sends[step]]))))
-        mine_got.append(near(mine_sends[step]))
+        mine_got[step] = [near(after(array)) for array in mine_got[step]]
+        if step and not step > 2:
+            other[step - 1] = wait(other[step - 1])
+
+    def stay(step):
+        mine.append(wait(close(keeps[step][0], *[wait(array) for array in mine_got[step]])))
 
     outs = []
 
     def put(step):
         pair = (dp // 2 - step) % n_ring
         where = jnp.stack([2 * pair + dp % 2, 2 * pair + 1 - dp % 2]).astype(jnp.int32) + token
-        return place(outs, n_dp * out_weight.shape[1], where, keeps[step][0], wait(mine_got[step]), wait(other[step]))
+        return place(outs, n_dp * out_weight.shape[1], where, mine[step], other[step])
 
     columns(0)
     for step in range(3, n_ring):
         turn(upper, step)
     rest[1] = wait(rest[1])
-    finish(0)
+    send(0)
     columns(1)
-    finish(1)
+    send(1)
+    stay(0)
     for step in range(2, n_ring, 2):
-        other[step - 2] = wait(other[step - 2])
         rest[1 + step // 2] = wait(rest[1 + step // 2])
         if step > 2:
             turn(beside, step)
         columns(step)
-        finish(step)
+        send(step)
+        stay(step - 1)
         turn(beside, step + 1)
         columns(step + 1)
-        other[step - 1] = wait(other[step - 1])
-        finish(step + 1)
-    other[-2] = wait(other[-2])
-    for step in range(n_ring):
-        outs = put(step)
-    return tuple(outs)
+        send(step + 1)
+        stay(step)
+    stay(n_ring - 1)
+    for step in range(n_ring - 1):
+        outs = [wait(out) for out in put(step)]
+    other[-1] = wait(other[-1])
+    return tuple(put(n_ring - 1))
 
 
 def solution(mesh):

time: 138 us -> 138 us (level)
  waiting for transfers between devices: 57.9 us -> 67.2 us
  local copies, waits for them, and re-layouts: 17.9 us -> 11.4 us
  Pallas kernels: 34.7 us -> 32.2 us
    unnamed x74 -> x58, local copies, waits for them, and re-layouts: 15 us -> 7.68 us
    ppermute x9, waiting for transfers between devices: 41.6 us -> 45.4 us  [onward(): return lax.ppermute(array, 'dp', [(i, (i + 2) % n_dp) for i in range(n_dp)])]
    ppermute x8, waiting for transfers between devices: 6.25 us -> 9.07 us  [far(): return lax.ppermute(array, 'seq', [(i, i ^ 2) for i in range(n_seq)])]
    ppermute x7, waiting for transfers between devices: 4.56 us -> 6.83 us  [across(): return lax.ppermute(array, 'dp', [(i, i ^ 1) for i in range(n_dp)])]
    pallas_call x4, Pallas kernels: 7.89 us -> 5.79 us  [place(): pl.pallas_call(place_kernel, grid_spec=pltpu.PrefetchScalarGridSpec(num_s...]
  transfers between devices with their start and end apart: 40 -> 40, of which waited for: 21 -> 26; matrix products, arithmetic and copies ran while one was open for 2% -> 2% of each run, Pallas kernels for 24% -> 22%
where the time goes in v9:
time: 138 us
  waiting for transfers between devices  67.2 us (49%)
  Pallas kernels  32.2 us (23%)
  starting transfers between devices  24.5 us (18%)
  local copies, waits for them, and re-layouts  11.4 us (8%)
  other arithmetic  1.4 us (1%)
    ppermute x9, waiting for transfers between devices, onward(): return lax.ppermute(array, 'dp', [(i, (i + 2) % n_dp) for i in range(n_dp)])  45.4 us
    pallas_call x4, Pallas kernels, project(): pl.pallas_call(functools.partial(project_kernel, len(acts), spans), in_sp...  14.4 us
    pallas_call x3, Pallas kernels, attend(): pl.pallas_call(functools.partial(attend_kernel, len(queries)), grid=(widt...  9.36 us
    ppermute x8, waiting for transfers between devices, far(): return lax.ppermute(array, 'seq', [(i, i ^ 2) for i in range(n_seq)])  9.07 us
    ppermute x7, starting transfers between devices, across(): return lax.ppermute(array, 'dp', [(i, i ^ 1) for i in range(n_dp)])  9.06 us
    ppermute x8, starting transfers between devices, far(): return lax.ppermute(array, 'seq', [(i, i ^ 2) for i in range(n_seq)])  7.84 us
    unnamed x58, local copies, waits for them, and re-layouts  7.68 us
    ppermute x7, waiting for transfers between devices, across(): return lax.ppermute(array, 'dp', [(i, i ^ 1) for i in range(n_dp)])  6.83 us
  transfers between devices with their start and end apart: 40, of which 26 were waited for; matrix products, arithmetic and copies ran while one was open for 2% of the time, Pallas kernels for 22%

profile of v9, /device:TPU:0, one launch (start us, length us, event | category | flops | bytes accessed | tf_op | source)
XLA Modules:
  0.0 137.7 jit_solution(3485900272076005974)
XLA Ops:
  0.7 2.0 %slice.6 = bf16[384,640]{1,0:T(8,128)(2,1)} slice(bf16[640,640]{1,0:T(8,128)(2,1)} %refs_6_.1), slice={[0:384], [0:640]} | slice | bytes 983040 | tf_op jit(solution)/shard_map/slice | solution.py:298
  2.6 2.9 %collective-permute-start = (bf16[384,640]{1,0:T(8,128)(2,1)}, bf16[384,640]{1,0:T(8,128)(2,1)S(1)}, u32[]{:S(2)}, u32[]{:S(2)}) collective-permute-start(bf16[384,640]{1,0:T(8,128)(2,1)} %slice.6), channel_id=1, source_target_pairs={{0,2},{1,3},{2,0},{3,1},{4,6},{5,7},{6,4},{7,5},{8,10},{9,11},{10,... | collective-permute-start | bytes 1474568 | tf_op jit(solution)/shard_map/ppermute | solution.py:272
  5.6 1.7 %slice.7 = bf16[256,640]{1,0:T(8,128)(2,1)} slice(bf16[640,640]{1,0:T(8,128)(2,1)} %refs_6_.1), slice={[384:640], [0:640]} | slice | bytes 655360 | tf_op jit(solution)/shard_map/slice | solution.py:298
  7.3 1.6 %collective-permute-start.2 = (bf16[256,640]{1,0:T(8,128)(2,1)}, bf16[256,640]{1,0:T(8,128)(2,1)}, u32[]{:S(2)}, u32[]{:S(2)}) collective-permute-start(bf16[256,640]{1,0:T(8,128)(2,1)} %slice.7), channel_id=1, source_target_pairs={{0,8},{4,12},{8,16},{12,20},{16,24},{20,28},{24,0},{28,4},{1,9},{5... | collective-permute-start | bytes 983048 | tf_op jit(solution)/shard_map/ppermute | solution.py:281
  13.3 2.0 %shard_map.104 = (bf16[2,128,1280]{2,1,0:T(8,128)(2,1)S(1)}, bf16[4,128,640]{2,1,0:T(8,128)(2,1)S(1)}, bf16[4,128,384]{2,1,0:T(8,128)(2,1)S(1)}, bf16[4,128,256]...) custom-call(s32[1]{0:T(128)} %bitcast.3.core_ref, ...), custom_call_target="tpu_custom_call" | custom-call | flops 1 | bytes 1 | tf_op jit(solution)/shard_map/pallas_call | solution.py:78
  15.4 1.6 %collective-permute-done.refs_7_ = bf16[384,640]{1,0:T(8,128)(2,1)S(1)} collective-permute-done((bf16[384,640]{1,0:T(8,128)(2,1)}, bf16[384,640]{1,0:T(8,128)(2,1)S(1)}, u32[]{:S(2)}, u32[]{:S(2)}) %collective-permute-start) | collective-permute-done | bytes 491552 | tf_op jit(solution)/shard_map/ppermute | solution.py:272
  17.0 1.7 %collective-permute-done.2.refs_7_ = bf16[256,640]{1,0:T(8,128)(2,1)} collective-permute-done((bf16[256,640]{1,0:T(8,128)(2,1)}, bf16[256,640]{1,0:T(8,128)(2,1)}, u32[]{:S(2)}, u32[]{:S(2)}) %collective-permute-start.2) | collective-permute-done | bytes 327712 | tf_op jit(solution)/shard_map/ppermute | solution.py:281
  24.3 8.0 %collective-permute-done.5.refs_7_ = bf16[256,640]{1,0:T(8,128)(2,1)S(1)} collective-permute-done((bf16[256,640]{1,0:T(8,128)(2,1)}, bf16[256,640]{1,0:T(8,128)(2,1)S(1)}, u32[]{:S(2)}, u32[]{:S(2)}) %collective-permute-start.5) | collective-permute-done | bytes 327712 | tf_op jit(solution)/shard_map/ppermute | solution.py:281
  33.0 9.8 %collective-permute-done.4.refs_6_ = bf16[384,640]{1,0:T(8,128)(2,1)S(1)} collective-permute-done((bf16[384,640]{1,0:T(8,128)(2,1)}, bf16[384,640]{1,0:T(8,128)(2,1)S(1)}, u32[]{:S(2)}, u32[]{:S(2)}) %collective-permute-start.4) | collective-permute-done | bytes 491552 | tf_op jit(solution)/shard_map/ppermute | solution.py:281
  42.9 10.5 %collective-permute-done.1.refs_8_ = bf16[384,640]{1,0:T(8,128)(2,1)S(1)} collective-permute-done((bf16[384,640]{1,0:T(8,128)(2,1)S(1)}, bf16[384,640]{1,0:T(8,128)(2,1)S(1)}, u32[]{:S(2)}, u32[]{:S(2)}) %collective-permute-start.1) | collective-permute-done | bytes 491552 | tf_op jit(solution)/shard_map/ppermute | solution.py:281
  53.3 4.7 %shard_map.105.refs_0_ = bf16[2,256,640]{2,1,0:T(8,128)(2,1)S(1)} custom-call(bf16[2,128,1280]{2,1,0:T(8,128)(2,1)S(1)} %get-tuple-element.236.refs_0_, bf16[2,128,1280]{2,1,0:T(8,128)(2,1)S(1)} %collective-permute-done.6.refs_1_, bf16[4,128,640]{2,1,0:T(8,128)(2,1)S(1)} %get-tuple-element.209.refs_2_, ...), custom_call_target="tpu_custom_call" | custom-call | flops 1 | bytes 1 | tf_op jit(solution)/shard_map/pallas_call | solution.py:129
  58.0 1.6 %collective-permute-start.17 = (bf16[2,256,640]{2,1,0:T(8,128)(2,1)S(1)}, bf16[2,256,640]{2,1,0:T(8,128)(2,1)S(1)}, u32[]{:S(2)}, u32[]{:S(2)}) collective-permute-start(bf16[2,256,640]{2,1,0:T(8,128)(2,1)S(1)} %shard_map.105.refs_0_), channel_id=1, source_target_pairs={{0,4},{4,0},{8,12},{12,8},{16,20},{20,16},{24,28},{28,24},{1,5},{5... | collective-permute-start | bytes 1966088 | tf_op jit(solution)/shard_map/ppermute | solution.py:278
  60.3 9.7 %collective-permute-done.13.refs_7_ = bf16[256,640]{1,0:T(8,128)(2,1)S(1)} collective-permute-done((bf16[256,640]{1,0:T(8,128)(2,1)S(1)}, bf16[256,640]{1,0:T(8,128)(2,1)S(1)}, u32[]{:S(2)}, u32[]{:S(2)}) %collective-permute-start.13) | collective-permute-done | bytes 327712 | tf_op jit(solution)/shard_map/ppermute | solution.py:281
  70.9 2.8 %shard_map.106.refs_1_ = bf16[2,256,384]{2,1,0:T(8,128)(2,1)S(1)} custom-call(bf16[2,128,1280]{2,1,0:T(8,128)(2,1)S(1)} %get-tuple-element.236.refs_0_, bf16[2,128,1280]{2,1,0:T(8,128)(2,1)S(1)} %collective-permute-done.6.refs_1_, bf16[4,128,384]{2,1,0:T(8,128)(2,1)S(1)} %get-tuple-element.238.refs_2_, ...), custom_call_target="tpu_custom_call" | custom-call | flops 1 | bytes 1 | tf_op jit(solution)/shard_map/pallas_call | solution.py:129
  73.7 1.6 %collective-permute-start.15 = (bf16[2,256,384]{2,1,0:T(8,128)(2,1)S(1)}, bf16[2,256,384]{2,1,0:T(8,128)(2,1)S(1)}, u32[]{:S(2)}, u32[]{:S(2)}) collective-permute-start(bf16[2,256,384]{2,1,0:T(8,128)(2,1)S(1)} %shard_map.106.refs_1_), channel_id=1, source_target_pairs={{0,4},{4,0},{8,12},{12,8},{16,20},{20,16},{24,28},{28,24},{1,5},{5... | collective-permute-start | bytes 1179656 | tf_op jit(solution)/shard_map/ppermute | solution.py:278
  76.8 3.7 %collective-permute-done.16.refs_4_ = bf16[8,128,256]{2,1,0:T(8,128)(2,1)S(1)} collective-permute-done((bf16[8,128,256]{2,1,0:T(8,128)(2,1)S(1)}, bf16[8,128,256]{2,1,0:T(8,128)(2,1)S(1)}, u32[]{:S(2)}, u32[]{:S(2)}) %collective-permute-start.16) | collective-permute-done | bytes 524320 | tf_op jit(solution)/shard_map/ppermute | solution.py:272
  80.5 1.9 %shard_map.107.refs_2_ = bf16[2,256,256]{2,1,0:T(8,128)(2,1)S(1)} custom-call(bf16[2,128,1280]{2,1,0:T(8,128)(2,1)S(1)} %get-tuple-element.236.refs_0_, bf16[2,128,1280]{2,1,0:T(8,128)(2,1)S(1)} %collective-permute-done.6.refs_1_, bf16[4,128,256]{2,1,0:T(8,128)(2,1)S(1)} %get-tuple-element.255.refs_2_, ...), custom_call_target="tpu_custom_call" | custom-call | flops 1 | bytes 1 | tf_op jit(solution)/shard_map/pallas_call | solution.py:129
  82.3 1.6 %collective-permute-start.19 = (bf16[2,256,256]{2,1,0:T(8,128)(2,1)S(1)}, bf16[2,256,256]{2,1,0:T(8,128)(2,1)S(1)}, u32[]{:S(2)}, u32[]{:S(2)}) collective-permute-start(bf16[2,256,256]{2,1,0:T(8,128)(2,1)S(1)} %shard_map.107.refs_2_), channel_id=1, source_target_pairs={{0,4},{4,0},{8,12},{12,8},{16,20},{20,16},{24,28},{28,24},{1,5},{5... | collective-permute-start | bytes 786440 | tf_op jit(solution)/shard_map/ppermute | solution.py:278
  84.2 1.8 %collective-permute-done.10.refs_8_ = bf16[384,640]{1,0:T(8,128)(2,1)} collective-permute-done((bf16[384,640]{1,0:T(8,128)(2,1)S(1)}, bf16[384,640]{1,0:T(8,128)(2,1)}, u32[]{:S(2)}, u32[]{:S(2)}) %collective-permute-start.10) | collective-permute-done | bytes 491552 | tf_op jit(solution)/shard_map/ppermute | solution.py:281
  86.5 1.5 %collective-permute-start.29 = (bf16[512,640]{1,0:T(8,128)(2,1)}, bf16[512,640]{1,0:T(8,128)(2,1)}, u32[]{:S(2)}, u32[]{:S(2)}) collective-permute-start(bf16[512,640]{1,0:T(8,128)(2,1)} %pad_maximum_fusion.1), channel_id=1, source_target_pairs={{0,2},{1,3},{2,0},{3,1},{4,6},{5,7},{6,4},{7,5},{8,10},{9,11},{10,... | collective-permute-start | bytes 1966088 | tf_op jit(solution)/shard_map/ppermute | solution.py:272
  88.0 1.6 %collective-permute-done.19.refs_5_ = bf16[2,256,256]{2,1,0:T(8,128)(2,1)S(1)} collective-permute-done((bf16[2,256,256]{2,1,0:T(8,128)(2,1)S(1)}, bf16[2,256,256]{2,1,0:T(8,128)(2,1)S(1)}, u32[]{:S(2)}, u32[]{:S(2)}) %collective-permute-start.19) | collective-permute-done | bytes 262176 | tf_op jit(solution)/shard_map/ppermute | solution.py:278
  90.6 3.3 %shard_map.108 = (f32[256,640]{1,0:T(8,128)S(1)}, f32[256,640]{1,0:T(8,128)S(1)}, bf16[256,640]{1,0:T(8,128)(2,1)S(1)}, bf16[128,640]{1,0:T(8,128)(2,1)S(1)}, bf16[128,640]{1,0:T(8,128)(2,1)S(1)}) custom-call(s32[1]{0:T(128)} %bitcast.2.flip_ref, bf16[2,256,640]{2,1,0:T(8,128)(2,1)S(1)} %shard_map.105.refs_0_, bf16[2,256,384]{2,1,0:T(8,128)(2,1)S(1)} %shard_map.106.refs_1_, ...), custom_call_target="tpu_custom_call" | custom-call | flops 1 | bytes 1 | tf_op jit(solution)/shard_map/pallas_call | solution.py:173
  94.6 2.3 %collective-permute-done.22.refs_9_ = bf16[256,640]{1,0:T(8,128)(2,1)} collective-permute-done((bf16[256,640]{1,0:T(8,128)(2,1)}, bf16[256,640]{1,0:T(8,128)(2,1)}, u32[]{:S(2)}, u32[]{:S(2)}) %collective-permute-start.22) | collective-permute-done | bytes 327712 | tf_op jit(solution)/shard_map/ppermute | solution.py:272
  97.0 1.6 %collective-permute-start.31 = (bf16[256,640]{1,0:T(8,128)(2,1)S(1)}, bf16[256,640]{1,0:T(8,128)(2,1)S(1)}, u32[]{:S(2)}, u32[]{:S(2)}) collective-permute-start(bf16[256,640]{1,0:T(8,128)(2,1)S(1)} %shard_map.109), channel_id=1, source_target_pairs={{0,4},{4,0},{8,12},{12,8},{16,20},{20,16},{24,28},{28,24},{1,5},{5... | collective-permute-start | bytes 983048 | tf_op jit(solution)/shard_map/ppermute | solution.py:278
  98.6 3.4 %shard_map.110 = (f32[256,640]{1,0:T(8,128)S(1)}, f32[256,640]{1,0:T(8,128)S(1)}, bf16[256,640]{1,0:T(8,128)(2,1)S(1)}, bf16[128,640]{1,0:T(8,128)(2,1)S(1)}, bf16[128,640]{1,0:T(8,128)(2,1)S(1)}) custom-call(s32[1]{0:T(128)} %bitcast.2.flip_ref, bf16[2,256,640]{2,1,0:T(8,128)(2,1)S(1)} %shard_map.105.refs_0_, bf16[2,256,384]{2,1,0:T(8,128)(2,1)S(1)} %shard_map.106.refs_1_, ...), custom_call_target="tpu_custom_call" | custom-call | flops 1 | bytes 1 | tf_op jit(solution)/shard_map/pallas_call | solution.py:173
  106.4 1.5 %collective-permute-done.29.refs_9_ = bf16[512,640]{1,0:T(8,128)(2,1)} collective-permute-done((bf16[512,640]{1,0:T(8,128)(2,1)}, bf16[512,640]{1,0:T(8,128)(2,1)}, u32[]{:S(2)}, u32[]{:S(2)}) %collective-permute-start.29) | collective-permute-done | bytes 655392 | tf_op jit(solution)/shard_map/ppermute | solution.py:272
  107.8 3.9 %shard_map.113 = (f32[256,640]{1,0:T(8,128)S(1)}, f32[256,640]{1,0:T(8,128)S(1)}, bf16[256,640]{1,0:T(8,128)(2,1)}, bf16[128,640]{1,0:T(8,128)(2,1)S(1)}, bf16[128,640]{1,0:T(8,128)(2,1)S(1)}) custom-call(s32[1]{0:T(128)} %bitcast.2.flip_ref, bf16[2,256,640]{2,1,0:T(8,128)(2,1)S(1)} %shard_map.105.refs_0_, bf16[2,256,384]{2,1,0:T(8,128)(2,1)S(1)} %shard_map.106.refs_1_, ...), custom_call_target="tpu_custom_call" | custom-call | flops 1 | bytes 1 | tf_op jit(solution)/shard_map/pallas_call | solution.py:173
  113.5 1.6 %collective-permute-start.35 = (bf16[256,640]{1,0:T(8,128)(2,1)S(1)}, bf16[256,640]{1,0:T(8,128)(2,1)S(1)}, u32[]{:S(2)}, u32[]{:S(2)}) collective-permute-start(bf16[256,640]{1,0:T(8,128)(2,1)S(1)} %shard_map.114), channel_id=1, source_target_pairs={{0,4},{4,0},{8,12},{12,8},{16,20},{20,16},{24,28},{28,24},{1,5},{5... | collective-permute-start | bytes 983048 | tf_op jit(solution)/shard_map/ppermute | solution.py:278
  115.2 4.0 %collective-permute-done.18.refs_8_ = bf16[384,640]{1,0:T(8,128)(2,1)S(1)} collective-permute-done((bf16[384,640]{1,0:T(8,128)(2,1)}, bf16[384,640]{1,0:T(8,128)(2,1)S(1)}, u32[]{:S(2)}, u32[]{:S(2)}) %collective-permute-start.18) | collective-permute-done | bytes 491552 | tf_op jit(solution)/shard_map/ppermute | solution.py:281
  119.1 3.8 %shard_map.116 = (f32[256,640]{1,0:T(8,128)S(1)}, f32[256,640]{1,0:T(8,128)S(1)}, bf16[256,640]{1,0:T(8,128)(2,1)}, bf16[128,640]{1,0:T(8,128)(2,1)S(1)}, bf16[128,640]{1,0:T(8,128)(2,1)S(1)}) custom-call(s32[1]{0:T(128)} %bitcast.2.flip_ref, bf16[2,256,640]{2,1,0:T(8,128)(2,1)S(1)} %shard_map.105.refs_0_, bf16[2,256,384]{2,1,0:T(8,128)(2,1)S(1)} %shard_map.106.refs_1_, ...), custom_call_target="tpu_custom_call" | custom-call | flops 1 | bytes 1 | tf_op jit(solution)/shard_map/pallas_call | solution.py:173
  127.6 1.4 %shard_map.120 = (bf16[128,5120]{1,0:T(8,128)(2,1)}, bf16[128,5120]{1,0:T(8,128)(2,1)}) custom-call(s32[2]{0:T(128)S(1)} %add_add_fusion.3.where_ref, bf16[256,640]{1,0:T(8,128)(2,1)S(1)} %shard_map.112.mine_ref, bf16[256,640]{1,0:T(8,128)(2,1)S(1)} %copy-done.22), custom_call_target="tpu_custom_call" | custom-call | flops 1 | bytes 1 | tf_op jit(solution)/shard_map/pallas_call | solution.py:231
  132.1 4.0 %collective-permute-done.37.other_ref = bf16[256,640]{1,0:T(8,128)(2,1)S(1)} collective-permute-done((bf16[256,640]{1,0:T(8,128)(2,1)S(1)}, bf16[256,640]{1,0:T(8,128)(2,1)S(1)}, u32[]{:S(2)}, u32[]{:S(2)}) %collective-permute-start.37) | collective-permute-done | bytes 327712 | tf_op jit(solution)/shard_map/ppermute | solution.py:278
  (138 shorter events, 31.9 us)
Async XLA Ops:
  2.6 14.4 %collective-permute-start = (bf16[384,640]{1,0:T(8,128)(2,1)}, bf16[384,640]{1,0:T(8,128)(2,1)S(1)}, u32[]{:S(2)}, u32[]{:S(2)}) collective-permute-start(bf16[384,640]{1,0:T(8,128)(2,1)} %slice.6), channel_id=1, source_target_pairs={{0,2},{1,3},{2,0},{3,1},{4,6},{5,7},{6,4},{7,5},{8,10},{9,11},{10,... | collective-permute-start | bytes 1474568 | tf_op jit(solution)/shard_map/ppermute | solution.py:272
  7.3 11.3 %collective-permute-start.2 = (bf16[256,640]{1,0:T(8,128)(2,1)}, bf16[256,640]{1,0:T(8,128)(2,1)}, u32[]{:S(2)}, u32[]{:S(2)}) collective-permute-start(bf16[256,640]{1,0:T(8,128)(2,1)} %slice.7), channel_id=1, source_target_pairs={{0,8},{4,12},{8,16},{12,20},{16,24},{20,28},{24,0},{28,4},{1,9},{5... | collective-permute-start | bytes 983048 | tf_op jit(solution)/shard_map/ppermute | solution.py:281
  18.6 2.1 %collective-permute-start.9 = (bf16[4,128,640]{2,1,0:T(8,128)(2,1)S(1)}, bf16[4,128,640]{2,1,0:T(8,128)(2,1)S(1)}, u32[]{:S(2)}, u32[]{:S(2)}) collective-permute-start(bf16[4,128,640]{2,1,0:T(8,128)(2,1)S(1)} %get-tuple-element.226), channel_id=1, source_target_pairs={{0,1},{1,0},{2,3},{3,2},{4,5},{5,4},{6,7},{7,6},{8,9},{9,8},{10,11... | collective-permute-start | bytes 1966088 | tf_op jit(solution)/shard_map/ppermute | solution.py:275
  18.6 13.7 %collective-permute-start.6 = (bf16[2,128,1280]{2,1,0:T(8,128)(2,1)S(1)}, bf16[2,128,1280]{2,1,0:T(8,128)(2,1)S(1)}, u32[]{:S(2)}, u32[]{:S(2)}) collective-permute-start(bf16[2,128,1280]{2,1,0:T(8,128)(2,1)S(1)} %get-tuple-element.217), channel_id=1, source_target_pairs={{0,1},{1,0},{2,3},{3,2},{4,5},{5,4},{6,7},{7,6},{8,9},{9,8},{10,11... | collective-permute-start | bytes 1966088 | tf_op jit(solution)/shard_map/ppermute | solution.py:275
  19.2 4.0 %collective-permute-start.8 = (bf16[4,128,384]{2,1,0:T(8,128)(2,1)S(1)}, bf16[4,128,384]{2,1,0:T(8,128)(2,1)S(1)}, u32[]{:S(2)}, u32[]{:S(2)}) collective-permute-start(bf16[4,128,384]{2,1,0:T(8,128)(2,1)S(1)} %get-tuple-element.225), channel_id=1, source_target_pairs={{0,1},{1,0},{2,3},{3,2},{4,5},{5,4},{6,7},{7,6},{8,9},{9,8},{10,11... | collective-permute-start | bytes 1179656 | tf_op jit(solution)/shard_map/ppermute | solution.py:275
  19.2 3.5 %collective-permute-start.7 = (bf16[4,128,256]{2,1,0:T(8,128)(2,1)S(1)}, bf16[4,128,256]{2,1,0:T(8,128)(2,1)S(1)}, u32[]{:S(2)}, u32[]{:S(2)}) collective-permute-start(bf16[4,128,256]{2,1,0:T(8,128)(2,1)S(1)} %get-tuple-element.224), channel_id=1, source_target_pairs={{0,1},{1,0},{2,3},{3,2},{4,5},{5,4},{6,7},{7,6},{8,9},{9,8},{10,11... | collective-permute-start | bytes 786440 | tf_op jit(solution)/shard_map/ppermute | solution.py:275
  19.7 12.6 %collective-permute-start.5 = (bf16[256,640]{1,0:T(8,128)(2,1)}, bf16[256,640]{1,0:T(8,128)(2,1)S(1)}, u32[]{:S(2)}, u32[]{:S(2)}) collective-permute-start(bf16[256,640]{1,0:T(8,128)(2,1)} %collective-permute-done.2.refs_7_), channel_id=1, source_target_pairs={{0,8},{4,12},{8,16},{12,20},{16,24},{20,28},{24,0},{28,4},{1,9},{5... | collective-permute-start | bytes 983048 | tf_op jit(solution)/shard_map/ppermute | solution.py:281
  20.7 22.1 %collective-permute-start.3 = (bf16[4,128,640]{2,1,0:T(8,128)(2,1)S(1)}, bf16[4,128,640]{2,1,0:T(8,128)(2,1)S(1)}, u32[]{:S(2)}, u32[]{:S(2)}) collective-permute-start(bf16[4,128,640]{2,1,0:T(8,128)(2,1)S(1)} %get-tuple-element.209.refs_2_), channel_id=1, source_target_pairs={{0,2},{1,3},{2,0},{3,1},{4,6},{5,7},{6,4},{7,5},{8,10},{9,11},{10,... | collective-permute-start | bytes 1966088 | tf_op jit(solution)/shard_map/ppermute | solution.py:272
  22.6 30.7 %collective-permute-start.14 = (bf16[4,128,640]{2,1,0:T(8,128)(2,1)S(1)}, bf16[4,128,640]{2,1,0:T(8,128)(2,1)S(1)}, u32[]{:S(2)}, u32[]{:S(2)}) collective-permute-start(bf16[4,128,640]{2,1,0:T(8,128)(2,1)S(1)} %collective-permute-done.9.refs_3_), channel_id=1, source_target_pairs={{0,2},{1,3},{2,0},{3,1},{4,6},{5,7},{6,4},{7,5},{8,10},{9,11},{10,... | collective-permute-start | bytes 1966088 | tf_op jit(solution)/shard_map/ppermute | solution.py:272
  23.2 19.6 %collective-permute-start.4 = (bf16[384,640]{1,0:T(8,128)(2,1)}, bf16[384,640]{1,0:T(8,128)(2,1)S(1)}, u32[]{:S(2)}, u32[]{:S(2)}) collective-permute-start(bf16[384,640]{1,0:T(8,128)(2,1)} %slice.6), channel_id=1, source_target_pairs={{0,8},{4,12},{8,16},{12,20},{16,24},{20,28},{24,0},{28,4},{1,9},{5... | collective-permute-start | bytes 1474568 | tf_op jit(solution)/shard_map/ppermute | solution.py:281
  32.3 21.1 %collective-permute-start.1 = (bf16[384,640]{1,0:T(8,128)(2,1)S(1)}, bf16[384,640]{1,0:T(8,128)(2,1)S(1)}, u32[]{:S(2)}, u32[]{:S(2)}) collective-permute-start(bf16[384,640]{1,0:T(8,128)(2,1)S(1)} %collective-permute-done.refs_7_), channel_id=1, source_target_pairs={{0,8},{4,12},{8,16},{12,20},{16,24},{20,28},{24,0},{28,4},{1,9},{5... | collective-permute-start | bytes 1474568 | tf_op jit(solution)/shard_map/ppermute | solution.py:281
  32.4 38.5 %collective-permute-start.11 = (bf16[8,128,384]{2,1,0:T(8,128)(2,1)S(1)}, bf16[8,128,384]{2,1,0:T(8,128)(2,1)S(1)}, u32[]{:S(2)}, u32[]{:S(2)}) collective-permute-start(bf16[8,128,384]{2,1,0:T(8,128)(2,1)S(1)} %pad_maximum_fusion), channel_id=1, source_target_pairs={{0,2},{1,3},{2,0},{3,1},{4,6},{5,7},{6,4},{7,5},{8,10},{9,11},{10,... | collective-permute-start | bytes 2359304 | tf_op jit(solution)/shard_map/ppermute | solution.py:272
  42.8 28.1 %collective-permute-start.12 = (bf16[384,640]{1,0:T(8,128)(2,1)S(1)}, bf16[384,640]{1,0:T(8,128)(2,1)}, u32[]{:S(2)}, u32[]{:S(2)}) collective-permute-start(bf16[384,640]{1,0:T(8,128)(2,1)S(1)} %collective-permute-done.4.refs_6_), channel_id=1, source_target_pairs={{0,8},{4,12},{8,16},{12,20},{16,24},{20,28},{24,0},{28,4},{1,9},{5... | collective-permute-start | bytes 1474568 | tf_op jit(solution)/shard_map/ppermute | solution.py:281
  42.8 27.1 %collective-permute-start.13 = (bf16[256,640]{1,0:T(8,128)(2,1)S(1)}, bf16[256,640]{1,0:T(8,128)(2,1)S(1)}, u32[]{:S(2)}, u32[]{:S(2)}) collective-permute-start(bf16[256,640]{1,0:T(8,128)(2,1)S(1)} %collective-permute-done.5.refs_7_), channel_id=1, source_target_pairs={{0,8},{4,12},{8,16},{12,20},{16,24},{20,28},{24,0},{28,4},{1,9},{5... | collective-permute-start | bytes 983048 | tf_op jit(solution)/shard_map/ppermute | solution.py:281
  58.0 17.8 %collective-permute-start.17 = (bf16[2,256,640]{2,1,0:T(8,128)(2,1)S(1)}, bf16[2,256,640]{2,1,0:T(8,128)(2,1)S(1)}, u32[]{:S(2)}, u32[]{:S(2)}) collective-permute-start(bf16[2,256,640]{2,1,0:T(8,128)(2,1)S(1)} %shard_map.105.refs_0_), channel_id=1, source_target_pairs={{0,4},{4,0},{8,12},{12,8},{16,20},{20,16},{24,28},{28,24},{1,5},{5... | collective-permute-start | bytes 1966088 | tf_op jit(solution)/shard_map/ppermute | solution.py:278
  59.7 20.8 %collective-permute-start.16 = (bf16[8,128,256]{2,1,0:T(8,128)(2,1)S(1)}, bf16[8,128,256]{2,1,0:T(8,128)(2,1)S(1)}, u32[]{:S(2)}, u32[]{:S(2)}) collective-permute-start(bf16[8,128,256]{2,1,0:T(8,128)(2,1)S(1)} %pad_maximum_fusion.2), channel_id=1, source_target_pairs={{0,2},{1,3},{2,0},{3,1},{4,6},{5,7},{6,4},{7,5},{8,10},{9,11},{10,... | collective-permute-start | bytes 1572872 | tf_op jit(solution)/shard_map/ppermute | solution.py:272
  69.9 16.1 %collective-permute-start.10 = (bf16[384,640]{1,0:T(8,128)(2,1)S(1)}, bf16[384,640]{1,0:T(8,128)(2,1)}, u32[]{:S(2)}, u32[]{:S(2)}) collective-permute-start(bf16[384,640]{1,0:T(8,128)(2,1)S(1)} %collective-permute-done.1.refs_8_), channel_id=1, source_target_pairs={{0,8},{4,12},{8,16},{12,20},{16,24},{20,28},{24,0},{28,4},{1,9},{5... | collective-permute-start | bytes 1474568 | tf_op jit(solution)/shard_map/ppermute | solution.py:281
  73.7 10.5 %collective-permute-start.15 = (bf16[2,256,384]{2,1,0:T(8,128)(2,1)S(1)}, bf16[2,256,384]{2,1,0:T(8,128)(2,1)S(1)}, u32[]{:S(2)}, u32[]{:S(2)}) collective-permute-start(bf16[2,256,384]{2,1,0:T(8,128)(2,1)S(1)} %shard_map.106.refs_1_), channel_id=1, source_target_pairs={{0,4},{4,0},{8,12},{12,8},{16,20},{20,16},{24,28},{28,24},{1,5},{5... | collective-permute-start | bytes 1179656 | tf_op jit(solution)/shard_map/ppermute | solution.py:278
  75.3 12.7 %collective-permute-start.20 = (bf16[256,640]{1,0:T(8,128)(2,1)}, bf16[256,640]{1,0:T(8,128)(2,1)}, u32[]{:S(2)}, u32[]{:S(2)}) collective-permute-start(bf16[256,640]{1,0:T(8,128)(2,1)} %slice.7), channel_id=1, source_target_pairs={{0,2},{1,3},{2,0},{3,1},{4,6},{5,7},{6,4},{7,5},{8,10},{9,11},{10,... | collective-permute-start | bytes 983048 | tf_op jit(solution)/shard_map/ppermute | solution.py:272
  75.8 18.8 %collective-permute-start.23 = (bf16[384,640]{1,0:T(8,128)(2,1)}, bf16[384,640]{1,0:T(8,128)(2,1)}, u32[]{:S(2)}, u32[]{:S(2)}) collective-permute-start(bf16[384,640]{1,0:T(8,128)(2,1)} %collective-permute-done.12.refs_6_), channel_id=1, source_target_pairs={{0,8},{4,12},{8,16},{12,20},{16,24},{20,28},{24,0},{28,4},{1,9},{5... | collective-permute-start | bytes 1474568 | tf_op jit(solution)/shard_map/ppermute | solution.py:281
  82.3 7.2 %collective-permute-start.19 = (bf16[2,256,256]{2,1,0:T(8,128)(2,1)S(1)}, bf16[2,256,256]{2,1,0:T(8,128)(2,1)S(1)}, u32[]{:S(2)}, u32[]{:S(2)}) collective-permute-start(bf16[2,256,256]{2,1,0:T(8,128)(2,1)S(1)} %shard_map.107.refs_2_), channel_id=1, source_target_pairs={{0,4},{4,0},{8,12},{12,8},{16,20},{20,16},{24,28},{28,24},{1,5},{5... | collective-permute-start | bytes 786440 | tf_op jit(solution)/shard_map/ppermute | solution.py:278
  86.0 11.0 %collective-permute-start.22 = (bf16[256,640]{1,0:T(8,128)(2,1)}, bf16[256,640]{1,0:T(8,128)(2,1)}, u32[]{:S(2)}, u32[]{:S(2)}) collective-permute-start(bf16[256,640]{1,0:T(8,128)(2,1)} %collective-permute-done.2.refs_7_), channel_id=1, source_target_pairs={{0,2},{1,3},{2,0},{3,1},{4,6},{5,7},{6,4},{7,5},{8,10},{9,11},{10,... | collective-permute-start | bytes 983048 | tf_op jit(solution)/shard_map/ppermute | solution.py:272
  86.5 21.3 %collective-permute-start.29 = (bf16[512,640]{1,0:T(8,128)(2,1)}, bf16[512,640]{1,0:T(8,128)(2,1)}, u32[]{:S(2)}, u32[]{:S(2)}) collective-permute-start(bf16[512,640]{1,0:T(8,128)(2,1)} %pad_maximum_fusion.1), channel_id=1, source_target_pairs={{0,2},{1,3},{2,0},{3,1},{4,6},{5,7},{6,4},{7,5},{8,10},{9,11},{10,... | collective-permute-start | bytes 1966088 | tf_op jit(solution)/shard_map/ppermute | solution.py:272
  93.9 3.0 %collective-permute-start.21 = (bf16[128,640]{1,0:T(8,128)(2,1)S(1)}, bf16[128,640]{1,0:T(8,128)(2,1)S(1)}, u32[]{:S(2)}, u32[]{:S(2)}) collective-permute-start(bf16[128,640]{1,0:T(8,128)(2,1)S(1)} %get-tuple-element.277), channel_id=1, source_target_pairs={{0,1},{1,0},{2,3},{3,2},{4,5},{5,4},{6,7},{7,6},{8,9},{9,8},{10,11... | collective-permute-start | bytes 491528 | tf_op jit(solution)/shard_map/ppermute | solution.py:275
  94.0 3.0 %collective-permute-start.24 = (bf16[128,640]{1,0:T(8,128)(2,1)S(1)}, bf16[128,640]{1,0:T(8,128)(2,1)S(1)}, u32[]{:S(2)}, u32[]{:S(2)}) collective-permute-start(bf16[128,640]{1,0:T(8,128)(2,1)S(1)} %get-tuple-element.288), channel_id=1, source_target_pairs={{0,1},{1,0},{2,3},{3,2},{4,5},{5,4},{6,7},{7,6},{8,9},{9,8},{10,11... | collective-permute-start | bytes 491528 | tf_op jit(solution)/shard_map/ppermute | solution.py:275
  97.0 8.6 %collective-permute-start.31 = (bf16[256,640]{1,0:T(8,128)(2,1)S(1)}, bf16[256,640]{1,0:T(8,128)(2,1)S(1)}, u32[]{:S(2)}, u32[]{:S(2)}) collective-permute-start(bf16[256,640]{1,0:T(8,128)(2,1)S(1)} %shard_map.109), channel_id=1, source_target_pairs={{0,4},{4,0},{8,12},{12,8},{16,20},{20,16},{24,28},{28,24},{1,5},{5... | collective-permute-start | bytes 983048 | tf_op jit(solution)/shard_map/ppermute | solution.py:278
  98.6 7.0 %collective-permute-start.30 = (bf16[256,640]{1,0:T(8,128)(2,1)S(1)}, bf16[256,640]{1,0:T(8,128)(2,1)S(1)}, u32[]{:S(2)}, u32[]{:S(2)}) collective-permute-start(bf16[256,640]{1,0:T(8,128)(2,1)S(1)} %get-tuple-element.317), channel_id=1, source_target_pairs={{0,1},{1,0},{2,3},{3,2},{4,5},{5,4},{6,7},{7,6},{8,9},{9,8},{10,11... | collective-permute-start | bytes 983048 | tf_op jit(solution)/shard_map/ppermute | solution.py:275
  103.6 15.5 %collective-permute-start.18 = (bf16[384,640]{1,0:T(8,128)(2,1)}, bf16[384,640]{1,0:T(8,128)(2,1)S(1)}, u32[]{:S(2)}, u32[]{:S(2)}) collective-permute-start(bf16[384,640]{1,0:T(8,128)(2,1)} %collective-permute-done.10.refs_8_), channel_id=1, source_target_pairs={{0,8},{4,12},{8,16},{12,20},{16,24},{20,28},{24,0},{28,4},{1,9},{5... | collective-permute-start | bytes 1474568 | tf_op jit(solution)/shard_map/ppermute | solution.py:281
  104.1 11.0 %collective-permute-start.28 = (bf16[256,640]{1,0:T(8,128)(2,1)S(1)}, bf16[256,640]{1,0:T(8,128)(2,1)S(1)}, u32[]{:S(2)}, u32[]{:S(2)}) collective-permute-start(bf16[256,640]{1,0:T(8,128)(2,1)S(1)} %shard_map.111), channel_id=1, source_target_pairs={{0,4},{4,0},{8,12},{12,8},{16,20},{20,16},{24,28},{28,24},{1,5},{5... | collective-permute-start | bytes 983048 | tf_op jit(solution)/shard_map/ppermute | solution.py:278
  105.7 9.4 %collective-permute-start.27 = (bf16[256,640]{1,0:T(8,128)(2,1)S(1)}, bf16[256,640]{1,0:T(8,128)(2,1)S(1)}, u32[]{:S(2)}, u32[]{:S(2)}) collective-permute-start(bf16[256,640]{1,0:T(8,128)(2,1)S(1)} %get-tuple-element.311), channel_id=1, source_target_pairs={{0,1},{1,0},{2,3},{3,2},{4,5},{5,4},{6,7},{7,6},{8,9},{9,8},{10,11... | collective-permute-start | bytes 983048 | tf_op jit(solution)/shard_map/ppermute | solution.py:275
  113.5 10.8 %collective-permute-start.35 = (bf16[256,640]{1,0:T(8,128)(2,1)S(1)}, bf16[256,640]{1,0:T(8,128)(2,1)S(1)}, u32[]{:S(2)}, u32[]{:S(2)}) collective-permute-start(bf16[256,640]{1,0:T(8,128)(2,1)S(1)} %shard_map.114), channel_id=1, source_target_pairs={{0,4},{4,0},{8,12},{12,8},{16,20},{20,16},{24,28},{28,24},{1,5},{5... | collective-permute-start | bytes 983048 | tf_op jit(solution)/shard_map/ppermute | solution.py:278
  126.2 9.9 %collective-permute-start.37 = (bf16[256,640]{1,0:T(8,128)(2,1)S(1)}, bf16[256,640]{1,0:T(8,128)(2,1)S(1)}, u32[]{:S(2)}, u32[]{:S(2)}) collective-permute-start(bf16[256,640]{1,0:T(8,128)(2,1)S(1)} %shard_map.117), channel_id=1, source_target_pairs={{0,4},{4,0},{8,12},{12,8},{16,20},{20,16},{24,28},{28,24},{1,5},{5... | collective-permute-start | bytes 983048 | tf_op jit(solution)/shard_map/ppermute | solution.py:278
  (37 other events, 224.4 us)

commit v10 on v9

--- a/solution.py
+++ b/solution.py
@@ -379,18 +379,18 @@
     send(0)
     columns(1)
     send(1)
-    stay(0)
     for step in range(2, n_ring, 2):
         rest[1 + step // 2] = wait(rest[1 + step // 2])
         if step > 2:
             turn(beside, step)
+        turn(beside, step + 1)
         columns(step)
         send(step)
+        stay(step - 2)
         stay(step - 1)
-        turn(beside, step + 1)
         columns(step + 1)
         send(step + 1)
-        stay(step)
+    stay(n_ring - 2)
     stay(n_ring - 1)
     for step in range(n_ring - 1):
         outs = [wait(out) for out in put(step)]

time: 138 us -> 139 us (level)
  waiting for transfers between devices: 67.2 us -> 65.7 us
    ppermute x7, waiting for transfers between devices: 6.83 us -> 8.98 us  [across(): return lax.ppermute(array, 'dp', [(i, i ^ 1) for i in range(n_dp)])]
    ppermute x9, waiting for transfers between devices: 45.4 us -> 43.3 us  [onward(): return lax.ppermute(array, 'dp', [(i, (i + 2) % n_dp) for i in range(n_dp)])]
    ppermute x16, waiting for transfers between devices: 5.89 us -> 4.3 us  [near(): return lax.ppermute(array, 'seq', [(i, i ^ 1) for i in range(n_seq)])]
  transfers between devices with their start and end apart: 40 -> 40, of which waited for: 26 -> 23; matrix products, arithmetic and copies ran while one was open for 2% -> 2% of each run, Pallas kernels for 22% -> 22%
where the time goes in v10:
time: 139 us; the launch traced here: 138 us
  waiting for transfers between devices  65.7 us (47%)
  Pallas kernels  32.1 us (23%)
  starting transfers between devices  25.2 us (18%)
  local copies, waits for them, and re-layouts  12.4 us (9%)
  other arithmetic  1.4 us (1%)
    ppermute x9, waiting for transfers between devices, onward(): return lax.ppermute(array, 'dp', [(i, (i + 2) % n_dp) for i in range(n_dp)])  43.3 us
    pallas_call x4, Pallas kernels, project(): pl.pallas_call(functools.partial(project_kernel, len(acts), spans), in_sp...  14.4 us
    ppermute x7, starting transfers between devices, across(): return lax.ppermute(array, 'dp', [(i, i ^ 1) for i in range(n_dp)])  10.1 us
    pallas_call x3, Pallas kernels, attend(): pl.pallas_call(functools.partial(attend_kernel, len(queries)), grid=(widt...  9.36 us
    ppermute x8, waiting for transfers between devices, far(): return lax.ppermute(array, 'seq', [(i, i ^ 2) for i in range(n_seq)])  9.06 us
    ppermute x7, waiting for transfers between devices, across(): return lax.ppermute(array, 'dp', [(i, i ^ 1) for i in range(n_dp)])  8.98 us
    ppermute x8, starting transfers between devices, far(): return lax.ppermute(array, 'seq', [(i, i ^ 2) for i in range(n_seq)])  8.77 us
    unnamed x58, local copies, waits for them, and re-layouts  8.68 us
  transfers between devices with their start and end apart: 40, of which 23 were waited for; matrix products, arithmetic and copies ran while one was open for 2% of the time, Pallas kernels for 22%

profile of v10, /device:TPU:0, one launch (start us, length us, event | category | flops | bytes accessed | tf_op | source)
XLA Modules:
  0.0 138.0 jit_solution(14081711979886246694)
XLA Ops:
  0.7 2.0 %slice.7 = bf16[384,640]{1,0:T(8,128)(2,1)} slice(bf16[640,640]{1,0:T(8,128)(2,1)} %refs_6_.1), slice={[0:384], [0:640]} | slice | bytes 983040 | tf_op jit(solution)/shard_map/slice | solution.py:298
  2.6 2.9 %collective-permute-start.1 = (bf16[384,640]{1,0:T(8,128)(2,1)}, bf16[384,640]{1,0:T(8,128)(2,1)S(1)}, u32[]{:S(2)}, u32[]{:S(2)}) collective-permute-start(bf16[384,640]{1,0:T(8,128)(2,1)} %slice.7), channel_id=1, source_target_pairs={{0,2},{1,3},{2,0},{3,1},{4,6},{5,7},{6,4},{7,5},{8,10},{9,11},{10,... | collective-permute-start | bytes 1474568 | tf_op jit(solution)/shard_map/ppermute | solution.py:272
  5.6 1.7 %slice.6 = bf16[256,640]{1,0:T(8,128)(2,1)} slice(bf16[640,640]{1,0:T(8,128)(2,1)} %refs_6_.1), slice={[384:640], [0:640]} | slice | bytes 655360 | tf_op jit(solution)/shard_map/slice | solution.py:298
  7.3 1.6 %collective-permute-start = (bf16[256,640]{1,0:T(8,128)(2,1)}, bf16[256,640]{1,0:T(8,128)(2,1)}, u32[]{:S(2)}, u32[]{:S(2)}) collective-permute-start(bf16[256,640]{1,0:T(8,128)(2,1)} %slice.6), channel_id=1, source_target_pairs={{0,8},{4,12},{8,16},{12,20},{16,24},{20,28},{24,0},{28,4},{1,9},{5... | collective-permute-start | bytes 983048 | tf_op jit(solution)/shard_map/ppermute | solution.py:281
  13.3 2.0 %shard_map.104 = (bf16[2,128,1280]{2,1,0:T(8,128)(2,1)S(1)}, bf16[4,128,640]{2,1,0:T(8,128)(2,1)S(1)}, bf16[4,128,384]{2,1,0:T(8,128)(2,1)S(1)}, bf16[4,128,256]...) custom-call(s32[1]{0:T(128)} %bitcast.3.core_ref, ...), custom_call_target="tpu_custom_call" | custom-call | flops 1 | bytes 1 | tf_op jit(solution)/shard_map/pallas_call | solution.py:78
  15.4 1.6 %collective-permute-done.1.refs_7_ = bf16[384,640]{1,0:T(8,128)(2,1)S(1)} collective-permute-done((bf16[384,640]{1,0:T(8,128)(2,1)}, bf16[384,640]{1,0:T(8,128)(2,1)S(1)}, u32[]{:S(2)}, u32[]{:S(2)}) %collective-permute-start.1) | collective-permute-done | bytes 491552 | tf_op jit(solution)/shard_map/ppermute | solution.py:272
  17.0 1.7 %collective-permute-done.refs_7_ = bf16[256,640]{1,0:T(8,128)(2,1)} collective-permute-done((bf16[256,640]{1,0:T(8,128)(2,1)}, bf16[256,640]{1,0:T(8,128)(2,1)}, u32[]{:S(2)}, u32[]{:S(2)}) %collective-permute-start) | collective-permute-done | bytes 327712 | tf_op jit(solution)/shard_map/ppermute | solution.py:281
  24.3 8.0 %collective-permute-done.9.refs_7_ = bf16[256,640]{1,0:T(8,128)(2,1)S(1)} collective-permute-done((bf16[256,640]{1,0:T(8,128)(2,1)}, bf16[256,640]{1,0:T(8,128)(2,1)S(1)}, u32[]{:S(2)}, u32[]{:S(2)}) %collective-permute-start.9) | collective-permute-done | bytes 327712 | tf_op jit(solution)/shard_map/ppermute | solution.py:281
  33.0 9.8 %collective-permute-done.8.refs_6_ = bf16[384,640]{1,0:T(8,128)(2,1)S(1)} collective-permute-done((bf16[384,640]{1,0:T(8,128)(2,1)}, bf16[384,640]{1,0:T(8,128)(2,1)S(1)}, u32[]{:S(2)}, u32[]{:S(2)}) %collective-permute-start.8) | collective-permute-done | bytes 491552 | tf_op jit(solution)/shard_map/ppermute | solution.py:281
  42.9 10.5 %collective-permute-done.11.refs_8_ = bf16[384,640]{1,0:T(8,128)(2,1)S(1)} collective-permute-done((bf16[384,640]{1,0:T(8,128)(2,1)S(1)}, bf16[384,640]{1,0:T(8,128)(2,1)S(1)}, u32[]{:S(2)}, u32[]{:S(2)}) %collective-permute-start.11) | collective-permute-done | bytes 491552 | tf_op jit(solution)/shard_map/ppermute | solution.py:281
  53.3 4.7 %shard_map.105.refs_0_ = bf16[2,256,640]{2,1,0:T(8,128)(2,1)S(1)} custom-call(bf16[2,128,1280]{2,1,0:T(8,128)(2,1)S(1)} %get-tuple-element.206.refs_0_, bf16[2,128,1280]{2,1,0:T(8,128)(2,1)S(1)} %collective-permute-done.2.refs_1_, bf16[4,128,640]{2,1,0:T(8,128)(2,1)S(1)} %get-tuple-element.232.refs_2_, ...), custom_call_target="tpu_custom_call" | custom-call | flops 1 | bytes 1 | tf_op jit(solution)/shard_map/pallas_call | solution.py:129
  58.0 1.6 %collective-permute-start.12 = (bf16[2,256,640]{2,1,0:T(8,128)(2,1)S(1)}, bf16[2,256,640]{2,1,0:T(8,128)(2,1)S(1)}, u32[]{:S(2)}, u32[]{:S(2)}) collective-permute-start(bf16[2,256,640]{2,1,0:T(8,128)(2,1)S(1)} %shard_map.105.refs_0_), channel_id=1, source_target_pairs={{0,4},{4,0},{8,12},{12,8},{16,20},{20,16},{24,28},{28,24},{1,5},{5... | collective-permute-start | bytes 1966088 | tf_op jit(solution)/shard_map/ppermute | solution.py:278
  60.3 9.7 %collective-permute-done.15.refs_7_ = bf16[256,640]{1,0:T(8,128)(2,1)S(1)} collective-permute-done((bf16[256,640]{1,0:T(8,128)(2,1)S(1)}, bf16[256,640]{1,0:T(8,128)(2,1)S(1)}, u32[]{:S(2)}, u32[]{:S(2)}) %collective-permute-start.15) | collective-permute-done | bytes 327712 | tf_op jit(solution)/shard_map/ppermute | solution.py:281
  70.9 2.8 %shard_map.106.refs_1_ = bf16[2,256,384]{2,1,0:T(8,128)(2,1)S(1)} custom-call(bf16[2,128,1280]{2,1,0:T(8,128)(2,1)S(1)} %get-tuple-element.206.refs_0_, bf16[2,128,1280]{2,1,0:T(8,128)(2,1)S(1)} %collective-permute-done.2.refs_1_, bf16[4,128,384]{2,1,0:T(8,128)(2,1)S(1)} %get-tuple-element.245.refs_2_, ...), custom_call_target="tpu_custom_call" | custom-call | flops 1 | bytes 1 | tf_op jit(solution)/shard_map/pallas_call | solution.py:129
  73.7 1.6 %collective-permute-start.19 = (bf16[2,256,384]{2,1,0:T(8,128)(2,1)S(1)}, bf16[2,256,384]{2,1,0:T(8,128)(2,1)S(1)}, u32[]{:S(2)}, u32[]{:S(2)}) collective-permute-start(bf16[2,256,384]{2,1,0:T(8,128)(2,1)S(1)} %shard_map.106.refs_1_), channel_id=1, source_target_pairs={{0,4},{4,0},{8,12},{12,8},{16,20},{20,16},{24,28},{28,24},{1,5},{5... | collective-permute-start | bytes 1179656 | tf_op jit(solution)/shard_map/ppermute | solution.py:278
  76.8 3.7 %collective-permute-done.6.refs_4_ = bf16[8,128,256]{2,1,0:T(8,128)(2,1)S(1)} collective-permute-done((bf16[8,128,256]{2,1,0:T(8,128)(2,1)S(1)}, bf16[8,128,256]{2,1,0:T(8,128)(2,1)S(1)}, u32[]{:S(2)}, u32[]{:S(2)}) %collective-permute-start.6) | collective-permute-done | bytes 524320 | tf_op jit(solution)/shard_map/ppermute | solution.py:272
  80.5 1.9 %shard_map.107.refs_2_ = bf16[2,256,256]{2,1,0:T(8,128)(2,1)S(1)} custom-call(bf16[2,128,1280]{2,1,0:T(8,128)(2,1)S(1)} %get-tuple-element.206.refs_0_, bf16[2,128,1280]{2,1,0:T(8,128)(2,1)S(1)} %collective-permute-done.2.refs_1_, bf16[4,128,256]{2,1,0:T(8,128)(2,1)S(1)} %get-tuple-element.230.refs_2_, ...), custom_call_target="tpu_custom_call" | custom-call | flops 1 | bytes 1 | tf_op jit(solution)/shard_map/pallas_call | solution.py:129
  82.3 1.6 %collective-permute-start.16 = (bf16[2,256,256]{2,1,0:T(8,128)(2,1)S(1)}, bf16[2,256,256]{2,1,0:T(8,128)(2,1)S(1)}, u32[]{:S(2)}, u32[]{:S(2)}) collective-permute-start(bf16[2,256,256]{2,1,0:T(8,128)(2,1)S(1)} %shard_map.107.refs_2_), channel_id=1, source_target_pairs={{0,4},{4,0},{8,12},{12,8},{16,20},{20,16},{24,28},{28,24},{1,5},{5... | collective-permute-start | bytes 786440 | tf_op jit(solution)/shard_map/ppermute | solution.py:278
  84.2 1.8 %collective-permute-done.18.refs_8_ = bf16[384,640]{1,0:T(8,128)(2,1)} collective-permute-done((bf16[384,640]{1,0:T(8,128)(2,1)S(1)}, bf16[384,640]{1,0:T(8,128)(2,1)}, u32[]{:S(2)}, u32[]{:S(2)}) %collective-permute-start.18) | collective-permute-done | bytes 491552 | tf_op jit(solution)/shard_map/ppermute | solution.py:281
  86.5 1.5 %collective-permute-start.30 = (bf16[512,640]{1,0:T(8,128)(2,1)}, bf16[512,640]{1,0:T(8,128)(2,1)}, u32[]{:S(2)}, u32[]{:S(2)}) collective-permute-start(bf16[512,640]{1,0:T(8,128)(2,1)} %pad_maximum_fusion.1), channel_id=1, source_target_pairs={{0,2},{1,3},{2,0},{3,1},{4,6},{5,7},{6,4},{7,5},{8,10},{9,11},{10,... | collective-permute-start | bytes 1966088 | tf_op jit(solution)/shard_map/ppermute | solution.py:272
  88.0 1.6 %collective-permute-done.16.refs_5_ = bf16[2,256,256]{2,1,0:T(8,128)(2,1)S(1)} collective-permute-done((bf16[2,256,256]{2,1,0:T(8,128)(2,1)S(1)}, bf16[2,256,256]{2,1,0:T(8,128)(2,1)S(1)}, u32[]{:S(2)}, u32[]{:S(2)}) %collective-permute-start.16) | collective-permute-done | bytes 262176 | tf_op jit(solution)/shard_map/ppermute | solution.py:278
  90.6 3.3 %shard_map.108 = (f32[256,640]{1,0:T(8,128)S(1)}, f32[256,640]{1,0:T(8,128)S(1)}, bf16[256,640]{1,0:T(8,128)(2,1)S(1)}, bf16[128,640]{1,0:T(8,128)(2,1)S(1)}, bf16[128,640]{1,0:T(8,128)(2,1)S(1)}) custom-call(s32[1]{0:T(128)} %bitcast.2.flip_ref, bf16[2,256,640]{2,1,0:T(8,128)(2,1)S(1)} %shard_map.105.refs_0_, bf16[2,256,384]{2,1,0:T(8,128)(2,1)S(1)} %shard_map.106.refs_1_, ...), custom_call_target="tpu_custom_call" | custom-call | flops 1 | bytes 1 | tf_op jit(solution)/shard_map/pallas_call | solution.py:173
  94.6 2.3 %collective-permute-done.21.refs_9_ = bf16[256,640]{1,0:T(8,128)(2,1)} collective-permute-done((bf16[256,640]{1,0:T(8,128)(2,1)}, bf16[256,640]{1,0:T(8,128)(2,1)}, u32[]{:S(2)}, u32[]{:S(2)}) %collective-permute-start.21) | collective-permute-done | bytes 327712 | tf_op jit(solution)/shard_map/ppermute | solution.py:272
  97.0 1.6 %collective-permute-start.31 = (bf16[256,640]{1,0:T(8,128)(2,1)S(1)}, bf16[256,640]{1,0:T(8,128)(2,1)S(1)}, u32[]{:S(2)}, u32[]{:S(2)}) collective-permute-start(bf16[256,640]{1,0:T(8,128)(2,1)S(1)} %shard_map.109), channel_id=1, source_target_pairs={{0,4},{4,0},{8,12},{12,8},{16,20},{20,16},{24,28},{28,24},{1,5},{5... | collective-permute-start | bytes 983048 | tf_op jit(solution)/shard_map/ppermute | solution.py:278
  98.6 3.4 %shard_map.110 = (f32[256,640]{1,0:T(8,128)S(1)}, f32[256,640]{1,0:T(8,128)S(1)}, bf16[256,640]{1,0:T(8,128)(2,1)S(1)}, bf16[128,640]{1,0:T(8,128)(2,1)S(1)}, bf16[128,640]{1,0:T(8,128)(2,1)S(1)}) custom-call(s32[1]{0:T(128)} %bitcast.2.flip_ref, bf16[2,256,640]{2,1,0:T(8,128)(2,1)S(1)} %shard_map.105.refs_0_, bf16[2,256,384]{2,1,0:T(8,128)(2,1)S(1)} %shard_map.106.refs_1_, ...), custom_call_target="tpu_custom_call" | custom-call | flops 1 | bytes 1 | tf_op jit(solution)/shard_map/pallas_call | solution.py:173
  107.8 1.9 %collective-permute-done.29.refs_8_ = bf16[384,640]{1,0:T(8,128)(2,1)S(1)} collective-permute-done((bf16[384,640]{1,0:T(8,128)(2,1)}, bf16[384,640]{1,0:T(8,128)(2,1)S(1)}, u32[]{:S(2)}, u32[]{:S(2)}) %collective-permute-start.29) | collective-permute-done | bytes 491552 | tf_op jit(solution)/shard_map/ppermute | solution.py:281
  109.7 3.9 %shard_map.112 = (f32[256,640]{1,0:T(8,128)S(1)}, f32[256,640]{1,0:T(8,128)S(1)}, bf16[256,640]{1,0:T(8,128)(2,1)}, bf16[128,640]{1,0:T(8,128)(2,1)S(1)}, bf16[128,640]{1,0:T(8,128)(2,1)S(1)}) custom-call(s32[1]{0:T(128)} %bitcast.2.flip_ref, bf16[2,256,640]{2,1,0:T(8,128)(2,1)S(1)} %shard_map.105.refs_0_, bf16[2,256,384]{2,1,0:T(8,128)(2,1)S(1)} %shard_map.106.refs_1_, ...), custom_call_target="tpu_custom_call" | custom-call | flops 1 | bytes 1 | tf_op jit(solution)/shard_map/pallas_call | solution.py:173
  115.4 1.6 %collective-permute-start.35 = (bf16[256,640]{1,0:T(8,128)(2,1)S(1)}, bf16[256,640]{1,0:T(8,128)(2,1)S(1)}, u32[]{:S(2)}, u32[]{:S(2)}) collective-permute-start(bf16[256,640]{1,0:T(8,128)(2,1)S(1)} %shard_map.113), channel_id=1, source_target_pairs={{0,4},{4,0},{8,12},{12,8},{16,20},{20,16},{24,28},{28,24},{1,5},{5... | collective-permute-start | bytes 983048 | tf_op jit(solution)/shard_map/ppermute | solution.py:278
  118.1 3.8 %shard_map.116 = (f32[256,640]{1,0:T(8,128)S(1)}, f32[256,640]{1,0:T(8,128)S(1)}, bf16[256,640]{1,0:T(8,128)(2,1)}, bf16[128,640]{1,0:T(8,128)(2,1)S(1)}, bf16[128,640]{1,0:T(8,128)(2,1)S(1)}) custom-call(s32[1]{0:T(128)} %bitcast.2.flip_ref, bf16[2,256,640]{2,1,0:T(8,128)(2,1)S(1)} %shard_map.105.refs_0_, bf16[2,256,384]{2,1,0:T(8,128)(2,1)S(1)} %shard_map.106.refs_1_, ...), custom_call_target="tpu_custom_call" | custom-call | flops 1 | bytes 1 | tf_op jit(solution)/shard_map/pallas_call | solution.py:173
  123.2 2.1 %collective-permute-done.35.other_ref = bf16[256,640]{1,0:T(8,128)(2,1)S(1)} collective-permute-done((bf16[256,640]{1,0:T(8,128)(2,1)S(1)}, bf16[256,640]{1,0:T(8,128)(2,1)S(1)}, u32[]{:S(2)}, u32[]{:S(2)}) %collective-permute-start.35) | collective-permute-done | bytes 327712 | tf_op jit(solution)/shard_map/ppermute | solution.py:278
  126.4 1.6 %collective-permute-start.37 = (bf16[256,640]{1,0:T(8,128)(2,1)S(1)}, bf16[256,640]{1,0:T(8,128)(2,1)S(1)}, u32[]{:S(2)}, u32[]{:S(2)}) collective-permute-start(bf16[256,640]{1,0:T(8,128)(2,1)S(1)} %shard_map.117), channel_id=1, source_target_pairs={{0,4},{4,0},{8,12},{12,8},{16,20},{20,16},{24,28},{28,24},{1,5},{5... | collective-permute-start | bytes 983048 | tf_op jit(solution)/shard_map/ppermute | solution.py:278
  132.7 3.8 %collective-permute-done.37.other_ref = bf16[256,640]{1,0:T(8,128)(2,1)S(1)} collective-permute-done((bf16[256,640]{1,0:T(8,128)(2,1)S(1)}, bf16[256,640]{1,0:T(8,128)(2,1)S(1)}, u32[]{:S(2)}, u32[]{:S(2)}) %collective-permute-start.37) | collective-permute-done | bytes 327712 | tf_op jit(solution)/shard_map/ppermute | solution.py:278
  (138 shorter events, 33.6 us)
Async XLA Ops:
  2.6 14.4 %collective-permute-start.1 = (bf16[384,640]{1,0:T(8,128)(2,1)}, bf16[384,640]{1,0:T(8,128)(2,1)S(1)}, u32[]{:S(2)}, u32[]{:S(2)}) collective-permute-start(bf16[384,640]{1,0:T(8,128)(2,1)} %slice.7), channel_id=1, source_target_pairs={{0,2},{1,3},{2,0},{3,1},{4,6},{5,7},{6,4},{7,5},{8,10},{9,11},{10,... | collective-permute-start | bytes 1474568 | tf_op jit(solution)/shard_map/ppermute | solution.py:272
  7.3 11.3 %collective-permute-start = (bf16[256,640]{1,0:T(8,128)(2,1)}, bf16[256,640]{1,0:T(8,128)(2,1)}, u32[]{:S(2)}, u32[]{:S(2)}) collective-permute-start(bf16[256,640]{1,0:T(8,128)(2,1)} %slice.6), channel_id=1, source_target_pairs={{0,8},{4,12},{8,16},{12,20},{16,24},{20,28},{24,0},{28,4},{1,9},{5... | collective-permute-start | bytes 983048 | tf_op jit(solution)/shard_map/ppermute | solution.py:281
  18.6 13.7 %collective-permute-start.2 = (bf16[2,128,1280]{2,1,0:T(8,128)(2,1)S(1)}, bf16[2,128,1280]{2,1,0:T(8,128)(2,1)S(1)}, u32[]{:S(2)}, u32[]{:S(2)}) collective-permute-start(bf16[2,128,1280]{2,1,0:T(8,128)(2,1)S(1)} %get-tuple-element.215), channel_id=1, source_target_pairs={{0,1},{1,0},{2,3},{3,2},{4,5},{5,4},{6,7},{7,6},{8,9},{9,8},{10,11... | collective-permute-start | bytes 1966088 | tf_op jit(solution)/shard_map/ppermute | solution.py:275
  19.2 4.0 %collective-permute-start.4 = (bf16[4,128,384]{2,1,0:T(8,128)(2,1)S(1)}, bf16[4,128,384]{2,1,0:T(8,128)(2,1)S(1)}, u32[]{:S(2)}, u32[]{:S(2)}) collective-permute-start(bf16[4,128,384]{2,1,0:T(8,128)(2,1)S(1)} %get-tuple-element.223), channel_id=1, source_target_pairs={{0,1},{1,0},{2,3},{3,2},{4,5},{5,4},{6,7},{7,6},{8,9},{9,8},{10,11... | collective-permute-start | bytes 1179656 | tf_op jit(solution)/shard_map/ppermute | solution.py:275
  19.2 3.5 %collective-permute-start.3 = (bf16[4,128,256]{2,1,0:T(8,128)(2,1)S(1)}, bf16[4,128,256]{2,1,0:T(8,128)(2,1)S(1)}, u32[]{:S(2)}, u32[]{:S(2)}) collective-permute-start(bf16[4,128,256]{2,1,0:T(8,128)(2,1)S(1)} %get-tuple-element.222), channel_id=1, source_target_pairs={{0,1},{1,0},{2,3},{3,2},{4,5},{5,4},{6,7},{7,6},{8,9},{9,8},{10,11... | collective-permute-start | bytes 786440 | tf_op jit(solution)/shard_map/ppermute | solution.py:275
  19.7 12.6 %collective-permute-start.9 = (bf16[256,640]{1,0:T(8,128)(2,1)}, bf16[256,640]{1,0:T(8,128)(2,1)S(1)}, u32[]{:S(2)}, u32[]{:S(2)}) collective-permute-start(bf16[256,640]{1,0:T(8,128)(2,1)} %collective-permute-done.refs_7_), channel_id=1, source_target_pairs={{0,8},{4,12},{8,16},{12,20},{16,24},{20,28},{24,0},{28,4},{1,9},{5... | collective-permute-start | bytes 983048 | tf_op jit(solution)/shard_map/ppermute | solution.py:281
  20.7 22.1 %collective-permute-start.7 = (bf16[4,128,640]{2,1,0:T(8,128)(2,1)S(1)}, bf16[4,128,640]{2,1,0:T(8,128)(2,1)S(1)}, u32[]{:S(2)}, u32[]{:S(2)}) collective-permute-start(bf16[4,128,640]{2,1,0:T(8,128)(2,1)S(1)} %get-tuple-element.232.refs_2_), channel_id=1, source_target_pairs={{0,2},{1,3},{2,0},{3,1},{4,6},{5,7},{6,4},{7,5},{8,10},{9,11},{10,... | collective-permute-start | bytes 1966088 | tf_op jit(solution)/shard_map/ppermute | solution.py:272
  22.6 30.7 %collective-permute-start.10 = (bf16[4,128,640]{2,1,0:T(8,128)(2,1)S(1)}, bf16[4,128,640]{2,1,0:T(8,128)(2,1)S(1)}, u32[]{:S(2)}, u32[]{:S(2)}) collective-permute-start(bf16[4,128,640]{2,1,0:T(8,128)(2,1)S(1)} %collective-permute-done.5.refs_3_), channel_id=1, source_target_pairs={{0,2},{1,3},{2,0},{3,1},{4,6},{5,7},{6,4},{7,5},{8,10},{9,11},{10,... | collective-permute-start | bytes 1966088 | tf_op jit(solution)/shard_map/ppermute | solution.py:272
  23.2 19.6 %collective-permute-start.8 = (bf16[384,640]{1,0:T(8,128)(2,1)}, bf16[384,640]{1,0:T(8,128)(2,1)S(1)}, u32[]{:S(2)}, u32[]{:S(2)}) collective-permute-start(bf16[384,640]{1,0:T(8,128)(2,1)} %slice.7), channel_id=1, source_target_pairs={{0,8},{4,12},{8,16},{12,20},{16,24},{20,28},{24,0},{28,4},{1,9},{5... | collective-permute-start | bytes 1474568 | tf_op jit(solution)/shard_map/ppermute | solution.py:281
  32.3 21.1 %collective-permute-start.11 = (bf16[384,640]{1,0:T(8,128)(2,1)S(1)}, bf16[384,640]{1,0:T(8,128)(2,1)S(1)}, u32[]{:S(2)}, u32[]{:S(2)}) collective-permute-start(bf16[384,640]{1,0:T(8,128)(2,1)S(1)} %collective-permute-done.1.refs_7_), channel_id=1, source_target_pairs={{0,8},{4,12},{8,16},{12,20},{16,24},{20,28},{24,0},{28,4},{1,9},{5... | collective-permute-start | bytes 1474568 | tf_op jit(solution)/shard_map/ppermute | solution.py:281
  32.4 38.5 %collective-permute-start.13 = (bf16[8,128,384]{2,1,0:T(8,128)(2,1)S(1)}, bf16[8,128,384]{2,1,0:T(8,128)(2,1)S(1)}, u32[]{:S(2)}, u32[]{:S(2)}) collective-permute-start(bf16[8,128,384]{2,1,0:T(8,128)(2,1)S(1)} %pad_maximum_fusion), channel_id=1, source_target_pairs={{0,2},{1,3},{2,0},{3,1},{4,6},{5,7},{6,4},{7,5},{8,10},{9,11},{10,... | collective-permute-start | bytes 2359304 | tf_op jit(solution)/shard_map/ppermute | solution.py:272
  42.8 28.1 %collective-permute-start.14 = (bf16[384,640]{1,0:T(8,128)(2,1)S(1)}, bf16[384,640]{1,0:T(8,128)(2,1)}, u32[]{:S(2)}, u32[]{:S(2)}) collective-permute-start(bf16[384,640]{1,0:T(8,128)(2,1)S(1)} %collective-permute-done.8.refs_6_), channel_id=1, source_target_pairs={{0,8},{4,12},{8,16},{12,20},{16,24},{20,28},{24,0},{28,4},{1,9},{5... | collective-permute-start | bytes 1474568 | tf_op jit(solution)/shard_map/ppermute | solution.py:281
  42.8 27.1 %collective-permute-start.15 = (bf16[256,640]{1,0:T(8,128)(2,1)S(1)}, bf16[256,640]{1,0:T(8,128)(2,1)S(1)}, u32[]{:S(2)}, u32[]{:S(2)}) collective-permute-start(bf16[256,640]{1,0:T(8,128)(2,1)S(1)} %collective-permute-done.9.refs_7_), channel_id=1, source_target_pairs={{0,8},{4,12},{8,16},{12,20},{16,24},{20,28},{24,0},{28,4},{1,9},{5... | collective-permute-start | bytes 983048 | tf_op jit(solution)/shard_map/ppermute | solution.py:281
  58.0 17.3 %collective-permute-start.12 = (bf16[2,256,640]{2,1,0:T(8,128)(2,1)S(1)}, bf16[2,256,640]{2,1,0:T(8,128)(2,1)S(1)}, u32[]{:S(2)}, u32[]{:S(2)}) collective-permute-start(bf16[2,256,640]{2,1,0:T(8,128)(2,1)S(1)} %shard_map.105.refs_0_), channel_id=1, source_target_pairs={{0,4},{4,0},{8,12},{12,8},{16,20},{20,16},{24,28},{28,24},{1,5},{5... | collective-permute-start | bytes 1966088 | tf_op jit(solution)/shard_map/ppermute | solution.py:278
  59.7 20.8 %collective-permute-start.6 = (bf16[8,128,256]{2,1,0:T(8,128)(2,1)S(1)}, bf16[8,128,256]{2,1,0:T(8,128)(2,1)S(1)}, u32[]{:S(2)}, u32[]{:S(2)}) collective-permute-start(bf16[8,128,256]{2,1,0:T(8,128)(2,1)S(1)} %pad_maximum_fusion.2), channel_id=1, source_target_pairs={{0,2},{1,3},{2,0},{3,1},{4,6},{5,7},{6,4},{7,5},{8,10},{9,11},{10,... | collective-permute-start | bytes 1572872 | tf_op jit(solution)/shard_map/ppermute | solution.py:272
  69.9 16.1 %collective-permute-start.18 = (bf16[384,640]{1,0:T(8,128)(2,1)S(1)}, bf16[384,640]{1,0:T(8,128)(2,1)}, u32[]{:S(2)}, u32[]{:S(2)}) collective-permute-start(bf16[384,640]{1,0:T(8,128)(2,1)S(1)} %collective-permute-done.11.refs_8_), channel_id=1, source_target_pairs={{0,8},{4,12},{8,16},{12,20},{16,24},{20,28},{24,0},{28,4},{1,9},{5... | collective-permute-start | bytes 1474568 | tf_op jit(solution)/shard_map/ppermute | solution.py:281
  73.7 10.5 %collective-permute-start.19 = (bf16[2,256,384]{2,1,0:T(8,128)(2,1)S(1)}, bf16[2,256,384]{2,1,0:T(8,128)(2,1)S(1)}, u32[]{:S(2)}, u32[]{:S(2)}) collective-permute-start(bf16[2,256,384]{2,1,0:T(8,128)(2,1)S(1)} %shard_map.106.refs_1_), channel_id=1, source_target_pairs={{0,4},{4,0},{8,12},{12,8},{16,20},{20,16},{24,28},{28,24},{1,5},{5... | collective-permute-start | bytes 1179656 | tf_op jit(solution)/shard_map/ppermute | solution.py:278
  75.3 19.3 %collective-permute-start.22 = (bf16[384,640]{1,0:T(8,128)(2,1)}, bf16[384,640]{1,0:T(8,128)(2,1)}, u32[]{:S(2)}, u32[]{:S(2)}) collective-permute-start(bf16[384,640]{1,0:T(8,128)(2,1)} %collective-permute-done.14.refs_6_), channel_id=1, source_target_pairs={{0,8},{4,12},{8,16},{12,20},{16,24},{20,28},{24,0},{28,4},{1,9},{5... | collective-permute-start | bytes 1474568 | tf_op jit(solution)/shard_map/ppermute | solution.py:281
  75.3 12.7 %collective-permute-start.17 = (bf16[256,640]{1,0:T(8,128)(2,1)}, bf16[256,640]{1,0:T(8,128)(2,1)}, u32[]{:S(2)}, u32[]{:S(2)}) collective-permute-start(bf16[256,640]{1,0:T(8,128)(2,1)} %slice.6), channel_id=1, source_target_pairs={{0,2},{1,3},{2,0},{3,1},{4,6},{5,7},{6,4},{7,5},{8,10},{9,11},{10,... | collective-permute-start | bytes 983048 | tf_op jit(solution)/shard_map/ppermute | solution.py:272
  82.3 7.2 %collective-permute-start.16 = (bf16[2,256,256]{2,1,0:T(8,128)(2,1)S(1)}, bf16[2,256,256]{2,1,0:T(8,128)(2,1)S(1)}, u32[]{:S(2)}, u32[]{:S(2)}) collective-permute-start(bf16[2,256,256]{2,1,0:T(8,128)(2,1)S(1)} %shard_map.107.refs_2_), channel_id=1, source_target_pairs={{0,4},{4,0},{8,12},{12,8},{16,20},{20,16},{24,28},{28,24},{1,5},{5... | collective-permute-start | bytes 786440 | tf_op jit(solution)/shard_map/ppermute | solution.py:278
  86.0 11.0 %collective-permute-start.21 = (bf16[256,640]{1,0:T(8,128)(2,1)}, bf16[256,640]{1,0:T(8,128)(2,1)}, u32[]{:S(2)}, u32[]{:S(2)}) collective-permute-start(bf16[256,640]{1,0:T(8,128)(2,1)} %collective-permute-done.refs_7_), channel_id=1, source_target_pairs={{0,2},{1,3},{2,0},{3,1},{4,6},{5,7},{6,4},{7,5},{8,10},{9,11},{10,... | collective-permute-start | bytes 983048 | tf_op jit(solution)/shard_map/ppermute | solution.py:272
  86.5 21.3 %collective-permute-start.30 = (bf16[512,640]{1,0:T(8,128)(2,1)}, bf16[512,640]{1,0:T(8,128)(2,1)}, u32[]{:S(2)}, u32[]{:S(2)}) collective-permute-start(bf16[512,640]{1,0:T(8,128)(2,1)} %pad_maximum_fusion.1), channel_id=1, source_target_pairs={{0,2},{1,3},{2,0},{3,1},{4,6},{5,7},{6,4},{7,5},{8,10},{9,11},{10,... | collective-permute-start | bytes 1966088 | tf_op jit(solution)/shard_map/ppermute | solution.py:272
  94.6 15.1 %collective-permute-start.29 = (bf16[384,640]{1,0:T(8,128)(2,1)}, bf16[384,640]{1,0:T(8,128)(2,1)S(1)}, u32[]{:S(2)}, u32[]{:S(2)}) collective-permute-start(bf16[384,640]{1,0:T(8,128)(2,1)} %collective-permute-done.18.refs_8_), channel_id=1, source_target_pairs={{0,8},{4,12},{8,16},{12,20},{16,24},{20,28},{24,0},{28,4},{1,9},{5... | collective-permute-start | bytes 1474568 | tf_op jit(solution)/shard_map/ppermute | solution.py:281
  97.0 8.6 %collective-permute-start.31 = (bf16[256,640]{1,0:T(8,128)(2,1)S(1)}, bf16[256,640]{1,0:T(8,128)(2,1)S(1)}, u32[]{:S(2)}, u32[]{:S(2)}) collective-permute-start(bf16[256,640]{1,0:T(8,128)(2,1)S(1)} %shard_map.109), channel_id=1, source_target_pairs={{0,4},{4,0},{8,12},{12,8},{16,20},{20,16},{24,28},{28,24},{1,5},{5... | collective-permute-start | bytes 983048 | tf_op jit(solution)/shard_map/ppermute | solution.py:278
  103.5 13.5 %collective-permute-start.27 = (bf16[256,640]{1,0:T(8,128)(2,1)S(1)}, bf16[256,640]{1,0:T(8,128)(2,1)S(1)}, u32[]{:S(2)}, u32[]{:S(2)}) collective-permute-start(bf16[256,640]{1,0:T(8,128)(2,1)S(1)} %get-tuple-element.313), channel_id=1, source_target_pairs={{0,1},{1,0},{2,3},{3,2},{4,5},{5,4},{6,7},{7,6},{8,9},{9,8},{10,11... | collective-permute-start | bytes 983048 | tf_op jit(solution)/shard_map/ppermute | solution.py:275
  103.8 13.2 %collective-permute-start.28 = (bf16[256,640]{1,0:T(8,128)(2,1)S(1)}, bf16[256,640]{1,0:T(8,128)(2,1)S(1)}, u32[]{:S(2)}, u32[]{:S(2)}) collective-permute-start(bf16[256,640]{1,0:T(8,128)(2,1)S(1)} %shard_map.111), channel_id=1, source_target_pairs={{0,4},{4,0},{8,12},{12,8},{16,20},{20,16},{24,28},{28,24},{1,5},{5... | collective-permute-start | bytes 983048 | tf_op jit(solution)/shard_map/ppermute | solution.py:278
  106.4 10.7 %collective-permute-start.26 = (bf16[256,640]{1,0:T(8,128)(2,1)S(1)}, bf16[256,640]{1,0:T(8,128)(2,1)S(1)}, u32[]{:S(2)}, u32[]{:S(2)}) collective-permute-start(bf16[256,640]{1,0:T(8,128)(2,1)S(1)} %get-tuple-element.310), channel_id=1, source_target_pairs={{0,1},{1,0},{2,3},{3,2},{4,5},{5,4},{6,7},{7,6},{8,9},{9,8},{10,11... | collective-permute-start | bytes 983048 | tf_op jit(solution)/shard_map/ppermute | solution.py:275
  115.4 10.0 %collective-permute-start.35 = (bf16[256,640]{1,0:T(8,128)(2,1)S(1)}, bf16[256,640]{1,0:T(8,128)(2,1)S(1)}, u32[]{:S(2)}, u32[]{:S(2)}) collective-permute-start(bf16[256,640]{1,0:T(8,128)(2,1)S(1)} %shard_map.113), channel_id=1, source_target_pairs={{0,4},{4,0},{8,12},{12,8},{16,20},{20,16},{24,28},{28,24},{1,5},{5... | collective-permute-start | bytes 983048 | tf_op jit(solution)/shard_map/ppermute | solution.py:278
  122.7 3.3 %collective-permute-start.34 = (bf16[128,640]{1,0:T(8,128)(2,1)S(1)}, bf16[128,640]{1,0:T(8,128)(2,1)S(1)}, u32[]{:S(2)}, u32[]{:S(2)}) collective-permute-start(bf16[128,640]{1,0:T(8,128)(2,1)S(1)} %get-tuple-element.350), channel_id=1, source_target_pairs={{0,1},{1,0},{2,3},{3,2},{4,5},{5,4},{6,7},{7,6},{8,9},{9,8},{10,11... | collective-permute-start | bytes 491528 | tf_op jit(solution)/shard_map/ppermute | solution.py:275
  122.7 3.3 %collective-permute-start.36 = (bf16[128,640]{1,0:T(8,128)(2,1)S(1)}, bf16[128,640]{1,0:T(8,128)(2,1)S(1)}, u32[]{:S(2)}, u32[]{:S(2)}) collective-permute-start(bf16[128,640]{1,0:T(8,128)(2,1)S(1)} %get-tuple-element.359), channel_id=1, source_target_pairs={{0,1},{1,0},{2,3},{3,2},{4,5},{5,4},{6,7},{7,6},{8,9},{9,8},{10,11... | collective-permute-start | bytes 491528 | tf_op jit(solution)/shard_map/ppermute | solution.py:275
  123.2 3.1 %collective-permute-start.39 = (bf16[256,640]{1,0:T(8,128)(2,1)}, bf16[256,640]{1,0:T(8,128)(2,1)S(1)}, u32[]{:S(2)}, u32[]{:S(2)}) collective-permute-start(bf16[256,640]{1,0:T(8,128)(2,1)} %get-tuple-element.370), channel_id=1, source_target_pairs={{0,1},{1,0},{2,3},{3,2},{4,5},{5,4},{6,7},{7,6},{8,9},{9,8},{10,11... | collective-permute-start | bytes 983048 | tf_op jit(solution)/shard_map/ppermute | solution.py:275
  126.4 10.1 %collective-permute-start.37 = (bf16[256,640]{1,0:T(8,128)(2,1)S(1)}, bf16[256,640]{1,0:T(8,128)(2,1)S(1)}, u32[]{:S(2)}, u32[]{:S(2)}) collective-permute-start(bf16[256,640]{1,0:T(8,128)(2,1)S(1)} %shard_map.117), channel_id=1, source_target_pairs={{0,4},{4,0},{8,12},{12,8},{16,20},{20,16},{24,28},{28,24},{1,5},{5... | collective-permute-start | bytes 983048 | tf_op jit(solution)/shard_map/ppermute | solution.py:278
  (37 other events, 221.7 us)

commit v11 on v10

--- a/solution.py
+++ b/solution.py
@@ -340,16 +340,16 @@
     rest[0] = wait(rest[0])
     swapped[2] = wait(swapped[2])
     acts = list(zip(acts, swapped))
-    flip = jnp.stack([seq // 2])
+    turned = jnp.stack([seq // 2])
 
     keeps, sends, mine_got, mine, other = [], [], [], [], []
 
-    def columns(step):
+    def columns(step, flip=None):
         own = [(upper[step], 0, cut), (lower[step], 0, depth - cut)] if step else [(out_weight, 0, depth)]
         start = step % 2 * (depth - cut) if step > 1 else 0
         got = rest[step] if step < 2 else rest[1 + step // 2]
         theirs = [(beside[step], 0, cut), (got, start, start + depth - cut)]
-        keep_mine, keep_other, *low = project(after(flip), acts, own + theirs)
+        keep_mine, keep_other, *low = project(after(turned) if flip is None else flip, acts, own + theirs)
         keeps.append((keep_mine, keep_other))
         sends.append([near(wait(array)) for array in low[1:]])
         mine_got.append([wait(array) for array in low[:1]])
@@ -383,8 +383,9 @@
         rest[1 + step // 2] = wait(rest[1 + step // 2])
         if step > 2:
             turn(beside, step)
+        flip = after(turned)
         turn(beside, step + 1)
-        columns(step)
+        columns(step, flip)
         send(step)
         stay(step - 2)
         stay(step - 1)

time: 139 us -> 137 us (0.986)
  waiting for transfers between devices: 65.7 us -> 61.4 us
  local copies, waits for them, and re-layouts: 12.4 us -> 13.8 us
    ppermute x9, waiting for transfers between devices: 43.3 us -> 41.2 us  [onward(): return lax.ppermute(array, 'dp', [(i, (i + 2) % n_dp) for i in range(n_dp)])]
    ppermute x7, waiting for transfers between devices: 8.98 us -> 7.48 us  [across(): return lax.ppermute(array, 'dp', [(i, i ^ 1) for i in range(n_dp)])]
    unnamed x58 -> x62, local copies, waits for them, and re-layouts: 8.68 us -> 10 us
where the time goes in v11:
time: 137 us; the launch traced here: 136 us
  waiting for transfers between devices  61.4 us (45%)
  Pallas kernels  32 us (23%)
  starting transfers between devices  26.2 us (19%)
  local copies, waits for them, and re-layouts  13.8 us (10%)
  other arithmetic  1.4 us (1%)
    ppermute x9, waiting for transfers between devices, onward(): return lax.ppermute(array, 'dp', [(i, (i + 2) % n_dp) for i in range(n_dp)])  41.2 us
    pallas_call x4, Pallas kernels, project(): pl.pallas_call(functools.partial(project_kernel, len(acts), spans), in_sp...  14.3 us
    ppermute x7, starting transfers between devices, across(): return lax.ppermute(array, 'dp', [(i, i ^ 1) for i in range(n_dp)])  10.8 us
    unnamed x62, local copies, waits for them, and re-layouts  10 us
    pallas_call x3, Pallas kernels, attend(): pl.pallas_call(functools.partial(attend_kernel, len(queries)), grid=(widt...  9.36 us
    ppermute x8, starting transfers between devices, far(): return lax.ppermute(array, 'seq', [(i, i ^ 2) for i in range(n_seq)])  8.77 us
    ppermute x8, waiting for transfers between devices, far(): return lax.ppermute(array, 'seq', [(i, i ^ 2) for i in range(n_seq)])  8.28 us
    ppermute x7, waiting for transfers between devices, across(): return lax.ppermute(array, 'dp', [(i, i ^ 1) for i in range(n_dp)])  7.48 us
  transfers between devices with their start and end apart: 40, of which 23 were waited for; matrix products, arithmetic and copies ran while one was open for 2% of the time, Pallas kernels for 22%

profile of v11, /device:TPU:0, one launch (start us, length us, event | category | flops | bytes accessed | tf_op | source)
XLA Modules:
  0.0 136.0 jit_solution(4974211900424353231)
XLA Ops:
  0.7 2.0 %slice.7 = bf16[384,640]{1,0:T(8,128)(2,1)} slice(bf16[640,640]{1,0:T(8,128)(2,1)} %refs_6_.1), slice={[0:384], [0:640]} | slice | bytes 983040 | tf_op jit(solution)/shard_map/slice | solution.py:298
  2.6 2.9 %collective-permute-start.1 = (bf16[384,640]{1,0:T(8,128)(2,1)}, bf16[384,640]{1,0:T(8,128)(2,1)S(1)}, u32[]{:S(2)}, u32[]{:S(2)}) collective-permute-start(bf16[384,640]{1,0:T(8,128)(2,1)} %slice.7), channel_id=1, source_target_pairs={{0,2},{1,3},{2,0},{3,1},{4,6},{5,7},{6,4},{7,5},{8,10},{9,11},{10,... | collective-permute-start | bytes 1474568 | tf_op jit(solution)/shard_map/ppermute | solution.py:272
  5.6 1.7 %slice.6 = bf16[256,640]{1,0:T(8,128)(2,1)} slice(bf16[640,640]{1,0:T(8,128)(2,1)} %refs_6_.1), slice={[384:640], [0:640]} | slice | bytes 655360 | tf_op jit(solution)/shard_map/slice | solution.py:298
  7.3 1.6 %collective-permute-start = (bf16[256,640]{1,0:T(8,128)(2,1)}, bf16[256,640]{1,0:T(8,128)(2,1)}, u32[]{:S(2)}, u32[]{:S(2)}) collective-permute-start(bf16[256,640]{1,0:T(8,128)(2,1)} %slice.6), channel_id=1, source_target_pairs={{0,8},{4,12},{8,16},{12,20},{16,24},{20,28},{24,0},{28,4},{1,9},{5... | collective-permute-start | bytes 983048 | tf_op jit(solution)/shard_map/ppermute | solution.py:281
  13.3 2.0 %shard_map.104 = (bf16[2,128,1280]{2,1,0:T(8,128)(2,1)S(1)}, bf16[4,128,640]{2,1,0:T(8,128)(2,1)S(1)}, bf16[4,128,384]{2,1,0:T(8,128)(2,1)S(1)}, bf16[4,128,256]...) custom-call(s32[1]{0:T(128)} %bitcast.3.core_ref, ...), custom_call_target="tpu_custom_call" | custom-call | flops 1 | bytes 1 | tf_op jit(solution)/shard_map/pallas_call | solution.py:78
  15.4 1.6 %collective-permute-done.1.refs_7_ = bf16[384,640]{1,0:T(8,128)(2,1)S(1)} collective-permute-done((bf16[384,640]{1,0:T(8,128)(2,1)}, bf16[384,640]{1,0:T(8,128)(2,1)S(1)}, u32[]{:S(2)}, u32[]{:S(2)}) %collective-permute-start.1) | collective-permute-done | bytes 491552 | tf_op jit(solution)/shard_map/ppermute | solution.py:272
  17.0 1.7 %collective-permute-done.refs_7_ = bf16[256,640]{1,0:T(8,128)(2,1)} collective-permute-done((bf16[256,640]{1,0:T(8,128)(2,1)}, bf16[256,640]{1,0:T(8,128)(2,1)}, u32[]{:S(2)}, u32[]{:S(2)}) %collective-permute-start) | collective-permute-done | bytes 327712 | tf_op jit(solution)/shard_map/ppermute | solution.py:281
  24.3 8.0 %collective-permute-done.9.refs_7_ = bf16[256,640]{1,0:T(8,128)(2,1)S(1)} collective-permute-done((bf16[256,640]{1,0:T(8,128)(2,1)}, bf16[256,640]{1,0:T(8,128)(2,1)S(1)}, u32[]{:S(2)}, u32[]{:S(2)}) %collective-permute-start.9) | collective-permute-done | bytes 327712 | tf_op jit(solution)/shard_map/ppermute | solution.py:281
  33.0 9.8 %collective-permute-done.8.refs_6_ = bf16[384,640]{1,0:T(8,128)(2,1)S(1)} collective-permute-done((bf16[384,640]{1,0:T(8,128)(2,1)}, bf16[384,640]{1,0:T(8,128)(2,1)S(1)}, u32[]{:S(2)}, u32[]{:S(2)}) %collective-permute-start.8) | collective-permute-done | bytes 491552 | tf_op jit(solution)/shard_map/ppermute | solution.py:281
  42.9 10.5 %collective-permute-done.11.refs_8_ = bf16[384,640]{1,0:T(8,128)(2,1)S(1)} collective-permute-done((bf16[384,640]{1,0:T(8,128)(2,1)S(1)}, bf16[384,640]{1,0:T(8,128)(2,1)S(1)}, u32[]{:S(2)}, u32[]{:S(2)}) %collective-permute-start.11) | collective-permute-done | bytes 491552 | tf_op jit(solution)/shard_map/ppermute | solution.py:281
  53.3 4.7 %shard_map.105.refs_0_ = bf16[2,256,640]{2,1,0:T(8,128)(2,1)S(1)} custom-call(bf16[2,128,1280]{2,1,0:T(8,128)(2,1)S(1)} %get-tuple-element.206.refs_0_, bf16[2,128,1280]{2,1,0:T(8,128)(2,1)S(1)} %collective-permute-done.2.refs_1_, bf16[4,128,640]{2,1,0:T(8,128)(2,1)S(1)} %get-tuple-element.232.refs_2_, ...), custom_call_target="tpu_custom_call" | custom-call | flops 1 | bytes 1 | tf_op jit(solution)/shard_map/pallas_call | solution.py:129
  58.0 1.6 %collective-permute-start.12 = (bf16[2,256,640]{2,1,0:T(8,128)(2,1)S(1)}, bf16[2,256,640]{2,1,0:T(8,128)(2,1)S(1)}, u32[]{:S(2)}, u32[]{:S(2)}) collective-permute-start(bf16[2,256,640]{2,1,0:T(8,128)(2,1)S(1)} %shard_map.105.refs_0_), channel_id=1, source_target_pairs={{0,4},{4,0},{8,12},{12,8},{16,20},{20,16},{24,28},{28,24},{1,5},{5... | collective-permute-start | bytes 1966088 | tf_op jit(solution)/shard_map/ppermute | solution.py:278
  60.3 9.7 %collective-permute-done.15.refs_7_ = bf16[256,640]{1,0:T(8,128)(2,1)S(1)} collective-permute-done((bf16[256,640]{1,0:T(8,128)(2,1)S(1)}, bf16[256,640]{1,0:T(8,128)(2,1)S(1)}, u32[]{:S(2)}, u32[]{:S(2)}) %collective-permute-start.15) | collective-permute-done | bytes 327712 | tf_op jit(solution)/shard_map/ppermute | solution.py:281
  70.9 2.8 %shard_map.106.refs_1_ = bf16[2,256,384]{2,1,0:T(8,128)(2,1)S(1)} custom-call(bf16[2,128,1280]{2,1,0:T(8,128)(2,1)S(1)} %get-tuple-element.206.refs_0_, bf16[2,128,1280]{2,1,0:T(8,128)(2,1)S(1)} %collective-permute-done.2.refs_1_, bf16[4,128,384]{2,1,0:T(8,128)(2,1)S(1)} %get-tuple-element.245.refs_2_, ...), custom_call_target="tpu_custom_call" | custom-call | flops 1 | bytes 1 | tf_op jit(solution)/shard_map/pallas_call | solution.py:129
  73.7 1.6 %collective-permute-start.19 = (bf16[2,256,384]{2,1,0:T(8,128)(2,1)S(1)}, bf16[2,256,384]{2,1,0:T(8,128)(2,1)S(1)}, u32[]{:S(2)}, u32[]{:S(2)}) collective-permute-start(bf16[2,256,384]{2,1,0:T(8,128)(2,1)S(1)} %shard_map.106.refs_1_), channel_id=1, source_target_pairs={{0,4},{4,0},{8,12},{12,8},{16,20},{20,16},{24,28},{28,24},{1,5},{5... | collective-permute-start | bytes 1179656 | tf_op jit(solution)/shard_map/ppermute | solution.py:278
  75.3 1.5 %collective-permute-start.17 = (bf16[256,640]{1,0:T(8,128)(2,1)}, bf16[256,640]{1,0:T(8,128)(2,1)}, u32[]{:S(2)}, u32[]{:S(2)}) collective-permute-start(bf16[256,640]{1,0:T(8,128)(2,1)} %slice.6), channel_id=1, source_target_pairs={{0,2},{1,3},{2,0},{3,1},{4,6},{5,7},{6,4},{7,5},{8,10},{9,11},{10,... | collective-permute-start | bytes 983048 | tf_op jit(solution)/shard_map/ppermute | solution.py:272
  76.8 3.7 %collective-permute-done.6.refs_4_ = bf16[8,128,256]{2,1,0:T(8,128)(2,1)S(1)} collective-permute-done((bf16[8,128,256]{2,1,0:T(8,128)(2,1)S(1)}, bf16[8,128,256]{2,1,0:T(8,128)(2,1)S(1)}, u32[]{:S(2)}, u32[]{:S(2)}) %collective-permute-start.6) | collective-permute-done | bytes 524320 | tf_op jit(solution)/shard_map/ppermute | solution.py:272
  80.5 1.9 %shard_map.107.refs_2_ = bf16[2,256,256]{2,1,0:T(8,128)(2,1)S(1)} custom-call(bf16[2,128,1280]{2,1,0:T(8,128)(2,1)S(1)} %get-tuple-element.206.refs_0_, bf16[2,128,1280]{2,1,0:T(8,128)(2,1)S(1)} %collective-permute-done.2.refs_1_, bf16[4,128,256]{2,1,0:T(8,128)(2,1)S(1)} %get-tuple-element.230.refs_2_, ...), custom_call_target="tpu_custom_call" | custom-call | flops 1 | bytes 1 | tf_op jit(solution)/shard_map/pallas_call | solution.py:129
  82.3 1.6 %collective-permute-start.16 = (bf16[2,256,256]{2,1,0:T(8,128)(2,1)S(1)}, bf16[2,256,256]{2,1,0:T(8,128)(2,1)S(1)}, u32[]{:S(2)}, u32[]{:S(2)}) collective-permute-start(bf16[2,256,256]{2,1,0:T(8,128)(2,1)S(1)} %shard_map.107.refs_2_), channel_id=1, source_target_pairs={{0,4},{4,0},{8,12},{12,8},{16,20},{20,16},{24,28},{28,24},{1,5},{5... | collective-permute-start | bytes 786440 | tf_op jit(solution)/shard_map/ppermute | solution.py:278
  84.3 1.6 %collective-permute-done.18.refs_8_ = bf16[384,640]{1,0:T(8,128)(2,1)S(1)} collective-permute-done((bf16[384,640]{1,0:T(8,128)(2,1)S(1)}, bf16[384,640]{1,0:T(8,128)(2,1)S(1)}, u32[]{:S(2)}, u32[]{:S(2)}) %collective-permute-start.18) | collective-permute-done | bytes 491552 | tf_op jit(solution)/shard_map/ppermute | solution.py:281
  87.2 1.5 %collective-permute-start.29 = (bf16[512,640]{1,0:T(8,128)(2,1)}, bf16[512,640]{1,0:T(8,128)(2,1)}, u32[]{:S(2)}, u32[]{:S(2)}) collective-permute-start(bf16[512,640]{1,0:T(8,128)(2,1)} %pad_maximum_fusion.1), channel_id=1, source_target_pairs={{0,2},{1,3},{2,0},{3,1},{4,6},{5,7},{6,4},{7,5},{8,10},{9,11},{10,... | collective-permute-start | bytes 1966088 | tf_op jit(solution)/shard_map/ppermute | solution.py:272
  90.6 3.3 %shard_map.108 = (f32[256,640]{1,0:T(8,128)S(1)}, f32[256,640]{1,0:T(8,128)S(1)}, bf16[256,640]{1,0:T(8,128)(2,1)S(1)}, bf16[128,640]{1,0:T(8,128)(2,1)S(1)}, bf16[128,640]{1,0:T(8,128)(2,1)S(1)}) custom-call(s32[1]{0:T(128)} %bitcast.2.flip_ref, bf16[2,256,640]{2,1,0:T(8,128)(2,1)S(1)} %shard_map.105.refs_0_, bf16[2,256,384]{2,1,0:T(8,128)(2,1)S(1)} %shard_map.106.refs_1_, ...), custom_call_target="tpu_custom_call" | custom-call | flops 1 | bytes 1 | tf_op jit(solution)/shard_map/pallas_call | solution.py:173
  94.6 3.0 %collective-permute-done.21.refs_9_ = bf16[256,640]{1,0:T(8,128)(2,1)} collective-permute-done((bf16[256,640]{1,0:T(8,128)(2,1)}, bf16[256,640]{1,0:T(8,128)(2,1)}, u32[]{:S(2)}, u32[]{:S(2)}) %collective-permute-start.21) | collective-permute-done | bytes 327712 | tf_op jit(solution)/shard_map/ppermute | solution.py:272
  97.7 1.6 %collective-permute-start.30 = (bf16[256,640]{1,0:T(8,128)(2,1)S(1)}, bf16[256,640]{1,0:T(8,128)(2,1)S(1)}, u32[]{:S(2)}, u32[]{:S(2)}) collective-permute-start(bf16[256,640]{1,0:T(8,128)(2,1)S(1)} %shard_map.109), channel_id=1, source_target_pairs={{0,4},{4,0},{8,12},{12,8},{16,20},{20,16},{24,28},{28,24},{1,5},{5... | collective-permute-start | bytes 983048 | tf_op jit(solution)/shard_map/ppermute | solution.py:278
  99.3 3.4 %shard_map.110 = (f32[256,640]{1,0:T(8,128)S(1)}, f32[256,640]{1,0:T(8,128)S(1)}, bf16[256,640]{1,0:T(8,128)(2,1)S(1)}, bf16[128,640]{1,0:T(8,128)(2,1)S(1)}, bf16[128,640]{1,0:T(8,128)(2,1)S(1)}) custom-call(s32[1]{0:T(128)} %bitcast.2.flip_ref, bf16[2,256,640]{2,1,0:T(8,128)(2,1)S(1)} %shard_map.105.refs_0_, bf16[2,256,384]{2,1,0:T(8,128)(2,1)S(1)} %shard_map.106.refs_1_, ...), custom_call_target="tpu_custom_call" | custom-call | flops 1 | bytes 1 | tf_op jit(solution)/shard_map/pallas_call | solution.py:173
  106.5 1.5 %collective-permute-start.28 = (bf16[256,640]{1,0:T(8,128)(2,1)S(1)}, bf16[256,640]{1,0:T(8,128)(2,1)S(1)}, u32[]{:S(2)}, u32[]{:S(2)}) collective-permute-start(bf16[256,640]{1,0:T(8,128)(2,1)S(1)} %shard_map.111), channel_id=1, source_target_pairs={{0,4},{4,0},{8,12},{12,8},{16,20},{20,16},{24,28},{28,24},{1,5},{5... | collective-permute-start | bytes 983048 | tf_op jit(solution)/shard_map/ppermute | solution.py:278
  108.0 3.8 %shard_map.112 = (f32[256,640]{1,0:T(8,128)S(1)}, f32[256,640]{1,0:T(8,128)S(1)}, bf16[256,640]{1,0:T(8,128)(2,1)}, bf16[128,640]{1,0:T(8,128)(2,1)S(1)}, bf16[128,640]{1,0:T(8,128)(2,1)S(1)}) custom-call(s32[1]{0:T(128)} %bitcast.2.flip_ref, bf16[2,256,640]{2,1,0:T(8,128)(2,1)S(1)} %shard_map.105.refs_0_, bf16[2,256,384]{2,1,0:T(8,128)(2,1)S(1)} %shard_map.106.refs_1_, ...), custom_call_target="tpu_custom_call" | custom-call | flops 1 | bytes 1 | tf_op jit(solution)/shard_map/pallas_call | solution.py:173
  113.5 1.5 %collective-permute-start.35 = (bf16[256,640]{1,0:T(8,128)(2,1)S(1)}, bf16[256,640]{1,0:T(8,128)(2,1)S(1)}, u32[]{:S(2)}, u32[]{:S(2)}) collective-permute-start(bf16[256,640]{1,0:T(8,128)(2,1)S(1)} %shard_map.113), channel_id=1, source_target_pairs={{0,4},{4,0},{8,12},{12,8},{16,20},{20,16},{24,28},{28,24},{1,5},{5... | collective-permute-start | bytes 983048 | tf_op jit(solution)/shard_map/ppermute | solution.py:278
  116.5 3.8 %shard_map.116 = (f32[256,640]{1,0:T(8,128)S(1)}, f32[256,640]{1,0:T(8,128)S(1)}, bf16[256,640]{1,0:T(8,128)(2,1)}, bf16[128,640]{1,0:T(8,128)(2,1)S(1)}, bf16[128,640]{1,0:T(8,128)(2,1)S(1)}) custom-call(s32[1]{0:T(128)} %bitcast.2.flip_ref, bf16[2,256,640]{2,1,0:T(8,128)(2,1)S(1)} %shard_map.105.refs_0_, bf16[2,256,384]{2,1,0:T(8,128)(2,1)S(1)} %shard_map.106.refs_1_, ...), custom_call_target="tpu_custom_call" | custom-call | flops 1 | bytes 1 | tf_op jit(solution)/shard_map/pallas_call | solution.py:173
  121.7 1.8 %collective-permute-done.35.other_ref = bf16[256,640]{1,0:T(8,128)(2,1)S(1)} collective-permute-done((bf16[256,640]{1,0:T(8,128)(2,1)S(1)}, bf16[256,640]{1,0:T(8,128)(2,1)S(1)}, u32[]{:S(2)}, u32[]{:S(2)}) %collective-permute-start.35) | collective-permute-done | bytes 327712 | tf_op jit(solution)/shard_map/ppermute | solution.py:278
  124.4 1.5 %collective-permute-start.37 = (bf16[256,640]{1,0:T(8,128)(2,1)S(1)}, bf16[256,640]{1,0:T(8,128)(2,1)S(1)}, u32[]{:S(2)}, u32[]{:S(2)}) collective-permute-start(bf16[256,640]{1,0:T(8,128)(2,1)S(1)} %shard_map.117), channel_id=1, source_target_pairs={{0,4},{4,0},{8,12},{12,8},{16,20},{20,16},{24,28},{28,24},{1,5},{5... | collective-permute-start | bytes 983048 | tf_op jit(solution)/shard_map/ppermute | solution.py:278
  131.4 3.1 %collective-permute-done.37.other_ref = bf16[256,640]{1,0:T(8,128)(2,1)S(1)} collective-permute-done((bf16[256,640]{1,0:T(8,128)(2,1)S(1)}, bf16[256,640]{1,0:T(8,128)(2,1)S(1)}, u32[]{:S(2)}, u32[]{:S(2)}) %collective-permute-start.37) | collective-permute-done | bytes 327712 | tf_op jit(solution)/shard_map/ppermute | solution.py:278
  (142 shorter events, 33.0 us)
Async XLA Ops:
  2.6 14.4 %collective-permute-start.1 = (bf16[384,640]{1,0:T(8,128)(2,1)}, bf16[384,640]{1,0:T(8,128)(2,1)S(1)}, u32[]{:S(2)}, u32[]{:S(2)}) collective-permute-start(bf16[384,640]{1,0:T(8,128)(2,1)} %slice.7), channel_id=1, source_target_pairs={{0,2},{1,3},{2,0},{3,1},{4,6},{5,7},{6,4},{7,5},{8,10},{9,11},{10,... | collective-permute-start | bytes 1474568 | tf_op jit(solution)/shard_map/ppermute | solution.py:272
  7.3 11.3 %collective-permute-start = (bf16[256,640]{1,0:T(8,128)(2,1)}, bf16[256,640]{1,0:T(8,128)(2,1)}, u32[]{:S(2)}, u32[]{:S(2)}) collective-permute-start(bf16[256,640]{1,0:T(8,128)(2,1)} %slice.6), channel_id=1, source_target_pairs={{0,8},{4,12},{8,16},{12,20},{16,24},{20,28},{24,0},{28,4},{1,9},{5... | collective-permute-start | bytes 983048 | tf_op jit(solution)/shard_map/ppermute | solution.py:281
  18.7 13.7 %collective-permute-start.2 = (bf16[2,128,1280]{2,1,0:T(8,128)(2,1)S(1)}, bf16[2,128,1280]{2,1,0:T(8,128)(2,1)S(1)}, u32[]{:S(2)}, u32[]{:S(2)}) collective-permute-start(bf16[2,128,1280]{2,1,0:T(8,128)(2,1)S(1)} %get-tuple-element.215), channel_id=1, source_target_pairs={{0,1},{1,0},{2,3},{3,2},{4,5},{5,4},{6,7},{7,6},{8,9},{9,8},{10,11... | collective-permute-start | bytes 1966088 | tf_op jit(solution)/shard_map/ppermute | solution.py:275
  19.2 4.0 %collective-permute-start.4 = (bf16[4,128,384]{2,1,0:T(8,128)(2,1)S(1)}, bf16[4,128,384]{2,1,0:T(8,128)(2,1)S(1)}, u32[]{:S(2)}, u32[]{:S(2)}) collective-permute-start(bf16[4,128,384]{2,1,0:T(8,128)(2,1)S(1)} %get-tuple-element.223), channel_id=1, source_target_pairs={{0,1},{1,0},{2,3},{3,2},{4,5},{5,4},{6,7},{7,6},{8,9},{9,8},{10,11... | collective-permute-start | bytes 1179656 | tf_op jit(solution)/shard_map/ppermute | solution.py:275
  19.2 3.5 %collective-permute-start.3 = (bf16[4,128,256]{2,1,0:T(8,128)(2,1)S(1)}, bf16[4,128,256]{2,1,0:T(8,128)(2,1)S(1)}, u32[]{:S(2)}, u32[]{:S(2)}) collective-permute-start(bf16[4,128,256]{2,1,0:T(8,128)(2,1)S(1)} %get-tuple-element.222), channel_id=1, source_target_pairs={{0,1},{1,0},{2,3},{3,2},{4,5},{5,4},{6,7},{7,6},{8,9},{9,8},{10,11... | collective-permute-start | bytes 786440 | tf_op jit(solution)/shard_map/ppermute | solution.py:275
  19.7 12.6 %collective-permute-start.9 = (bf16[256,640]{1,0:T(8,128)(2,1)}, bf16[256,640]{1,0:T(8,128)(2,1)S(1)}, u32[]{:S(2)}, u32[]{:S(2)}) collective-permute-start(bf16[256,640]{1,0:T(8,128)(2,1)} %collective-permute-done.refs_7_), channel_id=1, source_target_pairs={{0,8},{4,12},{8,16},{12,20},{16,24},{20,28},{24,0},{28,4},{1,9},{5... | collective-permute-start | bytes 983048 | tf_op jit(solution)/shard_map/ppermute | solution.py:281
  20.7 22.1 %collective-permute-start.7 = (bf16[4,128,640]{2,1,0:T(8,128)(2,1)S(1)}, bf16[4,128,640]{2,1,0:T(8,128)(2,1)S(1)}, u32[]{:S(2)}, u32[]{:S(2)}) collective-permute-start(bf16[4,128,640]{2,1,0:T(8,128)(2,1)S(1)} %get-tuple-element.232.refs_2_), channel_id=1, source_target_pairs={{0,2},{1,3},{2,0},{3,1},{4,6},{5,7},{6,4},{7,5},{8,10},{9,11},{10,... | collective-permute-start | bytes 1966088 | tf_op jit(solution)/shard_map/ppermute | solution.py:272
  22.6 30.7 %collective-permute-start.10 = (bf16[4,128,640]{2,1,0:T(8,128)(2,1)S(1)}, bf16[4,128,640]{2,1,0:T(8,128)(2,1)S(1)}, u32[]{:S(2)}, u32[]{:S(2)}) collective-permute-start(bf16[4,128,640]{2,1,0:T(8,128)(2,1)S(1)} %collective-permute-done.5.refs_3_), channel_id=1, source_target_pairs={{0,2},{1,3},{2,0},{3,1},{4,6},{5,7},{6,4},{7,5},{8,10},{9,11},{10,... | collective-permute-start | bytes 1966088 | tf_op jit(solution)/shard_map/ppermute | solution.py:272
  23.2 19.6 %collective-permute-start.8 = (bf16[384,640]{1,0:T(8,128)(2,1)}, bf16[384,640]{1,0:T(8,128)(2,1)S(1)}, u32[]{:S(2)}, u32[]{:S(2)}) collective-permute-start(bf16[384,640]{1,0:T(8,128)(2,1)} %slice.7), channel_id=1, source_target_pairs={{0,8},{4,12},{8,16},{12,20},{16,24},{20,28},{24,0},{28,4},{1,9},{5... | collective-permute-start | bytes 1474568 | tf_op jit(solution)/shard_map/ppermute | solution.py:281
  32.3 21.1 %collective-permute-start.11 = (bf16[384,640]{1,0:T(8,128)(2,1)S(1)}, bf16[384,640]{1,0:T(8,128)(2,1)S(1)}, u32[]{:S(2)}, u32[]{:S(2)}) collective-permute-start(bf16[384,640]{1,0:T(8,128)(2,1)S(1)} %collective-permute-done.1.refs_7_), channel_id=1, source_target_pairs={{0,8},{4,12},{8,16},{12,20},{16,24},{20,28},{24,0},{28,4},{1,9},{5... | collective-permute-start | bytes 1474568 | tf_op jit(solution)/shard_map/ppermute | solution.py:281
  32.4 38.5 %collective-permute-start.13 = (bf16[8,128,384]{2,1,0:T(8,128)(2,1)S(1)}, bf16[8,128,384]{2,1,0:T(8,128)(2,1)S(1)}, u32[]{:S(2)}, u32[]{:S(2)}) collective-permute-start(bf16[8,128,384]{2,1,0:T(8,128)(2,1)S(1)} %pad_maximum_fusion), channel_id=1, source_target_pairs={{0,2},{1,3},{2,0},{3,1},{4,6},{5,7},{6,4},{7,5},{8,10},{9,11},{10,... | collective-permute-start | bytes 2359304 | tf_op jit(solution)/shard_map/ppermute | solution.py:272
  42.8 28.1 %collective-permute-start.14 = (bf16[384,640]{1,0:T(8,128)(2,1)S(1)}, bf16[384,640]{1,0:T(8,128)(2,1)}, u32[]{:S(2)}, u32[]{:S(2)}) collective-permute-start(bf16[384,640]{1,0:T(8,128)(2,1)S(1)} %collective-permute-done.8.refs_6_), channel_id=1, source_target_pairs={{0,8},{4,12},{8,16},{12,20},{16,24},{20,28},{24,0},{28,4},{1,9},{5... | collective-permute-start | bytes 1474568 | tf_op jit(solution)/shard_map/ppermute | solution.py:281
  42.8 27.1 %collective-permute-start.15 = (bf16[256,640]{1,0:T(8,128)(2,1)S(1)}, bf16[256,640]{1,0:T(8,128)(2,1)S(1)}, u32[]{:S(2)}, u32[]{:S(2)}) collective-permute-start(bf16[256,640]{1,0:T(8,128)(2,1)S(1)} %collective-permute-done.9.refs_7_), channel_id=1, source_target_pairs={{0,8},{4,12},{8,16},{12,20},{16,24},{20,28},{24,0},{28,4},{1,9},{5... | collective-permute-start | bytes 983048 | tf_op jit(solution)/shard_map/ppermute | solution.py:281
  58.0 17.3 %collective-permute-start.12 = (bf16[2,256,640]{2,1,0:T(8,128)(2,1)S(1)}, bf16[2,256,640]{2,1,0:T(8,128)(2,1)S(1)}, u32[]{:S(2)}, u32[]{:S(2)}) collective-permute-start(bf16[2,256,640]{2,1,0:T(8,128)(2,1)S(1)} %shard_map.105.refs_0_), channel_id=1, source_target_pairs={{0,4},{4,0},{8,12},{12,8},{16,20},{20,16},{24,28},{28,24},{1,5},{5... | collective-permute-start | bytes 1966088 | tf_op jit(solution)/shard_map/ppermute | solution.py:278
  59.7 20.8 %collective-permute-start.6 = (bf16[8,128,256]{2,1,0:T(8,128)(2,1)S(1)}, bf16[8,128,256]{2,1,0:T(8,128)(2,1)S(1)}, u32[]{:S(2)}, u32[]{:S(2)}) collective-permute-start(bf16[8,128,256]{2,1,0:T(8,128)(2,1)S(1)} %pad_maximum_fusion.2), channel_id=1, source_target_pairs={{0,2},{1,3},{2,0},{3,1},{4,6},{5,7},{6,4},{7,5},{8,10},{9,11},{10,... | collective-permute-start | bytes 1572872 | tf_op jit(solution)/shard_map/ppermute | solution.py:272
  69.9 16.0 %collective-permute-start.18 = (bf16[384,640]{1,0:T(8,128)(2,1)S(1)}, bf16[384,640]{1,0:T(8,128)(2,1)S(1)}, u32[]{:S(2)}, u32[]{:S(2)}) collective-permute-start(bf16[384,640]{1,0:T(8,128)(2,1)S(1)} %collective-permute-done.11.refs_8_), channel_id=1, source_target_pairs={{0,8},{4,12},{8,16},{12,20},{16,24},{20,28},{24,0},{28,4},{1,9},{5... | collective-permute-start | bytes 1474568 | tf_op jit(solution)/shard_map/ppermute | solution.py:281
  73.7 10.6 %collective-permute-start.19 = (bf16[2,256,384]{2,1,0:T(8,128)(2,1)S(1)}, bf16[2,256,384]{2,1,0:T(8,128)(2,1)S(1)}, u32[]{:S(2)}, u32[]{:S(2)}) collective-permute-start(bf16[2,256,384]{2,1,0:T(8,128)(2,1)S(1)} %shard_map.106.refs_1_), channel_id=1, source_target_pairs={{0,4},{4,0},{8,12},{12,8},{16,20},{20,16},{24,28},{28,24},{1,5},{5... | collective-permute-start | bytes 1179656 | tf_op jit(solution)/shard_map/ppermute | solution.py:278
  75.3 19.3 %collective-permute-start.22 = (bf16[384,640]{1,0:T(8,128)(2,1)}, bf16[384,640]{1,0:T(8,128)(2,1)}, u32[]{:S(2)}, u32[]{:S(2)}) collective-permute-start(bf16[384,640]{1,0:T(8,128)(2,1)} %collective-permute-done.14.refs_6_), channel_id=1, source_target_pairs={{0,8},{4,12},{8,16},{12,20},{16,24},{20,28},{24,0},{28,4},{1,9},{5... | collective-permute-start | bytes 1474568 | tf_op jit(solution)/shard_map/ppermute | solution.py:281
  75.3 13.4 %collective-permute-start.17 = (bf16[256,640]{1,0:T(8,128)(2,1)}, bf16[256,640]{1,0:T(8,128)(2,1)}, u32[]{:S(2)}, u32[]{:S(2)}) collective-permute-start(bf16[256,640]{1,0:T(8,128)(2,1)} %slice.6), channel_id=1, source_target_pairs={{0,2},{1,3},{2,0},{3,1},{4,6},{5,7},{6,4},{7,5},{8,10},{9,11},{10,... | collective-permute-start | bytes 983048 | tf_op jit(solution)/shard_map/ppermute | solution.py:272
  82.3 7.2 %collective-permute-start.16 = (bf16[2,256,256]{2,1,0:T(8,128)(2,1)S(1)}, bf16[2,256,256]{2,1,0:T(8,128)(2,1)S(1)}, u32[]{:S(2)}, u32[]{:S(2)}) collective-permute-start(bf16[2,256,256]{2,1,0:T(8,128)(2,1)S(1)} %shard_map.107.refs_2_), channel_id=1, source_target_pairs={{0,4},{4,0},{8,12},{12,8},{16,20},{20,16},{24,28},{28,24},{1,5},{5... | collective-permute-start | bytes 786440 | tf_op jit(solution)/shard_map/ppermute | solution.py:278
  86.7 11.0 %collective-permute-start.21 = (bf16[256,640]{1,0:T(8,128)(2,1)}, bf16[256,640]{1,0:T(8,128)(2,1)}, u32[]{:S(2)}, u32[]{:S(2)}) collective-permute-start(bf16[256,640]{1,0:T(8,128)(2,1)} %collective-permute-done.refs_7_), channel_id=1, source_target_pairs={{0,2},{1,3},{2,0},{3,1},{4,6},{5,7},{6,4},{7,5},{8,10},{9,11},{10,... | collective-permute-start | bytes 983048 | tf_op jit(solution)/shard_map/ppermute | solution.py:272
  87.2 20.8 %collective-permute-start.29 = (bf16[512,640]{1,0:T(8,128)(2,1)}, bf16[512,640]{1,0:T(8,128)(2,1)}, u32[]{:S(2)}, u32[]{:S(2)}) collective-permute-start(bf16[512,640]{1,0:T(8,128)(2,1)} %pad_maximum_fusion.1), channel_id=1, source_target_pairs={{0,2},{1,3},{2,0},{3,1},{4,6},{5,7},{6,4},{7,5},{8,10},{9,11},{10,... | collective-permute-start | bytes 1966088 | tf_op jit(solution)/shard_map/ppermute | solution.py:272
  94.0 3.6 %collective-permute-start.20 = (bf16[128,640]{1,0:T(8,128)(2,1)S(1)}, bf16[128,640]{1,0:T(8,128)(2,1)S(1)}, u32[]{:S(2)}, u32[]{:S(2)}) collective-permute-start(bf16[128,640]{1,0:T(8,128)(2,1)S(1)} %get-tuple-element.276), channel_id=1, source_target_pairs={{0,1},{1,0},{2,3},{3,2},{4,5},{5,4},{6,7},{7,6},{8,9},{9,8},{10,11... | collective-permute-start | bytes 491528 | tf_op jit(solution)/shard_map/ppermute | solution.py:275
  94.1 3.6 %collective-permute-start.23 = (bf16[128,640]{1,0:T(8,128)(2,1)S(1)}, bf16[128,640]{1,0:T(8,128)(2,1)S(1)}, u32[]{:S(2)}, u32[]{:S(2)}) collective-permute-start(bf16[128,640]{1,0:T(8,128)(2,1)S(1)} %get-tuple-element.287), channel_id=1, source_target_pairs={{0,1},{1,0},{2,3},{3,2},{4,5},{5,4},{6,7},{7,6},{8,9},{9,8},{10,11... | collective-permute-start | bytes 491528 | tf_op jit(solution)/shard_map/ppermute | solution.py:275
  94.6 17.1 %collective-permute-start.31 = (bf16[384,640]{1,0:T(8,128)(2,1)S(1)}, bf16[384,640]{1,0:T(8,128)(2,1)S(1)}, u32[]{:S(2)}, u32[]{:S(2)}) collective-permute-start(bf16[384,640]{1,0:T(8,128)(2,1)S(1)} %copy-done.22), channel_id=1, source_target_pairs={{0,8},{4,12},{8,16},{12,20},{16,24},{20,28},{24,0},{28,4},{1,9},{5... | collective-permute-start | bytes 1474568 | tf_op jit(solution)/shard_map/ppermute | solution.py:281
  97.7 8.0 %collective-permute-start.30 = (bf16[256,640]{1,0:T(8,128)(2,1)S(1)}, bf16[256,640]{1,0:T(8,128)(2,1)S(1)}, u32[]{:S(2)}, u32[]{:S(2)}) collective-permute-start(bf16[256,640]{1,0:T(8,128)(2,1)S(1)} %shard_map.109), channel_id=1, source_target_pairs={{0,4},{4,0},{8,12},{12,8},{16,20},{20,16},{24,28},{28,24},{1,5},{5... | collective-permute-start | bytes 983048 | tf_op jit(solution)/shard_map/ppermute | solution.py:278
  104.2 11.3 %collective-permute-start.27 = (bf16[256,640]{1,0:T(8,128)(2,1)S(1)}, bf16[256,640]{1,0:T(8,128)(2,1)S(1)}, u32[]{:S(2)}, u32[]{:S(2)}) collective-permute-start(bf16[256,640]{1,0:T(8,128)(2,1)S(1)} %get-tuple-element.313), channel_id=1, source_target_pairs={{0,1},{1,0},{2,3},{3,2},{4,5},{5,4},{6,7},{7,6},{8,9},{9,8},{10,11... | collective-permute-start | bytes 983048 | tf_op jit(solution)/shard_map/ppermute | solution.py:275
  104.5 11.0 %collective-permute-start.26 = (bf16[256,640]{1,0:T(8,128)(2,1)S(1)}, bf16[256,640]{1,0:T(8,128)(2,1)S(1)}, u32[]{:S(2)}, u32[]{:S(2)}) collective-permute-start(bf16[256,640]{1,0:T(8,128)(2,1)S(1)} %get-tuple-element.310), channel_id=1, source_target_pairs={{0,1},{1,0},{2,3},{3,2},{4,5},{5,4},{6,7},{7,6},{8,9},{9,8},{10,11... | collective-permute-start | bytes 983048 | tf_op jit(solution)/shard_map/ppermute | solution.py:275
  106.5 9.0 %collective-permute-start.28 = (bf16[256,640]{1,0:T(8,128)(2,1)S(1)}, bf16[256,640]{1,0:T(8,128)(2,1)S(1)}, u32[]{:S(2)}, u32[]{:S(2)}) collective-permute-start(bf16[256,640]{1,0:T(8,128)(2,1)S(1)} %shard_map.111), channel_id=1, source_target_pairs={{0,4},{4,0},{8,12},{12,8},{16,20},{20,16},{24,28},{28,24},{1,5},{5... | collective-permute-start | bytes 983048 | tf_op jit(solution)/shard_map/ppermute | solution.py:278
  113.5 10.0 %collective-permute-start.35 = (bf16[256,640]{1,0:T(8,128)(2,1)S(1)}, bf16[256,640]{1,0:T(8,128)(2,1)S(1)}, u32[]{:S(2)}, u32[]{:S(2)}) collective-permute-start(bf16[256,640]{1,0:T(8,128)(2,1)S(1)} %shard_map.113), channel_id=1, source_target_pairs={{0,4},{4,0},{8,12},{12,8},{16,20},{20,16},{24,28},{28,24},{1,5},{5... | collective-permute-start | bytes 983048 | tf_op jit(solution)/shard_map/ppermute | solution.py:278
  121.7 4.2 %collective-permute-start.39 = (bf16[256,640]{1,0:T(8,128)(2,1)}, bf16[256,640]{1,0:T(8,128)(2,1)S(1)}, u32[]{:S(2)}, u32[]{:S(2)}) collective-permute-start(bf16[256,640]{1,0:T(8,128)(2,1)} %get-tuple-element.370), channel_id=1, source_target_pairs={{0,1},{1,0},{2,3},{3,2},{4,5},{5,4},{6,7},{7,6},{8,9},{9,8},{10,11... | collective-permute-start | bytes 983048 | tf_op jit(solution)/shard_map/ppermute | solution.py:275
  124.4 10.0 %collective-permute-start.37 = (bf16[256,640]{1,0:T(8,128)(2,1)S(1)}, bf16[256,640]{1,0:T(8,128)(2,1)S(1)}, u32[]{:S(2)}, u32[]{:S(2)}) collective-permute-start(bf16[256,640]{1,0:T(8,128)(2,1)S(1)} %shard_map.117), channel_id=1, source_target_pairs={{0,4},{4,0},{8,12},{12,8},{16,20},{20,16},{24,28},{28,24},{1,5},{5... | collective-permute-start | bytes 983048 | tf_op jit(solution)/shard_map/ppermute | solution.py:278
  (39 other events, 225.1 us)

commit v12 on v11

--- a/solution.py
+++ b/solution.py
@@ -355,9 +355,10 @@
         mine_got.append([wait(array) for array in low[:1]])
 
     def send(step):
+        closed = wait(close(keeps[step][1], *[wait(array) for array in sends[step]]))
         if step > 2:
             other[step - 1] = wait(other[step - 1])
-        other.append(across(wait(close(keeps[step][1], *[wait(array) for array in sends[step]]))))
+        other.append(across(after(closed)))
         mine_got[step] = [near(after(array)) for array in mine_got[step]]
         if step and not step > 2:
             other[step - 1] = wait(other[step - 1])

time: 137 us -> 136 us (level)
    ppermute x7, waiting for transfers between devices: 7.48 us -> 5.9 us  [across(): return lax.ppermute(array, 'dp', [(i, i ^ 1) for i in range(n_dp)])]
    ppermute x16, waiting for transfers between devices: 4.48 us -> 5.87 us  [near(): return lax.ppermute(array, 'seq', [(i, i ^ 1) for i in range(n_seq)])]
    ppermute x8, waiting for transfers between devices: 8.28 us -> 9.67 us  [far(): return lax.ppermute(array, 'seq', [(i, i ^ 2) for i in range(n_seq)])]
  transfers between devices with their start and end apart: 40 -> 40, of which waited for: 23 -> 25; matrix products, arithmetic and copies ran while one was open for 2% -> 2% of each run, Pallas kernels for 22% -> 23%
where the time goes in v12:
time: 136 us
  waiting for transfers between devices  62.6 us (46%)
  Pallas kernels  32 us (24%)
  starting transfers between devices  24.9 us (18%)
  local copies, waits for them, and re-layouts  13.7 us (10%)
  other arithmetic  1.4 us (1%)
    ppermute x9, waiting for transfers between devices, onward(): return lax.ppermute(array, 'dp', [(i, (i + 2) % n_dp) for i in range(n_dp)])  41.2 us
    pallas_call x4, Pallas kernels, project(): pl.pallas_call(functools.partial(project_kernel, len(acts), spans), in_sp...  14.3 us
    ppermute x7, starting transfers between devices, across(): return lax.ppermute(array, 'dp', [(i, i ^ 1) for i in range(n_dp)])  10 us
    unnamed x62, local copies, waits for them, and re-layouts  9.99 us
    ppermute x8, waiting for transfers between devices, far(): return lax.ppermute(array, 'seq', [(i, i ^ 2) for i in range(n_seq)])  9.67 us
    pallas_call x3, Pallas kernels, attend(): pl.pallas_call(functools.partial(attend_kernel, len(queries)), grid=(widt...  9.36 us
    ppermute x8, starting transfers between devices, far(): return lax.ppermute(array, 'seq', [(i, i ^ 2) for i in range(n_seq)])  8.77 us
    ppermute x7, waiting for transfers between devices, across(): return lax.ppermute(array, 'dp', [(i, i ^ 1) for i in range(n_dp)])  5.9 us
  transfers between devices with their start and end apart: 40, of which 25 were waited for; matrix products, arithmetic and copies ran while one was open for 2% of the time, Pallas kernels for 23%

profile of v12, /device:TPU:0, one launch (start us, length us, event | category | flops | bytes accessed | tf_op | source)
XLA Modules:
  0.0 135.7 jit_solution(227348451631846902)
XLA Ops:
  0.7 2.0 %slice.7 = bf16[384,640]{1,0:T(8,128)(2,1)} slice(bf16[640,640]{1,0:T(8,128)(2,1)} %refs_6_.1), slice={[0:384], [0:640]} | slice | bytes 983040 | tf_op jit(solution)/shard_map/slice | solution.py:298
  2.6 2.9 %collective-permute-start.1 = (bf16[384,640]{1,0:T(8,128)(2,1)}, bf16[384,640]{1,0:T(8,128)(2,1)S(1)}, u32[]{:S(2)}, u32[]{:S(2)}) collective-permute-start(bf16[384,640]{1,0:T(8,128)(2,1)} %slice.7), channel_id=1, source_target_pairs={{0,2},{1,3},{2,0},{3,1},{4,6},{5,7},{6,4},{7,5},{8,10},{9,11},{10,... | collective-permute-start | bytes 1474568 | tf_op jit(solution)/shard_map/ppermute | solution.py:272
  5.6 1.7 %slice.6 = bf16[256,640]{1,0:T(8,128)(2,1)} slice(bf16[640,640]{1,0:T(8,128)(2,1)} %refs_6_.1), slice={[384:640], [0:640]} | slice | bytes 655360 | tf_op jit(solution)/shard_map/slice | solution.py:298
  7.3 1.6 %collective-permute-start = (bf16[256,640]{1,0:T(8,128)(2,1)}, bf16[256,640]{1,0:T(8,128)(2,1)}, u32[]{:S(2)}, u32[]{:S(2)}) collective-permute-start(bf16[256,640]{1,0:T(8,128)(2,1)} %slice.6), channel_id=1, source_target_pairs={{0,8},{4,12},{8,16},{12,20},{16,24},{20,28},{24,0},{28,4},{1,9},{5... | collective-permute-start | bytes 983048 | tf_op jit(solution)/shard_map/ppermute | solution.py:281
  13.3 2.0 %shard_map.104 = (bf16[2,128,1280]{2,1,0:T(8,128)(2,1)S(1)}, bf16[4,128,640]{2,1,0:T(8,128)(2,1)S(1)}, bf16[4,128,384]{2,1,0:T(8,128)(2,1)S(1)}, bf16[4,128,256]...) custom-call(s32[1]{0:T(128)} %bitcast.3.core_ref, ...), custom_call_target="tpu_custom_call" | custom-call | flops 1 | bytes 1 | tf_op jit(solution)/shard_map/pallas_call | solution.py:78
  15.4 1.6 %collective-permute-done.1.refs_7_ = bf16[384,640]{1,0:T(8,128)(2,1)S(1)} collective-permute-done((bf16[384,640]{1,0:T(8,128)(2,1)}, bf16[384,640]{1,0:T(8,128)(2,1)S(1)}, u32[]{:S(2)}, u32[]{:S(2)}) %collective-permute-start.1) | collective-permute-done | bytes 491552 | tf_op jit(solution)/shard_map/ppermute | solution.py:272
  17.0 1.7 %collective-permute-done.refs_7_ = bf16[256,640]{1,0:T(8,128)(2,1)} collective-permute-done((bf16[256,640]{1,0:T(8,128)(2,1)}, bf16[256,640]{1,0:T(8,128)(2,1)}, u32[]{:S(2)}, u32[]{:S(2)}) %collective-permute-start) | collective-permute-done | bytes 327712 | tf_op jit(solution)/shard_map/ppermute | solution.py:281
  24.3 8.0 %collective-permute-done.9.refs_7_ = bf16[256,640]{1,0:T(8,128)(2,1)S(1)} collective-permute-done((bf16[256,640]{1,0:T(8,128)(2,1)}, bf16[256,640]{1,0:T(8,128)(2,1)S(1)}, u32[]{:S(2)}, u32[]{:S(2)}) %collective-permute-start.9) | collective-permute-done | bytes 327712 | tf_op jit(solution)/shard_map/ppermute | solution.py:281
  33.0 9.8 %collective-permute-done.8.refs_6_ = bf16[384,640]{1,0:T(8,128)(2,1)S(1)} collective-permute-done((bf16[384,640]{1,0:T(8,128)(2,1)}, bf16[384,640]{1,0:T(8,128)(2,1)S(1)}, u32[]{:S(2)}, u32[]{:S(2)}) %collective-permute-start.8) | collective-permute-done | bytes 491552 | tf_op jit(solution)/shard_map/ppermute | solution.py:281
  42.9 10.5 %collective-permute-done.11.refs_8_ = bf16[384,640]{1,0:T(8,128)(2,1)S(1)} collective-permute-done((bf16[384,640]{1,0:T(8,128)(2,1)S(1)}, bf16[384,640]{1,0:T(8,128)(2,1)S(1)}, u32[]{:S(2)}, u32[]{:S(2)}) %collective-permute-start.11) | collective-permute-done | bytes 491552 | tf_op jit(solution)/shard_map/ppermute | solution.py:281
  53.3 4.7 %shard_map.105.refs_0_ = bf16[2,256,640]{2,1,0:T(8,128)(2,1)S(1)} custom-call(bf16[2,128,1280]{2,1,0:T(8,128)(2,1)S(1)} %get-tuple-element.210.refs_0_, bf16[2,128,1280]{2,1,0:T(8,128)(2,1)S(1)} %collective-permute-done.2.refs_1_, bf16[4,128,640]{2,1,0:T(8,128)(2,1)S(1)} %get-tuple-element.236.refs_2_, ...), custom_call_target="tpu_custom_call" | custom-call | flops 1 | bytes 1 | tf_op jit(solution)/shard_map/pallas_call | solution.py:129
  58.0 1.6 %collective-permute-start.12 = (bf16[2,256,640]{2,1,0:T(8,128)(2,1)S(1)}, bf16[2,256,640]{2,1,0:T(8,128)(2,1)S(1)}, u32[]{:S(2)}, u32[]{:S(2)}) collective-permute-start(bf16[2,256,640]{2,1,0:T(8,128)(2,1)S(1)} %shard_map.105.refs_0_), channel_id=1, source_target_pairs={{0,4},{4,0},{8,12},{12,8},{16,20},{20,16},{24,28},{28,24},{1,5},{5... | collective-permute-start | bytes 1966088 | tf_op jit(solution)/shard_map/ppermute | solution.py:278
  60.3 9.7 %collective-permute-done.15.refs_7_ = bf16[256,640]{1,0:T(8,128)(2,1)S(1)} collective-permute-done((bf16[256,640]{1,0:T(8,128)(2,1)S(1)}, bf16[256,640]{1,0:T(8,128)(2,1)S(1)}, u32[]{:S(2)}, u32[]{:S(2)}) %collective-permute-start.15) | collective-permute-done | bytes 327712 | tf_op jit(solution)/shard_map/ppermute | solution.py:281
  70.9 2.8 %shard_map.106.refs_1_ = bf16[2,256,384]{2,1,0:T(8,128)(2,1)S(1)} custom-call(bf16[2,128,1280]{2,1,0:T(8,128)(2,1)S(1)} %get-tuple-element.210.refs_0_, bf16[2,128,1280]{2,1,0:T(8,128)(2,1)S(1)} %collective-permute-done.2.refs_1_, bf16[4,128,384]{2,1,0:T(8,128)(2,1)S(1)} %get-tuple-element.249.refs_2_, ...), custom_call_target="tpu_custom_call" | custom-call | flops 1 | bytes 1 | tf_op jit(solution)/shard_map/pallas_call | solution.py:129
  73.7 1.6 %collective-permute-start.19 = (bf16[2,256,384]{2,1,0:T(8,128)(2,1)S(1)}, bf16[2,256,384]{2,1,0:T(8,128)(2,1)S(1)}, u32[]{:S(2)}, u32[]{:S(2)}) collective-permute-start(bf16[2,256,384]{2,1,0:T(8,128)(2,1)S(1)} %shard_map.106.refs_1_), channel_id=1, source_target_pairs={{0,4},{4,0},{8,12},{12,8},{16,20},{20,16},{24,28},{28,24},{1,5},{5... | collective-permute-start | bytes 1179656 | tf_op jit(solution)/shard_map/ppermute | solution.py:278
  75.3 1.5 %collective-permute-start.17 = (bf16[256,640]{1,0:T(8,128)(2,1)}, bf16[256,640]{1,0:T(8,128)(2,1)}, u32[]{:S(2)}, u32[]{:S(2)}) collective-permute-start(bf16[256,640]{1,0:T(8,128)(2,1)} %slice.6), channel_id=1, source_target_pairs={{0,2},{1,3},{2,0},{3,1},{4,6},{5,7},{6,4},{7,5},{8,10},{9,11},{10,... | collective-permute-start | bytes 983048 | tf_op jit(solution)/shard_map/ppermute | solution.py:272
  76.8 3.7 %collective-permute-done.6.refs_4_ = bf16[8,128,256]{2,1,0:T(8,128)(2,1)S(1)} collective-permute-done((bf16[8,128,256]{2,1,0:T(8,128)(2,1)S(1)}, bf16[8,128,256]{2,1,0:T(8,128)(2,1)S(1)}, u32[]{:S(2)}, u32[]{:S(2)}) %collective-permute-start.6) | collective-permute-done | bytes 524320 | tf_op jit(solution)/shard_map/ppermute | solution.py:272
  80.5 1.9 %shard_map.107.refs_2_ = bf16[2,256,256]{2,1,0:T(8,128)(2,1)S(1)} custom-call(bf16[2,128,1280]{2,1,0:T(8,128)(2,1)S(1)} %get-tuple-element.210.refs_0_, bf16[2,128,1280]{2,1,0:T(8,128)(2,1)S(1)} %collective-permute-done.2.refs_1_, bf16[4,128,256]{2,1,0:T(8,128)(2,1)S(1)} %get-tuple-element.234.refs_2_, ...), custom_call_target="tpu_custom_call" | custom-call | flops 1 | bytes 1 | tf_op jit(solution)/shard_map/pallas_call | solution.py:129
  82.3 1.6 %collective-permute-start.16 = (bf16[2,256,256]{2,1,0:T(8,128)(2,1)S(1)}, bf16[2,256,256]{2,1,0:T(8,128)(2,1)S(1)}, u32[]{:S(2)}, u32[]{:S(2)}) collective-permute-start(bf16[2,256,256]{2,1,0:T(8,128)(2,1)S(1)} %shard_map.107.refs_2_), channel_id=1, source_target_pairs={{0,4},{4,0},{8,12},{12,8},{16,20},{20,16},{24,28},{28,24},{1,5},{5... | collective-permute-start | bytes 786440 | tf_op jit(solution)/shard_map/ppermute | solution.py:278
  84.3 1.6 %collective-permute-done.18.refs_8_ = bf16[384,640]{1,0:T(8,128)(2,1)S(1)} collective-permute-done((bf16[384,640]{1,0:T(8,128)(2,1)S(1)}, bf16[384,640]{1,0:T(8,128)(2,1)S(1)}, u32[]{:S(2)}, u32[]{:S(2)}) %collective-permute-start.18) | collective-permute-done | bytes 491552 | tf_op jit(solution)/shard_map/ppermute | solution.py:281
  87.2 1.5 %collective-permute-start.29 = (bf16[512,640]{1,0:T(8,128)(2,1)}, bf16[512,640]{1,0:T(8,128)(2,1)}, u32[]{:S(2)}, u32[]{:S(2)}) collective-permute-start(bf16[512,640]{1,0:T(8,128)(2,1)} %pad_maximum_fusion.1), channel_id=1, source_target_pairs={{0,2},{1,3},{2,0},{3,1},{4,6},{5,7},{6,4},{7,5},{8,10},{9,11},{10,... | collective-permute-start | bytes 1966088 | tf_op jit(solution)/shard_map/ppermute | solution.py:272
  90.6 3.3 %shard_map.108 = (f32[256,640]{1,0:T(8,128)S(1)}, f32[256,640]{1,0:T(8,128)S(1)}, bf16[256,640]{1,0:T(8,128)(2,1)S(1)}, bf16[128,640]{1,0:T(8,128)(2,1)S(1)}, bf16[128,640]{1,0:T(8,128)(2,1)S(1)}) custom-call(s32[1]{0:T(128)} %bitcast.2.flip_ref, bf16[2,256,640]{2,1,0:T(8,128)(2,1)S(1)} %shard_map.105.refs_0_, bf16[2,256,384]{2,1,0:T(8,128)(2,1)S(1)} %shard_map.106.refs_1_, ...), custom_call_target="tpu_custom_call" | custom-call | flops 1 | bytes 1 | tf_op jit(solution)/shard_map/pallas_call | solution.py:173
  94.6 3.0 %collective-permute-done.21.refs_9_ = bf16[256,640]{1,0:T(8,128)(2,1)} collective-permute-done((bf16[256,640]{1,0:T(8,128)(2,1)}, bf16[256,640]{1,0:T(8,128)(2,1)}, u32[]{:S(2)}, u32[]{:S(2)}) %collective-permute-start.21) | collective-permute-done | bytes 327712 | tf_op jit(solution)/shard_map/ppermute | solution.py:272
  97.7 1.6 %collective-permute-start.30 = (bf16[256,640]{1,0:T(8,128)(2,1)S(1)}, bf16[256,640]{1,0:T(8,128)(2,1)S(1)}, u32[]{:S(2)}, u32[]{:S(2)}) collective-permute-start(bf16[256,640]{1,0:T(8,128)(2,1)S(1)} %shard_map.109), channel_id=1, source_target_pairs={{0,4},{4,0},{8,12},{12,8},{16,20},{20,16},{24,28},{28,24},{1,5},{5... | collective-permute-start | bytes 983048 | tf_op jit(solution)/shard_map/ppermute | solution.py:278
  99.3 3.4 %shard_map.110 = (f32[256,640]{1,0:T(8,128)S(1)}, f32[256,640]{1,0:T(8,128)S(1)}, bf16[256,640]{1,0:T(8,128)(2,1)S(1)}, bf16[128,640]{1,0:T(8,128)(2,1)S(1)}, bf16[128,640]{1,0:T(8,128)(2,1)S(1)}) custom-call(s32[1]{0:T(128)} %bitcast.2.flip_ref, bf16[2,256,640]{2,1,0:T(8,128)(2,1)S(1)} %shard_map.105.refs_0_, bf16[2,256,384]{2,1,0:T(8,128)(2,1)S(1)} %shard_map.106.refs_1_, ...), custom_call_target="tpu_custom_call" | custom-call | flops 1 | bytes 1 | tf_op jit(solution)/shard_map/pallas_call | solution.py:173
  107.9 3.8 %shard_map.112 = (f32[256,640]{1,0:T(8,128)S(1)}, f32[256,640]{1,0:T(8,128)S(1)}, bf16[256,640]{1,0:T(8,128)(2,1)}, bf16[128,640]{1,0:T(8,128)(2,1)S(1)}, bf16[128,640]{1,0:T(8,128)(2,1)S(1)}) custom-call(s32[1]{0:T(128)} %bitcast.2.flip_ref, bf16[2,256,640]{2,1,0:T(8,128)(2,1)S(1)} %shard_map.105.refs_0_, bf16[2,256,384]{2,1,0:T(8,128)(2,1)S(1)} %shard_map.106.refs_1_, ...), custom_call_target="tpu_custom_call" | custom-call | flops 1 | bytes 1 | tf_op jit(solution)/shard_map/pallas_call | solution.py:173
  113.4 1.6 %collective-permute-start.36 = (bf16[256,640]{1,0:T(8,128)(2,1)S(1)}, bf16[256,640]{1,0:T(8,128)(2,1)S(1)}, u32[]{:S(2)}, u32[]{:S(2)}) collective-permute-start(bf16[256,640]{1,0:T(8,128)(2,1)S(1)} %shard_map.113), channel_id=1, source_target_pairs={{0,4},{4,0},{8,12},{12,8},{16,20},{20,16},{24,28},{28,24},{1,5},{5... | collective-permute-start | bytes 983048 | tf_op jit(solution)/shard_map/ppermute | solution.py:278
  116.0 3.8 %shard_map.116 = (f32[256,640]{1,0:T(8,128)S(1)}, f32[256,640]{1,0:T(8,128)S(1)}, bf16[256,640]{1,0:T(8,128)(2,1)}, bf16[128,640]{1,0:T(8,128)(2,1)S(1)}, bf16[128,640]{1,0:T(8,128)(2,1)S(1)}) custom-call(s32[1]{0:T(128)} %bitcast.2.flip_ref, bf16[2,256,640]{2,1,0:T(8,128)(2,1)S(1)} %shard_map.105.refs_0_, bf16[2,256,384]{2,1,0:T(8,128)(2,1)S(1)} %shard_map.106.refs_1_, ...), custom_call_target="tpu_custom_call" | custom-call | flops 1 | bytes 1 | tf_op jit(solution)/shard_map/pallas_call | solution.py:173
  124.1 1.5 %collective-permute-start.37 = (bf16[256,640]{1,0:T(8,128)(2,1)S(1)}, bf16[256,640]{1,0:T(8,128)(2,1)S(1)}, u32[]{:S(2)}, u32[]{:S(2)}) collective-permute-start(bf16[256,640]{1,0:T(8,128)(2,1)S(1)} %shard_map.117), channel_id=1, source_target_pairs={{0,4},{4,0},{8,12},{12,8},{16,20},{20,16},{24,28},{28,24},{1,5},{5... | collective-permute-start | bytes 983048 | tf_op jit(solution)/shard_map/ppermute | solution.py:278
  128.1 1.4 %shard_map.121 = (bf16[128,5120]{1,0:T(8,128)(2,1)}, bf16[128,5120]{1,0:T(8,128)(2,1)}) custom-call(s32[2]{0:T(128)S(1)} %add_add_fusion.2.where_ref, bf16[256,640]{1,0:T(8,128)(2,1)S(1)} %shard_map.115.mine_ref, bf16[256,640]{1,0:T(8,128)(2,1)S(1)} %copy-done.26, ...), custom_call_target="tpu_custom_call", output_to_operand_aliasing={{0}: (3, {}), {1}: (4, {})} | custom-call | flops 1 | bytes 1 | tf_op jit(solution)/shard_map/pallas_call | solution.py:231
  129.6 1.4 %shard_map.122 = (bf16[128,5120]{1,0:T(8,128)(2,1)}, bf16[128,5120]{1,0:T(8,128)(2,1)}) custom-call(s32[2]{0:T(128)S(1)} %add_add_fusion.1.where_ref, bf16[256,640]{1,0:T(8,128)(2,1)S(1)} %shard_map.118.mine_ref, bf16[256,640]{1,0:T(8,128)(2,1)S(1)} %copy-done.28, ...), custom_call_target="tpu_custom_call", output_to_operand_aliasing={{0}: (3, {}), {1}: (4, {})} | custom-call | flops 1 | bytes 1 | tf_op jit(solution)/shard_map/pallas_call | solution.py:231
  131.1 3.1 %collective-permute-done.37.other_ref = bf16[256,640]{1,0:T(8,128)(2,1)S(1)} collective-permute-done((bf16[256,640]{1,0:T(8,128)(2,1)S(1)}, bf16[256,640]{1,0:T(8,128)(2,1)S(1)}, u32[]{:S(2)}, u32[]{:S(2)}) %collective-permute-start.37) | collective-permute-done | bytes 327712 | tf_op jit(solution)/shard_map/ppermute | solution.py:278
  (142 shorter events, 32.9 us)
Async XLA Ops:
  2.6 14.4 %collective-permute-start.1 = (bf16[384,640]{1,0:T(8,128)(2,1)}, bf16[384,640]{1,0:T(8,128)(2,1)S(1)}, u32[]{:S(2)}, u32[]{:S(2)}) collective-permute-start(bf16[384,640]{1,0:T(8,128)(2,1)} %slice.7), channel_id=1, source_target_pairs={{0,2},{1,3},{2,0},{3,1},{4,6},{5,7},{6,4},{7,5},{8,10},{9,11},{10,... | collective-permute-start | bytes 1474568 | tf_op jit(solution)/shard_map/ppermute | solution.py:272
  7.3 11.3 %collective-permute-start = (bf16[256,640]{1,0:T(8,128)(2,1)}, bf16[256,640]{1,0:T(8,128)(2,1)}, u32[]{:S(2)}, u32[]{:S(2)}) collective-permute-start(bf16[256,640]{1,0:T(8,128)(2,1)} %slice.6), channel_id=1, source_target_pairs={{0,8},{4,12},{8,16},{12,20},{16,24},{20,28},{24,0},{28,4},{1,9},{5... | collective-permute-start | bytes 983048 | tf_op jit(solution)/shard_map/ppermute | solution.py:281
  18.7 13.7 %collective-permute-start.2 = (bf16[2,128,1280]{2,1,0:T(8,128)(2,1)S(1)}, bf16[2,128,1280]{2,1,0:T(8,128)(2,1)S(1)}, u32[]{:S(2)}, u32[]{:S(2)}) collective-permute-start(bf16[2,128,1280]{2,1,0:T(8,128)(2,1)S(1)} %get-tuple-element.219), channel_id=1, source_target_pairs={{0,1},{1,0},{2,3},{3,2},{4,5},{5,4},{6,7},{7,6},{8,9},{9,8},{10,11... | collective-permute-start | bytes 1966088 | tf_op jit(solution)/shard_map/ppermute | solution.py:275
  19.2 4.0 %collective-permute-start.4 = (bf16[4,128,384]{2,1,0:T(8,128)(2,1)S(1)}, bf16[4,128,384]{2,1,0:T(8,128)(2,1)S(1)}, u32[]{:S(2)}, u32[]{:S(2)}) collective-permute-start(bf16[4,128,384]{2,1,0:T(8,128)(2,1)S(1)} %get-tuple-element.227), channel_id=1, source_target_pairs={{0,1},{1,0},{2,3},{3,2},{4,5},{5,4},{6,7},{7,6},{8,9},{9,8},{10,11... | collective-permute-start | bytes 1179656 | tf_op jit(solution)/shard_map/ppermute | solution.py:275
  19.2 3.5 %collective-permute-start.3 = (bf16[4,128,256]{2,1,0:T(8,128)(2,1)S(1)}, bf16[4,128,256]{2,1,0:T(8,128)(2,1)S(1)}, u32[]{:S(2)}, u32[]{:S(2)}) collective-permute-start(bf16[4,128,256]{2,1,0:T(8,128)(2,1)S(1)} %get-tuple-element.226), channel_id=1, source_target_pairs={{0,1},{1,0},{2,3},{3,2},{4,5},{5,4},{6,7},{7,6},{8,9},{9,8},{10,11... | collective-permute-start | bytes 786440 | tf_op jit(solution)/shard_map/ppermute | solution.py:275
  19.7 12.6 %collective-permute-start.9 = (bf16[256,640]{1,0:T(8,128)(2,1)}, bf16[256,640]{1,0:T(8,128)(2,1)S(1)}, u32[]{:S(2)}, u32[]{:S(2)}) collective-permute-start(bf16[256,640]{1,0:T(8,128)(2,1)} %collective-permute-done.refs_7_), channel_id=1, source_target_pairs={{0,8},{4,12},{8,16},{12,20},{16,24},{20,28},{24,0},{28,4},{1,9},{5... | collective-permute-start | bytes 983048 | tf_op jit(solution)/shard_map/ppermute | solution.py:281
  20.7 22.1 %collective-permute-start.7 = (bf16[4,128,640]{2,1,0:T(8,128)(2,1)S(1)}, bf16[4,128,640]{2,1,0:T(8,128)(2,1)S(1)}, u32[]{:S(2)}, u32[]{:S(2)}) collective-permute-start(bf16[4,128,640]{2,1,0:T(8,128)(2,1)S(1)} %get-tuple-element.236.refs_2_), channel_id=1, source_target_pairs={{0,2},{1,3},{2,0},{3,1},{4,6},{5,7},{6,4},{7,5},{8,10},{9,11},{10,... | collective-permute-start | bytes 1966088 | tf_op jit(solution)/shard_map/ppermute | solution.py:272
  22.6 30.7 %collective-permute-start.10 = (bf16[4,128,640]{2,1,0:T(8,128)(2,1)S(1)}, bf16[4,128,640]{2,1,0:T(8,128)(2,1)S(1)}, u32[]{:S(2)}, u32[]{:S(2)}) collective-permute-start(bf16[4,128,640]{2,1,0:T(8,128)(2,1)S(1)} %collective-permute-done.5.refs_3_), channel_id=1, source_target_pairs={{0,2},{1,3},{2,0},{3,1},{4,6},{5,7},{6,4},{7,5},{8,10},{9,11},{10,... | collective-permute-start | bytes 1966088 | tf_op jit(solution)/shard_map/ppermute | solution.py:272
  23.2 19.6 %collective-permute-start.8 = (bf16[384,640]{1,0:T(8,128)(2,1)}, bf16[384,640]{1,0:T(8,128)(2,1)S(1)}, u32[]{:S(2)}, u32[]{:S(2)}) collective-permute-start(bf16[384,640]{1,0:T(8,128)(2,1)} %slice.7), channel_id=1, source_target_pairs={{0,8},{4,12},{8,16},{12,20},{16,24},{20,28},{24,0},{28,4},{1,9},{5... | collective-permute-start | bytes 1474568 | tf_op jit(solution)/shard_map/ppermute | solution.py:281
  32.3 21.1 %collective-permute-start.11 = (bf16[384,640]{1,0:T(8,128)(2,1)S(1)}, bf16[384,640]{1,0:T(8,128)(2,1)S(1)}, u32[]{:S(2)}, u32[]{:S(2)}) collective-permute-start(bf16[384,640]{1,0:T(8,128)(2,1)S(1)} %collective-permute-done.1.refs_7_), channel_id=1, source_target_pairs={{0,8},{4,12},{8,16},{12,20},{16,24},{20,28},{24,0},{28,4},{1,9},{5... | collective-permute-start | bytes 1474568 | tf_op jit(solution)/shard_map/ppermute | solution.py:281
  32.4 38.5 %collective-permute-start.13 = (bf16[8,128,384]{2,1,0:T(8,128)(2,1)S(1)}, bf16[8,128,384]{2,1,0:T(8,128)(2,1)S(1)}, u32[]{:S(2)}, u32[]{:S(2)}) collective-permute-start(bf16[8,128,384]{2,1,0:T(8,128)(2,1)S(1)} %pad_maximum_fusion), channel_id=1, source_target_pairs={{0,2},{1,3},{2,0},{3,1},{4,6},{5,7},{6,4},{7,5},{8,10},{9,11},{10,... | collective-permute-start | bytes 2359304 | tf_op jit(solution)/shard_map/ppermute | solution.py:272
  42.8 28.1 %collective-permute-start.14 = (bf16[384,640]{1,0:T(8,128)(2,1)S(1)}, bf16[384,640]{1,0:T(8,128)(2,1)}, u32[]{:S(2)}, u32[]{:S(2)}) collective-permute-start(bf16[384,640]{1,0:T(8,128)(2,1)S(1)} %collective-permute-done.8.refs_6_), channel_id=1, source_target_pairs={{0,8},{4,12},{8,16},{12,20},{16,24},{20,28},{24,0},{28,4},{1,9},{5... | collective-permute-start | bytes 1474568 | tf_op jit(solution)/shard_map/ppermute | solution.py:281
  42.8 27.1 %collective-permute-start.15 = (bf16[256,640]{1,0:T(8,128)(2,1)S(1)}, bf16[256,640]{1,0:T(8,128)(2,1)S(1)}, u32[]{:S(2)}, u32[]{:S(2)}) collective-permute-start(bf16[256,640]{1,0:T(8,128)(2,1)S(1)} %collective-permute-done.9.refs_7_), channel_id=1, source_target_pairs={{0,8},{4,12},{8,16},{12,20},{16,24},{20,28},{24,0},{28,4},{1,9},{5... | collective-permute-start | bytes 983048 | tf_op jit(solution)/shard_map/ppermute | solution.py:281
  58.0 17.3 %collective-permute-start.12 = (bf16[2,256,640]{2,1,0:T(8,128)(2,1)S(1)}, bf16[2,256,640]{2,1,0:T(8,128)(2,1)S(1)}, u32[]{:S(2)}, u32[]{:S(2)}) collective-permute-start(bf16[2,256,640]{2,1,0:T(8,128)(2,1)S(1)} %shard_map.105.refs_0_), channel_id=1, source_target_pairs={{0,4},{4,0},{8,12},{12,8},{16,20},{20,16},{24,28},{28,24},{1,5},{5... | collective-permute-start | bytes 1966088 | tf_op jit(solution)/shard_map/ppermute | solution.py:278
  59.7 20.8 %collective-permute-start.6 = (bf16[8,128,256]{2,1,0:T(8,128)(2,1)S(1)}, bf16[8,128,256]{2,1,0:T(8,128)(2,1)S(1)}, u32[]{:S(2)}, u32[]{:S(2)}) collective-permute-start(bf16[8,128,256]{2,1,0:T(8,128)(2,1)S(1)} %pad_maximum_fusion.2), channel_id=1, source_target_pairs={{0,2},{1,3},{2,0},{3,1},{4,6},{5,7},{6,4},{7,5},{8,10},{9,11},{10,... | collective-permute-start | bytes 1572872 | tf_op jit(solution)/shard_map/ppermute | solution.py:272
  69.9 16.0 %collective-permute-start.18 = (bf16[384,640]{1,0:T(8,128)(2,1)S(1)}, bf16[384,640]{1,0:T(8,128)(2,1)S(1)}, u32[]{:S(2)}, u32[]{:S(2)}) collective-permute-start(bf16[384,640]{1,0:T(8,128)(2,1)S(1)} %collective-permute-done.11.refs_8_), channel_id=1, source_target_pairs={{0,8},{4,12},{8,16},{12,20},{16,24},{20,28},{24,0},{28,4},{1,9},{5... | collective-permute-start | bytes 1474568 | tf_op jit(solution)/shard_map/ppermute | solution.py:281
  73.7 10.6 %collective-permute-start.19 = (bf16[2,256,384]{2,1,0:T(8,128)(2,1)S(1)}, bf16[2,256,384]{2,1,0:T(8,128)(2,1)S(1)}, u32[]{:S(2)}, u32[]{:S(2)}) collective-permute-start(bf16[2,256,384]{2,1,0:T(8,128)(2,1)S(1)} %shard_map.106.refs_1_), channel_id=1, source_target_pairs={{0,4},{4,0},{8,12},{12,8},{16,20},{20,16},{24,28},{28,24},{1,5},{5... | collective-permute-start | bytes 1179656 | tf_op jit(solution)/shard_map/ppermute | solution.py:278
  75.3 19.3 %collective-permute-start.22 = (bf16[384,640]{1,0:T(8,128)(2,1)}, bf16[384,640]{1,0:T(8,128)(2,1)}, u32[]{:S(2)}, u32[]{:S(2)}) collective-permute-start(bf16[384,640]{1,0:T(8,128)(2,1)} %collective-permute-done.14.refs_6_), channel_id=1, source_target_pairs={{0,8},{4,12},{8,16},{12,20},{16,24},{20,28},{24,0},{28,4},{1,9},{5... | collective-permute-start | bytes 1474568 | tf_op jit(solution)/shard_map/ppermute | solution.py:281
  75.3 13.4 %collective-permute-start.17 = (bf16[256,640]{1,0:T(8,128)(2,1)}, bf16[256,640]{1,0:T(8,128)(2,1)}, u32[]{:S(2)}, u32[]{:S(2)}) collective-permute-start(bf16[256,640]{1,0:T(8,128)(2,1)} %slice.6), channel_id=1, source_target_pairs={{0,2},{1,3},{2,0},{3,1},{4,6},{5,7},{6,4},{7,5},{8,10},{9,11},{10,... | collective-permute-start | bytes 983048 | tf_op jit(solution)/shard_map/ppermute | solution.py:272
  82.3 7.2 %collective-permute-start.16 = (bf16[2,256,256]{2,1,0:T(8,128)(2,1)S(1)}, bf16[2,256,256]{2,1,0:T(8,128)(2,1)S(1)}, u32[]{:S(2)}, u32[]{:S(2)}) collective-permute-start(bf16[2,256,256]{2,1,0:T(8,128)(2,1)S(1)} %shard_map.107.refs_2_), channel_id=1, source_target_pairs={{0,4},{4,0},{8,12},{12,8},{16,20},{20,16},{24,28},{28,24},{1,5},{5... | collective-permute-start | bytes 786440 | tf_op jit(solution)/shard_map/ppermute | solution.py:278
  86.7 11.0 %collective-permute-start.21 = (bf16[256,640]{1,0:T(8,128)(2,1)}, bf16[256,640]{1,0:T(8,128)(2,1)}, u32[]{:S(2)}, u32[]{:S(2)}) collective-permute-start(bf16[256,640]{1,0:T(8,128)(2,1)} %collective-permute-done.refs_7_), channel_id=1, source_target_pairs={{0,2},{1,3},{2,0},{3,1},{4,6},{5,7},{6,4},{7,5},{8,10},{9,11},{10,... | collective-permute-start | bytes 983048 | tf_op jit(solution)/shard_map/ppermute | solution.py:272
  87.2 20.7 %collective-permute-start.29 = (bf16[512,640]{1,0:T(8,128)(2,1)}, bf16[512,640]{1,0:T(8,128)(2,1)}, u32[]{:S(2)}, u32[]{:S(2)}) collective-permute-start(bf16[512,640]{1,0:T(8,128)(2,1)} %pad_maximum_fusion.1), channel_id=1, source_target_pairs={{0,2},{1,3},{2,0},{3,1},{4,6},{5,7},{6,4},{7,5},{8,10},{9,11},{10,... | collective-permute-start | bytes 1966088 | tf_op jit(solution)/shard_map/ppermute | solution.py:272
  94.0 3.6 %collective-permute-start.20 = (bf16[128,640]{1,0:T(8,128)(2,1)S(1)}, bf16[128,640]{1,0:T(8,128)(2,1)S(1)}, u32[]{:S(2)}, u32[]{:S(2)}) collective-permute-start(bf16[128,640]{1,0:T(8,128)(2,1)S(1)} %get-tuple-element.280), channel_id=1, source_target_pairs={{0,1},{1,0},{2,3},{3,2},{4,5},{5,4},{6,7},{7,6},{8,9},{9,8},{10,11... | collective-permute-start | bytes 491528 | tf_op jit(solution)/shard_map/ppermute | solution.py:275
  94.1 3.6 %collective-permute-start.23 = (bf16[128,640]{1,0:T(8,128)(2,1)S(1)}, bf16[128,640]{1,0:T(8,128)(2,1)S(1)}, u32[]{:S(2)}, u32[]{:S(2)}) collective-permute-start(bf16[128,640]{1,0:T(8,128)(2,1)S(1)} %get-tuple-element.291), channel_id=1, source_target_pairs={{0,1},{1,0},{2,3},{3,2},{4,5},{5,4},{6,7},{7,6},{8,9},{9,8},{10,11... | collective-permute-start | bytes 491528 | tf_op jit(solution)/shard_map/ppermute | solution.py:275
  94.6 17.0 %collective-permute-start.31 = (bf16[384,640]{1,0:T(8,128)(2,1)S(1)}, bf16[384,640]{1,0:T(8,128)(2,1)S(1)}, u32[]{:S(2)}, u32[]{:S(2)}) collective-permute-start(bf16[384,640]{1,0:T(8,128)(2,1)S(1)} %copy-done.22), channel_id=1, source_target_pairs={{0,8},{4,12},{8,16},{12,20},{16,24},{20,28},{24,0},{28,4},{1,9},{5... | collective-permute-start | bytes 1474568 | tf_op jit(solution)/shard_map/ppermute | solution.py:281
  97.7 8.0 %collective-permute-start.30 = (bf16[256,640]{1,0:T(8,128)(2,1)S(1)}, bf16[256,640]{1,0:T(8,128)(2,1)S(1)}, u32[]{:S(2)}, u32[]{:S(2)}) collective-permute-start(bf16[256,640]{1,0:T(8,128)(2,1)S(1)} %shard_map.109), channel_id=1, source_target_pairs={{0,4},{4,0},{8,12},{12,8},{16,20},{20,16},{24,28},{28,24},{1,5},{5... | collective-permute-start | bytes 983048 | tf_op jit(solution)/shard_map/ppermute | solution.py:278
  104.5 10.5 %collective-permute-start.28 = (bf16[256,640]{1,0:T(8,128)(2,1)S(1)}, bf16[256,640]{1,0:T(8,128)(2,1)S(1)}, u32[]{:S(2)}, u32[]{:S(2)}) collective-permute-start(bf16[256,640]{1,0:T(8,128)(2,1)S(1)} %shard_map.111), channel_id=1, source_target_pairs={{0,4},{4,0},{8,12},{12,8},{16,20},{20,16},{24,28},{28,24},{1,5},{5... | collective-permute-start | bytes 983048 | tf_op jit(solution)/shard_map/ppermute | solution.py:278
  105.1 9.9 %collective-permute-start.27 = (bf16[256,640]{1,0:T(8,128)(2,1)S(1)}, bf16[256,640]{1,0:T(8,128)(2,1)S(1)}, u32[]{:S(2)}, u32[]{:S(2)}) collective-permute-start(bf16[256,640]{1,0:T(8,128)(2,1)S(1)} %get-tuple-element.317), channel_id=1, source_target_pairs={{0,1},{1,0},{2,3},{3,2},{4,5},{5,4},{6,7},{7,6},{8,9},{9,8},{10,11... | collective-permute-start | bytes 983048 | tf_op jit(solution)/shard_map/ppermute | solution.py:275
  106.5 8.6 %collective-permute-start.26 = (bf16[256,640]{1,0:T(8,128)(2,1)S(1)}, bf16[256,640]{1,0:T(8,128)(2,1)S(1)}, u32[]{:S(2)}, u32[]{:S(2)}) collective-permute-start(bf16[256,640]{1,0:T(8,128)(2,1)S(1)} %get-tuple-element.314), channel_id=1, source_target_pairs={{0,1},{1,0},{2,3},{3,2},{4,5},{5,4},{6,7},{7,6},{8,9},{9,8},{10,11... | collective-permute-start | bytes 983048 | tf_op jit(solution)/shard_map/ppermute | solution.py:275
  113.4 10.0 %collective-permute-start.36 = (bf16[256,640]{1,0:T(8,128)(2,1)S(1)}, bf16[256,640]{1,0:T(8,128)(2,1)S(1)}, u32[]{:S(2)}, u32[]{:S(2)}) collective-permute-start(bf16[256,640]{1,0:T(8,128)(2,1)S(1)} %shard_map.113), channel_id=1, source_target_pairs={{0,4},{4,0},{8,12},{12,8},{16,20},{20,16},{24,28},{28,24},{1,5},{5... | collective-permute-start | bytes 983048 | tf_op jit(solution)/shard_map/ppermute | solution.py:278
  121.2 4.4 %collective-permute-start.39 = (bf16[256,640]{1,0:T(8,128)(2,1)}, bf16[256,640]{1,0:T(8,128)(2,1)S(1)}, u32[]{:S(2)}, u32[]{:S(2)}) collective-permute-start(bf16[256,640]{1,0:T(8,128)(2,1)} %get-tuple-element.375), channel_id=1, source_target_pairs={{0,1},{1,0},{2,3},{3,2},{4,5},{5,4},{6,7},{7,6},{8,9},{9,8},{10,11... | collective-permute-start | bytes 983048 | tf_op jit(solution)/shard_map/ppermute | solution.py:275
  124.1 10.1 %collective-permute-start.37 = (bf16[256,640]{1,0:T(8,128)(2,1)S(1)}, bf16[256,640]{1,0:T(8,128)(2,1)S(1)}, u32[]{:S(2)}, u32[]{:S(2)}) collective-permute-start(bf16[256,640]{1,0:T(8,128)(2,1)S(1)} %shard_map.117), channel_id=1, source_target_pairs={{0,4},{4,0},{8,12},{12,8},{16,20},{20,16},{24,28},{28,24},{1,5},{5... | collective-permute-start | bytes 983048 | tf_op jit(solution)/shard_map/ppermute | solution.py:278
  (39 other events, 223.3 us)

commit v13 on v12

--- a/solution.py
+++ b/solution.py
@@ -294,7 +294,7 @@
             ring.append(onward(ring[step]))
 
     depth = out_weight.shape[0]
-    cut = depth * 3 // 5 // 16 * 16
+    cut = depth * 13 // 20 // 16 * 16
     upper, lower = [out_weight[:cut]], [out_weight[cut:]]
     lower.append(onward(lower[0]))
     upper.append(onward(upper[0]))

time: 136 us -> 144 us (1.059)
  starting transfers between devices: 24.9 us -> 29.1 us
  waiting for transfers between devices: 62.6 us -> 66.6 us
    ppermute x7, waiting for transfers between devices: 5.9 us -> 13 us  [across(): return lax.ppermute(array, 'dp', [(i, i ^ 1) for i in range(n_dp)])]
    ppermute x8, waiting for transfers between devices: 9.67 us -> 3.18 us  [far(): return lax.ppermute(array, 'seq', [(i, i ^ 2) for i in range(n_seq)])]
    ppermute x9, waiting for transfers between devices: 41.2 us -> 45.3 us  [onward(): return lax.ppermute(array, 'dp', [(i, (i + 2) % n_dp) for i in range(n_dp)])]
    ppermute x8, starting transfers between devices: 8.77 us -> 12.4 us  [far(): return lax.ppermute(array, 'seq', [(i, i ^ 2) for i in range(n_seq)])]
    ppermute x9, starting transfers between devices: 2.96 us -> 4.76 us  [onward(): return lax.ppermute(array, 'dp', [(i, (i + 2) % n_dp) for i in range(n_dp)])]
    unnamed x62 -> x66, local copies, waits for them, and re-layouts: 9.99 us -> 11.1 us
  transfers between devices with their start and end apart: 40 -> 40, of which waited for: 25 -> 18; matrix products, arithmetic and copies ran while one was open for 2% -> 2% of each run, Pallas kernels for 23% -> 21%
where the time goes in v13:
time: 144 us
  waiting for transfers between devices  66.6 us (46%)
  Pallas kernels  31.3 us (22%)
  starting transfers between devices  29.1 us (20%)
  local copies, waits for them, and re-layouts  14.1 us (10%)
    ppermute x9, waiting for transfers between devices, onward(): return lax.ppermute(array, 'dp', [(i, (i + 2) % n_dp) for i in range(n_dp)])  45.3 us
    pallas_call x4, Pallas kernels, project(): pl.pallas_call(functools.partial(project_kernel, len(acts), spans), in_sp...  13.6 us
    ppermute x7, waiting for transfers between devices, across(): return lax.ppermute(array, 'dp', [(i, i ^ 1) for i in range(n_dp)])  13 us
    ppermute x8, starting transfers between devices, far(): return lax.ppermute(array, 'seq', [(i, i ^ 2) for i in range(n_seq)])  12.4 us
    unnamed x66, local copies, waits for them, and re-layouts  11.1 us
    pallas_call x3, Pallas kernels, attend(): pl.pallas_call(functools.partial(attend_kernel, len(queries)), grid=(widt...  9.38 us
    ppermute x7, starting transfers between devices, across(): return lax.ppermute(array, 'dp', [(i, i ^ 1) for i in range(n_dp)])  9.19 us
    pallas_call x4, Pallas kernels, place(): pl.pallas_call(place_kernel, grid_spec=pltpu.PrefetchScalarGridSpec(num_s...  5.79 us
  transfers between devices with their start and end apart: 40, of which 18 were waited for; matrix products, arithmetic and copies ran while one was open for 2% of the time, Pallas kernels for 21%

profile of v13, /device:TPU:0, one launch (start us, length us, event | category | flops | bytes accessed | tf_op | source)
XLA Modules:
  0.0 143.5 jit_solution(16573660135511621356)
XLA Ops:
  0.7 2.0 %slice.7 = bf16[416,640]{1,0:T(8,128)(2,1)} slice(bf16[640,640]{1,0:T(8,128)(2,1)} %refs_6_.1), slice={[0:416], [0:640]} | slice | bytes 1064960 | tf_op jit(solution)/shard_map/slice | solution.py:298
  2.7 2.9 %collective-permute-start.1 = (bf16[416,640]{1,0:T(8,128)(2,1)}, bf16[416,640]{1,0:T(8,128)(2,1)S(1)}, u32[]{:S(2)}, u32[]{:S(2)}) collective-permute-start(bf16[416,640]{1,0:T(8,128)(2,1)} %slice.7), channel_id=1, source_target_pairs={{0,2},{1,3},{2,0},{3,1},{4,6},{5,7},{6,4},{7,5},{8,10},{9,11},{10,... | collective-permute-start | bytes 1597448 | tf_op jit(solution)/shard_map/ppermute | solution.py:272
  6.6 1.6 %collective-permute-start = (bf16[224,640]{1,0:T(8,128)(2,1)S(1)}, bf16[224,640]{1,0:T(8,128)(2,1)}, u32[]{:S(2)}, u32[]{:S(2)}) collective-permute-start(bf16[224,640]{1,0:T(8,128)(2,1)S(1)} %slice.6), channel_id=1, source_target_pairs={{0,8},{4,12},{8,16},{12,20},{16,24},{20,28},{24,0},{28,4},{1,9},{5... | collective-permute-start | bytes 860168 | tf_op jit(solution)/shard_map/ppermute | solution.py:281
  12.7 2.0 %shard_map.104 = (bf16[2,128,1280]{2,1,0:T(8,128)(2,1)S(1)}, bf16[4,128,640]{2,1,0:T(8,128)(2,1)S(1)}, bf16[4,128,384]{2,1,0:T(8,128)(2,1)S(1)}, bf16[4,128,256]...) custom-call(s32[1]{0:T(128)} %bitcast.3.core_ref, ...), custom_call_target="tpu_custom_call" | custom-call | flops 1 | bytes 1 | tf_op jit(solution)/shard_map/pallas_call | solution.py:78
  14.7 3.2 %collective-permute-done.1.refs_7_ = bf16[416,640]{1,0:T(8,128)(2,1)S(1)} collective-permute-done((bf16[416,640]{1,0:T(8,128)(2,1)}, bf16[416,640]{1,0:T(8,128)(2,1)S(1)}, u32[]{:S(2)}, u32[]{:S(2)}) %collective-permute-start.1) | collective-permute-done | bytes 532512 | tf_op jit(solution)/shard_map/ppermute | solution.py:272
  18.9 1.8 %collective-permute-start.9 = (bf16[224,640]{1,0:T(8,128)(2,1)}, bf16[224,640]{1,0:T(8,128)(2,1)S(1)}, u32[]{:S(2)}, u32[]{:S(2)}) collective-permute-start(bf16[224,640]{1,0:T(8,128)(2,1)} %collective-permute-done.refs_7_), channel_id=1, source_target_pairs={{0,8},{4,12},{8,16},{12,20},{16,24},{20,28},{24,0},{28,4},{1,9},{5... | collective-permute-start | bytes 860168 | tf_op jit(solution)/shard_map/ppermute | solution.py:281
  20.8 1.5 %collective-permute-start.7 = (bf16[4,128,640]{2,1,0:T(8,128)(2,1)S(1)}, bf16[4,128,640]{2,1,0:T(8,128)(2,1)S(1)}, u32[]{:S(2)}, u32[]{:S(2)}) collective-permute-start(bf16[4,128,640]{2,1,0:T(8,128)(2,1)S(1)} %get-tuple-element.236.refs_2_), channel_id=1, source_target_pairs={{0,2},{1,3},{2,0},{3,1},{4,6},{5,7},{6,4},{7,5},{8,10},{9,11},{10,... | collective-permute-start | bytes 1966088 | tf_op jit(solution)/shard_map/ppermute | solution.py:272
  23.6 6.4 %collective-permute-done.9.refs_7_ = bf16[224,640]{1,0:T(8,128)(2,1)S(1)} collective-permute-done((bf16[224,640]{1,0:T(8,128)(2,1)}, bf16[224,640]{1,0:T(8,128)(2,1)S(1)}, u32[]{:S(2)}, u32[]{:S(2)}) %collective-permute-start.9) | collective-permute-done | bytes 286752 | tf_op jit(solution)/shard_map/ppermute | solution.py:281
  31.5 1.6 %collective-permute-start.13 = (bf16[8,128,384]{2,1,0:T(8,128)(2,1)S(1)}, bf16[8,128,384]{2,1,0:T(8,128)(2,1)S(1)}, u32[]{:S(2)}, u32[]{:S(2)}) collective-permute-start(bf16[8,128,384]{2,1,0:T(8,128)(2,1)S(1)} %pad_maximum_fusion), channel_id=1, source_target_pairs={{0,2},{1,3},{2,0},{3,1},{4,6},{5,7},{6,4},{7,5},{8,10},{9,11},{10,... | collective-permute-start | bytes 2359304 | tf_op jit(solution)/shard_map/ppermute | solution.py:272
  33.0 14.1 %collective-permute-done.8.refs_6_ = bf16[416,640]{1,0:T(8,128)(2,1)S(1)} collective-permute-done((bf16[416,640]{1,0:T(8,128)(2,1)}, bf16[416,640]{1,0:T(8,128)(2,1)S(1)}, u32[]{:S(2)}, u32[]{:S(2)}) %collective-permute-start.8) | collective-permute-done | bytes 532512 | tf_op jit(solution)/shard_map/ppermute | solution.py:281
  47.1 11.4 %collective-permute-done.11.refs_8_ = bf16[416,640]{1,0:T(8,128)(2,1)S(1)} collective-permute-done((bf16[416,640]{1,0:T(8,128)(2,1)S(1)}, bf16[416,640]{1,0:T(8,128)(2,1)S(1)}, u32[]{:S(2)}, u32[]{:S(2)}) %collective-permute-start.11) | collective-permute-done | bytes 532512 | tf_op jit(solution)/shard_map/ppermute | solution.py:281
  58.5 4.7 %shard_map.105.refs_0_ = bf16[2,256,640]{2,1,0:T(8,128)(2,1)S(1)} custom-call(bf16[2,128,1280]{2,1,0:T(8,128)(2,1)S(1)} %get-tuple-element.210.refs_0_, bf16[2,128,1280]{2,1,0:T(8,128)(2,1)S(1)} %collective-permute-done.2.refs_1_, bf16[4,128,640]{2,1,0:T(8,128)(2,1)S(1)} %get-tuple-element.236.refs_2_, ...), custom_call_target="tpu_custom_call" | custom-call | flops 1 | bytes 1 | tf_op jit(solution)/shard_map/pallas_call | solution.py:129
  63.2 1.6 %collective-permute-start.12 = (bf16[2,256,640]{2,1,0:T(8,128)(2,1)S(1)}, bf16[2,256,640]{2,1,0:T(8,128)(2,1)S(1)}, u32[]{:S(2)}, u32[]{:S(2)}) collective-permute-start(bf16[2,256,640]{2,1,0:T(8,128)(2,1)S(1)} %shard_map.105.refs_0_), channel_id=1, source_target_pairs={{0,4},{4,0},{8,12},{12,8},{16,20},{20,16},{24,28},{28,24},{1,5},{5... | collective-permute-start | bytes 1966088 | tf_op jit(solution)/shard_map/ppermute | solution.py:278
  64.9 1.6 %collective-permute-start.6 = (bf16[8,128,256]{2,1,0:T(8,128)(2,1)S(1)}, bf16[8,128,256]{2,1,0:T(8,128)(2,1)S(1)}, u32[]{:S(2)}, u32[]{:S(2)}) collective-permute-start(bf16[8,128,256]{2,1,0:T(8,128)(2,1)S(1)} %pad_maximum_fusion.2), channel_id=1, source_target_pairs={{0,2},{1,3},{2,0},{3,1},{4,6},{5,7},{6,4},{7,5},{8,10},{9,11},{10,... | collective-permute-start | bytes 1572872 | tf_op jit(solution)/shard_map/ppermute | solution.py:272
  66.4 8.2 %collective-permute-done.15.refs_7_ = bf16[224,640]{1,0:T(8,128)(2,1)S(1)} collective-permute-done((bf16[224,640]{1,0:T(8,128)(2,1)S(1)}, bf16[224,640]{1,0:T(8,128)(2,1)S(1)}, u32[]{:S(2)}, u32[]{:S(2)}) %collective-permute-start.15) | collective-permute-done | bytes 286752 | tf_op jit(solution)/shard_map/ppermute | solution.py:281
  75.5 2.8 %shard_map.106.refs_1_ = bf16[2,256,384]{2,1,0:T(8,128)(2,1)S(1)} custom-call(bf16[2,128,1280]{2,1,0:T(8,128)(2,1)S(1)} %get-tuple-element.210.refs_0_, bf16[2,128,1280]{2,1,0:T(8,128)(2,1)S(1)} %collective-permute-done.2.refs_1_, bf16[4,128,384]{2,1,0:T(8,128)(2,1)S(1)} %get-tuple-element.249.refs_2_, ...), custom_call_target="tpu_custom_call" | custom-call | flops 1 | bytes 1 | tf_op jit(solution)/shard_map/pallas_call | solution.py:129
  79.7 1.5 %collective-permute-start.17 = (bf16[224,640]{1,0:T(8,128)(2,1)S(1)}, bf16[224,640]{1,0:T(8,128)(2,1)S(1)}, u32[]{:S(2)}, u32[]{:S(2)}) collective-permute-start(bf16[224,640]{1,0:T(8,128)(2,1)S(1)} %copy-done.30), channel_id=1, source_target_pairs={{0,2},{1,3},{2,0},{3,1},{4,6},{5,7},{6,4},{7,5},{8,10},{9,11},{10,... | collective-permute-start | bytes 860168 | tf_op jit(solution)/shard_map/ppermute | solution.py:272
  81.2 1.9 %shard_map.107.refs_2_ = bf16[2,256,256]{2,1,0:T(8,128)(2,1)S(1)} custom-call(bf16[2,128,1280]{2,1,0:T(8,128)(2,1)S(1)} %get-tuple-element.210.refs_0_, bf16[2,128,1280]{2,1,0:T(8,128)(2,1)S(1)} %collective-permute-done.2.refs_1_, bf16[4,128,256]{2,1,0:T(8,128)(2,1)S(1)} %get-tuple-element.234.refs_2_, ...), custom_call_target="tpu_custom_call" | custom-call | flops 1 | bytes 1 | tf_op jit(solution)/shard_map/pallas_call | solution.py:129
  83.7 6.8 %collective-permute-done.19.refs_4_ = bf16[2,256,384]{2,1,0:T(8,128)(2,1)S(1)} collective-permute-done((bf16[2,256,384]{2,1,0:T(8,128)(2,1)S(1)}, bf16[2,256,384]{2,1,0:T(8,128)(2,1)S(1)}, u32[]{:S(2)}, u32[]{:S(2)}) %collective-permute-start.19) | collective-permute-done | bytes 393248 | tf_op jit(solution)/shard_map/ppermute | solution.py:278
  96.3 2.3 %shard_map.108 = (f32[256,640]{1,0:T(8,128)S(1)}, f32[256,640]{1,0:T(8,128)S(1)}, bf16[256,640]{1,0:T(8,128)(2,1)S(1)}, bf16[128,640]{1,0:T(8,128)(2,1)S(1)}, bf16[128,640]{1,0:T(8,128)(2,1)S(1)}) custom-call(s32[1]{0:T(128)} %bitcast.2.flip_ref, bf16[2,256,640]{2,1,0:T(8,128)(2,1)S(1)} %shard_map.105.refs_0_, bf16[2,256,384]{2,1,0:T(8,128)(2,1)S(1)} %shard_map.106.refs_1_, ...), custom_call_target="tpu_custom_call" | custom-call | flops 1 | bytes 1 | tf_op jit(solution)/shard_map/pallas_call | solution.py:173
  98.7 4.2 %collective-permute-done.22.refs_6_ = bf16[416,640]{1,0:T(8,128)(2,1)} collective-permute-done((bf16[416,640]{1,0:T(8,128)(2,1)}, bf16[416,640]{1,0:T(8,128)(2,1)}, u32[]{:S(2)}, u32[]{:S(2)}) %collective-permute-start.22) | collective-permute-done | bytes 532512 | tf_op jit(solution)/shard_map/ppermute | solution.py:281
  105.8 3.4 %shard_map.110 = (f32[256,640]{1,0:T(8,128)S(1)}, f32[256,640]{1,0:T(8,128)S(1)}, bf16[256,640]{1,0:T(8,128)(2,1)S(1)}, bf16[128,640]{1,0:T(8,128)(2,1)S(1)}, bf16[128,640]{1,0:T(8,128)(2,1)S(1)}) custom-call(s32[1]{0:T(128)} %bitcast.2.flip_ref, bf16[2,256,640]{2,1,0:T(8,128)(2,1)S(1)} %shard_map.105.refs_0_, bf16[2,256,384]{2,1,0:T(8,128)(2,1)S(1)} %shard_map.106.refs_1_, ...), custom_call_target="tpu_custom_call" | custom-call | flops 1 | bytes 1 | tf_op jit(solution)/shard_map/pallas_call | solution.py:173
  111.7 2.8 %collective-permute-done.30.other_ref = bf16[256,640]{1,0:T(8,128)(2,1)S(1)} collective-permute-done((bf16[256,640]{1,0:T(8,128)(2,1)S(1)}, bf16[256,640]{1,0:T(8,128)(2,1)S(1)}, u32[]{:S(2)}, u32[]{:S(2)}) %collective-permute-start.30) | collective-permute-done | bytes 327712 | tf_op jit(solution)/shard_map/ppermute | solution.py:278
  115.3 3.9 %shard_map.112 = (f32[256,640]{1,0:T(8,128)S(1)}, f32[256,640]{1,0:T(8,128)S(1)}, bf16[256,640]{1,0:T(8,128)(2,1)}, bf16[128,640]{1,0:T(8,128)(2,1)S(1)}, bf16[128,640]{1,0:T(8,128)(2,1)S(1)}) custom-call(s32[1]{0:T(128)} %bitcast.2.flip_ref, bf16[2,256,640]{2,1,0:T(8,128)(2,1)S(1)} %shard_map.105.refs_0_, bf16[2,256,384]{2,1,0:T(8,128)(2,1)S(1)} %shard_map.106.refs_1_, ...), custom_call_target="tpu_custom_call" | custom-call | flops 1 | bytes 1 | tf_op jit(solution)/shard_map/pallas_call | solution.py:173
  121.2 1.8 %collective-permute-start.36 = (bf16[256,640]{1,0:T(8,128)(2,1)S(1)}, bf16[256,640]{1,0:T(8,128)(2,1)S(1)}, u32[]{:S(2)}, u32[]{:S(2)}) collective-permute-start(bf16[256,640]{1,0:T(8,128)(2,1)S(1)} %shard_map.113), channel_id=1, source_target_pairs={{0,4},{4,0},{8,12},{12,8},{16,20},{20,16},{24,28},{28,24},{1,5},{5... | collective-permute-start | bytes 983048 | tf_op jit(solution)/shard_map/ppermute | solution.py:278
  124.1 4.0 %shard_map.116 = (f32[256,640]{1,0:T(8,128)S(1)}, f32[256,640]{1,0:T(8,128)S(1)}, bf16[256,640]{1,0:T(8,128)(2,1)}, bf16[128,640]{1,0:T(8,128)(2,1)S(1)}, bf16[128,640]{1,0:T(8,128)(2,1)S(1)}) custom-call(s32[1]{0:T(128)} %bitcast.2.flip_ref, bf16[2,256,640]{2,1,0:T(8,128)(2,1)S(1)} %shard_map.105.refs_0_, bf16[2,256,384]{2,1,0:T(8,128)(2,1)S(1)} %shard_map.106.refs_1_, ...), custom_call_target="tpu_custom_call" | custom-call | flops 1 | bytes 1 | tf_op jit(solution)/shard_map/pallas_call | solution.py:173
  131.9 1.7 %collective-permute-start.37 = (bf16[256,640]{1,0:T(8,128)(2,1)S(1)}, bf16[256,640]{1,0:T(8,128)(2,1)S(1)}, u32[]{:S(2)}, u32[]{:S(2)}) collective-permute-start(bf16[256,640]{1,0:T(8,128)(2,1)S(1)} %shard_map.117), channel_id=1, source_target_pairs={{0,4},{4,0},{8,12},{12,8},{16,20},{20,16},{24,28},{28,24},{1,5},{5... | collective-permute-start | bytes 983048 | tf_op jit(solution)/shard_map/ppermute | solution.py:278
  134.6 1.4 %shard_map.120 = (bf16[128,5120]{1,0:T(8,128)(2,1)}, bf16[128,5120]{1,0:T(8,128)(2,1)}) custom-call(s32[2]{0:T(128)S(1)} %add_add_fusion.3.where_ref, bf16[256,640]{1,0:T(8,128)(2,1)S(1)} %shard_map.114.mine_ref, bf16[256,640]{1,0:T(8,128)(2,1)S(1)} %copy-done.22), custom_call_target="tpu_custom_call" | custom-call | flops 1 | bytes 1 | tf_op jit(solution)/shard_map/pallas_call | solution.py:231
  136.1 1.4 %shard_map.121 = (bf16[128,5120]{1,0:T(8,128)(2,1)}, bf16[128,5120]{1,0:T(8,128)(2,1)}) custom-call(s32[2]{0:T(128)S(1)} %add_add_fusion.2.where_ref, bf16[256,640]{1,0:T(8,128)(2,1)S(1)} %shard_map.115.mine_ref, bf16[256,640]{1,0:T(8,128)(2,1)S(1)} %copy-done.24, ...), custom_call_target="tpu_custom_call", output_to_operand_aliasing={{0}: (3, {}), {1}: (4, {})} | custom-call | flops 1 | bytes 1 | tf_op jit(solution)/shard_map/pallas_call | solution.py:231
  137.7 1.4 %shard_map.122 = (bf16[128,5120]{1,0:T(8,128)(2,1)}, bf16[128,5120]{1,0:T(8,128)(2,1)}) custom-call(s32[2]{0:T(128)S(1)} %add_add_fusion.1.where_ref, bf16[256,640]{1,0:T(8,128)(2,1)S(1)} %shard_map.118.mine_ref, bf16[256,640]{1,0:T(8,128)(2,1)S(1)} %copy-done.26, ...), custom_call_target="tpu_custom_call", output_to_operand_aliasing={{0}: (3, {}), {1}: (4, {})} | custom-call | flops 1 | bytes 1 | tf_op jit(solution)/shard_map/pallas_call | solution.py:231
  139.1 2.9 %collective-permute-done.37.other_ref = bf16[256,640]{1,0:T(8,128)(2,1)S(1)} collective-permute-done((bf16[256,640]{1,0:T(8,128)(2,1)S(1)}, bf16[256,640]{1,0:T(8,128)(2,1)S(1)}, u32[]{:S(2)}, u32[]{:S(2)}) %collective-permute-start.37) | collective-permute-done | bytes 327712 | tf_op jit(solution)/shard_map/ppermute | solution.py:278
  142.1 1.4 %shard_map.123 = (bf16[128,5120]{1,0:T(8,128)(2,1)}, bf16[128,5120]{1,0:T(8,128)(2,1)}) custom-call(s32[2]{0:T(128)S(1)} %add_add_fusion.where_ref, bf16[256,640]{1,0:T(8,128)(2,1)S(1)} %shard_map.119.mine_ref, bf16[256,640]{1,0:T(8,128)(2,1)S(1)} %collective-permute-done.37.other_ref, ...), custom_call_target="tpu_custom_call", output_to_operand_aliasing={{0}: (3, {}), {1}: (4, {})} | custom-call | flops 1 | bytes 1 | tf_op jit(solution)/shard_map/pallas_call | solution.py:231
  (146 shorter events, 32.1 us)
Async XLA Ops:
  2.7 15.2 %collective-permute-start.1 = (bf16[416,640]{1,0:T(8,128)(2,1)}, bf16[416,640]{1,0:T(8,128)(2,1)S(1)}, u32[]{:S(2)}, u32[]{:S(2)}) collective-permute-start(bf16[416,640]{1,0:T(8,128)(2,1)} %slice.7), channel_id=1, source_target_pairs={{0,2},{1,3},{2,0},{3,1},{4,6},{5,7},{6,4},{7,5},{8,10},{9,11},{10,... | collective-permute-start | bytes 1597448 | tf_op jit(solution)/shard_map/ppermute | solution.py:272
  6.6 11.3 %collective-permute-start = (bf16[224,640]{1,0:T(8,128)(2,1)S(1)}, bf16[224,640]{1,0:T(8,128)(2,1)}, u32[]{:S(2)}, u32[]{:S(2)}) collective-permute-start(bf16[224,640]{1,0:T(8,128)(2,1)S(1)} %slice.6), channel_id=1, source_target_pairs={{0,8},{4,12},{8,16},{12,20},{16,24},{20,28},{24,0},{28,4},{1,9},{5... | collective-permute-start | bytes 860168 | tf_op jit(solution)/shard_map/ppermute | solution.py:281
  17.9 2.9 %collective-permute-start.5 = (bf16[4,128,640]{2,1,0:T(8,128)(2,1)S(1)}, bf16[4,128,640]{2,1,0:T(8,128)(2,1)S(1)}, u32[]{:S(2)}, u32[]{:S(2)}) collective-permute-start(bf16[4,128,640]{2,1,0:T(8,128)(2,1)S(1)} %get-tuple-element.228), channel_id=1, source_target_pairs={{0,1},{1,0},{2,3},{3,2},{4,5},{5,4},{6,7},{7,6},{8,9},{9,8},{10,11... | collective-permute-start | bytes 1966088 | tf_op jit(solution)/shard_map/ppermute | solution.py:275
  17.9 13.5 %collective-permute-start.2 = (bf16[2,128,1280]{2,1,0:T(8,128)(2,1)S(1)}, bf16[2,128,1280]{2,1,0:T(8,128)(2,1)S(1)}, u32[]{:S(2)}, u32[]{:S(2)}) collective-permute-start(bf16[2,128,1280]{2,1,0:T(8,128)(2,1)S(1)} %get-tuple-element.219), channel_id=1, source_target_pairs={{0,1},{1,0},{2,3},{3,2},{4,5},{5,4},{6,7},{7,6},{8,9},{9,8},{10,11... | collective-permute-start | bytes 1966088 | tf_op jit(solution)/shard_map/ppermute | solution.py:275
  18.4 11.6 %collective-permute-start.4 = (bf16[4,128,384]{2,1,0:T(8,128)(2,1)S(1)}, bf16[4,128,384]{2,1,0:T(8,128)(2,1)S(1)}, u32[]{:S(2)}, u32[]{:S(2)}) collective-permute-start(bf16[4,128,384]{2,1,0:T(8,128)(2,1)S(1)} %get-tuple-element.227), channel_id=1, source_target_pairs={{0,1},{1,0},{2,3},{3,2},{4,5},{5,4},{6,7},{7,6},{8,9},{9,8},{10,11... | collective-permute-start | bytes 1179656 | tf_op jit(solution)/shard_map/ppermute | solution.py:275
  18.5 3.8 %collective-permute-start.3 = (bf16[4,128,256]{2,1,0:T(8,128)(2,1)S(1)}, bf16[4,128,256]{2,1,0:T(8,128)(2,1)S(1)}, u32[]{:S(2)}, u32[]{:S(2)}) collective-permute-start(bf16[4,128,256]{2,1,0:T(8,128)(2,1)S(1)} %get-tuple-element.226), channel_id=1, source_target_pairs={{0,1},{1,0},{2,3},{3,2},{4,5},{5,4},{6,7},{7,6},{8,9},{9,8},{10,11... | collective-permute-start | bytes 786440 | tf_op jit(solution)/shard_map/ppermute | solution.py:275
  18.9 11.1 %collective-permute-start.9 = (bf16[224,640]{1,0:T(8,128)(2,1)}, bf16[224,640]{1,0:T(8,128)(2,1)S(1)}, u32[]{:S(2)}, u32[]{:S(2)}) collective-permute-start(bf16[224,640]{1,0:T(8,128)(2,1)} %collective-permute-done.refs_7_), channel_id=1, source_target_pairs={{0,8},{4,12},{8,16},{12,20},{16,24},{20,28},{24,0},{28,4},{1,9},{5... | collective-permute-start | bytes 860168 | tf_op jit(solution)/shard_map/ppermute | solution.py:281
  20.8 26.3 %collective-permute-start.7 = (bf16[4,128,640]{2,1,0:T(8,128)(2,1)S(1)}, bf16[4,128,640]{2,1,0:T(8,128)(2,1)S(1)}, u32[]{:S(2)}, u32[]{:S(2)}) collective-permute-start(bf16[4,128,640]{2,1,0:T(8,128)(2,1)S(1)} %get-tuple-element.236.refs_2_), channel_id=1, source_target_pairs={{0,2},{1,3},{2,0},{3,1},{4,6},{5,7},{6,4},{7,5},{8,10},{9,11},{10,... | collective-permute-start | bytes 1966088 | tf_op jit(solution)/shard_map/ppermute | solution.py:272
  22.3 36.3 %collective-permute-start.10 = (bf16[4,128,640]{2,1,0:T(8,128)(2,1)S(1)}, bf16[4,128,640]{2,1,0:T(8,128)(2,1)S(1)}, u32[]{:S(2)}, u32[]{:S(2)}) collective-permute-start(bf16[4,128,640]{2,1,0:T(8,128)(2,1)S(1)} %collective-permute-done.5.refs_3_), channel_id=1, source_target_pairs={{0,2},{1,3},{2,0},{3,1},{4,6},{5,7},{6,4},{7,5},{8,10},{9,11},{10,... | collective-permute-start | bytes 1966088 | tf_op jit(solution)/shard_map/ppermute | solution.py:272
  30.1 17.0 %collective-permute-start.8 = (bf16[416,640]{1,0:T(8,128)(2,1)}, bf16[416,640]{1,0:T(8,128)(2,1)S(1)}, u32[]{:S(2)}, u32[]{:S(2)}) collective-permute-start(bf16[416,640]{1,0:T(8,128)(2,1)} %slice.7), channel_id=1, source_target_pairs={{0,8},{4,12},{8,16},{12,20},{16,24},{20,28},{24,0},{28,4},{1,9},{5... | collective-permute-start | bytes 1597448 | tf_op jit(solution)/shard_map/ppermute | solution.py:281
  30.1 28.4 %collective-permute-start.11 = (bf16[416,640]{1,0:T(8,128)(2,1)S(1)}, bf16[416,640]{1,0:T(8,128)(2,1)S(1)}, u32[]{:S(2)}, u32[]{:S(2)}) collective-permute-start(bf16[416,640]{1,0:T(8,128)(2,1)S(1)} %collective-permute-done.1.refs_7_), channel_id=1, source_target_pairs={{0,8},{4,12},{8,16},{12,20},{16,24},{20,28},{24,0},{28,4},{1,9},{5... | collective-permute-start | bytes 1597448 | tf_op jit(solution)/shard_map/ppermute | solution.py:281
  31.5 44.0 %collective-permute-start.13 = (bf16[8,128,384]{2,1,0:T(8,128)(2,1)S(1)}, bf16[8,128,384]{2,1,0:T(8,128)(2,1)S(1)}, u32[]{:S(2)}, u32[]{:S(2)}) collective-permute-start(bf16[8,128,384]{2,1,0:T(8,128)(2,1)S(1)} %pad_maximum_fusion), channel_id=1, source_target_pairs={{0,2},{1,3},{2,0},{3,1},{4,6},{5,7},{6,4},{7,5},{8,10},{9,11},{10,... | collective-permute-start | bytes 2359304 | tf_op jit(solution)/shard_map/ppermute | solution.py:272
  47.1 28.4 %collective-permute-start.14 = (bf16[416,640]{1,0:T(8,128)(2,1)S(1)}, bf16[416,640]{1,0:T(8,128)(2,1)}, u32[]{:S(2)}, u32[]{:S(2)}) collective-permute-start(bf16[416,640]{1,0:T(8,128)(2,1)S(1)} %collective-permute-done.8.refs_6_), channel_id=1, source_target_pairs={{0,8},{4,12},{8,16},{12,20},{16,24},{20,28},{24,0},{28,4},{1,9},{5... | collective-permute-start | bytes 1597448 | tf_op jit(solution)/shard_map/ppermute | solution.py:281
  63.2 16.5 %collective-permute-start.12 = (bf16[2,256,640]{2,1,0:T(8,128)(2,1)S(1)}, bf16[2,256,640]{2,1,0:T(8,128)(2,1)S(1)}, u32[]{:S(2)}, u32[]{:S(2)}) collective-permute-start(bf16[2,256,640]{2,1,0:T(8,128)(2,1)S(1)} %shard_map.105.refs_0_), channel_id=1, source_target_pairs={{0,4},{4,0},{8,12},{12,8},{16,20},{20,16},{24,28},{28,24},{1,5},{5... | collective-permute-start | bytes 1966088 | tf_op jit(solution)/shard_map/ppermute | solution.py:278
  64.8 9.8 %collective-permute-start.15 = (bf16[224,640]{1,0:T(8,128)(2,1)S(1)}, bf16[224,640]{1,0:T(8,128)(2,1)S(1)}, u32[]{:S(2)}, u32[]{:S(2)}) collective-permute-start(bf16[224,640]{1,0:T(8,128)(2,1)S(1)} %collective-permute-done.9.refs_7_), channel_id=1, source_target_pairs={{0,8},{4,12},{8,16},{12,20},{16,24},{20,28},{24,0},{28,4},{1,9},{5... | collective-permute-start | bytes 860168 | tf_op jit(solution)/shard_map/ppermute | solution.py:281
  64.9 16.4 %collective-permute-start.6 = (bf16[8,128,256]{2,1,0:T(8,128)(2,1)S(1)}, bf16[8,128,256]{2,1,0:T(8,128)(2,1)S(1)}, u32[]{:S(2)}, u32[]{:S(2)}) collective-permute-start(bf16[8,128,256]{2,1,0:T(8,128)(2,1)S(1)} %pad_maximum_fusion.2), channel_id=1, source_target_pairs={{0,2},{1,3},{2,0},{3,1},{4,6},{5,7},{6,4},{7,5},{8,10},{9,11},{10,... | collective-permute-start | bytes 1572872 | tf_op jit(solution)/shard_map/ppermute | solution.py:272
  74.6 16.9 %collective-permute-start.18 = (bf16[416,640]{1,0:T(8,128)(2,1)S(1)}, bf16[416,640]{1,0:T(8,128)(2,1)}, u32[]{:S(2)}, u32[]{:S(2)}) collective-permute-start(bf16[416,640]{1,0:T(8,128)(2,1)S(1)} %collective-permute-done.11.refs_8_), channel_id=1, source_target_pairs={{0,8},{4,12},{8,16},{12,20},{16,24},{20,28},{24,0},{28,4},{1,9},{5... | collective-permute-start | bytes 1597448 | tf_op jit(solution)/shard_map/ppermute | solution.py:281
  75.5 27.4 %collective-permute-start.22 = (bf16[416,640]{1,0:T(8,128)(2,1)}, bf16[416,640]{1,0:T(8,128)(2,1)}, u32[]{:S(2)}, u32[]{:S(2)}) collective-permute-start(bf16[416,640]{1,0:T(8,128)(2,1)} %collective-permute-done.14.refs_6_), channel_id=1, source_target_pairs={{0,8},{4,12},{8,16},{12,20},{16,24},{20,28},{24,0},{28,4},{1,9},{5... | collective-permute-start | bytes 1597448 | tf_op jit(solution)/shard_map/ppermute | solution.py:281
  78.4 12.1 %collective-permute-start.19 = (bf16[2,256,384]{2,1,0:T(8,128)(2,1)S(1)}, bf16[2,256,384]{2,1,0:T(8,128)(2,1)S(1)}, u32[]{:S(2)}, u32[]{:S(2)}) collective-permute-start(bf16[2,256,384]{2,1,0:T(8,128)(2,1)S(1)} %shard_map.106.refs_1_), channel_id=1, source_target_pairs={{0,4},{4,0},{8,12},{12,8},{16,20},{20,16},{24,28},{28,24},{1,5},{5... | collective-permute-start | bytes 1179656 | tf_op jit(solution)/shard_map/ppermute | solution.py:278
  79.7 13.8 %collective-permute-start.17 = (bf16[224,640]{1,0:T(8,128)(2,1)S(1)}, bf16[224,640]{1,0:T(8,128)(2,1)S(1)}, u32[]{:S(2)}, u32[]{:S(2)}) collective-permute-start(bf16[224,640]{1,0:T(8,128)(2,1)S(1)} %copy-done.30), channel_id=1, source_target_pairs={{0,2},{1,3},{2,0},{3,1},{4,6},{5,7},{6,4},{7,5},{8,10},{9,11},{10,... | collective-permute-start | bytes 860168 | tf_op jit(solution)/shard_map/ppermute | solution.py:272
  83.1 11.2 %collective-permute-start.16 = (bf16[2,256,256]{2,1,0:T(8,128)(2,1)S(1)}, bf16[2,256,256]{2,1,0:T(8,128)(2,1)S(1)}, u32[]{:S(2)}, u32[]{:S(2)}) collective-permute-start(bf16[2,256,256]{2,1,0:T(8,128)(2,1)S(1)} %shard_map.107.refs_2_), channel_id=1, source_target_pairs={{0,4},{4,0},{8,12},{12,8},{16,20},{20,16},{24,28},{28,24},{1,5},{5... | collective-permute-start | bytes 786440 | tf_op jit(solution)/shard_map/ppermute | solution.py:278
  91.5 11.4 %collective-permute-start.21 = (bf16[224,640]{1,0:T(8,128)(2,1)}, bf16[224,640]{1,0:T(8,128)(2,1)}, u32[]{:S(2)}, u32[]{:S(2)}) collective-permute-start(bf16[224,640]{1,0:T(8,128)(2,1)} %collective-permute-done.refs_7_), channel_id=1, source_target_pairs={{0,2},{1,3},{2,0},{3,1},{4,6},{5,7},{6,4},{7,5},{8,10},{9,11},{10,... | collective-permute-start | bytes 860168 | tf_op jit(solution)/shard_map/ppermute | solution.py:272
  92.8 22.5 %collective-permute-start.29 = (bf16[448,640]{1,0:T(8,128)(2,1)}, bf16[448,640]{1,0:T(8,128)(2,1)}, u32[]{:S(2)}, u32[]{:S(2)}) collective-permute-start(bf16[448,640]{1,0:T(8,128)(2,1)} %pad_maximum_fusion.1), channel_id=1, source_target_pairs={{0,2},{1,3},{2,0},{3,1},{4,6},{5,7},{6,4},{7,5},{8,10},{9,11},{10,... | collective-permute-start | bytes 1720328 | tf_op jit(solution)/shard_map/ppermute | solution.py:272
  94.3 25.0 %collective-permute-start.31 = (bf16[416,640]{1,0:T(8,128)(2,1)}, bf16[416,640]{1,0:T(8,128)(2,1)}, u32[]{:S(2)}, u32[]{:S(2)}) collective-permute-start(bf16[416,640]{1,0:T(8,128)(2,1)} %collective-permute-done.18.refs_8_), channel_id=1, source_target_pairs={{0,8},{4,12},{8,16},{12,20},{16,24},{20,28},{24,0},{28,4},{1,9},{5... | collective-permute-start | bytes 1597448 | tf_op jit(solution)/shard_map/ppermute | solution.py:281
  98.7 4.3 %collective-permute-start.20 = (bf16[128,640]{1,0:T(8,128)(2,1)S(1)}, bf16[128,640]{1,0:T(8,128)(2,1)S(1)}, u32[]{:S(2)}, u32[]{:S(2)}) collective-permute-start(bf16[128,640]{1,0:T(8,128)(2,1)S(1)} %get-tuple-element.280), channel_id=1, source_target_pairs={{0,1},{1,0},{2,3},{3,2},{4,5},{5,4},{6,7},{7,6},{8,9},{9,8},{10,11... | collective-permute-start | bytes 491528 | tf_op jit(solution)/shard_map/ppermute | solution.py:275
  104.4 10.2 %collective-permute-start.30 = (bf16[256,640]{1,0:T(8,128)(2,1)S(1)}, bf16[256,640]{1,0:T(8,128)(2,1)S(1)}, u32[]{:S(2)}, u32[]{:S(2)}) collective-permute-start(bf16[256,640]{1,0:T(8,128)(2,1)S(1)} %shard_map.109), channel_id=1, source_target_pairs={{0,4},{4,0},{8,12},{12,8},{16,20},{20,16},{24,28},{28,24},{1,5},{5... | collective-permute-start | bytes 983048 | tf_op jit(solution)/shard_map/ppermute | solution.py:278
  110.9 12.1 %collective-permute-start.28 = (bf16[256,640]{1,0:T(8,128)(2,1)S(1)}, bf16[256,640]{1,0:T(8,128)(2,1)S(1)}, u32[]{:S(2)}, u32[]{:S(2)}) collective-permute-start(bf16[256,640]{1,0:T(8,128)(2,1)S(1)} %shard_map.111), channel_id=1, source_target_pairs={{0,4},{4,0},{8,12},{12,8},{16,20},{20,16},{24,28},{28,24},{1,5},{5... | collective-permute-start | bytes 983048 | tf_op jit(solution)/shard_map/ppermute | solution.py:278
  111.7 11.3 %collective-permute-start.27 = (bf16[256,640]{1,0:T(8,128)(2,1)S(1)}, bf16[256,640]{1,0:T(8,128)(2,1)S(1)}, u32[]{:S(2)}, u32[]{:S(2)}) collective-permute-start(bf16[256,640]{1,0:T(8,128)(2,1)S(1)} %get-tuple-element.317), channel_id=1, source_target_pairs={{0,1},{1,0},{2,3},{3,2},{4,5},{5,4},{6,7},{7,6},{8,9},{9,8},{10,11... | collective-permute-start | bytes 983048 | tf_op jit(solution)/shard_map/ppermute | solution.py:275
  115.3 7.8 %collective-permute-start.26 = (bf16[256,640]{1,0:T(8,128)(2,1)S(1)}, bf16[256,640]{1,0:T(8,128)(2,1)S(1)}, u32[]{:S(2)}, u32[]{:S(2)}) collective-permute-start(bf16[256,640]{1,0:T(8,128)(2,1)S(1)} %get-tuple-element.314), channel_id=1, source_target_pairs={{0,1},{1,0},{2,3},{3,2},{4,5},{5,4},{6,7},{7,6},{8,9},{9,8},{10,11... | collective-permute-start | bytes 983048 | tf_op jit(solution)/shard_map/ppermute | solution.py:275
  121.2 9.9 %collective-permute-start.36 = (bf16[256,640]{1,0:T(8,128)(2,1)S(1)}, bf16[256,640]{1,0:T(8,128)(2,1)S(1)}, u32[]{:S(2)}, u32[]{:S(2)}) collective-permute-start(bf16[256,640]{1,0:T(8,128)(2,1)S(1)} %shard_map.113), channel_id=1, source_target_pairs={{0,4},{4,0},{8,12},{12,8},{16,20},{20,16},{24,28},{28,24},{1,5},{5... | collective-permute-start | bytes 983048 | tf_op jit(solution)/shard_map/ppermute | solution.py:278
  129.4 4.2 %collective-permute-start.39 = (bf16[256,640]{1,0:T(8,128)(2,1)}, bf16[256,640]{1,0:T(8,128)(2,1)S(1)}, u32[]{:S(2)}, u32[]{:S(2)}) collective-permute-start(bf16[256,640]{1,0:T(8,128)(2,1)} %get-tuple-element.375), channel_id=1, source_target_pairs={{0,1},{1,0},{2,3},{3,2},{4,5},{5,4},{6,7},{7,6},{8,9},{9,8},{10,11... | collective-permute-start | bytes 983048 | tf_op jit(solution)/shard_map/ppermute | solution.py:275
  131.9 10.1 %collective-permute-start.37 = (bf16[256,640]{1,0:T(8,128)(2,1)S(1)}, bf16[256,640]{1,0:T(8,128)(2,1)S(1)}, u32[]{:S(2)}, u32[]{:S(2)}) collective-permute-start(bf16[256,640]{1,0:T(8,128)(2,1)S(1)} %shard_map.117), channel_id=1, source_target_pairs={{0,4},{4,0},{8,12},{12,8},{16,20},{20,16},{24,28},{28,24},{1,5},{5... | collective-permute-start | bytes 983048 | tf_op jit(solution)/shard_map/ppermute | solution.py:278
  (41 other events, 245.1 us)
